TPU v7x, 32 devices: a whole 2x2x4 slice. The times are simulated.
32 devices in a mesh: fsdp: 8 (over z, y), seq: 4 (over x, core).
Axes of the slice: x: 2, y: 2, z: 4, core: 2. Of those that a mesh axis runs over, the one named last changes fastest.
Arguments:
- tokens: bfloat16 [16, 2048, 768], P('fsdp', 'seq'), may hold values from -6 to 6
- counts: int32 [16, 4], P('fsdp'), may hold values from 256 to 512, as said below
- norm1_gain: bfloat16 [768], P('fsdp'), may hold values from 0.5 to 1.5
- norm1_bias: bfloat16 [768], P('fsdp'), may hold values from -4 to 4
- qkv_weight: bfloat16 [768, 2304], P('fsdp'), may hold values from -0.21875 to 0.21875
- query_bias: bfloat16 [768], P('fsdp'), may hold values from -4 to 4
- value_bias: bfloat16 [768], P('fsdp'), may hold values from -4 to 4
- proj_weight: bfloat16 [768, 768], P('fsdp'), may hold values from -0.875 to 0.875
- proj_bias: bfloat16 [768], P('fsdp'), may hold values from -4 to 4
- norm2_gain: bfloat16 [768], P('fsdp'), may hold values from 0.5 to 1.5
- norm2_bias: bfloat16 [768], P('fsdp'), may hold values from -4 to 4
- fc1_weight: bfloat16 [768, 3072], P('fsdp'), may hold values from -0.21875 to 0.21875
- fc1_bias: bfloat16 [3072], P('fsdp'), may hold values from -4 to 4
- fc2_weight: bfloat16 [3072, 768], P('fsdp'), may hold values from -0.109375 to 0.109375
- fc2_bias: bfloat16 [768], P('fsdp'), may hold values from -4 to 4
- cotangent: bfloat16 [16, 2048, 768], P('fsdp', 'seq'), may hold values from -6 to 6
Outputs:
- output: bfloat16 [16, 2048, 768], P('fsdp', 'seq')
- input_grad: float32 [16, 2048, 768], P('fsdp', 'seq')
- grad_norm1_gain: float32 [768], P('fsdp')
- grad_norm1_bias: float32 [768], P('fsdp')
- grad_qkv_weight: float32 [768, 2304], P('fsdp')
- grad_query_bias: float32 [768], P('fsdp')
- grad_value_bias: float32 [768], P('fsdp')
- grad_proj_weight: float32 [768, 768], P('fsdp')
- grad_proj_bias: float32 [768], P('fsdp')
- grad_norm2_gain: float32 [768], P('fsdp')
- grad_norm2_bias: float32 [768], P('fsdp')
- grad_fc1_weight: float32 [768, 3072], P('fsdp')
- grad_fc1_bias: float32 [3072], P('fsdp')
- grad_fc2_weight: float32 [3072, 768], P('fsdp')
- grad_fc2_bias: float32 [768], P('fsdp')
Inputs may be any that keep to these rules, and one draw needn't show every extreme that they name: `counts`: in every image the first device along seq keeps all 512 of its slots; every other keeps at least half of them and fewer than all.
All inputs are finite; a program needn't handle non-finite values.
Results may differ from a plain program's by a relative error of at most 0.018.
Values may be sent and summed in bfloat16 or wider, within the bound.
No kernel may reach another device: no remote copies, remote signals or barrier semaphores. Data moves between devices by JAX's collectives and lax.ppermute only.
A program may use at most 320 MiB of HBM per device.

v0:
```python
import jax
import jax.numpy as jnp
from jax import lax
from jax.sharding import PartitionSpec as P

HEADS = 12
HEAD_DIM = 64


EPSILON = 1e-06
MASKED = -1e30


def layer_norm(values, gain, offset):
    center_mean = jnp.mean(values, axis=-1, keepdims=True)
    centred = values - center_mean
    variance = jnp.mean(centred * centred, axis=-1, keepdims=True)
    return centred * lax.rsqrt(variance + EPSILON) * gain + offset


def gelu_exact(values):
    return jax.nn.gelu(values, approximate=False)


def inner_rows(left, right):
    return lax.dot_general(
        left, right, (((0,), (0,)), ((), ())), preferred_element_type=jnp.float32
    )


def inner_cols(left, right):
    return lax.dot_general(
        left, right, (((1,), (1,)), ((), ())), preferred_element_type=jnp.float32
    )


def column_sums(values):
    return jnp.sum(values.astype(jnp.float32), axis=0)


def per_device(
    tokens,
    counts,
    norm1_gain,
    norm1_bias,
    qkv_weight,
    query_bias,
    value_bias,
    proj_weight,
    proj_bias,
    norm2_gain,
    norm2_bias,
    fc1_weight,
    fc1_bias,
    fc2_weight,
    fc2_bias,
    cotangent,
):
    images, slots, width = tokens.shape
    groups = lax.axis_size("seq")
    heads_here = HEADS // groups
    scale_factor = HEAD_DIM ** (-0.5)
    rows = images * slots
    gain_one, bias_one, w_qkv, bias_query, bias_value, w_proj, bias_proj = (
        lax.all_gather(norm1_gain, "fsdp", axis=0, tiled=True),
        lax.all_gather(norm1_bias, "fsdp", axis=0, tiled=True),
        lax.all_gather(qkv_weight, "fsdp", axis=0, tiled=True),
        lax.all_gather(query_bias, "fsdp", axis=0, tiled=True),
        lax.all_gather(value_bias, "fsdp", axis=0, tiled=True),
        lax.all_gather(proj_weight, "fsdp", axis=0, tiled=True),
        lax.all_gather(proj_bias, "fsdp", axis=0, tiled=True),
    )
    gain_two, bias_two, w_fc1, bias_fc1, w_fc2, bias_fc2 = (
        lax.all_gather(norm2_gain, "fsdp", axis=0, tiled=True),
        lax.all_gather(norm2_bias, "fsdp", axis=0, tiled=True),
        lax.all_gather(fc1_weight, "fsdp", axis=0, tiled=True),
        lax.all_gather(fc1_bias, "fsdp", axis=0, tiled=True),
        lax.all_gather(fc2_weight, "fsdp", axis=0, tiled=True),
        lax.all_gather(fc2_bias, "fsdp", axis=0, tiled=True),
    )
    places = jnp.arange(slots, dtype=jnp.int32)
    valid = (counts[:, :, None] > places[None, None, :]).reshape(images, groups * slots)

    def split_heads(packed):
        length = packed.shape[0]
        query_part = packed[:, 0].reshape(length, heads_here, HEAD_DIM)
        key_part = packed[:, 1].reshape(length, heads_here, HEAD_DIM)
        value_part = packed[:, 2].reshape(length, heads_here, HEAD_DIM)
        return (query_part, key_part, value_part)

    def score_block(query_part, key_part, keep):
        scores = (
            jnp.einsum("qhe,khe->hqk", query_part, key_part, preferred_element_type=jnp.float32)
            * scale_factor
        )
        return jnp.where(keep[None, None, :], scores, MASKED)

    def attend_forward(element):
        packed, keep = element
        query_part, key_part, value_part = split_heads(packed)
        scores = score_block(query_part, key_part, keep)
        highest = jnp.max(scores, axis=-1, keepdims=True)
        raised = jnp.exp(scores - highest)
        totals = jnp.sum(raised, axis=-1, keepdims=True)
        probs_low = (raised / totals).astype(jnp.bfloat16)
        result = jnp.einsum(
            "hqk,khe->qhe", probs_low, value_part, preferred_element_type=jnp.float32
        )
        return (
            result.astype(jnp.bfloat16).reshape(packed.shape[0], -1),
            (highest + jnp.log(totals))[..., 0],
        )

    def attend_backward(element):
        packed, keep, log_total, grad_result = element
        length = packed.shape[0]
        query_part, key_part, value_part = split_heads(packed)
        probs = jnp.exp(score_block(query_part, key_part, keep) - log_total[..., None])
        grad_heads = grad_result.reshape(length, heads_here, HEAD_DIM)
        grad_value = jnp.einsum(
            "hqk,qhe->khe",
            probs.astype(jnp.bfloat16),
            grad_heads,
            preferred_element_type=jnp.float32,
        )
        grad_probs = jnp.einsum(
            "qhe,khe->hqk", grad_heads, value_part, preferred_element_type=jnp.float32
        )
        row_delta = jnp.sum(probs * grad_probs, axis=-1, keepdims=True)
        grad_scores = (probs * (grad_probs - row_delta)).astype(jnp.bfloat16)
        grad_query = (
            jnp.einsum("hqk,khe->qhe", grad_scores, key_part, preferred_element_type=jnp.float32)
            * scale_factor
        )
        grad_key = (
            jnp.einsum("hqk,qhe->khe", grad_scores, query_part, preferred_element_type=jnp.float32)
            * scale_factor
        )
        stacked = jnp.stack([grad_query, grad_key, grad_value], axis=1).astype(jnp.bfloat16)
        return stacked.reshape(length, 3, heads_here * HEAD_DIM)

    gain_one_f = gain_one.astype(jnp.float32)
    bias_one_f = bias_one.astype(jnp.float32)
    gain_two_f = gain_two.astype(jnp.float32)
    bias_two_f = bias_two.astype(jnp.float32)
    inputs = tokens.astype(jnp.float32).reshape(rows, width)
    normed_low = layer_norm(inputs, gain_one_f, bias_one_f).astype(jnp.bfloat16)
    qkv_bias = jnp.concatenate([bias_query, jnp.zeros_like(bias_query), bias_value]).astype(
        jnp.float32
    )
    packed_all = jnp.dot(normed_low, w_qkv, preferred_element_type=jnp.float32) + qkv_bias
    packed_low = packed_all.astype(jnp.bfloat16).reshape(images, slots, 3, width)
    packed_heads = lax.all_to_all(packed_low, "seq", split_axis=3, concat_axis=1, tiled=True)
    result_heads, log_totals = lax.map(attend_forward, (packed_heads, valid))
    mixed = lax.all_to_all(result_heads, "seq", split_axis=1, concat_axis=2, tiled=True).reshape(
        rows, width
    )
    middle = (
        inputs
        + jnp.dot(mixed, w_proj, preferred_element_type=jnp.float32)
        + bias_proj.astype(jnp.float32)
    )
    normed_two = layer_norm(middle, gain_two_f, bias_two_f).astype(jnp.bfloat16)
    hidden = jnp.dot(normed_two, w_fc1, preferred_element_type=jnp.float32) + bias_fc1.astype(
        jnp.float32
    )
    active = gelu_exact(hidden).astype(jnp.bfloat16)
    result = (
        middle
        + jnp.dot(active, w_fc2, preferred_element_type=jnp.float32)
        + bias_fc2.astype(jnp.float32)
    )
    output = result.astype(jnp.bfloat16).reshape(images, slots, width)
    gain_one, w_qkv, w_proj = (
        lax.all_gather(norm1_gain, "fsdp", axis=0, tiled=True),
        lax.all_gather(qkv_weight, "fsdp", axis=0, tiled=True),
        lax.all_gather(proj_weight, "fsdp", axis=0, tiled=True),
    )
    gain_two, w_fc1, w_fc2 = (
        lax.all_gather(norm2_gain, "fsdp", axis=0, tiled=True),
        lax.all_gather(fc1_weight, "fsdp", axis=0, tiled=True),
        lax.all_gather(fc2_weight, "fsdp", axis=0, tiled=True),
    )
    gain_one_f = gain_one.astype(jnp.float32)
    gain_two_f = gain_two.astype(jnp.float32)
    grad_top = cotangent.reshape(rows, width)
    grad_fc2_bias = column_sums(grad_top)
    grad_fc2_weight = inner_rows(active, grad_top)
    grad_active = inner_cols(grad_top, w_fc2)
    grad_hidden = jax.vjp(gelu_exact, hidden)[1](grad_active)[0].astype(jnp.bfloat16)
    grad_fc1_bias = column_sums(grad_hidden)
    grad_fc1_weight = inner_rows(normed_two, grad_hidden)
    grad_normed_two = inner_cols(grad_hidden, w_fc1)
    norm_pull_two = jax.vjp(layer_norm, middle, gain_two_f, bias_two_f)[1]
    grad_middle_norm, grad_norm2_gain, grad_norm2_bias = norm_pull_two(grad_normed_two)
    grad_middle = grad_top.astype(jnp.float32) + grad_middle_norm
    grad_branch = grad_middle.astype(jnp.bfloat16)
    grad_proj_bias = column_sums(grad_branch)
    grad_proj_weight = inner_rows(mixed, grad_branch)
    grad_mixed = inner_cols(grad_branch, w_proj).astype(jnp.bfloat16).reshape(images, slots, width)
    grad_mixed_heads = lax.all_to_all(grad_mixed, "seq", split_axis=2, concat_axis=1, tiled=True)
    grad_packed_heads = lax.map(
        attend_backward, (packed_heads, valid, log_totals, grad_mixed_heads)
    )
    grad_packed = lax.all_to_all(
        grad_packed_heads, "seq", split_axis=1, concat_axis=3, tiled=True
    ).reshape(rows, 3 * width)
    grad_query_bias = column_sums(grad_packed[:, :width])
    grad_value_bias = column_sums(grad_packed[:, 2 * width :])
    grad_qkv_weight = inner_rows(normed_low, grad_packed)
    grad_normed_one = inner_cols(grad_packed, w_qkv)
    norm_pull_one = jax.vjp(layer_norm, inputs, gain_one_f, bias_one_f)[1]
    grad_input_norm, grad_norm1_gain, grad_norm1_bias = norm_pull_one(grad_normed_one)
    input_grad = (grad_middle + grad_input_norm).reshape(images, slots, width)
    owned = (
        lax.psum_scatter(
            grad_norm1_gain.astype(jnp.bfloat16), "fsdp", scatter_dimension=0, tiled=True
        ).astype(jnp.float32),
        lax.psum_scatter(
            grad_norm1_bias.astype(jnp.bfloat16), "fsdp", scatter_dimension=0, tiled=True
        ).astype(jnp.float32),
        lax.psum_scatter(
            grad_qkv_weight.astype(jnp.bfloat16), "fsdp", scatter_dimension=0, tiled=True
        ).astype(jnp.float32),
        lax.psum_scatter(
            grad_query_bias.astype(jnp.bfloat16), "fsdp", scatter_dimension=0, tiled=True
        ).astype(jnp.float32),
        lax.psum_scatter(
            grad_value_bias.astype(jnp.bfloat16), "fsdp", scatter_dimension=0, tiled=True
        ).astype(jnp.float32),
        lax.psum_scatter(
            grad_proj_weight.astype(jnp.bfloat16), "fsdp", scatter_dimension=0, tiled=True
        ).astype(jnp.float32),
        lax.psum_scatter(
            grad_proj_bias.astype(jnp.bfloat16), "fsdp", scatter_dimension=0, tiled=True
        ).astype(jnp.float32),
        lax.psum_scatter(
            grad_norm2_gain.astype(jnp.bfloat16), "fsdp", scatter_dimension=0, tiled=True
        ).astype(jnp.float32),
        lax.psum_scatter(
            grad_norm2_bias.astype(jnp.bfloat16), "fsdp", scatter_dimension=0, tiled=True
        ).astype(jnp.float32),
        lax.psum_scatter(
            grad_fc1_weight.astype(jnp.bfloat16), "fsdp", scatter_dimension=0, tiled=True
        ).astype(jnp.float32),
        lax.psum_scatter(
            grad_fc1_bias.astype(jnp.bfloat16), "fsdp", scatter_dimension=0, tiled=True
        ).astype(jnp.float32),
        lax.psum_scatter(
            grad_fc2_weight.astype(jnp.bfloat16), "fsdp", scatter_dimension=0, tiled=True
        ).astype(jnp.float32),
        lax.psum_scatter(
            grad_fc2_bias.astype(jnp.bfloat16), "fsdp", scatter_dimension=0, tiled=True
        ).astype(jnp.float32),
    )
    (
        own_g1,
        own_b1,
        own_qkv,
        own_qb,
        own_vb,
        own_proj,
        own_pb,
        own_g2,
        own_b2,
        own_fc1,
        own_fb1,
        own_fc2,
        own_fb2,
    ) = owned
    summed = (
        lax.psum(own_g1.astype(jnp.bfloat16), "seq").astype(jnp.float32),
        lax.psum(own_b1.astype(jnp.bfloat16), "seq").astype(jnp.float32),
        lax.psum(own_qkv.astype(jnp.bfloat16), "seq").astype(jnp.float32),
        lax.psum(own_qb.astype(jnp.bfloat16), "seq").astype(jnp.float32),
        lax.psum(own_vb.astype(jnp.bfloat16), "seq").astype(jnp.float32),
        lax.psum(own_proj.astype(jnp.bfloat16), "seq").astype(jnp.float32),
        lax.psum(own_pb.astype(jnp.bfloat16), "seq").astype(jnp.float32),
        lax.psum(own_g2.astype(jnp.bfloat16), "seq").astype(jnp.float32),
        lax.psum(own_b2.astype(jnp.bfloat16), "seq").astype(jnp.float32),
        lax.psum(own_fc1.astype(jnp.bfloat16), "seq").astype(jnp.float32),
        lax.psum(own_fb1.astype(jnp.bfloat16), "seq").astype(jnp.float32),
        lax.psum(own_fc2.astype(jnp.bfloat16), "seq").astype(jnp.float32),
        lax.psum(own_fb2.astype(jnp.bfloat16), "seq").astype(jnp.float32),
    )
    return (
        output,
        input_grad,
        summed[0],
        summed[1],
        summed[2],
        summed[3],
        summed[4],
        summed[5],
        summed[6],
        summed[7],
        summed[8],
        summed[9],
        summed[10],
        summed[11],
        summed[12],
    )


def solution(mesh):
    placed = (
        P("fsdp", "seq", None),
        P("fsdp", None),
        P("fsdp"),
        P("fsdp"),
        P("fsdp", None),
        P("fsdp"),
        P("fsdp"),
        P("fsdp", None),
        P("fsdp"),
        P("fsdp"),
        P("fsdp"),
        P("fsdp", None),
        P("fsdp"),
        P("fsdp", None),
        P("fsdp"),
        P("fsdp", "seq", None),
    )
    return jax.shard_map(
        per_device,
        mesh=mesh,
        in_specs=placed,
        out_specs=(
            P("fsdp", "seq", None),
            P("fsdp", "seq", None),
            P("fsdp"),
            P("fsdp"),
            P("fsdp", None),
            P("fsdp"),
            P("fsdp"),
            P("fsdp", None),
            P("fsdp"),
            P("fsdp"),
            P("fsdp"),
            P("fsdp", None),
            P("fsdp"),
            P("fsdp", None),
            P("fsdp"),
        ),
        check_vma=False,
    )
```

profile of v0, /device:TPU:0, one launch (start us, length us, event | category | flops | bytes accessed | tf_op | source)
XLA Modules:
  0.0 1029.8 jit_solution(587260707456812918)
XLA Ops:
  15.8 40.2 %all-reduce.18 = (bf16[768]{0:T(1024)(128)(2,1)S(1)}, bf16[768]{0:T(1024)(128)(2,1)S(1)}, bf16[768]{0:T(1024)(128)(2,1)S(1)}, bf16[768]{0:T(1024)(128)(2,1)S(1)}...) all-reduce(bf16[768]{0:T(1024)(128)(2,1)S(1)} %dynamic-update-slice, ...), channel_id=1, replica_groups=mesh['fsdp'=8,'seq'=4] {'fsdp'}, use_global_device_ids=true, to_apply=%add.1 | all-reduce | flops 5376 | bytes 21504
  120.4 52.2 %all-to-all-done = bf16[2,512,3,768]{1,0,2,3:T(2,128)(2,1)} async-done(((bf16[2,512,3,768]{1,0,2,3:T(2,128)(2,1)}), bf16[2,512,3,768]{1,0,2,3:T(2,128)(2,1)}, u32[]{:S(2)}, u32[]{:S(2)}) %all-to-all-start) | async-done | bytes 4718624 | tf_op jit(solution)/shard_map/all_to_all | solution.py:153
  178.5 128.5 %while.22 = (s32[]{:T(128)}, bf16[2,2048,192]{1,2,0:T(8,128)(2,1)}, f32[2,3,2048]{2,1,0:T(4,128)S(1)}, bf16[2,2048,3,192]{1,3,2,0:T(8,128)(2,1)}, pred[2,2048]{1,0:T(4,128)(4,1)S(1)}, /*index=5*/s32[]{:T(128)}) while((s32[]{:T(128)}, bf16[2,2048,192]{1,2,0:T(8,128)(2,1)}, f32[2,3,2048]{2,1,0:T(4,128)S(1)}, ...), condition=%wide.region_5.6_spmd, body=%wide.region_2.5_spmd.sunk | while | flops 3372607488 | bytes 177965184 | solution.py:154
  180.7 18.3 %fusion.117 = (f32[3,2048]{1,0:T(4,128)S(1)}, f32[3,2048,2048]{1,2,0:T(8,128)}) fusion(pred[2048]{0:T(1024)(128)(4,1)S(1)} %dynamic-slice_reduce_fusion.4, bf16[2048,3,64]{0,2,1:T(8,128)(2,1)S(1)} %bitcast.202, bf16[2048,3,64]{0,2,1:T(8,128)(2,1)S(1)} %bitcast.201), kind=kOutput, calls=%fused_computation.3.clone.1 | convolution fusion | flops 1648355328 | bytes 51931136 | tf_op jit(solution)/shard_map/while/body/eval_jaxpr/qhe,khe->hqk/dot_general | solution.py:93
  198.9 22.8 %fusion.118 = f32[3,2048]{1,0:T(4,128)S(1)} fusion(f32[3,2048,2048]{1,2,0:T(8,128)} %get-tuple-element.243, f32[3,2048]{1,0:T(4,128)S(1)} %get-tuple-element.244, pred[2048]{0:T(1024)(128)(4,1)S(1)} %dynamic-slice_reduce_fusion.4), kind=kLoop, calls=%fused_computation.4.clone.1 | loop fusion | flops 50325504 | bytes 50382848 | tf_op jit(solution)/shard_map/while/body/eval_jaxpr/reduce_sum | solution.py:104
  221.7 20.1 %fusion.119 = bf16[3,64,2048]{2,1,0:T(8,128)(2,1)S(1)} fusion(bf16[2048,3,64]{0,2,1:T(8,128)(2,1)S(1)} %bitcast.203, f32[3,2048,2048]{1,2,0:T(8,128)} %get-tuple-element.243, f32[3,2048]{1,0:T(4,128)S(1)} %fusion.118, f32[3,2048]{1,0:T(4,128)S(1)} %get-tuple-element.244, pred[2048]{0:T(1024)(128)(4,1)S(1)} %dynamic-slice_reduce_fusion.4), kind=kOutput, calls=%fused_computation.6.clone.1 | convolution fusion | flops 1673920512 | bytes 51955712 | tf_op jit(solution)/shard_map/while/body/eval_jaxpr/hqk,khe->qhe/dot_general | solution.py:106
  263.3 22.5 %fusion.118 = f32[3,2048]{1,0:T(4,128)S(1)} fusion(f32[3,2048,2048]{1,2,0:T(8,128)} %get-tuple-element.243, f32[3,2048]{1,0:T(4,128)S(1)} %get-tuple-element.244, pred[2048]{0:T(1024)(128)(4,1)S(1)} %dynamic-slice_reduce_fusion.4), kind=kLoop, calls=%fused_computation.4.clone.1 | loop fusion | flops 50325504 | bytes 50382848 | tf_op jit(solution)/shard_map/while/body/eval_jaxpr/reduce_sum | solution.py:104
  285.9 19.9 %fusion.119 = bf16[3,64,2048]{2,1,0:T(8,128)(2,1)S(1)} fusion(bf16[2048,3,64]{0,2,1:T(8,128)(2,1)S(1)} %bitcast.203, f32[3,2048,2048]{1,2,0:T(8,128)} %get-tuple-element.243, f32[3,2048]{1,0:T(4,128)S(1)} %fusion.118, f32[3,2048]{1,0:T(4,128)S(1)} %get-tuple-element.244, pred[2048]{0:T(1024)(128)(4,1)S(1)} %dynamic-slice_reduce_fusion.4), kind=kOutput, calls=%fused_computation.6.clone.1 | convolution fusion | flops 1673920512 | bytes 51955712 | tf_op jit(solution)/shard_map/while/body/eval_jaxpr/hqk,khe->qhe/dot_general | solution.py:106
  318.4 26.3 %all-gather = bf16[8,1,384]{2,1,0:T(2,128)(2,1)S(1)} all-gather(bf16[1,1,384]{2,1,0:T(2,128)(2,1)S(1)} %reshape.302), channel_id=1, replica_groups=mesh['fsdp'=8,'seq'=4] {'fsdp'}, dimensions={0}, use_global_device_ids=true | all-gather | bytes 6912 | tf_op jit(solution)/shard_map/all_gather | solution.py:77
  361.6 38.1 %multiply_convert_fusion.1 = (bf16[1024,3072]{1,0:T(8,128)(2,1)}, f32[1024,3072]{1,0:T(8,128)}, f32[1024,3072]{1,0:T(8,128)}) fusion(f32[3072]{0:T(1024)S(1)} %bitcast.229, bf16[768,3072]{1,0:T(8,128)(2,1)} %all-gather.10.cloned.1.call-done, f32[1024,768]{1,0:T(8,128)} %copy-done.9, f32[768]{0:T(1024)S(1)} %convert_element_type.195, ...), kind=kOutput, calls=%fused_computation.34 | convolution fusion | flops 5043388416 | bytes 39348224 | tf_op jit(solution)/shard_map/dot_general | solution.py:164
  477.9 287.0 %while.23 = (s32[]{:T(128)}, bf16[2,2048,3,192]{1,3,2,0:T(8,128)(2,1)}, bf16[2,2048,3,192]{1,3,2,0:T(8,128)(2,1)}, pred[2,2048]{1,0:T(4,128)(4,1)S(1)}, f32[2,3,...) while((s32[]{:T(128)}, bf16[2,2048,3,192]{1,3,2,0:T(8,128)(2,1)}, ...), condition=%wide.region_12.13_spmd, body=%wide.region_10.12_spmd.sunk | while | flops 8250845184 | bytes 401263200 | solution.py:202
  480.1 19.6 %fusion.131 = f32[3,2048,2048]{1,2,0:T(8,128)} fusion(bf16[2048,3,64]{0,2,1:T(8,128)(2,1)S(1)} %bitcast.193, bf16[2048,3,64]{0,2,1:T(8,128)(2,1)S(1)} %bitcast.191), kind=kOutput, calls=%fused_computation.112.clone.1 | convolution fusion | flops 1610612736 | bytes 51904512 | tf_op jit(solution)/shard_map/while/body/eval_jaxpr/qhe,khe->hqk/dot_general | solution.py:93
  501.0 34.7 %multiply_reduce_fusion.5 = (f32[3,2048]{1,0:T(4,128)S(1)}, f32[3,2048,2048]{1,2,0:T(8,128)}) fusion(f32[3,2048,2048]{1,2,0:T(8,128)} %fusion.131, f32[3,2048]{1,0:T(4,128)S(1)} %dynamic-slice_bitcast_fusion.8, pred[2048]{0:T(1024)(128)(4,1)S(1)} %dynamic-slice_reduce_fusion.5, bf16[2048,3,64]{0,2,1:T(8,128)(2,1)S(1)} %bitcast.199, ...), kind=kOutput, calls=%fused_computation.14.clone.1 | convolution fusion | flops 1673521152 | bytes 102287360 | tf_op jit(solution)/shard_map/while/body/eval_jaxpr/qhe,khe->hqk/dot_general | solution.py:126
  535.6 41.3 %multiply_convert_fusion.3 = bf16[3,2048,2048]{1,2,0:T(8,128)(2,1)} fusion(f32[3,2048,2048]{1,2,0:T(8,128)} %get-tuple-element.254, f32[3,2048,2048]{1,2,0:T(8,128)} %fusion.131, f32[3,2048]{1,0:T(4,128)S(1)} %get-tuple-element.255, f32[3,2048]{1,0:T(4,128)S(1)} %dynamic-slice_bitcast_fusion.8, pred[2048]{0:T(1024)(128)(4,1)S(1)} %dynamic-slice_reduce_fusion.5), kind=kLoop, calls=%fused_computation.13.clone.1 | loop fusion | flops 75497472 | bytes 125880320 | tf_op jit(solution)/shard_map/while/body/eval_jaxpr/convert_element_type | solution.py:130
  600.3 19.7 %fusion.132 = bf16[3,64,2048]{2,1,0:T(8,128)(2,1)S(1)} fusion(bf16[2048,3,64]{0,2,1:T(8,128)(2,1)S(1)} %bitcast.200, f32[3,2048,2048]{1,2,0:T(8,128)} %fusion.131, f32[3,2048]{1,0:T(4,128)S(1)} %dynamic-slice_bitcast_fusion.8, pred[2048]{0:T(1024)(128)(4,1)S(1)} %dynamic-slice_reduce_fusion.5), kind=kOutput, calls=%fused_computation.21.clone.1 | convolution fusion | flops 1661337600 | bytes 51931136 | tf_op jit(solution)/shard_map/while/body/eval_jaxpr/hqk,qhe->khe/dot_general | solution.py:120
  623.7 20.0 %fusion.131 = f32[3,2048,2048]{1,2,0:T(8,128)} fusion(bf16[2048,3,64]{0,2,1:T(8,128)(2,1)S(1)} %bitcast.193, bf16[2048,3,64]{0,2,1:T(8,128)(2,1)S(1)} %bitcast.191), kind=kOutput, calls=%fused_computation.112.clone.1 | convolution fusion | flops 1610612736 | bytes 51904512 | tf_op jit(solution)/shard_map/while/body/eval_jaxpr/qhe,khe->hqk/dot_general | solution.py:93
  645.0 34.9 %multiply_reduce_fusion.5 = (f32[3,2048]{1,0:T(4,128)S(1)}, f32[3,2048,2048]{1,2,0:T(8,128)}) fusion(f32[3,2048,2048]{1,2,0:T(8,128)} %fusion.131, f32[3,2048]{1,0:T(4,128)S(1)} %dynamic-slice_bitcast_fusion.8, pred[2048]{0:T(1024)(128)(4,1)S(1)} %dynamic-slice_reduce_fusion.5, bf16[2048,3,64]{0,2,1:T(8,128)(2,1)S(1)} %bitcast.199, ...), kind=kOutput, calls=%fused_computation.14.clone.1 | convolution fusion | flops 1673521152 | bytes 102287360 | tf_op jit(solution)/shard_map/while/body/eval_jaxpr/qhe,khe->hqk/dot_general | solution.py:126
  679.9 40.7 %multiply_convert_fusion.3 = bf16[3,2048,2048]{1,2,0:T(8,128)(2,1)} fusion(f32[3,2048,2048]{1,2,0:T(8,128)} %get-tuple-element.254, f32[3,2048,2048]{1,2,0:T(8,128)} %fusion.131, f32[3,2048]{1,0:T(4,128)S(1)} %get-tuple-element.255, f32[3,2048]{1,0:T(4,128)S(1)} %dynamic-slice_bitcast_fusion.8, pred[2048]{0:T(1024)(128)(4,1)S(1)} %dynamic-slice_reduce_fusion.5), kind=kLoop, calls=%fused_computation.13.clone.1 | loop fusion | flops 75497472 | bytes 125880320 | tf_op jit(solution)/shard_map/while/body/eval_jaxpr/convert_element_type | solution.py:130
  743.7 19.3 %fusion.132 = bf16[3,64,2048]{2,1,0:T(8,128)(2,1)S(1)} fusion(bf16[2048,3,64]{0,2,1:T(8,128)(2,1)S(1)} %bitcast.200, f32[3,2048,2048]{1,2,0:T(8,128)} %fusion.131, f32[3,2048]{1,0:T(4,128)S(1)} %dynamic-slice_bitcast_fusion.8, pred[2048]{0:T(1024)(128)(4,1)S(1)} %dynamic-slice_reduce_fusion.5), kind=kOutput, calls=%fused_computation.21.clone.1 | convolution fusion | flops 1661337600 | bytes 51931136 | tf_op jit(solution)/shard_map/while/body/eval_jaxpr/hqk,qhe->khe/dot_general | solution.py:120
  788.3 68.8 %all-to-all-done.3 = bf16[2,2048,3,192]{3,0,2,1:T(2,128)(2,1)} async-done(((bf16[2,2048,3,192]{3,0,2,1:T(2,128)(2,1)}), bf16[2,2048,3,192]{3,0,2,1:T(2,128)(2,1)}, u32[]{:S(2)}, u32[]{:S(2)}) %all-to-all-start.3) | async-done | bytes 4718624 | tf_op jit(solution)/shard_map/all_to_all | solution.py:205
  857.1 21.2 %copy.86 = bf16[2,4,512,3,192]{2,0,4,1,3:T(2,128)(2,1)} copy(bf16[2,4,512,3,192]{4,0,3,2,1:T(2,128)(2,1)} %bitcast.31) | data formatting | bytes 9437184 | tf_op jit(solution)/shard_map/all_to_all | solution.py:205
  904.7 35.0 %all-reduce.17 = (bf16[768]{0:T(1024)(128)(2,1)S(1)}, bf16[768]{0:T(1024)(128)(2,1)S(1)}, bf16[768]{0:T(1024)(128)(2,1)S(1)}, bf16[768]{0:T(1024)(128)(2,1)S(1)}...) all-reduce(bf16[768]{0:T(1024)(128)(2,1)S(1)} %dynamic-update-slice, ...), channel_id=1, replica_groups=mesh['fsdp'=8,'seq'=4] {'fsdp'}, use_global_device_ids=true, to_apply=%add.7 | all-reduce | flops 9984 | bytes 39936
  939.8 27.0 %reduce-scatter.5.cloned.1.call-done = bf16[96,2304]{1,0:T(8,128)(2,1)} async-done(((bf16[768,2304]{1,0:T(8,128)(2,1)}), bf16[96,2304]{1,0:T(8,128)(2,1)}) %reduce-scatter.5.cloned.1.call-update) | async-done | bytes 442384 | tf_op jit(solution)/shard_map/reduce_scatter | solution.py:222
  994.3 21.6 %all-reduce.23.cloned.1.call-done = (bf16[96,2304]{1,0:T(8,128)(2,1)}, bf16[96,768]{1,0:T(8,128)(2,1)}, bf16[96,3072]{1,0:T(8,128)(2,1)}, bf16[384,768]{1,0:T(8,128)(2,1)}) async-done(((bf16[96,2304]{1,0:T(8,128)(2,1)}, bf16[96,768]{1,0:T(8,128)(2,1)}, bf16[96,3072]{1,0:T(8,128)(2,1)}, bf16[384,768]{1,0:T(8,128)(2,1)}), (bf16[96,2304]{1,0:T(8,128)(2,1)}, bf16[96,768]{1,0:T(8,128)(2,1)}, ...) | async-done | bytes 1769488 | tf_op jit(solution)/shard_map/psum | solution.py:274
  (257 shorter events, 348.2 us)
Async XLA Ops:
  7.2 113.1 %copy-start = (s32[2,4]{1,0:T(2,128)S(1)}, s32[2,4]{1,0:T(2,128)}, u32[]{:S(2)}) copy-start(s32[2,4]{1,0:T(2,128)} %param.21) | copy-start | bytes 100
  7.2 54.3 %copy-start.2 = (bf16[2,512,768]{2,1,0:T(8,128)(2,1)S(1)}, bf16[2,512,768]{2,1,0:T(8,128)(2,1)}, u32[]{:S(2)}) copy-start(bf16[2,512,768]{2,1,0:T(8,128)(2,1)} %param.20) | copy-start | bytes 4718596
  7.2 71.3 %all-gather.6.cloned.1.call-start = ((), (), s32[]{:S(2)}) async-start(), calls=%async_computation.8 | async-start | bytes 3981312 | tf_op jit(solution)/shard_map/all_gather | solution.py:67
  113.8 58.8 %all-to-all-start = ((bf16[2,512,3,768]{1,0,2,3:T(2,128)(2,1)}), bf16[2,512,3,768]{1,0,2,3:T(2,128)(2,1)}, u32[]{:S(2)}, u32[]{:S(2)}) async-start(bf16[2,512,3,768]{1,0,2,3:T(2,128)(2,1)} %copy.77), calls=%async_computation | async-start | bytes 9437184 | tf_op jit(solution)/shard_map/all_to_all | solution.py:153
  118.8 236.8 %all-gather.8.cloned.1.call-start = ((), (), s32[]{:S(2)}) async-start(), calls=%async_computation.9 | async-start | bytes 1327104 | tf_op jit(solution)/shard_map/all_gather | solution.py:70
  119.5 242.1 %all-gather.10.cloned.1.call-start = ((), (), s32[]{:S(2)}) async-start(), calls=%async_computation.10 | async-start | bytes 5308416 | tf_op jit(solution)/shard_map/all_gather | solution.py:76
  221.7 20.1 %copy-start.12 = (bf16[2,2048,192]{1,2,0:T(8,128)(2,1)S(1)}, bf16[2,2048,192]{1,2,0:T(8,128)(2,1)}, u32[]{:S(2)}) copy-start(bf16[2,2048,192]{1,2,0:T(8,128)(2,1)} %get-tuple-element.263) | copy-start | bytes 4718596 | tf_op jit(solution)/shard_map/while
  285.9 19.9 %copy-start.12 = (bf16[2,2048,192]{1,2,0:T(8,128)(2,1)S(1)}, bf16[2,2048,192]{1,2,0:T(8,128)(2,1)}, u32[]{:S(2)}) copy-start(bf16[2,2048,192]{1,2,0:T(8,128)(2,1)} %get-tuple-element.263) | copy-start | bytes 4718596 | tf_op jit(solution)/shard_map/while
  307.0 37.7 %copy-start.17 = (pred[2,2048]{1,0:T(4,128)(4,1)}, pred[2,2048]{1,0:T(4,128)(4,1)S(1)}, u32[]{:S(2)}) copy-start(pred[2,2048]{1,0:T(4,128)(4,1)S(1)} %get-tuple-element.327) | copy-start | bytes 12292
  307.0 37.7 %copy-start.19 = (f32[2,3,2048]{2,1,0:T(4,128)}, f32[2,3,2048]{2,1,0:T(4,128)S(1)}, u32[]{:S(2)}) copy-start(f32[2,3,2048]{2,1,0:T(4,128)S(1)} %get-tuple-element.278) | copy-start | bytes 147460
  313.2 31.5 %all-to-all-start.1 = ((bf16[2,2048,192]{2,0,1:T(2,128)(2,1)}), bf16[2,2048,192]{2,0,1:T(2,128)(2,1)}, u32[]{:S(2)}, u32[]{:S(2)}) async-start(bf16[2,2048,192]{2,0,1:T(2,128)(2,1)} %copy.80), calls=%async_computation.1 | async-start | bytes 4194304 | tf_op jit(solution)/shard_map/all_to_all | solution.py:155
  317.7 38.0 %copy-start.3 = (bf16[2,512,768]{2,1,0:T(8,128)(2,1)S(1)}, bf16[2,512,768]{2,1,0:T(8,128)(2,1)}, u32[]{:S(2)}) copy-start(bf16[2,512,768]{2,1,0:T(8,128)(2,1)} %param.20) | copy-start | bytes 4718596
  317.7 82.2 %all-gather.12.cloned.1.call-start = ((), (), s32[]{:S(2)}) async-start(), calls=%async_computation.11 | async-start | bytes 5308416 | tf_op jit(solution)/shard_map/all_gather | solution.py:78
  318.2 621.5 %reduce-scatter.7.cloned.1.call-start = ((), (), s32[]{:S(2)}) async-start(), calls=%async_computation.13 | async-start | bytes 1327104 | tf_op jit(solution)/shard_map/reduce_scatter | solution.py:231
  361.6 38.3 %copy-start.6 = (bf16[2,512,768]{2,1,0:T(8,128)(2,1)S(1)}, bf16[2,512,768]{2,1,0:T(8,128)(2,1)}, u32[]{:S(2)}) copy-start(bf16[2,512,768]{2,1,0:T(8,128)(2,1)} %param.35) | copy-start | bytes 4718596
  399.9 18.0 %copy-start.10 = (f32[1024,768]{1,0:T(8,128)S(1)}, f32[1024,768]{1,0:T(8,128)}, u32[]{:S(2)}) copy-start(f32[1024,768]{1,0:T(8,128)} %copy-done.9) | copy-start | bytes 9437188
  435.8 504.0 %reduce-scatter.9.cloned.1.call-start = ((), (), s32[]{:S(2)}) async-start(), calls=%async_computation.14 | async-start | bytes 5308416 | tf_op jit(solution)/shard_map/reduce_scatter | solution.py:243
  452.6 23.6 %all-to-all-start.2 = ((bf16[2,512,768]{1,0,2:T(2,128)(2,1)}), bf16[2,512,768]{1,0,2:T(2,128)(2,1)S(1)}, u32[]{:S(2)}, u32[]{:S(2)}) async-start(bf16[2,512,768]{1,0,2:T(2,128)(2,1)} %copy.82), calls=%async_computation.2 | async-start | bytes 3145728 | tf_op jit(solution)/shard_map/all_to_all | solution.py:201
  456.2 483.6 %reduce-scatter.11.cloned.1.call-start = ((), (), s32[]{:S(2)}) async-start(), calls=%async_computation.15 | async-start | bytes 5308416 | tf_op jit(solution)/shard_map/reduce_scatter | solution.py:249
  781.0 76.1 %all-to-all-start.3 = ((bf16[2,2048,3,192]{3,0,2,1:T(2,128)(2,1)}), bf16[2,2048,3,192]{3,0,2,1:T(2,128)(2,1)}, u32[]{:S(2)}, u32[]{:S(2)}) async-start(bf16[2,2048,3,192]{3,0,2,1:T(2,128)(2,1)} %copy.85), calls=%async_computation.3 | async-start | bytes 12582912 | tf_op jit(solution)/shard_map/all_to_all | solution.py:205
  786.4 180.5 %reduce-scatter.5.cloned.1.call-start = ((), (), s32[]{:S(2)}) async-start(), calls=%async_computation.12 | async-start | bytes 3981312 | tf_op jit(solution)/shard_map/reduce_scatter | solution.py:222
  889.9 126.1 %all-reduce.23.cloned.1.call-start = ((), (), s32[]{:S(2)}) async-start(), calls=%async_computation.16 | async-start | bytes 3538944 | tf_op jit(solution)/shard_map/psum | solution.py:274
  966.9 22.6 %copy-start.33 = (f32[1024]{0:T(1024)S(1)}, f32[1024]{0:T(1024)}, u32[]{:S(2)}) copy-start(f32[1024]{0:T(1024)} %copy-done.32) | copy-start | bytes 12292
  989.5 33.5 %copy-start.1 = (s32[2,4]{1,0:T(2,128)S(1)}, s32[2,4]{1,0:T(2,128)}, u32[]{:S(2)}) copy-start(s32[2,4]{1,0:T(2,128)} %param.21) | copy-start | bytes 100
  (37 other events, 196.0 us)
Sparse Core Ops, SparseCore 0:
  10.2 68.2 all-gather.5
  121.8 40.1 all-gather.7
  164.2 78.6 all-gather.9
  320.4 79.4 all-gather.11
  435.9 62.2 reduce-scatter.6
  501.7 94.2 reduce-scatter.8
  599.6 95.0 reduce-scatter.10
  890.0 76.8 reduce-scatter.4
  969.5 46.4 all-reduce.22
where the time goes:
time: 1040 us; the launch traced here: 1030 us
  matrix products  397 us (38%)
  waiting for transfers between devices  199 us (19%)
  other arithmetic  163 us (16%)
  local copies, waits for them, and re-layouts  126 us (12%)
  blocking collectives  109 us (10%)
  starting transfers between devices  18.9 us (2%)
  between operations  16.7 us (2%)
    convert_element_type x2, other arithmetic, attend_backward(): grad_scores = (probs * (grad_probs - row_delta)).astype(jnp.bfloat16)  82 us
    dot_general x4, matrix products, score_block(): jnp.einsum('qhe,khe->hqk', query_part, key_part, preferred_element_type=j...  76 us
    unnamed x2, blocking collectives  75.2 us
    dot_general x2, matrix products, attend_backward(): jnp.einsum('qhe,khe->hqk', grad_heads, value_part, preferred_element_type...  69.6 us
    all_to_all x1, waiting for transfers between devices, per_device(): lax.all_to_all(grad_packed_heads, 'seq', split_axis=1, concat_axis=3, til...  68.8 us
    all_to_all x1, waiting for transfers between devices, per_device(): lax.all_to_all(packed_low, 'seq', split_axis=3, concat_axis=1, tiled=True)  52.2 us
    reduce_sum x2, other arithmetic, attend_forward(): totals = jnp.sum(raised, axis=-1, keepdims=True)  45.3 us
    dot_general x2, matrix products, attend_forward(): jnp.einsum('hqk,khe->qhe', probs_low, value_part, preferred_element_type=...  40 us
  transfers between devices with their start and end apart: 13, of which 7 were waited for; matrix products, arithmetic and copies ran while one was open for 58% of the time, Pallas kernels for 0%

commit v1 on v0

v1 whole, which is shorter than its diff:
```python
import functools

import jax
import jax.numpy as jnp
from jax import lax
from jax.experimental import pallas as pl
from jax.experimental.pallas import tpu as pltpu
from jax.sharding import PartitionSpec as P

HEADS = 12
HEAD_DIM = 64
EPSILON = 1e-06
MASKED = -1e30
BF = jnp.bfloat16
F32 = jnp.float32
VMEM_BYTES = 60 * 1024 * 1024
PAIR = 2 * HEAD_DIM
VEC_ROWS = 16


def params(*semantics):
    return pltpu.CompilerParams(
        dimension_semantics=semantics, vmem_limit_bytes=VMEM_BYTES
    )


def dot(left, right, left_dim=1, right_dim=0):
    return lax.dot_general(
        left, right, (((left_dim,), (right_dim,)), ((), ())), preferred_element_type=F32
    )


def cost(flops, bytes_accessed, transcendentals=0):
    return pl.CostEstimate(
        flops=int(flops), bytes_accessed=int(bytes_accessed), transcendentals=int(transcendentals)
    )


def whole(shape):
    return pl.BlockSpec(shape, lambda *_: tuple(0 for _ in shape))


def key_bias(counts_ref, keys, slots):
    row = lax.broadcasted_iota(jnp.int32, (slots, PAIR), 0)
    parts = [
        jnp.where(row < counts_ref[at], 0.0, MASKED).astype(F32) for at in range(keys // slots)
    ]
    return jnp.concatenate(parts, axis=0)


def augment_keys(pair, bias, which, ones):
    lane = lax.broadcasted_iota(jnp.int32, pair.shape, 1)
    mine = (lane < HEAD_DIM) if which == 0 else (lane >= HEAD_DIM)
    start = HEAD_DIM if which == 0 else 0
    extra = jnp.where(
        lane == start, bias, jnp.where((lane > start) & (lane <= start + ones), 1.0, 0.0)
    )
    return jnp.where(mine, pair.astype(F32), extra).astype(BF)


def augment_values(pair, which, ones):
    lane = lax.broadcasted_iota(jnp.int32, pair.shape, 1)
    mine = (lane < HEAD_DIM) if which == 0 else (lane >= HEAD_DIM)
    start = HEAD_DIM if which == 0 else 0
    extra = jnp.where((lane >= start) & (lane < start + ones), 1.0, 0.0)
    return jnp.where(mine, pair.astype(F32), extra).astype(BF)


def pieces(value):
    first = value.astype(BF).astype(F32)
    rest = value - first
    second = rest.astype(BF).astype(F32)
    return first, second, rest - second


def extra_rows(rows, width):
    place = lax.broadcasted_iota(jnp.int32, (HEAD_DIM, width), 0)
    out = jnp.zeros((HEAD_DIM, width), F32)
    for at, row in enumerate(rows):
        out = jnp.where(place == at, row, out)
    return out.astype(BF)


def place_rows(head, extra, which):
    return jnp.concatenate([head, extra] if which == 0 else [extra, head], axis=0)


def attend_forward_kernel(
    slots, bq, chunk, counts_ref, k_ref, qt_ref, vt_ref, mixed_ref, ot_ref, lse_ref,
    kaug, vaug, s_a, s_b, m_a, m_b
):
    keys = k_ref.shape[0]
    step = pl.program_id(1)
    steps = pl.num_programs(1)
    scores = (s_a, s_b)
    peaks = (m_a, m_b)
    ones_row = extra_rows([jnp.ones((1, bq), F32)], bq)

    @pl.when(step == 0)
    def _():
        bias = key_bias(counts_ref, keys, slots)
        ones = jnp.ones((16, keys), BF)
        for which in range(2):
            kaug[which] = augment_keys(k_ref[...], bias, which, 0)
            vaug[which] = jnp.concatenate(
                [vt_ref[which * HEAD_DIM : (which + 1) * HEAD_DIM, :], ones], axis=0
            )

    def query_block(at, which):
        head = qt_ref[which * HEAD_DIM : (which + 1) * HEAD_DIM, pl.ds(at * bq, bq)]
        head = (head.astype(F32) * HEAD_DIM ** (-0.5)).astype(BF)
        return place_rows(head, ones_row, which)

    def score_chunk(query, which, at, peak):
        rows = slice(at * chunk, (at + 1) * chunk)
        s = dot(kaug[which, rows, :], query)
        scores[which][rows, :] = s
        top = jnp.max(s.reshape(chunk // 8, 8, bq), axis=0)
        return top if peak is None else jnp.maximum(peak, top)

    def weigh_chunk(which, at, peak, total):
        rows = slice(at * chunk, (at + 1) * chunk)
        p = jnp.exp(scores[which][rows, :] - peak).astype(BF)
        o = dot(vaug[which, :, rows], p)
        return o if total is None else total + o

    @pl.when(step == 0)
    def _():
        query = query_block(0, 0)
        peak = None
        for at in range(keys // chunk):
            peak = score_chunk(query, 0, at, peak)
        m_a[...] = peak

    later = jnp.minimum(step + 1, steps - 1)
    outs = []
    for which in range(2):
        other = 1 - which
        query = query_block(step if which == 0 else later, other)
        peak = jnp.max(peaks[which][...], axis=0, keepdims=True)
        next_peak, total = None, None
        for at in range(keys // chunk):
            next_peak = score_chunk(query, other, at, next_peak)
            total = weigh_chunk(which, at, peak, total)
        peaks[other][...] = next_peak
        norm = total[HEAD_DIM : HEAD_DIM + 1, :]
        outs.append(total[:HEAD_DIM, :] * (1.0 / norm))
        lse_ref[0, which : which + 1, :] = peak + jnp.log(norm)
    both = jnp.concatenate(outs, axis=0)
    ot_ref[...] = both
    mixed_ref[...] = both.T.astype(BF)


def attend_forward(counts, packed, packed_t, slots):
    keys, width = packed.shape
    width //= 3
    pairs = width // PAIR
    bq, chunk = 256, 256
    kernel = functools.partial(attend_forward_kernel, slots, bq, chunk)
    return pl.pallas_call(
        kernel,
        grid=(pairs, keys // bq),
        in_specs=[
            pl.BlockSpec(memory_space=pltpu.SMEM),
            pl.BlockSpec((keys, PAIR), lambda p, i: (0, pairs + p)),
            pl.BlockSpec((PAIR, keys), lambda p, i: (p, 0)),
            pl.BlockSpec((PAIR, keys), lambda p, i: (2 * pairs + p, 0)),
        ],
        out_specs=[
            pl.BlockSpec((bq, PAIR), lambda p, i: (i, p)),
            pl.BlockSpec((PAIR, bq), lambda p, i: (p, i)),
            pl.BlockSpec((1, 8, bq), lambda p, i: (p, 0, i)),
        ],
        out_shape=[
            jax.ShapeDtypeStruct((keys, width), BF),
            jax.ShapeDtypeStruct((width, keys), F32),
            jax.ShapeDtypeStruct((pairs, 8, keys), F32),
        ],
        scratch_shapes=[
            pltpu.VMEM((2, keys, PAIR), BF),
            pltpu.VMEM((2, HEAD_DIM + 16, keys), BF),
            pltpu.VMEM((keys, bq), F32),
            pltpu.VMEM((keys, bq), F32),
            pltpu.VMEM((8, bq), F32),
            pltpu.VMEM((8, bq), F32),
        ],
        compiler_params=params("arbitrary", "arbitrary"),
        cost_estimate=cost(
            2 * pairs * 2 * 2 * keys * keys * 256, 12 * keys * width, 2 * pairs * keys * keys
        ),
        name="attend_forward",
    )(counts, packed, packed_t, packed_t)


def attend_backward_kernel(
    slots, bq, chunk, counts_ref, q_ref, k_ref, v_ref, qt_ref, kt_ref, do_ref, dot_ref, ot_ref,
    lse_ref, gq_ref, gk_ref, gv_ref, kaug, vaug, acc_k, acc_v
):
    keys = k_ref.shape[0]
    step = pl.program_id(1)
    steps = pl.num_programs(1)
    scale = HEAD_DIM ** (-0.5)

    @pl.when(step == 0)
    def _():
        bias = key_bias(counts_ref, keys, slots)
        for which in range(2):
            kaug[which] = augment_keys(k_ref[...], bias, which, 3)
            vaug[which] = augment_values(v_ref[...], which, 3)
        acc_k[...] = jnp.zeros_like(acc_k)
        acc_v[...] = jnp.zeros_like(acc_v)

    ones_row = jnp.ones((1, bq), F32)
    queries, grads = [], []
    for which in range(2):
        rows = slice(which * HEAD_DIM, (which + 1) * HEAD_DIM)
        head = (qt_ref[rows, :].astype(F32) * scale).astype(BF)
        log_total = lse_ref[0, which : which + 1, :]
        queries.append(
            place_rows(head, extra_rows([ones_row, *pieces(-log_total)], bq), which)
        )
        grad = dot_ref[rows, :]
        delta = jnp.sum(grad.astype(F32) * ot_ref[rows, :], axis=0, keepdims=True)
        grads.append(place_rows(grad, extra_rows(list(pieces(-delta)), bq), which))

    do_pair = do_ref[...]
    q_pair = q_ref[...]
    totals = [None, None]
    for at in range(keys // chunk):
        rows = slice(at * chunk, (at + 1) * chunk)
        for which in range(2):
            p = jnp.exp(dot(kaug[which, rows, :], queries[which]))
            dp = dot(vaug[which, rows, :], grads[which])
            p_low = p.astype(BF)
            ds = (p * dp).astype(BF)
            acc_v[which, rows, :] += dot(p_low, do_pair)
            acc_k[which, rows, :] += dot(ds, q_pair)
            part = dot(kt_ref[which * HEAD_DIM : (which + 1) * HEAD_DIM, rows], ds)
            totals[which] = part if totals[which] is None else totals[which] + part
    both = jnp.concatenate(totals, axis=0) * scale
    gq_ref[...] = both.T.astype(BF)

    @pl.when(step == steps - 1)
    def _():
        lane = lax.broadcasted_iota(jnp.int32, (keys, PAIR), 1)
        gk_ref[...] = (jnp.where(lane < HEAD_DIM, acc_k[0], acc_k[1]) * scale).astype(BF)
        gv_ref[...] = jnp.where(lane < HEAD_DIM, acc_v[0], acc_v[1]).astype(BF)


def attend_backward(counts, packed, packed_t, grad, grad_t, result_t, log_total, slots):
    keys, width = packed.shape
    width //= 3
    pairs = width // PAIR
    bq, chunk = 512, 256
    kernel = functools.partial(attend_backward_kernel, slots, bq, chunk)
    return pl.pallas_call(
        kernel,
        grid=(pairs, keys // bq),
        in_specs=[
            pl.BlockSpec(memory_space=pltpu.SMEM),
            pl.BlockSpec((bq, PAIR), lambda p, i: (i, p)),
            pl.BlockSpec((keys, PAIR), lambda p, i: (0, pairs + p)),
            pl.BlockSpec((keys, PAIR), lambda p, i: (0, 2 * pairs + p)),
            pl.BlockSpec((PAIR, bq), lambda p, i: (p, i)),
            pl.BlockSpec((PAIR, keys), lambda p, i: (pairs + p, 0)),
            pl.BlockSpec((bq, PAIR), lambda p, i: (i, p)),
            pl.BlockSpec((PAIR, bq), lambda p, i: (p, i)),
            pl.BlockSpec((PAIR, bq), lambda p, i: (p, i)),
            pl.BlockSpec((1, 8, bq), lambda p, i: (p, 0, i)),
        ],
        out_specs=[
            pl.BlockSpec((bq, PAIR), lambda p, i: (i, p)),
            pl.BlockSpec((keys, PAIR), lambda p, i: (0, p)),
            pl.BlockSpec((keys, PAIR), lambda p, i: (0, p)),
        ],
        out_shape=[jax.ShapeDtypeStruct((keys, width), BF)] * 3,
        scratch_shapes=[
            pltpu.VMEM((2, keys, PAIR), BF),
            pltpu.VMEM((2, keys, PAIR), BF),
            pltpu.VMEM((2, keys, PAIR), F32),
            pltpu.VMEM((2, keys, PAIR), F32),
        ],
        compiler_params=params("arbitrary", "arbitrary"),
        cost_estimate=cost(
            2 * pairs * 5 * 2 * keys * keys * 256, 24 * keys * width, 2 * pairs * keys * keys
        ),
        name="attend_backward",
    )(counts, packed, packed, packed, packed_t, packed_t, grad, grad_t, result_t, log_total)


def normalised(values):
    centred = values - jnp.mean(values, axis=-1, keepdims=True)
    variance = jnp.mean(centred * centred, axis=-1, keepdims=True)
    inverse = lax.rsqrt(variance + EPSILON)
    return centred * inverse, inverse


def norm_pull(grad, gain, unit, inverse):
    scaled = grad * gain
    mean = jnp.mean(scaled, axis=-1, keepdims=True)
    along = jnp.mean(scaled * unit, axis=-1, keepdims=True)
    return inverse * (scaled - mean - unit * along)


def fold(values):
    return jnp.sum(values.reshape(values.shape[0] // 8, 8, values.shape[1]), axis=0)


def feed_forward_kernel(
    chunk, tok_ref, mo_ref, ms_ref, cot_ref, wpo_ref, wps_ref, g2_ref, vec_ref, f1b_ref,
    mid_ref, out_ref, gn_ref, dw1_ref, dw2_ref, gf1_ref, gf2_ref, acc1, acc2, accb, accc
):
    step = pl.program_id(0)
    steps = pl.num_programs(0)
    width = tok_ref.shape[1]
    half = f1b_ref.shape[1]

    @pl.when(step == 0)
    def _():
        acc1[...] = jnp.zeros_like(acc1)
        acc2[...] = jnp.zeros_like(acc2)
        accb[...] = jnp.zeros_like(accb)
        accc[...] = jnp.zeros_like(accc)

    middle = (
        tok_ref[...].astype(F32)
        + dot(mo_ref[...], wpo_ref[...])
        + dot(ms_ref[...], wps_ref[...])
        + vec_ref[0:1, :]
    )
    mid_ref[...] = middle
    unit, _ = normalised(middle)
    normed = (unit * vec_ref[1:2, :] + vec_ref[2:3, :]).astype(BF)
    cot = cot_ref[...]
    out = None
    grad = None
    for at in range(half // chunk):
        cols = slice(at * chunk, (at + 1) * chunk)
        w1 = g2_ref[:, width + at * chunk : width + (at + 1) * chunk]
        piece, row = divmod(at * chunk, width)
        start = width + half + piece * width
        w2 = g2_ref[row : row + chunk, start : start + width]
        hidden = dot(normed, w1) + f1b_ref[0:1, cols]
        below = 0.5 + 0.5 * lax.erf(hidden * (0.5**0.5))
        slope = below + hidden * (jnp.exp(hidden * hidden * -0.5) * 0.3989422804014327)
        active = (hidden * below).astype(BF)
        grad_hidden = (dot(cot, w2, 1, 1) * slope).astype(BF)
        more = dot(active, w2)
        out = more if out is None else out + more
        more = dot(grad_hidden, w1, 1, 1)
        grad = more if grad is None else grad + more
        acc1[:, cols] += dot(normed, grad_hidden, 0, 0)
        acc2[cols, :] += dot(active, cot, 0, 0)
        accb[:, cols] += fold(grad_hidden.astype(F32))
    accc[...] += fold(cot.astype(F32))
    out_ref[...] = out.astype(BF)
    gn_ref[...] = grad.astype(BF)

    @pl.when(step == steps - 1)
    def _():
        dw1_ref[...] = acc1[...].astype(BF)
        dw2_ref[...] = acc2[...].astype(BF)
        gf1_ref[...] = accb[...]
        gf2_ref[...] = accc[...]


def feed_forward(tokens, mixed_own, mixed_sib, cot, wp_own, wp_sib, weights, vec, f1b):
    rows, width = tokens.shape
    half = f1b.shape[1]
    heads = mixed_own.shape[1]
    bt, chunk = 256, 384
    blocks = rows // bt
    kernel = functools.partial(feed_forward_kernel, chunk)
    return pl.pallas_call(
        kernel,
        grid=(blocks,),
        in_specs=[
            pl.BlockSpec((bt, width), lambda i: (i, 0)),
            pl.BlockSpec((bt, heads), lambda i: (i, 0)),
            pl.BlockSpec((bt, heads), lambda i: (lax.rem(i + blocks // 2, blocks), 0)),
            pl.BlockSpec((bt, width), lambda i: (i, 0)),
            whole(wp_own.shape),
            whole(wp_sib.shape),
            whole(weights.shape),
            whole(vec.shape),
            whole(f1b.shape),
        ],
        out_specs=[
            pl.BlockSpec((bt, width), lambda i: (i, 0)),
            pl.BlockSpec((bt, width), lambda i: (i, 0)),
            pl.BlockSpec((bt, width), lambda i: (i, 0)),
            whole((width, half)),
            whole((half, width)),
            whole((8, half)),
            whole((8, width)),
        ],
        out_shape=[
            jax.ShapeDtypeStruct((rows, width), F32),
            jax.ShapeDtypeStruct((rows, width), BF),
            jax.ShapeDtypeStruct((rows, width), BF),
            jax.ShapeDtypeStruct((width, half), BF),
            jax.ShapeDtypeStruct((half, width), BF),
            jax.ShapeDtypeStruct((8, half), F32),
            jax.ShapeDtypeStruct((8, width), F32),
        ],
        scratch_shapes=[
            pltpu.VMEM((width, half), F32),
            pltpu.VMEM((half, width), F32),
            pltpu.VMEM((8, half), F32),
            pltpu.VMEM((8, width), F32),
        ],
        compiler_params=params("arbitrary"),
        cost_estimate=cost(
            2 * rows * width * (6 * half + width), 20 * rows * width + 8 * width * half,
            2 * rows * half,
        ),
        name="feed_forward",
    )(tokens, mixed_own, mixed_sib, cot, wp_own, wp_sib, weights, vec, f1b)


def branch_kernel(
    core_ref, mid_ref, ga_ref, gb_ref, cot_ref, mo_ref, ms_ref, wpo_ref, vec_ref,
    gm_ref, do_ref, dot_ref, dwo_ref, dws_ref, vecs_ref, acco, accs, accv, low_ref
):
    step = pl.program_id(0)
    steps = pl.num_programs(0)
    half = do_ref.shape[1]

    @pl.when(step == 0)
    def _():
        acco[...] = jnp.zeros_like(acco)
        accs[...] = jnp.zeros_like(accs)
        accv[...] = jnp.zeros_like(accv)

    unit, inverse = normalised(mid_ref[...])
    grad = ga_ref[...].astype(F32) + gb_ref[...].astype(F32)
    accv[0:8, :] += fold(grad * unit)
    accv[8:16, :] += fold(grad)
    grad_middle = cot_ref[...].astype(F32) + norm_pull(grad, vec_ref[1:2, :], unit, inverse)

    @pl.when(step < steps // 2)
    def _():
        gm_ref[...] = grad_middle

    low = grad_middle.astype(BF)
    low_ref[...] = low
    accv[16:24, :] += fold(low.astype(F32))
    do_ref[...] = dot(low, wpo_ref[...], 1, 1).astype(BF)
    dot_ref[...] = dot(wpo_ref[...], low, 1, 1).astype(BF)
    mine = low_ref[:, pl.ds(pl.multiple_of(core_ref[0] * half, half), half)]
    acco[...] += dot(mo_ref[...], mine, 0, 0)
    accs[...] += dot(ms_ref[...], mine, 0, 0)

    @pl.when(step == steps - 1)
    def _():
        dwo_ref[...] = acco[...].astype(BF)
        dws_ref[...] = accs[...].astype(BF)
        vecs_ref[...] = accv[...]


def branch(core, middle, grad_own, grad_sib, cot, mixed_own, mixed_sib, wp_own, vec):
    rows, width = middle.shape
    half = mixed_own.shape[1]
    bt = 256
    blocks = rows // bt
    swap = lambda i: (lax.rem(i + blocks // 2, blocks), 0)
    straight = lambda i: (i, 0)
    return pl.pallas_call(
        branch_kernel,
        grid=(blocks,),
        in_specs=[
            pl.BlockSpec(memory_space=pltpu.SMEM),
            pl.BlockSpec((bt, width), straight),
            pl.BlockSpec((bt, width), straight),
            pl.BlockSpec((bt, width), swap),
            pl.BlockSpec((bt, width), straight),
            pl.BlockSpec((bt, half), straight),
            pl.BlockSpec((bt, half), swap),
            whole(wp_own.shape),
            whole(vec.shape),
        ],
        out_specs=[
            pl.BlockSpec((bt, width), lambda i: (jnp.minimum(i, blocks // 2 - 1), 0)),
            pl.BlockSpec((bt, half), straight),
            pl.BlockSpec((half, bt), lambda i: (0, i)),
            whole((half, half)),
            whole((half, half)),
            whole((24, width)),
        ],
        out_shape=[
            jax.ShapeDtypeStruct((rows // 2, width), F32),
            jax.ShapeDtypeStruct((rows, half), BF),
            jax.ShapeDtypeStruct((half, rows), BF),
            jax.ShapeDtypeStruct((half, half), BF),
            jax.ShapeDtypeStruct((half, half), BF),
            jax.ShapeDtypeStruct((24, width), F32),
        ],
        scratch_shapes=[
            pltpu.VMEM((half, half), F32),
            pltpu.VMEM((half, half), F32),
            pltpu.VMEM((24, width), F32),
            pltpu.VMEM((bt, width), BF),
        ],
        compiler_params=params("arbitrary"),
        cost_estimate=cost(2 * rows * width * 3 * half, 18 * rows * width),
        name="branch",
    )(core, middle, grad_own, grad_sib, cot, mixed_own, mixed_sib, wp_own, vec)


def project_back_kernel(
    tok_ref, gq_ref, gk_ref, gv_ref, w_ref, vec_ref,
    own_ref, sib_ref, dw_ref, vecs_ref, qv_ref, accw, accv, accqv
):
    step = pl.program_id(0)
    steps = pl.num_programs(0)
    part = gq_ref.shape[1]

    @pl.when(step == 0)
    def _():
        accw[...] = jnp.zeros_like(accw)
        accv[...] = jnp.zeros_like(accv)
        accqv[...] = jnp.zeros_like(accqv)

    unit, _ = normalised(tok_ref[...].astype(F32))
    normed = (unit * vec_ref[0:1, :] + vec_ref[1:2, :]).astype(BF)
    grad = None
    for at, ref in enumerate((gq_ref, gk_ref, gv_ref)):
        cols = slice(at * part, (at + 1) * part)
        value = ref[...]
        more = dot(value, w_ref[:, cols], 1, 1)
        grad = more if grad is None else grad + more
        accw[:, cols] += dot(normed, value, 0, 0)
        if at != 1:
            here = 0 if at == 0 else 8
            accqv[here : here + 8, :] += fold(value.astype(F32))
    accv[0:8, :] += fold(grad * unit)
    accv[8:16, :] += fold(grad)

    @pl.when(step < steps // 2)
    def _():
        own_ref[...] = grad

    @pl.when(step >= steps // 2)
    def _():
        sib_ref[...] = grad.astype(BF)

    @pl.when(step == steps - 1)
    def _():
        dw_ref[...] = accw[...].astype(BF)
        vecs_ref[...] = accv[...]
        qv_ref[...] = accqv[...]


def project_back(tokens, gq, gk, gv, weight, vec):
    rows, width = tokens.shape
    part = gq.shape[1]
    bt = 256
    blocks = rows // bt
    straight = lambda i: (i, 0)
    return pl.pallas_call(
        project_back_kernel,
        grid=(blocks,),
        in_specs=[
            pl.BlockSpec((bt, width), straight),
            pl.BlockSpec((bt, part), straight),
            pl.BlockSpec((bt, part), straight),
            pl.BlockSpec((bt, part), straight),
            whole(weight.shape),
            whole(vec.shape),
        ],
        out_specs=[
            pl.BlockSpec((bt, width), lambda i: (jnp.minimum(i, blocks // 2 - 1), 0)),
            pl.BlockSpec((bt, width), lambda i: (jnp.maximum(i - blocks // 2, 0), 0)),
            whole((width, 3 * part)),
            whole((16, width)),
            whole((16, part)),
        ],
        out_shape=[
            jax.ShapeDtypeStruct((rows // 2, width), F32),
            jax.ShapeDtypeStruct((rows // 2, width), BF),
            jax.ShapeDtypeStruct((width, 3 * part), BF),
            jax.ShapeDtypeStruct((16, width), F32),
            jax.ShapeDtypeStruct((16, part), F32),
        ],
        scratch_shapes=[
            pltpu.VMEM((width, 3 * part), F32),
            pltpu.VMEM((16, width), F32),
            pltpu.VMEM((16, part), F32),
        ],
        compiler_params=params("arbitrary"),
        cost_estimate=cost(2 * rows * width * 6 * part, 14 * rows * width),
        name="project_back",
    )(tokens, gq, gk, gv, weight, vec)


def per_device(
    tokens,
    counts,
    norm1_gain,
    norm1_bias,
    qkv_weight,
    query_bias,
    value_bias,
    proj_weight,
    proj_bias,
    norm2_gain,
    norm2_bias,
    fc1_weight,
    fc1_bias,
    fc2_weight,
    fc2_bias,
    cotangent,
):
    images, slots, width = tokens.shape
    owners = lax.axis_size("fsdp")
    seq = lax.axis_size("seq")
    place = lax.axis_index("seq")
    core = lax.rem(place, 2)
    image = place // 2
    part = width // 2
    shard = width // owners
    ff = fc1_weight.shape[1]
    ff_shard = ff // owners
    quarter = ff_shard // 4
    half = ff // 2
    to_sibling = [(at, at ^ 1) for at in range(seq)]
    to_partner = [(at, at ^ 2) for at in range(seq)]

    def sibling(value):
        return lax.ppermute(value, "seq", to_sibling)

    def partner(value):
        return lax.ppermute(value, "seq", to_partner)

    def pick(value, at, axis):
        return lax.dynamic_index_in_dim(value, at, axis, keepdims=False)

    qkv_half = pick(qkv_weight.reshape(shard, 3, 2, part), core, 2).reshape(shard, 3 * part)
    small = jnp.concatenate(
        [
            norm1_gain, norm1_bias, query_bias, value_bias, proj_bias, norm2_gain, norm2_bias,
            fc2_bias, fc1_bias,
        ]
    )
    small_row = jnp.zeros((VEC_ROWS, 3 * part), BF).at[0, : small.shape[0]].set(small)
    first = lax.all_gather(
        jnp.concatenate([qkv_half, small_row], axis=0), "fsdp", axis=0, tiled=False
    )
    fc1_half = pick(fc1_weight.reshape(shard, owners, 2, 2, quarter), core, 2)
    fc1_half = fc1_half.transpose(0, 2, 1, 3).reshape(shard, half)
    fc2_half = lax.dynamic_slice_in_dim(fc2_weight, core * 2 * quarter, 2 * quarter, 0)
    fc2_half = fc2_half.reshape(2, quarter, width).transpose(1, 0, 2).reshape(shard, 2 * width)
    second = lax.all_gather(
        jnp.concatenate([proj_weight, fc1_half, fc2_half], axis=1), "fsdp", axis=0, tiled=True
    )

    def collect(value):
        mine = pick(value, image, 0)
        theirs = partner(pick(value, 1 - image, 0))
        return jnp.concatenate([mine, theirs, sibling(mine), sibling(theirs)], axis=0)

    tok = collect(tokens)
    kept = pick(counts, image, 0)
    kept = jnp.stack([pick(kept, place ^ at, 0) for at in (0, 2, 1, 3)])
    core_row = core.reshape(1).astype(jnp.int32)

    w_qkv = first[:, :shard].reshape(width, 3 * part)
    vecs = first[:, shard, : small.shape[0]].astype(F32)
    g1, b1, qb, vb, pb, g2, b2, f2b = (
        vecs[:, at * shard : (at + 1) * shard].reshape(width) for at in range(8)
    )
    f1b = pick(vecs[:, 8 * shard :].reshape(owners, 2, 2, quarter), core, 1)
    f1b = f1b.transpose(1, 0, 2).reshape(1, half)

    def mine_of(vector):
        return lax.dynamic_slice_in_dim(vector, core * part, part, 0)

    qkv_bias = jnp.concatenate([mine_of(qb), jnp.zeros((part,), F32), mine_of(vb)])
    unit, _ = normalised(tok.astype(F32))
    normed = (unit * g1 + b1).astype(BF)
    packed = (jnp.dot(normed, w_qkv, preferred_element_type=F32) + qkv_bias).astype(BF)
    packed_t = packed.T
    mixed, result_t, log_total = attend_forward(kept, packed, packed_t, slots)
    mixed_sib = sibling(mixed)

    cot = collect(cotangent)
    wp = second[:, :width]
    wp_own = lax.dynamic_slice_in_dim(wp, core * part, part, 0)
    wp_sib = lax.dynamic_slice_in_dim(wp, (1 - core) * part, part, 0)
    vec_two = jnp.concatenate([jnp.stack([pb, g2, b2]), jnp.zeros((5, width), F32)])
    middle, out_part, gn_part, dw1, dw2, gf1, gf2 = feed_forward(
        tok, mixed, mixed_sib, cot, wp_own, wp_sib, second, vec_two, f1b
    )
    gn_sib = sibling(gn_part)
    rows_own = 2 * slots
    out_sib = sibling(out_part[rows_own:])
    out_own = (
        middle[:rows_own] + out_part[:rows_own].astype(F32) + out_sib.astype(F32) + f2b
    ).astype(BF)

    def hand_back(own, sent):
        kept_part = own[:slots]
        came = partner(sent).astype(own.dtype)
        straight = jnp.stack([kept_part, came])
        crossed = jnp.stack([came, kept_part])
        return jnp.where(image == 0, straight, crossed)

    output = hand_back(out_own, out_own[slots:])
    grad_middle, grad_mixed, grad_mixed_t, dwp_own, dwp_sib, vec_back = branch(
        core_row, middle, gn_part, gn_sib, cot, mixed, mixed_sib, wp_own, vec_two
    )
    dwp = jnp.where(
        core == 0,
        jnp.concatenate([dwp_own, dwp_sib], axis=0),
        jnp.concatenate([dwp_sib, dwp_own], axis=0),
    )
    dw2 = dw2.reshape(2, owners, quarter, width).transpose(1, 2, 0, 3).reshape(width, 2 * width)
    scattered_one = lax.psum_scatter(
        jnp.concatenate([dwp, dw1, dw2], axis=1), "fsdp", scatter_dimension=0, tiled=True
    )
    gq, gk, gv = attend_backward(
        kept, packed, packed_t, grad_mixed, grad_mixed_t, result_t, log_total, slots
    )
    vec_one = jnp.concatenate([jnp.stack([g1, b1]), jnp.zeros((6, width), F32)])
    gn1_own, gn1_send, dw_qkv, vec_first, vec_qv = project_back(tok, gq, gk, gv, w_qkv, vec_one)

    def spread(vector):
        both = jnp.zeros((2, part), F32)
        return lax.dynamic_update_index_in_dim(both, vector, core, 0).reshape(width)

    def rows_of(block):
        return jnp.sum(block.reshape(block.shape[0] // 8, 8, block.shape[1]), axis=1)

    once = (core == 0).astype(F32)
    gg1, gb1 = rows_of(vec_first)
    gqb, gvb = rows_of(vec_qv)
    gg2, gb2, gpb = rows_of(vec_back) * once
    gf2b = jnp.sum(gf2, axis=0) * once
    gf1b = jnp.sum(gf1, axis=0).reshape(2, owners, quarter).transpose(1, 0, 2)
    gf1b = lax.dynamic_update_index_in_dim(
        jnp.zeros((owners, 2, 2, quarter), F32), gf1b, core, 1
    ).reshape(owners, ff_shard)
    small_grads = jnp.concatenate(
        [
            vector.reshape(owners, shard)
            for vector in (gg1, gb1, spread(gqb), spread(gvb), gpb, gg2, gb2, gf2b)
        ]
        + [gf1b],
        axis=1,
    ).astype(BF)
    small_block = (
        jnp.zeros((owners, VEC_ROWS, 3 * part), BF).at[:, 0, : small.shape[0]].set(small_grads)
    )
    scattered_two = lax.psum_scatter(
        jnp.concatenate([dw_qkv.reshape(owners, shard, 3 * part), small_block], axis=1),
        "fsdp",
        scatter_dimension=0,
        tiled=False,
    )

    gn1 = gn1_own + sibling(gn1_send).astype(F32)
    unit_own, inverse_own = normalised(tok[:rows_own].astype(F32))
    input_own = grad_middle + norm_pull(gn1, g1, unit_own, inverse_own)
    input_grad = hand_back(input_own, input_own[slots:].astype(BF))

    def finish(value):
        total = value.astype(F32) + partner(value).astype(F32)
        other = sibling(total.astype(BF)).astype(F32)
        return total, other

    def in_order(mine, other):
        return jnp.where(core == 0, mine, other), jnp.where(core == 0, other, mine)

    one_mine, one_other = finish(scattered_one)
    lower, upper = in_order(one_mine, one_other)
    grad_proj = jnp.concatenate([lower[:, :part], upper[:, :part]], axis=1)

    def fc1_of(value):
        return value[:, part : part + half].reshape(shard, 2, owners, quarter).transpose(0, 2, 1, 3)

    grad_fc1 = jnp.stack([fc1_of(lower), fc1_of(upper)], axis=2).reshape(shard, ff)

    def fc2_of(value):
        return value[:, part + half :].reshape(quarter, 2, width).transpose(1, 0, 2)

    grad_fc2 = jnp.stack([fc2_of(lower), fc2_of(upper)]).reshape(ff_shard, width)
    two_mine, two_other = finish(scattered_two)
    lower, upper = in_order(two_mine[:shard], two_other[:shard])
    grad_qkv = jnp.stack(
        [lower.reshape(shard, 3, part), upper.reshape(shard, 3, part)], axis=2
    ).reshape(shard, 6 * part)
    small_sum = two_mine[shard] + two_other[shard]
    s = [small_sum[at * shard : (at + 1) * shard] for at in range(8)]
    grad_f1b = small_sum[8 * shard : 8 * shard + ff_shard]
    return (
        output,
        input_grad,
        s[0],
        s[1],
        grad_qkv,
        s[2],
        s[3],
        grad_proj,
        s[4],
        s[5],
        s[6],
        grad_fc1,
        grad_f1b,
        grad_fc2,
        s[7],
    )


def solution(mesh):
    placed = (
        P("fsdp", "seq", None),
        P("fsdp", None),
        P("fsdp"),
        P("fsdp"),
        P("fsdp", None),
        P("fsdp"),
        P("fsdp"),
        P("fsdp", None),
        P("fsdp"),
        P("fsdp"),
        P("fsdp"),
        P("fsdp", None),
        P("fsdp"),
        P("fsdp", None),
        P("fsdp"),
        P("fsdp", "seq", None),
    )
    return jax.shard_map(
        per_device,
        mesh=mesh,
        in_specs=placed,
        out_specs=(
            P("fsdp", "seq", None),
            P("fsdp", "seq", None),
            P("fsdp"),
            P("fsdp"),
            P("fsdp", None),
            P("fsdp"),
            P("fsdp"),
            P("fsdp", None),
            P("fsdp"),
            P("fsdp"),
            P("fsdp"),
            P("fsdp", None),
            P("fsdp"),
            P("fsdp", None),
            P("fsdp"),
        ),
        check_vma=False,
    )
```

time: 1040 us -> 547 us (0.53)
  matrix products: 397 us -> 8.83 us
  Pallas kernels: 0 us -> 200 us
  other arithmetic: 163 us -> 41.4 us
  blocking collectives: 109 us -> 0 us
  local copies, waits for them, and re-layouts: 126 us -> 55.8 us
    dot_general x26 -> x1, matrix products: 397 us -> 8.83 us  [per_device(): jnp.dot(normed, w_qkv, preferred_element_type=F32) + qkv_bias]
    pallas_call x0 -> x5, Pallas kernels: none -> 200 us  [the longest x1 66.9 us: attend_backward(): pl.pallas_call(kernel, grid=(pairs, keys // bq), in_specs=[pl.BlockSpec(m...]
    all_to_all x4 -> x0, waiting for transfers between devices: 131 us -> none  [the longest x1 68.8 us: per_device(): lax.all_to_all(grad_packed_heads, 'seq', split_axis=1, concat_axis=3, til...]
    convert_element_type x25 -> x4, other arithmetic: 96.2 us -> 4.11 us  [the longest x1 2.98 us: per_device(): out_own = (middle[:rows_own] + out_part[:rows_own].astype(F32) + out_sib....]
    reduce_scatter x4 -> x2, waiting for transfers between devices: 27.1 us -> 111 us  [the longest x1 96.4 us: per_device(): lax.psum_scatter(jnp.concatenate([dwp, dw1, dw2], axis=1), 'fsdp', scatte...]
    unnamed x2 -> x0, blocking collectives: 75.2 us -> none
    ppermute x0 -> x16, waiting for transfers between devices: none -> 63.8 us  [the longest x6 52.1 us: partner(): return lax.ppermute(value, 'seq', to_partner)]
    reduce_sum x10, other arithmetic: 57.7 us -> 11.6 us  [the longest x1 3.73 us: norm_pull(): mean = jnp.mean(scaled, axis=-1, keepdims=True)]
  transfers between devices with their start and end apart: 13 -> 20, of which waited for: 7 -> 13; matrix products, arithmetic and copies ran while one was open for 58% -> 14% of each run, Pallas kernels for 0% -> 8%
where the time goes in v1:
time: 547 us; the launch traced here: 542 us
  waiting for transfers between devices  209 us (38%)
  Pallas kernels  200 us (37%)
  local copies, waits for them, and re-layouts  55.8 us (10%)
  other arithmetic  41.4 us (8%)
  between operations  14.7 us (3%)
  starting transfers between devices  12.5 us (2%)
  matrix products  8.83 us (2%)
    reduce_scatter x1, waiting for transfers between devices, per_device(): lax.psum_scatter(jnp.concatenate([dwp, dw1, dw2], axis=1), 'fsdp', scatte...  96.4 us
    pallas_call x1, Pallas kernels, attend_backward(): pl.pallas_call(kernel, grid=(pairs, keys // bq), in_specs=[pl.BlockSpec(m...  66.9 us
    pallas_call x1, Pallas kernels, feed_forward(): pl.pallas_call(kernel, grid=(blocks,), in_specs=[pl.BlockSpec((bt, width)...  55.7 us
    ppermute x6, waiting for transfers between devices, partner(): return lax.ppermute(value, 'seq', to_partner)  52.1 us
    pallas_call x1, Pallas kernels, attend_forward(): pl.pallas_call(kernel, grid=(pairs, keys // bq), in_specs=[pl.BlockSpec(m...  42.1 us
    all_gather x1, waiting for transfers between devices, per_device(): lax.all_gather(jnp.concatenate([proj_weight, fc1_half, fc2_half], axis=1)...  21.9 us
    pallas_call x1, Pallas kernels, project_back(): pl.pallas_call(project_back_kernel, grid=(blocks,), in_specs=[pl.BlockSpe...  18.5 us
    pallas_call x1, Pallas kernels, branch(): pl.pallas_call(branch_kernel, grid=(blocks,), in_specs=[pl.BlockSpec(memo...  16.4 us
  transfers between devices with their start and end apart: 20, of which 13 were waited for; matrix products, arithmetic and copies ran while one was open for 14% of the time, Pallas kernels for 8%

profile of v1, /device:TPU:0, one launch (start us, length us, event | category | flops | bytes accessed | tf_op | source)
XLA Modules:
  0.0 542.3 jit_solution(7245928864462865698)
XLA Ops:
  7.3 6.2 %concatenate.74 = bf16[1152]{0:T(1024)(128)(2,1)S(1)} concatenate(bf16[96]{0:T(256)(128)(2,1)} %param.22, bf16[96]{0:T(256)(128)(2,1)} %param.23, bf16[96]{0:T(256)(128)(2,1)} %param.25, bf16[96]{0:T(256)(128)(2,1)} %param.26, bf16[96]{0:T(256)(128)(2,1)} %param.28, bf16[96]{0:T(256)(128)(2,1)} %param.29, bf16[96]{0:T(256)(128)(2,1)} %param.30, bf16[96]{0:T(256)(128)(2,1)} %param.34, ...), dimensions={0} | concatenate | bytes 4608 | tf_op jit(solution)/shard_map/concatenate | solution.py:639
  16.9 3.4 reshape.331
  25.5 17.5 %collective-permute-done = bf16[512,768]{1,0:T(8,128)(2,1)S(1)} collective-permute-done((bf16[512,768]{1,0:T(8,128)(2,1)S(1)}, bf16[512,768]{1,0:T(8,128)(2,1)S(1)}, u32[]{:S(2)}, u32[]{:S(2)}) %collective-permute-start) | collective-permute-done | bytes 786464 | tf_op jit(solution)/shard_map/ppermute | solution.py:633
  48.0 3.2 pad_add_fusion.counts_ref
  56.5 12.3 %all-gather.6.cloned.1.call-done = bf16[896,1152]{1,0:T(8,128)(2,1)} async-done(((bf16[112,1152]{1,0:T(8,128)(2,1)}), bf16[896,1152]{1,0:T(8,128)(2,1)}) %all-gather.6.cloned.1.call-update) | async-done | bytes 2064400 | tf_op jit(solution)/shard_map/all_gather | solution.py:646
  73.7 8.8 %add_convert_fusion = bf16[2048,1152]{0,1:T(8,128)(2,1)} fusion(bf16[768,1152]{1,0:T(8,128)(2,1)} %bitcast.107, f32[1152]{0:T(1024)S(1)} %pad_maximum_fusion.9, bf16[2048,768]{1,0:T(8,128)(2,1)} %copy-done.6, f32[768]{0:T(1024)S(1)} %add.153, f32[768]{0:T(1024)S(1)} %mul.90, f32[2048]{0:T(1024)S(1)} %add_rsqrt_fusion, f32[2048]{0:T(1024)S(1)} %broadcast_multiply_fusion), kind=kOutput, calls=%fused_computation | convolution fusion | flops 3638034432 | bytes 9660928 | tf_op jit(solution)/shard_map/dot_general | solution.py:681
  82.6 6.7 %copy.60.k_ref.q_ref.v_ref = bf16[2048,1152]{1,0:T(8,128)(2,1)} copy(bf16[2048,1152]{0,1:T(8,128)(2,1)} %add_convert_fusion) | data formatting | bytes 9437184 | tf_op jit(solution)/shard_map/convert_element_type | solution.py:681
  89.3 42.1 %attend_forward.1 = (bf16[2048,384]{1,0:T(8,128)(2,1)}, f32[384,2048]{1,0:T(8,128)}, f32[3,8,2048]{2,1,0:T(8,128)}) custom-call(s32[4]{0:T(128)} %pad_add_fusion.counts_ref, bf16[2048,1152]{1,0:T(8,128)(2,1)} %copy.60.k_ref.q_ref.v_ref, bf16[1152,2048]{1,0:T(8,128)(2,1)} %bitcast.98, bf16[1152,2048]{1,0:T(8,128)(2,1)} %bitcast.99), custom_call_target="tpu_custom_call" | custom-call | flops 25769803776 | bytes 9437184 | tf_op jit(solution)/shard_map/attend_forward/pallas_call | solution.py:160
  132.1 4.6 collective-permute-done.5
  141.8 21.9 %all-gather.4.cloned.1.call-done.g2_ref = bf16[768,3840]{1,0:T(8,128)(2,1)} async-done(((bf16[96,3840]{1,0:T(8,128)(2,1)}), bf16[768,3840]{1,0:T(8,128)(2,1)}) %all-gather.4.cloned.1.call-update) | async-done | bytes 5898256 | tf_op jit(solution)/shard_map/all_gather | solution.py:653
  166.1 55.7 %feed_forward.1 = (f32[2048,768]{1,0:T(8,128)}, bf16[2048,768]{1,0:T(8,128)(2,1)}, bf16[2048,768]{1,0:T(8,128)(2,1)}, bf16[768,1536]{1,0:T(8,128)(2,1)}, bf16[15...) custom-call(bf16[2048,768]{1,0:T(8,128)(2,1)} %copy-done.6, bf16[2048,384]{1,0:T(8,128)(2,1)} %get-tuple-element.63.mo_ref, ...), custom_call_target="tpu_custom_call" | custom-call | flops 31406948352 | bytes 40894464 | tf_op jit(solution)/shard_map/feed_forward/pallas_call | solution.py:374
  224.7 3.2 collective-permute-done.9.gb_ref
  227.9 16.4 %branch.1 = (f32[1024,768]{1,0:T(8,128)}, bf16[2048,384]{1,0:T(8,128)(2,1)}, bf16[384,2048]{1,0:T(8,128)(2,1)}, bf16[384,384]{1,0:T(8,128)(2,1)}, bf16[384,384]{1,0:T(8,128)(2,1)}, /*index=5*/f32[24,768]{1,0:T(8,128)}) custom-call(s32[1]{0:T(128)} %bitcast.19.core_ref, f32[2048,768]{1,0:T(8,128)} %get-tuple-element.64.mid_ref, ...), custom_call_target="tpu_custom_call" | custom-call | flops 3623878656 | bytes 28311552 | tf_op jit(solution)/shard_map/branch/pallas_call | solution.py:468
  244.3 66.9 %attend_backward.1 = (bf16[2048,384]{1,0:T(8,128)(2,1)}, bf16[2048,384]{1,0:T(8,128)(2,1)}, bf16[2048,384]{1,0:T(8,128)(2,1)}) custom-call(s32[4]{0:T(128)} %pad_add_fusion.counts_ref, bf16[2048,1152]{1,0:T(8,128)(2,1)} %copy.60.k_ref.q_ref.v_ref, bf16[2048,1152]{1,0:T(8,128)(2,1)} %copy.60.k_ref.q_ref.v_ref, bf16[2048,1152]{1,0:T(8,128)(2,1)} %copy.60.k_ref.q_ref.v_ref, ...), custom_call_target="tpu_custom_call" | custom-call | flops 64424509440 | bytes 18874368 | tf_op jit(solution)/shard_map/attend_backward/pallas_call | solution.py:256
  311.2 18.5 %project_back.1 = (f32[1024,768]{1,0:T(8,128)}, bf16[1024,768]{1,0:T(8,128)(2,1)}, bf16[768,1152]{1,0:T(8,128)(2,1)}, f32[16,768]{1,0:T(8,128)}, f32[16,384]{1,0:T(8,128)}) custom-call(bf16[2048,768]{1,0:T(8,128)(2,1)} %copy-done.6, bf16[2048,384]{1,0:T(8,128)(2,1)} %get-tuple-element.72.gq_ref, bf16[2048,384]{1,0:T(8,128)(2,1)} %get-tuple-element.73.gk_ref, ...), custom_call_target="tpu_custom_call" | custom-call | flops 7247757312 | bytes 22020096 | tf_op jit(solution)/shard_map/project_back/pallas_call | solution.py:560
  345.9 3.2 collective-permute-done.7
  355.6 17.4 %collective-permute-done.8 = bf16[512,768]{1,0:T(8,128)(2,1)} collective-permute-done((bf16[512,768]{1,0:T(8,128)(2,1)}, bf16[512,768]{1,0:T(8,128)(2,1)}, u32[]{:S(2)}, u32[]{:S(2)}) %collective-permute-start.8) | collective-permute-done | bytes 786464 | tf_op jit(solution)/shard_map/ppermute | solution.py:633
  375.8 3.7 fusion.23
  379.5 3.1 fusion.14
  386.0 14.8 %reduce-scatter.3.cloned.1.call-done = bf16[1,112,1152]{2,1,0:T(8,128)(2,1)} async-done(((bf16[8,112,1152]{2,1,0:T(8,128)(2,1)}), bf16[1,112,1152]{2,1,0:T(8,128)(2,1)}) %reduce-scatter.3.cloned.1.call-update) | async-done | bytes 258064 | tf_op jit(solution)/shard_map/reduce_scatter | solution.py:754
  403.7 5.0 collective-permute-done.12
  410.9 96.4 %reduce-scatter.5.cloned.1.call-done = bf16[96,3456]{1,0:T(8,128)(2,1)} async-done(((bf16[768,3456]{1,0:T(8,128)(2,1)}), bf16[96,3456]{1,0:T(8,128)(2,1)}) %reduce-scatter.5.cloned.1.call-update) | async-done | bytes 663568 | tf_op jit(solution)/shard_map/reduce_scatter | solution.py:718
  511.8 12.2 %collective-permute-done.14 = bf16[96,3456]{1,0:T(8,128)(2,1)S(1)} collective-permute-done((bf16[96,3456]{1,0:T(8,128)(2,1)}, bf16[96,3456]{1,0:T(8,128)(2,1)S(1)}, u32[]{:S(2)}, u32[]{:S(2)}) %collective-permute-start.14) | collective-permute-done | bytes 663584 | tf_op jit(solution)/shard_map/ppermute | solution.py:633
  531.6 3.2 reshape.348
  (205 shorter events, 81.2 us)
Async XLA Ops:
  7.2 61.6 %all-gather.6.cloned.1.call-start = ((), (), s32[]{:S(2)}) async-start(), calls=%async_computation.5 | async-start | bytes 2322432 | tf_op jit(solution)/shard_map/all_gather | solution.py:646
  16.8 146.9 %all-gather.4.cloned.1.call-start = ((), (), s32[]{:S(2)}) async-start(), calls=%async_computation.2 | async-start | bytes 6635520 | tf_op jit(solution)/shard_map/all_gather | solution.py:653
  22.0 378.7 %reduce-scatter.3.cloned.1.call-start = ((), (), s32[]{:S(2)}) async-start(), calls=%async_computation.3 | async-start | bytes 2322432 | tf_op jit(solution)/shard_map/reduce_scatter | solution.py:754
  22.3 25.1 %copy-start.24 = (s32[2,4]{1,0:T(2,128)S(1)}, s32[2,4]{1,0:T(2,128)}, u32[]{:S(2)}) copy-start(s32[2,4]{1,0:T(2,128)} %param.21) | copy-start | bytes 100
  22.5 31.3 %copy-start.2 = (bf16[512,768]{1,0:T(8,128)(2,1)}, bf16[512,768]{1,0:T(8,128)(2,1)S(1)}, u32[]{:S(2)}) copy-start(bf16[512,768]{1,0:T(8,128)(2,1)S(1)} %get-tuple-element.102) | copy-start | bytes 2359300
  22.5 20.5 %collective-permute-start = (bf16[512,768]{1,0:T(8,128)(2,1)S(1)}, bf16[512,768]{1,0:T(8,128)(2,1)S(1)}, u32[]{:S(2)}, u32[]{:S(2)}) collective-permute-start(bf16[512,768]{1,0:T(8,128)(2,1)S(1)} %get-tuple-element.103), channel_id=1, source_target_pairs={{0,2},{1,3},{2,0},{3,1},{4,6},{5,7},{6,4},{7,5},{8,10},{9,11},{10,... | collective-permute-start | bytes 2359304 | tf_op jit(solution)/shard_map/ppermute | solution.py:633
  25.5 25.7 %collective-permute-start.1 = (bf16[512,768]{1,0:T(8,128)(2,1)S(1)}, bf16[512,768]{1,0:T(8,128)(2,1)}, u32[]{:S(2)}, u32[]{:S(2)}) collective-permute-start(bf16[512,768]{1,0:T(8,128)(2,1)S(1)} %get-tuple-element.102), channel_id=1, source_target_pairs={{0,1},{1,0},{2,3},{3,2},{4,5},{5,4},{6,7},{7,6},{8,9},{9,8},{10,11... | collective-permute-start | bytes 2359304 | tf_op jit(solution)/shard_map/ppermute | solution.py:630
  43.0 8.2 %collective-permute-start.2 = (bf16[512,768]{1,0:T(8,128)(2,1)S(1)}, bf16[512,768]{1,0:T(8,128)(2,1)}, u32[]{:S(2)}, u32[]{:S(2)}) collective-permute-start(bf16[512,768]{1,0:T(8,128)(2,1)S(1)} %collective-permute-done), channel_id=1, source_target_pairs={{0,1},{1,0},{2,3},{3,2},{4,5},{5,4},{6,7},{7,6},{8,9},{9,8},{10,11... | collective-permute-start | bytes 2359304 | tf_op jit(solution)/shard_map/ppermute | solution.py:630
  45.7 86.3 %collective-permute-start.4 = (bf16[512,768]{1,0:T(8,128)(2,1)}, bf16[512,768]{1,0:T(8,128)(2,1)}, u32[]{:S(2)}, u32[]{:S(2)}) collective-permute-start(bf16[512,768]{1,0:T(8,128)(2,1)} %get-tuple-element.101), channel_id=1, source_target_pairs={{0,2},{1,3},{2,0},{3,1},{4,6},{5,7},{6,4},{7,5},{8,10},{9,11},{10,... | collective-permute-start | bytes 2359304 | tf_op jit(solution)/shard_map/ppermute | solution.py:633
  131.4 34.7 %collective-permute-start.3 = (bf16[2048,384]{1,0:T(8,128)(2,1)}, bf16[2048,384]{1,0:T(8,128)(2,1)}, u32[]{:S(2)}, u32[]{:S(2)}) collective-permute-start(bf16[2048,384]{1,0:T(8,128)(2,1)} %get-tuple-element.63.mo_ref), channel_id=1, source_target_pairs={{0,1},{1,0},{2,3},{3,2},{4,5},{5,4},{6,7},{7,6},{8,9},{9,8},{10,11... | collective-permute-start | bytes 4718600 | tf_op jit(solution)/shard_map/ppermute | solution.py:630
  131.4 5.3 collective-permute-start.5
  131.9 5.4 collective-permute-start.6
  221.9 6.1 %collective-permute-start.9 = (bf16[2048,768]{1,0:T(8,128)(2,1)}, bf16[2048,768]{1,0:T(8,128)(2,1)}, u32[]{:S(2)}, u32[]{:S(2)}) collective-permute-start(bf16[2048,768]{1,0:T(8,128)(2,1)} %get-tuple-element.66.ga_ref), channel_id=1, source_target_pairs={{0,1},{1,0},{2,3},{3,2},{4,5},{5,4},{6,7},{7,6},{8,9},{9,8},{10,11... | collective-permute-start | bytes 9437192 | tf_op jit(solution)/shard_map/ppermute | solution.py:630
  335.4 171.9 %reduce-scatter.5.cloned.1.call-start = ((), (), s32[]{:S(2)}) async-start(), calls=%async_computation.4 | async-start | bytes 5971968 | tf_op jit(solution)/shard_map/reduce_scatter | solution.py:718
  345.3 3.8 collective-permute-start.7
  345.5 30.2 %collective-permute-start.10 = (bf16[1024,768]{1,0:T(8,128)(2,1)}, bf16[1024,768]{1,0:T(8,128)(2,1)}, u32[]{:S(2)}, u32[]{:S(2)}) collective-permute-start(bf16[1024,768]{1,0:T(8,128)(2,1)} %get-tuple-element.76), channel_id=1, source_target_pairs={{0,1},{1,0},{2,3},{3,2},{4,5},{5,4},{6,7},{7,6},{8,9},{9,8},{10,11... | collective-permute-start | bytes 4718600 | tf_op jit(solution)/shard_map/ppermute | solution.py:630
  353.1 19.9 %collective-permute-start.8 = (bf16[512,768]{1,0:T(8,128)(2,1)}, bf16[512,768]{1,0:T(8,128)(2,1)}, u32[]{:S(2)}, u32[]{:S(2)}) collective-permute-start(bf16[512,768]{1,0:T(8,128)(2,1)} %get-tuple-element.99), channel_id=1, source_target_pairs={{0,2},{1,3},{2,0},{3,1},{4,6},{5,7},{6,4},{7,5},{8,10},{9,11},{10,... | collective-permute-start | bytes 2359304 | tf_op jit(solution)/shard_map/ppermute | solution.py:633
  354.7 21.1 %copy-start.22 = (f32[768]{0:T(1024)S(1)}, f32[768]{0:T(1024)}, u32[]{:S(2)}) copy-start(f32[768]{0:T(1024)} %copy-done.21) | copy-start | bytes 9220
  384.4 24.5 %collective-permute-start.11 = (bf16[512,768]{1,0:T(8,128)(2,1)S(1)}, bf16[512,768]{1,0:T(8,128)(2,1)S(1)}, u32[]{:S(2)}, u32[]{:S(2)}) collective-permute-start(bf16[512,768]{1,0:T(8,128)(2,1)S(1)} %slice.280), channel_id=1, source_target_pairs={{0,2},{1,3},{2,0},{3,1},{4,6},{5,7},{6,4},{7,5},{8,10},{9,11},{10,... | collective-permute-start | bytes 2359304 | tf_op jit(solution)/shard_map/ppermute | solution.py:633
  400.8 7.9 %collective-permute-start.12 = (bf16[112,1152]{1,0:T(8,128)(2,1)}, bf16[112,1152]{1,0:T(8,128)(2,1)S(1)}, u32[]{:S(2)}, u32[]{:S(2)}) collective-permute-start(bf16[112,1152]{1,0:T(8,128)(2,1)} %bitcast.118), channel_id=1, source_target_pairs={{0,2},{1,3},{2,0},{3,1},{4,6},{5,7},{6,4},{7,5},{8,10},{9,11},{10,... | collective-permute-start | bytes 774152 | tf_op jit(solution)/shard_map/ppermute | solution.py:633
  408.8 2.1 collective-permute-start.13
  410.9 98.0 %copy-start.13 = (f32[112,1152]{1,0:T(8,128)}, f32[112,1152]{1,0:T(8,128)S(1)}, u32[]{:S(2)}) copy-start(f32[112,1152]{1,0:T(8,128)S(1)} %convert_element_type.82) | copy-start | bytes 1548292
  507.3 16.7 %collective-permute-start.14 = (bf16[96,3456]{1,0:T(8,128)(2,1)}, bf16[96,3456]{1,0:T(8,128)(2,1)S(1)}, u32[]{:S(2)}, u32[]{:S(2)}) collective-permute-start(bf16[96,3456]{1,0:T(8,128)(2,1)} %reduce-scatter.5.cloned.1.call-done), channel_id=1, source_target_pairs={{0,2},{1,3},{2,0},{3,1},{4,6},{5,7},{6,4},{7,5},{8,10},{9,11},{10,... | collective-permute-start | bytes 1990664 | tf_op jit(solution)/shard_map/ppermute | solution.py:633
  524.2 2.2 collective-permute-start.15
  (22 other events, 138.8 us)
Sparse Core Ops, SparseCore 0:
  16.9 51.8 all-gather.5
  71.0 92.7 all-gather.3
  335.5 65.1 reduce-scatter.2
  404.2 103.0 reduce-scatter.4

commit v2 on v1

--- a/solution.py
+++ b/solution.py
@@ -16,6 +16,7 @@
 VMEM_BYTES = 60 * 1024 * 1024
 PAIR = 2 * HEAD_DIM
 VEC_ROWS = 16
+SLOT_ORDER = (0, 2, 1, 3)
 
 
 def params(*semantics):
@@ -40,11 +41,13 @@
     return pl.BlockSpec(shape, lambda *_: tuple(0 for _ in shape))
 
 
-def key_bias(counts_ref, keys, slots):
+def key_bias(counts_ref, place_ref, keys, slots):
     row = lax.broadcasted_iota(jnp.int32, (slots, PAIR), 0)
-    parts = [
-        jnp.where(row < counts_ref[at], 0.0, MASKED).astype(F32) for at in range(keys // slots)
-    ]
+    place = place_ref[0]
+    parts = []
+    for flip in SLOT_ORDER:
+        kept = counts_ref[place // 2, jnp.bitwise_xor(place, flip)]
+        parts.append(jnp.where(row < kept, 0.0, MASKED).astype(F32))
     return jnp.concatenate(parts, axis=0)
 
 
@@ -86,7 +89,7 @@
 
 
 def attend_forward_kernel(
-    slots, bq, chunk, counts_ref, k_ref, qt_ref, vt_ref, mixed_ref, ot_ref, lse_ref,
+    slots, bq, chunk, counts_ref, place_ref, k_ref, qt_ref, vt_ref, mixed_ref, ot_ref, lse_ref,
     kaug, vaug, s_a, s_b, m_a, m_b
 ):
     keys = k_ref.shape[0]
@@ -98,7 +101,7 @@
 
     @pl.when(step == 0)
     def _():
-        bias = key_bias(counts_ref, keys, slots)
+        bias = key_bias(counts_ref, place_ref, keys, slots)
         ones = jnp.ones((16, keys), BF)
         for which in range(2):
             kaug[which] = augment_keys(k_ref[...], bias, which, 0)
@@ -151,7 +154,7 @@
     mixed_ref[...] = both.T.astype(BF)
 
 
-def attend_forward(counts, packed, packed_t, slots):
+def attend_forward(counts, place, packed, packed_t, slots):
     keys, width = packed.shape
     width //= 3
     pairs = width // PAIR
@@ -162,6 +165,7 @@
         grid=(pairs, keys // bq),
         in_specs=[
             pl.BlockSpec(memory_space=pltpu.SMEM),
+            pl.BlockSpec(memory_space=pltpu.SMEM),
             pl.BlockSpec((keys, PAIR), lambda p, i: (0, pairs + p)),
             pl.BlockSpec((PAIR, keys), lambda p, i: (p, 0)),
             pl.BlockSpec((PAIR, keys), lambda p, i: (2 * pairs + p, 0)),
@@ -189,11 +193,11 @@
             2 * pairs * 2 * 2 * keys * keys * 256, 12 * keys * width, 2 * pairs * keys * keys
         ),
         name="attend_forward",
-    )(counts, packed, packed_t, packed_t)
+    )(counts, place, packed, packed_t, packed_t)
 
 
 def attend_backward_kernel(
-    slots, bq, chunk, counts_ref, q_ref, k_ref, v_ref, qt_ref, kt_ref, do_ref, dot_ref, ot_ref,
+    slots, bq, chunk, counts_ref, place_ref, q_ref, k_ref, v_ref, qt_ref, kt_ref, do_ref, dot_ref, ot_ref,
     lse_ref, gq_ref, gk_ref, gv_ref, kaug, vaug, acc_k, acc_v
 ):
     keys = k_ref.shape[0]
@@ -203,7 +207,7 @@
 
     @pl.when(step == 0)
     def _():
-        bias = key_bias(counts_ref, keys, slots)
+        bias = key_bias(counts_ref, place_ref, keys, slots)
         for which in range(2):
             kaug[which] = augment_keys(k_ref[...], bias, which, 3)
             vaug[which] = augment_values(v_ref[...], which, 3)
@@ -247,7 +251,7 @@
         gv_ref[...] = jnp.where(lane < HEAD_DIM, acc_v[0], acc_v[1]).astype(BF)
 
 
-def attend_backward(counts, packed, packed_t, grad, grad_t, result_t, log_total, slots):
+def attend_backward(counts, place, packed, packed_t, grad, grad_t, result_t, log_total, slots):
     keys, width = packed.shape
     width //= 3
     pairs = width // PAIR
@@ -258,6 +262,7 @@
         grid=(pairs, keys // bq),
         in_specs=[
             pl.BlockSpec(memory_space=pltpu.SMEM),
+            pl.BlockSpec(memory_space=pltpu.SMEM),
             pl.BlockSpec((bq, PAIR), lambda p, i: (i, p)),
             pl.BlockSpec((keys, PAIR), lambda p, i: (0, pairs + p)),
             pl.BlockSpec((keys, PAIR), lambda p, i: (0, 2 * pairs + p)),
@@ -285,7 +290,7 @@
             2 * pairs * 5 * 2 * keys * keys * 256, 24 * keys * width, 2 * pairs * keys * keys
         ),
         name="attend_backward",
-    )(counts, packed, packed, packed, packed_t, packed_t, grad, grad_t, result_t, log_total)
+    )(counts, place, packed, packed, packed, packed_t, packed_t, grad, grad_t, result_t, log_total)
 
 
 def normalised(values):
@@ -308,7 +313,7 @@
 
 def feed_forward_kernel(
     chunk, tok_ref, mo_ref, ms_ref, cot_ref, wpo_ref, wps_ref, g2_ref, vec_ref, f1b_ref,
-    mid_ref, out_ref, gn_ref, dw1_ref, dw2_ref, gf1_ref, gf2_ref, acc1, acc2, accb, accc
+    mid_ref, out_ref, gn_ref, dw_ref, gf1_ref, gf2_ref, acc1, acc2, accb, accc
 ):
     step = pl.program_id(0)
     steps = pl.num_programs(0)
@@ -331,6 +336,7 @@
     mid_ref[...] = middle
     unit, _ = normalised(middle)
     normed = (unit * vec_ref[1:2, :] + vec_ref[2:3, :]).astype(BF)
+    normed_t = normed.T
     cot = cot_ref[...]
     out = None
     grad = None
@@ -349,7 +355,7 @@
         out = more if out is None else out + more
         more = dot(grad_hidden, w1, 1, 1)
         grad = more if grad is None else grad + more
-        acc1[:, cols] += dot(normed, grad_hidden, 0, 0)
+        acc1[:, cols] += dot(normed_t, grad_hidden)
         acc2[cols, :] += dot(active, cot, 0, 0)
         accb[:, cols] += fold(grad_hidden.astype(F32))
     accc[...] += fold(cot.astype(F32))
@@ -358,8 +364,11 @@
 
     @pl.when(step == steps - 1)
     def _():
-        dw1_ref[...] = acc1[...].astype(BF)
-        dw2_ref[...] = acc2[...].astype(BF)
+        dw_ref[:, :half] = acc1[...].astype(BF)
+        for piece in range(half // width):
+            dw_ref[:, half + piece * width : half + (piece + 1) * width] = acc2[
+                piece * width : (piece + 1) * width, :
+            ].astype(BF)
         gf1_ref[...] = accb[...]
         gf2_ref[...] = accc[...]
 
@@ -389,8 +398,7 @@
             pl.BlockSpec((bt, width), lambda i: (i, 0)),
             pl.BlockSpec((bt, width), lambda i: (i, 0)),
             pl.BlockSpec((bt, width), lambda i: (i, 0)),
-            whole((width, half)),
-            whole((half, width)),
+            whole((width, 2 * half)),
             whole((8, half)),
             whole((8, width)),
         ],
@@ -398,8 +406,7 @@
             jax.ShapeDtypeStruct((rows, width), F32),
             jax.ShapeDtypeStruct((rows, width), BF),
             jax.ShapeDtypeStruct((rows, width), BF),
-            jax.ShapeDtypeStruct((width, half), BF),
-            jax.ShapeDtypeStruct((half, width), BF),
+            jax.ShapeDtypeStruct((width, 2 * half), BF),
             jax.ShapeDtypeStruct((8, half), F32),
             jax.ShapeDtypeStruct((8, width), F32),
         ],
@@ -522,14 +529,14 @@
         accqv[...] = jnp.zeros_like(accqv)
 
     unit, _ = normalised(tok_ref[...].astype(F32))
-    normed = (unit * vec_ref[0:1, :] + vec_ref[1:2, :]).astype(BF)
+    normed_t = (unit * vec_ref[0:1, :] + vec_ref[1:2, :]).astype(BF).T
     grad = None
     for at, ref in enumerate((gq_ref, gk_ref, gv_ref)):
         cols = slice(at * part, (at + 1) * part)
         value = ref[...]
         more = dot(value, w_ref[:, cols], 1, 1)
         grad = more if grad is None else grad + more
-        accw[:, cols] += dot(normed, value, 0, 0)
+        accw[:, cols] += dot(normed_t, value)
         if at != 1:
             here = 0 if at == 0 else 8
             accqv[here : here + 8, :] += fold(value.astype(F32))
@@ -591,6 +598,120 @@
         cost_estimate=cost(2 * rows * width * 6 * part, 14 * rows * width),
         name="project_back",
     )(tokens, gq, gk, gv, weight, vec)
+
+
+def pack_kernel(core_ref, qkv_ref, small_ref, proj_ref, fc1_ref, fc2_ref, one_ref, two_ref):
+    first_core = core_ref[0] == 0
+    shard, width = proj_ref.shape
+    part = width // 2
+    ff = fc1_ref.shape[1]
+    owners = width // shard
+    quarter = ff // owners // 4
+    half = ff // 2
+    one_ref[:VEC_ROWS, :] = small_ref[...]
+
+    for at in range(3):
+        low = qkv_ref[:, at * width : at * width + part]
+        high = qkv_ref[:, at * width + part : (at + 1) * width]
+        one_ref[VEC_ROWS:, at * part : (at + 1) * part] = jnp.where(first_core, low, high)
+    two_ref[:, :width] = proj_ref[...]
+    pieces_low, pieces_high = [], []
+    for piece in range(2):
+        for owner in range(owners):
+            base = owner * 4 * quarter + piece * quarter
+            pieces_low.append(fc1_ref[:, base : base + quarter])
+            pieces_high.append(fc1_ref[:, base + 2 * quarter : base + 3 * quarter])
+    two_ref[:, width : width + half] = jnp.where(
+        first_core, jnp.concatenate(pieces_low, axis=1), jnp.concatenate(pieces_high, axis=1)
+    )
+    for piece in range(2):
+        low = fc2_ref[piece * quarter : (piece + 1) * quarter, :]
+        high = fc2_ref[(2 + piece) * quarter : (3 + piece) * quarter, :]
+        start = width + half + piece * width
+        two_ref[:, start : start + width] = jnp.where(first_core, low, high)
+
+
+def pack_weights(core, qkv, small, proj, fc1, fc2):
+    shard, width = proj.shape
+    half = fc1.shape[1] // 2
+    return pl.pallas_call(
+        pack_kernel,
+        grid=(1,),
+        in_specs=[pl.BlockSpec(memory_space=pltpu.SMEM)]
+        + [whole(value.shape) for value in (qkv, small, proj, fc1, fc2)],
+        out_specs=[whole((VEC_ROWS + shard, 3 * width // 2)), whole((shard, 3 * width + half))],
+        out_shape=[
+            jax.ShapeDtypeStruct((VEC_ROWS + shard, 3 * width // 2), BF),
+            jax.ShapeDtypeStruct((shard, 3 * width + half), BF),
+        ],
+        compiler_params=params("arbitrary"),
+        cost_estimate=cost(0, 5 * shard * width * 8),
+        name="pack_weights",
+    )(core, qkv, small, proj, fc1, fc2)
+
+
+def project_kernel(tok_ref, w_ref, bias_ref, vec_ref, out_ref, out_t_ref):
+    unit, _ = normalised(tok_ref[...].astype(F32))
+    normed = (unit * vec_ref[0:1, :] + vec_ref[1:2, :]).astype(BF)
+    packed = dot(normed, w_ref[...]) + bias_ref[0:1, :]
+    out_ref[...] = packed.astype(BF)
+    out_t_ref[...] = packed.T.astype(BF)
+
+
+def project(tokens, weight, bias, vec):
+    rows, width = tokens.shape
+    wide = weight.shape[1]
+    bt = 256
+    return pl.pallas_call(
+        project_kernel,
+        grid=(rows // bt,),
+        in_specs=[
+            pl.BlockSpec((bt, width), lambda i: (i, 0)),
+            whole(weight.shape),
+            whole(bias.shape),
+            whole(vec.shape),
+        ],
+        out_specs=[
+            pl.BlockSpec((bt, wide), lambda i: (i, 0)),
+            pl.BlockSpec((wide, bt), lambda i: (0, i)),
+        ],
+        out_shape=[
+            jax.ShapeDtypeStruct((rows, wide), BF),
+            jax.ShapeDtypeStruct((wide, rows), BF),
+        ],
+        compiler_params=params("arbitrary"),
+        cost_estimate=cost(2 * rows * width * wide, 12 * rows * width),
+        name="project",
+    )(tokens, weight, bias, vec)
+
+
+def gather_line(value):
+    owners = lax.axis_size("fsdp")
+    lines = owners // 2
+    at = lax.axis_index("fsdp")
+    line, odd = at // 2, lax.rem(at, 2)
+    other = lax.ppermute(value, "fsdp", [(f, f ^ 1) for f in range(owners)])
+    pair = jnp.stack([jnp.where(odd == 0, value, other), jnp.where(odd == 0, other, value)])
+    ups, downs = [pair], [pair]
+    for hop in range(1, lines):
+        up = [(f, f + 2) for f in range(owners - 2) if f // 2 >= hop - 1]
+        down = [(f, f - 2) for f in range(2, owners) if f // 2 <= lines - hop]
+        ups.append(lax.ppermute(ups[-1], "fsdp", up))
+        downs.append(lax.ppermute(downs[-1], "fsdp", down))
+    gathered = []
+    for target in range(lines):
+        options = [
+            downs[target - here] if here < target else ups[here - target] for here in range(lines)
+        ]
+        gathered.append(choose_at(line, options))
+    return jnp.stack(gathered).reshape(owners, *value.shape)
+
+
+def choose_at(index, options):
+    out = options[-1]
+    for at in range(len(options) - 2, -1, -1):
+        out = jnp.where(index == at, options[at], out)
+    return out
 
 
 def per_device(
@@ -635,62 +756,50 @@
     def pick(value, at, axis):
         return lax.dynamic_index_in_dim(value, at, axis, keepdims=False)
 
-    qkv_half = pick(qkv_weight.reshape(shard, 3, 2, part), core, 2).reshape(shard, 3 * part)
-    small = jnp.concatenate(
-        [
-            norm1_gain, norm1_bias, query_bias, value_bias, proj_bias, norm2_gain, norm2_bias,
-            fc2_bias, fc1_bias,
-        ]
-    )
-    small_row = jnp.zeros((VEC_ROWS, 3 * part), BF).at[0, : small.shape[0]].set(small)
-    first = lax.all_gather(
-        jnp.concatenate([qkv_half, small_row], axis=0), "fsdp", axis=0, tiled=False
-    )
-    fc1_half = pick(fc1_weight.reshape(shard, owners, 2, 2, quarter), core, 2)
-    fc1_half = fc1_half.transpose(0, 2, 1, 3).reshape(shard, half)
-    fc2_half = lax.dynamic_slice_in_dim(fc2_weight, core * 2 * quarter, 2 * quarter, 0)
-    fc2_half = fc2_half.reshape(2, quarter, width).transpose(1, 0, 2).reshape(shard, 2 * width)
-    second = lax.all_gather(
-        jnp.concatenate([proj_weight, fc1_half, fc2_half], axis=1), "fsdp", axis=0, tiled=True
-    )
-
-    def collect(value):
+    place_row = place.reshape(1).astype(jnp.int32)
+    core_row = core.reshape(1).astype(jnp.int32)
+    small = [
+        norm1_gain, norm1_bias, query_bias, value_bias, proj_bias, norm2_gain, norm2_bias,
+        fc2_bias, fc1_bias,
+    ]
+    small_rows = jnp.stack([jnp.pad(vector, (0, 3 * part - vector.shape[0])) for vector in small])
+    small_rows = jnp.pad(small_rows, ((0, VEC_ROWS - len(small)), (0, 0)))
+    one, two = pack_weights(core_row, qkv_weight, small_rows, proj_weight, fc1_weight, fc2_weight)
+    second = lax.all_gather(two, "fsdp", axis=0, tiled=True)
+    first = gather_line(one)
+
+    def collect(value, theirs):
         mine = pick(value, image, 0)
-        theirs = partner(pick(value, 1 - image, 0))
         return jnp.concatenate([mine, theirs, sibling(mine), sibling(theirs)], axis=0)
 
-    tok = collect(tokens)
-    kept = pick(counts, image, 0)
-    kept = jnp.stack([pick(kept, place ^ at, 0) for at in (0, 2, 1, 3)])
-    core_row = core.reshape(1).astype(jnp.int32)
-
-    w_qkv = first[:, :shard].reshape(width, 3 * part)
-    vecs = first[:, shard, : small.shape[0]].astype(F32)
-    g1, b1, qb, vb, pb, g2, b2, f2b = (
-        vecs[:, at * shard : (at + 1) * shard].reshape(width) for at in range(8)
-    )
-    f1b = pick(vecs[:, 8 * shard :].reshape(owners, 2, 2, quarter), core, 1)
+    tok = collect(tokens, partner(pick(tokens, 1 - image, 0)))
+    w_qkv = first[:, VEC_ROWS:].reshape(width, 3 * part)
+    vecs = first[:, :8, :shard].astype(F32).transpose(1, 0, 2).reshape(8, width)
+    g1, b1, qb, vb, pb, g2, b2, f2b = vecs
+    f1b = first[:, 8, :ff_shard].astype(F32)
+    f1b = pick(f1b.reshape(owners, 2, 2, quarter), core, 1)
     f1b = f1b.transpose(1, 0, 2).reshape(1, half)
 
     def mine_of(vector):
         return lax.dynamic_slice_in_dim(vector, core * part, part, 0)
 
     qkv_bias = jnp.concatenate([mine_of(qb), jnp.zeros((part,), F32), mine_of(vb)])
-    unit, _ = normalised(tok.astype(F32))
-    normed = (unit * g1 + b1).astype(BF)
-    packed = (jnp.dot(normed, w_qkv, preferred_element_type=F32) + qkv_bias).astype(BF)
-    packed_t = packed.T
-    mixed, result_t, log_total = attend_forward(kept, packed, packed_t, slots)
+    vec_one = jnp.concatenate([jnp.stack([g1, b1]), jnp.zeros((6, width), F32)])
+    packed, packed_t = project(tok, w_qkv, qkv_bias.reshape(1, 3 * part), vec_one)
+    cot_theirs = partner(pick(cotangent, 1 - image, 0))
+    packed, cot_theirs = lax.optimization_barrier((packed, cot_theirs))
+    mixed, result_t, log_total = attend_forward(counts, place_row, packed, packed_t, slots)
     mixed_sib = sibling(mixed)
 
-    cot = collect(cotangent)
+    cot = collect(cotangent, cot_theirs)
     wp = second[:, :width]
     wp_own = lax.dynamic_slice_in_dim(wp, core * part, part, 0)
     wp_sib = lax.dynamic_slice_in_dim(wp, (1 - core) * part, part, 0)
     vec_two = jnp.concatenate([jnp.stack([pb, g2, b2]), jnp.zeros((5, width), F32)])
-    middle, out_part, gn_part, dw1, dw2, gf1, gf2 = feed_forward(
+    middle, out_part, gn_part, dw_ff, gf1, gf2 = feed_forward(
         tok, mixed, mixed_sib, cot, wp_own, wp_sib, second, vec_two, f1b
     )
+    scattered_one = lax.psum_scatter(dw_ff, "fsdp", scatter_dimension=0, tiled=True)
     gn_sib = sibling(gn_part)
     rows_own = 2 * slots
     out_sib = sibling(out_part[rows_own:])
@@ -714,14 +823,10 @@
         jnp.concatenate([dwp_own, dwp_sib], axis=0),
         jnp.concatenate([dwp_sib, dwp_own], axis=0),
     )
-    dw2 = dw2.reshape(2, owners, quarter, width).transpose(1, 2, 0, 3).reshape(width, 2 * width)
-    scattered_one = lax.psum_scatter(
-        jnp.concatenate([dwp, dw1, dw2], axis=1), "fsdp", scatter_dimension=0, tiled=True
-    )
+    grad_mixed, output = lax.optimization_barrier((grad_mixed, output))
     gq, gk, gv = attend_backward(
-        kept, packed, packed_t, grad_mixed, grad_mixed_t, result_t, log_total, slots
-    )
-    vec_one = jnp.concatenate([jnp.stack([g1, b1]), jnp.zeros((6, width), F32)])
+        counts, place_row, packed, packed_t, grad_mixed, grad_mixed_t, result_t, log_total, slots
+    )
     gn1_own, gn1_send, dw_qkv, vec_first, vec_qv = project_back(tok, gq, gk, gv, w_qkv, vec_one)
 
     def spread(vector):
@@ -740,23 +845,21 @@
     gf1b = lax.dynamic_update_index_in_dim(
         jnp.zeros((owners, 2, 2, quarter), F32), gf1b, core, 1
     ).reshape(owners, ff_shard)
-    small_grads = jnp.concatenate(
+    wide = 4 * part
+    small_grads = jnp.stack(
+        [gg1, gb1, spread(gqb), spread(gvb), gpb, gg2, gb2, gf2b]
+    ).reshape(8, owners, shard).transpose(1, 0, 2)
+    small_block = jnp.concatenate(
         [
-            vector.reshape(owners, shard)
-            for vector in (gg1, gb1, spread(gqb), spread(gvb), gpb, gg2, gb2, gf2b)
-        ]
-        + [gf1b],
+            jnp.pad(small_grads, ((0, 0), (0, 0), (0, wide - shard))),
+            jnp.pad(gf1b[:, None], ((0, 0), (0, VEC_ROWS - 9), (0, wide - ff_shard))),
+        ],
         axis=1,
     ).astype(BF)
-    small_block = (
-        jnp.zeros((owners, VEC_ROWS, 3 * part), BF).at[:, 0, : small.shape[0]].set(small_grads)
-    )
-    scattered_two = lax.psum_scatter(
-        jnp.concatenate([dw_qkv.reshape(owners, shard, 3 * part), small_block], axis=1),
-        "fsdp",
-        scatter_dimension=0,
-        tiled=False,
-    )
+    dw_attend = jnp.concatenate([dw_qkv, dwp], axis=1).reshape(owners, shard, wide)
+    block_two = jnp.concatenate([small_block, dw_attend], axis=1)
+    block_two, scattered_one = lax.optimization_barrier((block_two, scattered_one))
+    scattered_two = lax.psum_scatter(block_two, "fsdp", scatter_dimension=0, tiled=False)
 
     gn1 = gn1_own + sibling(gn1_send).astype(F32)
     unit_own, inverse_own = normalised(tok[:rows_own].astype(F32))
@@ -773,25 +876,30 @@
 
     one_mine, one_other = finish(scattered_one)
     lower, upper = in_order(one_mine, one_other)
-    grad_proj = jnp.concatenate([lower[:, :part], upper[:, :part]], axis=1)
 
     def fc1_of(value):
-        return value[:, part : part + half].reshape(shard, 2, owners, quarter).transpose(0, 2, 1, 3)
+        return value[:, :half].reshape(shard, 2, owners, quarter).transpose(0, 2, 1, 3)
 
     grad_fc1 = jnp.stack([fc1_of(lower), fc1_of(upper)], axis=2).reshape(shard, ff)
 
     def fc2_of(value):
-        return value[:, part + half :].reshape(quarter, 2, width).transpose(1, 0, 2)
+        return value[:, half:].reshape(quarter, 2, width).transpose(1, 0, 2)
 
     grad_fc2 = jnp.stack([fc2_of(lower), fc2_of(upper)]).reshape(ff_shard, width)
     two_mine, two_other = finish(scattered_two)
-    lower, upper = in_order(two_mine[:shard], two_other[:shard])
-    grad_qkv = jnp.stack(
-        [lower.reshape(shard, 3, part), upper.reshape(shard, 3, part)], axis=2
-    ).reshape(shard, 6 * part)
-    small_sum = two_mine[shard] + two_other[shard]
-    s = [small_sum[at * shard : (at + 1) * shard] for at in range(8)]
-    grad_f1b = small_sum[8 * shard : 8 * shard + ff_shard]
+    lower, upper = in_order(two_mine[VEC_ROWS:], two_other[VEC_ROWS:])
+    grad_qkv = jnp.concatenate(
+        [
+            value[:, at * part : (at + 1) * part]
+            for at in range(3)
+            for value in (lower, upper)
+        ],
+        axis=1,
+    )
+    grad_proj = jnp.concatenate([lower[:, 3 * part :], upper[:, 3 * part :]], axis=1)
+    small_sum = two_mine[:VEC_ROWS] + two_other[:VEC_ROWS]
+    s = [small_sum[at, :shard] for at in range(8)]
+    grad_f1b = small_sum[8, :ff_shard]
     return (
         output,
         input_grad,

time: 547 us -> 513 us (0.938)
  local copies, waits for them, and re-layouts: 55.8 us -> 30 us
  waiting for transfers between devices: 209 us -> 186 us
  Pallas kernels: 200 us -> 214 us
  starting transfers between devices: 12.5 us -> 23.6 us
  matrix products: 8.83 us -> 0 us
    ppermute x0 -> x7, waiting for transfers between devices: none -> 78.1 us  [the longest x3 74.1 us: gather_line(): downs.append(lax.ppermute(downs[-1], 'fsdp', down))]
    reduce_scatter x2, waiting for transfers between devices: 111 us -> 38.1 us  [the longest x1 38.1 us: per_device(): lax.psum_scatter(block_two, 'fsdp', scatter_dimension=0, tiled=False)]
    all_gather x2 -> x1, waiting for transfers between devices: 34.1 us -> 0.01 us  [per_device(): second = lax.all_gather(two, 'fsdp', axis=0, tiled=True)]
    ppermute x0 -> x7, starting transfers between devices: none -> 14.4 us  [the longest x3 7.53 us: gather_line(): ups.append(lax.ppermute(ups[-1], 'fsdp', up))]
    pallas_call x0 -> x2, Pallas kernels: none -> 14.2 us  [the longest x1 11.6 us: project(): pl.pallas_call(project_kernel, grid=(rows // bt,), in_specs=[pl.BlockSpec...]
    dot_general x1 -> x0, matrix products: 8.83 us -> none  [per_device(): jnp.dot(normed, w_qkv, preferred_element_type=F32) + qkv_bias]
    ppermute x6, waiting for transfers between devices: 52.1 us -> 60 us  [partner(): return lax.ppermute(value, 'seq', to_partner)]
    concatenate x11 -> x0, local copies, waits for them, and re-layouts: 7.02 us -> none  [the longest x1 6.16 us: per_device(): jnp.concatenate([norm1_gain, norm1_bias, query_bias, value_bias, proj_bia...]
  transfers between devices with their start and end apart: 20 -> 26, of which waited for: 13 -> 14; matrix products, arithmetic and copies ran while one was open for 14% -> 10% of each run, Pallas kernels for 8% -> 31%
where the time goes in v2:
time: 513 us; the launch traced here: 505 us
  Pallas kernels  214 us (42%)
  waiting for transfers between devices  186 us (36%)
  other arithmetic  36.9 us (7%)
  local copies, waits for them, and re-layouts  30 us (6%)
  starting transfers between devices  23.6 us (5%)
  between operations  14.9 us (3%)
    ppermute x3, waiting for transfers between devices, gather_line(): downs.append(lax.ppermute(downs[-1], 'fsdp', down))  74.1 us
    pallas_call x1, Pallas kernels, attend_backward(): pl.pallas_call(kernel, grid=(pairs, keys // bq), in_specs=[pl.BlockSpec(m...  66.7 us
    ppermute x6, waiting for transfers between devices, partner(): return lax.ppermute(value, 'seq', to_partner)  60 us
    pallas_call x1, Pallas kernels, feed_forward(): pl.pallas_call(kernel, grid=(blocks,), in_specs=[pl.BlockSpec((bt, width)...  55.7 us
    pallas_call x1, Pallas kernels, attend_forward(): pl.pallas_call(kernel, grid=(pairs, keys // bq), in_specs=[pl.BlockSpec(m...  42.2 us
    reduce_scatter x1, waiting for transfers between devices, per_device(): lax.psum_scatter(block_two, 'fsdp', scatter_dimension=0, tiled=False)  38.1 us
    pallas_call x1, Pallas kernels, project_back(): pl.pallas_call(project_back_kernel, grid=(blocks,), in_specs=[pl.BlockSpe...  18.5 us
    pallas_call x1, Pallas kernels, branch(): pl.pallas_call(branch_kernel, grid=(blocks,), in_specs=[pl.BlockSpec(memo...  16.7 us
  transfers between devices with their start and end apart: 26, of which 14 were waited for; matrix products, arithmetic and copies ran while one was open for 10% of the time, Pallas kernels for 31%

profile of v2, /device:TPU:0, one launch (start us, length us, event | category | flops | bytes accessed | tf_op | source)
XLA Modules:
  0.0 504.9 jit_solution(13825139941545453962)
XLA Ops:
  16.9 3.0 collective-permute-start.3
  22.4 3.9 collective-permute-done.3
  27.8 4.6 collective-permute-start.4
  32.4 7.7 %collective-permute-done = bf16[512,768]{1,0:T(8,128)(2,1)S(1)} collective-permute-done((bf16[512,768]{1,0:T(8,128)(2,1)}, bf16[512,768]{1,0:T(8,128)(2,1)S(1)}, u32[]{:S(2)}, u32[]{:S(2)}) %collective-permute-start) | collective-permute-done | bytes 786464 | tf_op jit(solution)/shard_map/ppermute | solution.py:754
  40.1 23.4 %collective-permute-done.7 = bf16[2,112,1152]{2,1,0:T(8,128)(2,1)S(1)} collective-permute-done((bf16[2,112,1152]{2,1,0:T(8,128)(2,1)S(1)}, bf16[2,112,1152]{2,1,0:T(8,128)(2,1)S(1)}, u32[]{:S(2)}, u32[]{:S(2)}) %collective-permute-start.7) | collective-permute-done | bytes 516128 | tf_op jit(solution)/shard_map/ppermute | solution.py:700
  66.3 21.8 %collective-permute-done.8 = bf16[2,112,1152]{2,1,0:T(8,128)(2,1)} collective-permute-done((bf16[2,112,1152]{2,1,0:T(8,128)(2,1)S(1)}, bf16[2,112,1152]{2,1,0:T(8,128)(2,1)}, u32[]{:S(2)}, u32[]{:S(2)}) %collective-permute-start.8) | collective-permute-done | bytes 516128 | tf_op jit(solution)/shard_map/ppermute | solution.py:700
  94.5 6.5 %pad_maximum_fusion.tok_ref = bf16[2048,768]{1,0:T(8,128)(2,1)} fusion(bf16[512,768]{1,0:T(8,128)(2,1)} %collective-permute-done.2, bf16[512,768]{1,0:T(8,128)(2,1)} %collective-permute-done.1, bf16[512,768]{1,0:T(8,128)(2,1)S(1)} %collective-permute-done, bf16[512,768]{1,0:T(8,128)(2,1)S(1)} %get-tuple-element.89), kind=kLoop, calls=%fused_computation.17 | loop fusion | flops 12582912 | bytes 6291456 | tf_op jit(solution)/shard_map/concatenate | solution.py:773
  101.0 28.9 %collective-permute-done.9 = bf16[2,112,1152]{2,1,0:T(8,128)(2,1)} collective-permute-done((bf16[2,112,1152]{2,1,0:T(8,128)(2,1)}, bf16[2,112,1152]{2,1,0:T(8,128)(2,1)}, u32[]{:S(2)}, u32[]{:S(2)}) %collective-permute-start.9) | collective-permute-done | bytes 516128 | tf_op jit(solution)/shard_map/ppermute | solution.py:700
  135.3 11.6 %project.1 = (bf16[2048,1152]{1,0:T(8,128)(2,1)}, bf16[1152,2048]{1,0:T(8,128)(2,1)}) custom-call(bf16[2048,768]{1,0:T(8,128)(2,1)} %pad_maximum_fusion.tok_ref, bf16[768,1152]{1,0:T(8,128)(2,1)} %bitcast.91, f32[1,1152]{1,0:T(1,128)} %reshape.150.bias_ref, f32[8,768]{1,0:T(8,128)} %maximum_maximum_fusion.vec_ref), custom_call_target="tpu_custom_call" | custom-call | flops 3623878656 | bytes 18874368 | tf_op jit(solution)/shard_map/project/pallas_call | solution.py:665
  146.9 42.2 %attend_forward.1 = (bf16[2048,384]{1,0:T(8,128)(2,1)}, f32[384,2048]{1,0:T(8,128)}, f32[3,8,2048]{2,1,0:T(8,128)}) custom-call(s32[2,4]{1,0:T(2,128)} %counts_ref.3, s32[1]{0:T(128)} %bitcast.3.place_ref, bf16[2048,1152]{1,0:T(8,128)(2,1)} %get-tuple-element.50.k_ref.q_ref.v_ref, bf16[1152,2048]{1,0:T(8,128)(2,1)} %get-tuple-element.51.qt_ref.vt_ref.kt_ref, ...), custom_call_target="tpu_custom_call" | custom-call | flops 25769803776 | bytes 9437184 | tf_op jit(solution)/shard_map/attend_forward/pallas_call | solution.py:163
  191.5 3.0 collective-permute-done.12
  195.1 3.1 pad_maximum_fusion.1.cot_ref
  200.6 55.7 %feed_forward.1 = (f32[2048,768]{1,0:T(8,128)}, bf16[2048,768]{1,0:T(8,128)(2,1)}, bf16[2048,768]{1,0:T(8,128)(2,1)}, bf16[768,3072]{1,0:T(8,128)(2,1)}, f32[8,1536]{1,0:T(8,128)}, /*index=5*/f32[8,768]{1,0:T(8,128)}) custom-call(bf16[2048,768]{1,0:T(8,128)(2,1)} %pad_maximum_fusion.tok_ref, bf16[2048,384]{1,0:T(8,128)(2,1)} %get-tuple-element.52.mo_ref, ...), custom_call_target="tpu_custom_call" | custom-call | flops 31406948352 | bytes 40894464 | tf_op jit(solution)/shard_map/feed_forward/pallas_call | solution.py:383
  259.7 3.2 collective-permute-done.15
  267.9 17.7 %collective-permute-done.16 = bf16[512,768]{1,0:T(8,128)(2,1)S(1)} collective-permute-done((bf16[512,768]{1,0:T(8,128)(2,1)S(1)}, bf16[512,768]{1,0:T(8,128)(2,1)S(1)}, u32[]{:S(2)}, u32[]{:S(2)}) %collective-permute-start.16) | collective-permute-done | bytes 786464 | tf_op jit(solution)/shard_map/ppermute | solution.py:754
  287.0 16.7 %branch.1 = (f32[1024,768]{1,0:T(8,128)}, bf16[2048,384]{1,0:T(8,128)(2,1)}, bf16[384,2048]{1,0:T(8,128)(2,1)}, bf16[384,384]{1,0:T(8,128)(2,1)}, bf16[384,384]{1,0:T(8,128)(2,1)}, /*index=5*/f32[24,768]{1,0:T(8,128)}) custom-call(s32[1]{0:T(128)} %bitcast.core_ref, f32[2048,768]{1,0:T(8,128)} %get-tuple-element.55.mid_ref, ...), custom_call_target="tpu_custom_call" | custom-call | flops 3623878656 | bytes 28311552 | tf_op jit(solution)/shard_map/branch/pallas_call | solution.py:475
  303.7 66.7 %attend_backward.1 = (bf16[2048,384]{1,0:T(8,128)(2,1)}, bf16[2048,384]{1,0:T(8,128)(2,1)}, bf16[2048,384]{1,0:T(8,128)(2,1)}) custom-call(s32[2,4]{1,0:T(2,128)} %counts_ref.3, s32[1]{0:T(128)} %bitcast.3.place_ref, bf16[2048,1152]{1,0:T(8,128)(2,1)} %get-tuple-element.50.k_ref.q_ref.v_ref, bf16[2048,1152]{1,0:T(8,128)(2,1)} %get-tuple-element.50.k_ref.q_ref.v_ref, ...), custom_call_target="tpu_custom_call" | custom-call | flops 64424509440 | bytes 18874368 | tf_op jit(solution)/shard_map/attend_backward/pallas_call | solution.py:260
  370.4 18.5 %project_back.1 = (f32[1024,768]{1,0:T(8,128)}, bf16[1024,768]{1,0:T(8,128)(2,1)}, bf16[768,1152]{1,0:T(8,128)(2,1)}, f32[16,768]{1,0:T(8,128)}, f32[16,384]{1,0:T(8,128)}) custom-call(bf16[2048,768]{1,0:T(8,128)(2,1)} %pad_maximum_fusion.tok_ref, bf16[2048,384]{1,0:T(8,128)(2,1)} %get-tuple-element.65.gq_ref, bf16[2048,384]{1,0:T(8,128)(2,1)} %get-tuple-element.66.gk_ref, ...), custom_call_target="tpu_custom_call" | custom-call | flops 7247757312 | bytes 22020096 | tf_op jit(solution)/shard_map/project_back/pallas_call | solution.py:567
  398.7 3.9 fusion.15
  407.1 12.0 %collective-permute-done.21 = bf16[96,3072]{1,0:T(8,128)(2,1)S(1)} collective-permute-done((bf16[96,3072]{1,0:T(8,128)(2,1)}, bf16[96,3072]{1,0:T(8,128)(2,1)S(1)}, u32[]{:S(2)}, u32[]{:S(2)}) %collective-permute-start.21) | collective-permute-done | bytes 589856 | tf_op jit(solution)/shard_map/ppermute | solution.py:754
  420.0 15.1 %collective-permute-done.18 = bf16[512,768]{1,0:T(8,128)(2,1)S(1)} collective-permute-done((bf16[512,768]{1,0:T(8,128)(2,1)S(1)}, bf16[512,768]{1,0:T(8,128)(2,1)S(1)}, u32[]{:S(2)}, u32[]{:S(2)}) %collective-permute-start.18) | collective-permute-done | bytes 786464 | tf_op jit(solution)/shard_map/ppermute | solution.py:754
  437.2 38.1 %reduce-scatter.5.cloned.1.call-done = bf16[1,112,1536]{2,1,0:T(8,128)(2,1)} async-done(((bf16[8,112,1536]{2,1,0:T(8,128)(2,1)}), bf16[1,112,1536]{2,1,0:T(8,128)(2,1)}) %reduce-scatter.5.cloned.1.call-update) | async-done | bytes 344080 | tf_op jit(solution)/shard_map/reduce_scatter | solution.py:862
  477.0 7.4 %collective-permute-done.19 = bf16[112,1536]{1,0:T(8,128)(2,1)S(1)} collective-permute-done((bf16[112,1536]{1,0:T(8,128)(2,1)}, bf16[112,1536]{1,0:T(8,128)(2,1)S(1)}, u32[]{:S(2)}, u32[]{:S(2)}) %collective-permute-start.19) | collective-permute-done | bytes 344096 | tf_op jit(solution)/shard_map/ppermute | solution.py:754
  491.3 3.2 reshape.159
  (224 shorter events, 72.1 us)
Async XLA Ops:
  7.2 191.0 %all-gather.2.cloned.1.call-start = ((), (), s32[]{:S(2)}) async-start(), calls=%async_computation.2 | async-start | bytes 6635520 | tf_op jit(solution)/shard_map/all_gather | solution.py:768
  16.8 378.2 %reduce-scatter.3.cloned.1.call-start = ((), (), s32[]{:S(2)}) async-start(), calls=%async_computation.3 | async-start | bytes 5308416 | tf_op jit(solution)/shard_map/reduce_scatter | solution.py:802
  16.9 9.5 %collective-permute-start.3 = (bf16[112,1152]{1,0:T(8,128)(2,1)}, bf16[112,1152]{1,0:T(8,128)(2,1)S(1)}, u32[]{:S(2)}, u32[]{:S(2)}) collective-permute-start(bf16[112,1152]{1,0:T(8,128)(2,1)} %get-tuple-element.48), channel_id=1, source_target_pairs={{0,4},{4,0},{8,12},{12,8},{16,20},{20,16},{24,28},{28,24},{1,5},{5... | collective-permute-start | bytes 774152 | tf_op jit(solution)/shard_map/ppermute | solution.py:693
  20.9 19.2 %collective-permute-start = (bf16[512,768]{1,0:T(8,128)(2,1)}, bf16[512,768]{1,0:T(8,128)(2,1)S(1)}, u32[]{:S(2)}, u32[]{:S(2)}) collective-permute-start(bf16[512,768]{1,0:T(8,128)(2,1)} %get-tuple-element.90), channel_id=1, source_target_pairs={{0,2},{1,3},{2,0},{3,1},{4,6},{5,7},{6,4},{7,5},{8,10},{9,11},{10,... | collective-permute-start | bytes 2359304 | tf_op jit(solution)/shard_map/ppermute | solution.py:754
  26.4 37.1 %collective-permute-start.7 = (bf16[2,112,1152]{2,1,0:T(8,128)(2,1)S(1)}, bf16[2,112,1152]{2,1,0:T(8,128)(2,1)S(1)}, u32[]{:S(2)}, u32[]{:S(2)}) collective-permute-start(bf16[2,112,1152]{2,1,0:T(8,128)(2,1)S(1)} %pad_maximum_fusion.7), channel_id=1, source_target_pairs={{8,0},{12,4},{16,8},{20,12},{24,16},{28,20},{9,1},{13,5},{17,9},{2... | collective-permute-start | bytes 1548296 | tf_op jit(solution)/shard_map/ppermute | solution.py:700
  27.8 37.1 %collective-permute-start.4 = (bf16[2,112,1152]{2,1,0:T(8,128)(2,1)S(1)}, bf16[2,112,1152]{2,1,0:T(8,128)(2,1)S(1)}, u32[]{:S(2)}, u32[]{:S(2)}) collective-permute-start(bf16[2,112,1152]{2,1,0:T(8,128)(2,1)S(1)} %pad_maximum_fusion.7), channel_id=1, source_target_pairs={{0,8},{4,12},{8,16},{12,20},{16,24},{20,28},{1,9},{5,13},{9,17},{1... | collective-permute-start | bytes 1548296 | tf_op jit(solution)/shard_map/ppermute | solution.py:699
  32.3 62.2 %collective-permute-start.1 = (bf16[512,768]{1,0:T(8,128)(2,1)S(1)}, bf16[512,768]{1,0:T(8,128)(2,1)}, u32[]{:S(2)}, u32[]{:S(2)}) collective-permute-start(bf16[512,768]{1,0:T(8,128)(2,1)S(1)} %get-tuple-element.89), channel_id=1, source_target_pairs={{0,1},{1,0},{2,3},{3,2},{4,5},{5,4},{6,7},{7,6},{8,9},{9,8},{10,11... | collective-permute-start | bytes 2359304 | tf_op jit(solution)/shard_map/ppermute | solution.py:751
  40.1 54.4 %collective-permute-start.2 = (bf16[512,768]{1,0:T(8,128)(2,1)S(1)}, bf16[512,768]{1,0:T(8,128)(2,1)}, u32[]{:S(2)}, u32[]{:S(2)}) collective-permute-start(bf16[512,768]{1,0:T(8,128)(2,1)S(1)} %collective-permute-done), channel_id=1, source_target_pairs={{0,1},{1,0},{2,3},{3,2},{4,5},{5,4},{6,7},{7,6},{8,9},{9,8},{10,11... | collective-permute-start | bytes 2359304 | tf_op jit(solution)/shard_map/ppermute | solution.py:751
  63.5 24.6 %collective-permute-start.8 = (bf16[2,112,1152]{2,1,0:T(8,128)(2,1)S(1)}, bf16[2,112,1152]{2,1,0:T(8,128)(2,1)}, u32[]{:S(2)}, u32[]{:S(2)}) collective-permute-start(bf16[2,112,1152]{2,1,0:T(8,128)(2,1)S(1)} %collective-permute-done.7), channel_id=1, source_target_pairs={{8,0},{12,4},{16,8},{20,12},{9,1},{13,5},{17,9},{21,13},{10,2},{14... | collective-permute-start | bytes 1548296 | tf_op jit(solution)/shard_map/ppermute | solution.py:700
  64.9 24.5 %collective-permute-start.5 = (bf16[2,112,1152]{2,1,0:T(8,128)(2,1)S(1)}, bf16[2,112,1152]{2,1,0:T(8,128)(2,1)}, u32[]{:S(2)}, u32[]{:S(2)}) collective-permute-start(bf16[2,112,1152]{2,1,0:T(8,128)(2,1)S(1)} %collective-permute-done.4), channel_id=1, source_target_pairs={{8,16},{12,20},{16,24},{20,28},{9,17},{13,21},{17,25},{21,29},{10,... | collective-permute-start | bytes 1548296 | tf_op jit(solution)/shard_map/ppermute | solution.py:699
  88.1 41.8 %collective-permute-start.9 = (bf16[2,112,1152]{2,1,0:T(8,128)(2,1)}, bf16[2,112,1152]{2,1,0:T(8,128)(2,1)}, u32[]{:S(2)}, u32[]{:S(2)}) collective-permute-start(bf16[2,112,1152]{2,1,0:T(8,128)(2,1)} %collective-permute-done.8), channel_id=1, source_target_pairs={{8,0},{12,4},{9,1},{13,5},{10,2},{14,6},{11,3},{15,7}} | collective-permute-start | bytes 1548296 | tf_op jit(solution)/shard_map/ppermute | solution.py:700
  89.4 40.5 %collective-permute-start.6 = (bf16[2,112,1152]{2,1,0:T(8,128)(2,1)}, bf16[2,112,1152]{2,1,0:T(8,128)(2,1)}, u32[]{:S(2)}, u32[]{:S(2)}) collective-permute-start(bf16[2,112,1152]{2,1,0:T(8,128)(2,1)} %collective-permute-done.5), channel_id=1, source_target_pairs={{16,24},{20,28},{17,25},{21,29},{18,26},{22,30},{19,27},{23,31}} | collective-permute-start | bytes 1548296 | tf_op jit(solution)/shard_map/ppermute | solution.py:699
  93.2 53.6 %collective-permute-start.10 = (bf16[512,768]{1,0:T(8,128)(2,1)}, bf16[512,768]{1,0:T(8,128)(2,1)}, u32[]{:S(2)}, u32[]{:S(2)}) collective-permute-start(bf16[512,768]{1,0:T(8,128)(2,1)} %get-tuple-element.88), channel_id=1, source_target_pairs={{0,2},{1,3},{2,0},{3,1},{4,6},{5,7},{6,4},{7,5},{8,10},{9,11},{10,... | collective-permute-start | bytes 2359304 | tf_op jit(solution)/shard_map/ppermute | solution.py:754
  189.1 11.5 %collective-permute-start.11 = (bf16[2048,384]{1,0:T(8,128)(2,1)}, bf16[2048,384]{1,0:T(8,128)(2,1)}, u32[]{:S(2)}, u32[]{:S(2)}) collective-permute-start(bf16[2048,384]{1,0:T(8,128)(2,1)} %get-tuple-element.52.mo_ref), channel_id=1, source_target_pairs={{0,1},{1,0},{2,3},{3,2},{4,5},{5,4},{6,7},{7,6},{8,9},{9,8},{10,11... | collective-permute-start | bytes 4718600 | tf_op jit(solution)/shard_map/ppermute | solution.py:751
  189.1 5.4 %collective-permute-start.12 = (bf16[512,768]{1,0:T(8,128)(2,1)S(1)}, bf16[512,768]{1,0:T(8,128)(2,1)}, u32[]{:S(2)}, u32[]{:S(2)}) collective-permute-start(bf16[512,768]{1,0:T(8,128)(2,1)S(1)} %get-tuple-element.87), channel_id=1, source_target_pairs={{0,1},{1,0},{2,3},{3,2},{4,5},{5,4},{6,7},{7,6},{8,9},{9,8},{10,11... | collective-permute-start | bytes 2359304 | tf_op jit(solution)/shard_map/ppermute | solution.py:751
  189.6 5.5 %collective-permute-start.13 = (bf16[512,768]{1,0:T(8,128)(2,1)}, bf16[512,768]{1,0:T(8,128)(2,1)}, u32[]{:S(2)}, u32[]{:S(2)}) collective-permute-start(bf16[512,768]{1,0:T(8,128)(2,1)} %collective-permute-done.10), channel_id=1, source_target_pairs={{0,1},{1,0},{2,3},{3,2},{4,5},{5,4},{6,7},{7,6},{8,9},{9,8},{10,11... | collective-permute-start | bytes 2359304 | tf_op jit(solution)/shard_map/ppermute | solution.py:751
  259.2 27.7 %collective-permute-start.14 = (bf16[2048,768]{1,0:T(8,128)(2,1)}, bf16[2048,768]{1,0:T(8,128)(2,1)}, u32[]{:S(2)}, u32[]{:S(2)}) collective-permute-start(bf16[2048,768]{1,0:T(8,128)(2,1)} %get-tuple-element.56.ga_ref), channel_id=1, source_target_pairs={{0,1},{1,0},{2,3},{3,2},{4,5},{5,4},{6,7},{7,6},{8,9},{9,8},{10,11... | collective-permute-start | bytes 9437192 | tf_op jit(solution)/shard_map/ppermute | solution.py:751
  266.0 19.6 %collective-permute-start.16 = (bf16[512,768]{1,0:T(8,128)(2,1)S(1)}, bf16[512,768]{1,0:T(8,128)(2,1)S(1)}, u32[]{:S(2)}, u32[]{:S(2)}) collective-permute-start(bf16[512,768]{1,0:T(8,128)(2,1)S(1)} %get-tuple-element.86), channel_id=1, source_target_pairs={{0,2},{1,3},{2,0},{3,1},{4,6},{5,7},{6,4},{7,5},{8,10},{9,11},{10,... | collective-permute-start | bytes 2359304 | tf_op jit(solution)/shard_map/ppermute | solution.py:754
  267.6 207.7 %reduce-scatter.5.cloned.1.call-start = ((), (), s32[]{:S(2)}) async-start(), calls=%async_computation.4 | async-start | bytes 3096576 | tf_op jit(solution)/shard_map/reduce_scatter | solution.py:862
  402.7 16.4 %collective-permute-start.21 = (bf16[96,3072]{1,0:T(8,128)(2,1)}, bf16[96,3072]{1,0:T(8,128)(2,1)S(1)}, u32[]{:S(2)}, u32[]{:S(2)}) collective-permute-start(bf16[96,3072]{1,0:T(8,128)(2,1)} %reduce-scatter.3.cloned.1.call-done), channel_id=1, source_target_pairs={{0,2},{1,3},{2,0},{3,1},{4,6},{5,7},{6,4},{7,5},{8,10},{9,11},{10,... | collective-permute-start | bytes 1769480 | tf_op jit(solution)/shard_map/ppermute | solution.py:754
  406.4 28.7 %collective-permute-start.18 = (bf16[512,768]{1,0:T(8,128)(2,1)S(1)}, bf16[512,768]{1,0:T(8,128)(2,1)S(1)}, u32[]{:S(2)}, u32[]{:S(2)}) collective-permute-start(bf16[512,768]{1,0:T(8,128)(2,1)S(1)} %slice.220), channel_id=1, source_target_pairs={{0,2},{1,3},{2,0},{3,1},{4,6},{5,7},{6,4},{7,5},{8,10},{9,11},{10,... | collective-permute-start | bytes 2359304 | tf_op jit(solution)/shard_map/ppermute | solution.py:754
  419.9 56.8 %collective-permute-start.22 = (bf16[96,3072]{1,0:T(8,128)(2,1)S(1)}, bf16[96,3072]{1,0:T(8,128)(2,1)S(1)}, u32[]{:S(2)}, u32[]{:S(2)}) collective-permute-start(bf16[96,3072]{1,0:T(8,128)(2,1)S(1)} %fusion.14), channel_id=1, source_target_pairs={{0,1},{1,0},{2,3},{3,2},{4,5},{5,4},{6,7},{7,6},{8,9},{9,8},{10,11... | collective-permute-start | bytes 1769480 | tf_op jit(solution)/shard_map/ppermute | solution.py:751
  475.2 9.2 %collective-permute-start.19 = (bf16[112,1536]{1,0:T(8,128)(2,1)}, bf16[112,1536]{1,0:T(8,128)(2,1)S(1)}, u32[]{:S(2)}, u32[]{:S(2)}) collective-permute-start(bf16[112,1536]{1,0:T(8,128)(2,1)} %bitcast.95), channel_id=1, source_target_pairs={{0,2},{1,3},{2,0},{3,1},{4,6},{5,7},{6,4},{7,5},{8,10},{9,11},{10,... | collective-permute-start | bytes 1032200 | tf_op jit(solution)/shard_map/ppermute | solution.py:754
  485.3 9.2 %collective-permute-start.20 = (bf16[112,1536]{1,0:T(8,128)(2,1)}, bf16[112,1536]{1,0:T(8,128)(2,1)}, u32[]{:S(2)}, u32[]{:S(2)}) collective-permute-start(bf16[112,1536]{1,0:T(8,128)(2,1)} %get-tuple-element.104), channel_id=1, source_target_pairs={{0,1},{1,0},{2,3},{3,2},{4,5},{5,4},{6,7},{7,6},{8,9},{9,8},{10,11... | collective-permute-start | bytes 1032200 | tf_op jit(solution)/shard_map/ppermute | solution.py:751
  (29 other events, 504.8 us)
Sparse Core Ops, SparseCore 0:
  16.9 118.2 all-gather.1
  267.7 103.2 reduce-scatter.2
  395.2 80.0 reduce-scatter.4

commit v3 on v2

--- a/solution.py
+++ b/solution.py
@@ -251,34 +251,37 @@
         gv_ref[...] = jnp.where(lane < HEAD_DIM, acc_v[0], acc_v[1]).astype(BF)
 
 
-def attend_backward(counts, place, packed, packed_t, grad, grad_t, result_t, log_total, slots):
+def attend_backward(
+    counts, place, packed, packed_t, grad, grad_t, result_t, log_total, slots, start, count
+):
     keys, width = packed.shape
     width //= 3
     pairs = width // PAIR
     bq, chunk = 512, 256
     kernel = functools.partial(attend_backward_kernel, slots, bq, chunk)
+    at = lambda p: p + start
     return pl.pallas_call(
         kernel,
-        grid=(pairs, keys // bq),
+        grid=(count, keys // bq),
         in_specs=[
             pl.BlockSpec(memory_space=pltpu.SMEM),
             pl.BlockSpec(memory_space=pltpu.SMEM),
-            pl.BlockSpec((bq, PAIR), lambda p, i: (i, p)),
-            pl.BlockSpec((keys, PAIR), lambda p, i: (0, pairs + p)),
-            pl.BlockSpec((keys, PAIR), lambda p, i: (0, 2 * pairs + p)),
-            pl.BlockSpec((PAIR, bq), lambda p, i: (p, i)),
-            pl.BlockSpec((PAIR, keys), lambda p, i: (pairs + p, 0)),
-            pl.BlockSpec((bq, PAIR), lambda p, i: (i, p)),
-            pl.BlockSpec((PAIR, bq), lambda p, i: (p, i)),
-            pl.BlockSpec((PAIR, bq), lambda p, i: (p, i)),
-            pl.BlockSpec((1, 8, bq), lambda p, i: (p, 0, i)),
+            pl.BlockSpec((bq, PAIR), lambda p, i: (i, at(p))),
+            pl.BlockSpec((keys, PAIR), lambda p, i: (0, pairs + at(p))),
+            pl.BlockSpec((keys, PAIR), lambda p, i: (0, 2 * pairs + at(p))),
+            pl.BlockSpec((PAIR, bq), lambda p, i: (at(p), i)),
+            pl.BlockSpec((PAIR, keys), lambda p, i: (pairs + at(p), 0)),
+            pl.BlockSpec((bq, PAIR), lambda p, i: (i, at(p))),
+            pl.BlockSpec((PAIR, bq), lambda p, i: (at(p), i)),
+            pl.BlockSpec((PAIR, bq), lambda p, i: (at(p), i)),
+            pl.BlockSpec((1, 8, bq), lambda p, i: (at(p), 0, i)),
         ],
         out_specs=[
             pl.BlockSpec((bq, PAIR), lambda p, i: (i, p)),
             pl.BlockSpec((keys, PAIR), lambda p, i: (0, p)),
             pl.BlockSpec((keys, PAIR), lambda p, i: (0, p)),
         ],
-        out_shape=[jax.ShapeDtypeStruct((keys, width), BF)] * 3,
+        out_shape=[jax.ShapeDtypeStruct((keys, count * PAIR), BF)] * 3,
         scratch_shapes=[
             pltpu.VMEM((2, keys, PAIR), BF),
             pltpu.VMEM((2, keys, PAIR), BF),
@@ -287,7 +290,8 @@
         ],
         compiler_params=params("arbitrary", "arbitrary"),
         cost_estimate=cost(
-            2 * pairs * 5 * 2 * keys * keys * 256, 24 * keys * width, 2 * pairs * keys * keys
+            2 * count * 5 * 2 * keys * keys * 256, 24 * keys * count * PAIR,
+            2 * count * keys * keys,
         ),
         name="attend_backward",
     )(counts, place, packed, packed, packed, packed_t, packed_t, grad, grad_t, result_t, log_total)
@@ -312,13 +316,14 @@
 
 
 def feed_forward_kernel(
-    chunk, tok_ref, mo_ref, ms_ref, cot_ref, wpo_ref, wps_ref, g2_ref, vec_ref, f1b_ref,
-    mid_ref, out_ref, gn_ref, dw_ref, gf1_ref, gf2_ref, acc1, acc2, accb, accc
+    chunk, core_ref, tok_ref, mo_ref, ms_ref, cot_ref, wpx_ref, g2_ref, vec_ref, f1b_ref,
+    mid_ref, out_ref, gn_ref, dw_ref, gf1_ref, gf2_ref, wpo_ref, acc1, acc2, accb, accc, wps_ref
 ):
     step = pl.program_id(0)
     steps = pl.num_programs(0)
     width = tok_ref.shape[1]
     half = f1b_ref.shape[1]
+    part = width // 2
 
     @pl.when(step == 0)
     def _():
@@ -326,6 +331,12 @@
         acc2[...] = jnp.zeros_like(acc2)
         accb[...] = jnp.zeros_like(accb)
         accc[...] = jnp.zeros_like(accc)
+        here = pl.ds(pl.multiple_of(core_ref[0] * part, part), part)
+        there = pl.ds(pl.multiple_of((1 - core_ref[0]) * part, part), part)
+        wpo_ref[:, here] = g2_ref[here, :part]
+        wpo_ref[:, there] = wpx_ref[here, :]
+        wps_ref[:, here] = g2_ref[there, :part]
+        wps_ref[:, there] = wpx_ref[there, :]
 
     middle = (
         tok_ref[...].astype(F32)
@@ -342,9 +353,9 @@
     grad = None
     for at in range(half // chunk):
         cols = slice(at * chunk, (at + 1) * chunk)
-        w1 = g2_ref[:, width + at * chunk : width + (at + 1) * chunk]
+        w1 = g2_ref[:, part + at * chunk : part + (at + 1) * chunk]
         piece, row = divmod(at * chunk, width)
-        start = width + half + piece * width
+        start = part + half + piece * width
         w2 = g2_ref[row : row + chunk, start : start + width]
         hidden = dot(normed, w1) + f1b_ref[0:1, cols]
         below = 0.5 + 0.5 * lax.erf(hidden * (0.5**0.5))
@@ -373,7 +384,7 @@
         gf2_ref[...] = accc[...]
 
 
-def feed_forward(tokens, mixed_own, mixed_sib, cot, wp_own, wp_sib, weights, vec, f1b):
+def feed_forward(core, tokens, mixed_own, mixed_sib, cot, wp_other, weights, vec, f1b):
     rows, width = tokens.shape
     half = f1b.shape[1]
     heads = mixed_own.shape[1]
@@ -384,12 +395,12 @@
         kernel,
         grid=(blocks,),
         in_specs=[
+            pl.BlockSpec(memory_space=pltpu.SMEM),
             pl.BlockSpec((bt, width), lambda i: (i, 0)),
             pl.BlockSpec((bt, heads), lambda i: (i, 0)),
             pl.BlockSpec((bt, heads), lambda i: (lax.rem(i + blocks // 2, blocks), 0)),
             pl.BlockSpec((bt, width), lambda i: (i, 0)),
-            whole(wp_own.shape),
-            whole(wp_sib.shape),
+            whole(wp_other.shape),
             whole(weights.shape),
             whole(vec.shape),
             whole(f1b.shape),
@@ -401,6 +412,7 @@
             whole((width, 2 * half)),
             whole((8, half)),
             whole((8, width)),
+            whole((width // 2, width)),
         ],
         out_shape=[
             jax.ShapeDtypeStruct((rows, width), F32),
@@ -409,12 +421,14 @@
             jax.ShapeDtypeStruct((width, 2 * half), BF),
             jax.ShapeDtypeStruct((8, half), F32),
             jax.ShapeDtypeStruct((8, width), F32),
+            jax.ShapeDtypeStruct((width // 2, width), BF),
         ],
         scratch_shapes=[
             pltpu.VMEM((width, half), F32),
             pltpu.VMEM((half, width), F32),
             pltpu.VMEM((8, half), F32),
             pltpu.VMEM((8, width), F32),
+            pltpu.VMEM((width // 2, width), BF),
         ],
         compiler_params=params("arbitrary"),
         cost_estimate=cost(
@@ -422,7 +436,7 @@
             2 * rows * half,
         ),
         name="feed_forward",
-    )(tokens, mixed_own, mixed_sib, cot, wp_own, wp_sib, weights, vec, f1b)
+    )(core, tokens, mixed_own, mixed_sib, cot, wp_other, weights, vec, f1b)
 
 
 def branch_kernel(
@@ -514,13 +528,68 @@
     )(core, middle, grad_own, grad_sib, cot, mixed_own, mixed_sib, wp_own, vec)
 
 
+def weight_grad_kernel(tok_ref, gq_ref, gk_ref, gv_ref, vec_ref, dw_ref, qv_ref, accw, accqv):
+    step = pl.program_id(0)
+    steps = pl.num_programs(0)
+    part = gq_ref.shape[1]
+
+    @pl.when(step == 0)
+    def _():
+        accw[...] = jnp.zeros_like(accw)
+        accqv[...] = jnp.zeros_like(accqv)
+
+    unit, _ = normalised(tok_ref[...].astype(F32))
+    normed_t = (unit * vec_ref[0:1, :] + vec_ref[1:2, :]).astype(BF).T
+    for at, ref in enumerate((gq_ref, gk_ref, gv_ref)):
+        cols = slice(at * part, (at + 1) * part)
+        value = ref[...]
+        accw[:, cols] += dot(normed_t, value)
+        if at != 1:
+            here = 0 if at == 0 else 8
+            accqv[here : here + 8, :] += fold(value.astype(F32))
+
+    @pl.when(step == steps - 1)
+    def _():
+        dw_ref[...] = accw[...].astype(BF)
+        qv_ref[...] = accqv[...]
+
+
+def weight_grad(tokens, gq, gk, gv, vec):
+    rows, width = tokens.shape
+    part = gq.shape[1]
+    bt = 256
+    straight = lambda i: (i, 0)
+    return pl.pallas_call(
+        weight_grad_kernel,
+        grid=(rows // bt,),
+        in_specs=[
+            pl.BlockSpec((bt, width), straight),
+            pl.BlockSpec((bt, part), straight),
+            pl.BlockSpec((bt, part), straight),
+            pl.BlockSpec((bt, part), straight),
+            whole(vec.shape),
+        ],
+        out_specs=[whole((width, 3 * part)), whole((16, part))],
+        out_shape=[
+            jax.ShapeDtypeStruct((width, 3 * part), BF),
+            jax.ShapeDtypeStruct((16, part), F32),
+        ],
+        scratch_shapes=[pltpu.VMEM((width, 3 * part), F32), pltpu.VMEM((16, part), F32)],
+        compiler_params=params("arbitrary"),
+        cost_estimate=cost(2 * rows * width * 3 * part, 2 * rows * (width + 3 * part)),
+        name="weight_grad",
+    )(tokens, gq, gk, gv, vec)
+
+
 def project_back_kernel(
-    tok_ref, gq_ref, gk_ref, gv_ref, w_ref, vec_ref,
+    tok_ref, gqa_ref, gka_ref, gva_ref, gq_ref, gk_ref, gv_ref, w_ref, vec_ref,
     own_ref, sib_ref, dw_ref, vecs_ref, qv_ref, accw, accv, accqv
 ):
     step = pl.program_id(0)
     steps = pl.num_programs(0)
+    early = gqa_ref.shape[1]
     part = gq_ref.shape[1]
+    wide = early + part
 
     @pl.when(step == 0)
     def _():
@@ -531,10 +600,14 @@
     unit, _ = normalised(tok_ref[...].astype(F32))
     normed_t = (unit * vec_ref[0:1, :] + vec_ref[1:2, :]).astype(BF).T
     grad = None
+    before = (gqa_ref, gka_ref, gva_ref)
     for at, ref in enumerate((gq_ref, gk_ref, gv_ref)):
         cols = slice(at * part, (at + 1) * part)
         value = ref[...]
-        more = dot(value, w_ref[:, cols], 1, 1)
+        more = dot(
+            jnp.concatenate([before[at][...], value], axis=1),
+            w_ref[:, at * wide : (at + 1) * wide], 1, 1,
+        )
         grad = more if grad is None else grad + more
         accw[:, cols] += dot(normed_t, value)
         if at != 1:
@@ -558,23 +631,19 @@
         qv_ref[...] = accqv[...]
 
 
-def project_back(tokens, gq, gk, gv, weight, vec):
+def project_back(tokens, before, grads, weight, vec):
     rows, width = tokens.shape
-    part = gq.shape[1]
+    early, part = before[0].shape[1], grads[0].shape[1]
     bt = 256
     blocks = rows // bt
     straight = lambda i: (i, 0)
     return pl.pallas_call(
         project_back_kernel,
         grid=(blocks,),
-        in_specs=[
-            pl.BlockSpec((bt, width), straight),
-            pl.BlockSpec((bt, part), straight),
-            pl.BlockSpec((bt, part), straight),
-            pl.BlockSpec((bt, part), straight),
-            whole(weight.shape),
-            whole(vec.shape),
-        ],
+        in_specs=[pl.BlockSpec((bt, width), straight)]
+        + [pl.BlockSpec((bt, early), straight)] * 3
+        + [pl.BlockSpec((bt, part), straight)] * 3
+        + [whole(weight.shape), whole(vec.shape)],
         out_specs=[
             pl.BlockSpec((bt, width), lambda i: (jnp.minimum(i, blocks // 2 - 1), 0)),
             pl.BlockSpec((bt, width), lambda i: (jnp.maximum(i - blocks // 2, 0), 0)),
@@ -595,59 +664,69 @@
             pltpu.VMEM((16, part), F32),
         ],
         compiler_params=params("arbitrary"),
-        cost_estimate=cost(2 * rows * width * 6 * part, 14 * rows * width),
+        cost_estimate=cost(2 * rows * width * (6 * part + 3 * early), 14 * rows * width),
         name="project_back",
-    )(tokens, gq, gk, gv, weight, vec)
-
-
-def pack_kernel(core_ref, qkv_ref, small_ref, proj_ref, fc1_ref, fc2_ref, one_ref, two_ref):
-    first_core = core_ref[0] == 0
+    )(tokens, *before, *grads, weight, vec)
+
+
+def pack_kernel(place_ref, *refs):
+    vectors, (qkv_ref, proj_ref, fc1_ref, fc2_ref, one_ref, two_ref) = refs[:-6], refs[-6:]
+    first_core = lax.rem(place_ref[0], 2) == 0
+    first_chip = place_ref[0] // 2 == 0
     shard, width = proj_ref.shape
     part = width // 2
     ff = fc1_ref.shape[1]
-    owners = width // shard
+    owners = one_ref.shape[0]
     quarter = ff // owners // 4
     half = ff // 2
-    one_ref[:VEC_ROWS, :] = small_ref[...]
-
+    one_ref[0, :VEC_ROWS, :] = jnp.zeros((VEC_ROWS, 3 * part), BF)
+    for at, ref in enumerate(vectors):
+        one_ref[0, at : at + 1, : ref.shape[1]] = ref[...]
     for at in range(3):
         low = qkv_ref[:, at * width : at * width + part]
         high = qkv_ref[:, at * width + part : (at + 1) * width]
-        one_ref[VEC_ROWS:, at * part : (at + 1) * part] = jnp.where(first_core, low, high)
-    two_ref[:, :width] = proj_ref[...]
+        mine = jnp.where(first_core, low, high)
+        mine = jnp.where(first_chip, mine[: shard // 2], mine[shard // 2 :])
+        one_ref[0, VEC_ROWS:, at * part : (at + 1) * part] = mine
+    for owner in range(1, owners):
+        one_ref[owner] = one_ref[0]
+    two_ref[:, :part] = jnp.where(first_core, proj_ref[:, :part], proj_ref[:, part:])
     pieces_low, pieces_high = [], []
     for piece in range(2):
         for owner in range(owners):
             base = owner * 4 * quarter + piece * quarter
             pieces_low.append(fc1_ref[:, base : base + quarter])
             pieces_high.append(fc1_ref[:, base + 2 * quarter : base + 3 * quarter])
-    two_ref[:, width : width + half] = jnp.where(
+    two_ref[:, part : part + half] = jnp.where(
         first_core, jnp.concatenate(pieces_low, axis=1), jnp.concatenate(pieces_high, axis=1)
     )
     for piece in range(2):
         low = fc2_ref[piece * quarter : (piece + 1) * quarter, :]
         high = fc2_ref[(2 + piece) * quarter : (3 + piece) * quarter, :]
-        start = width + half + piece * width
+        start = part + half + piece * width
         two_ref[:, start : start + width] = jnp.where(first_core, low, high)
 
 
-def pack_weights(core, qkv, small, proj, fc1, fc2):
+def pack_weights(place, owners, vectors, qkv, proj, fc1, fc2):
     shard, width = proj.shape
     half = fc1.shape[1] // 2
+    part = width // 2
+    vectors = [vector.reshape(1, -1) for vector in vectors]
+    values = (*vectors, qkv, proj, fc1, fc2)
+    rows = VEC_ROWS + shard // 2
     return pl.pallas_call(
         pack_kernel,
         grid=(1,),
-        in_specs=[pl.BlockSpec(memory_space=pltpu.SMEM)]
-        + [whole(value.shape) for value in (qkv, small, proj, fc1, fc2)],
-        out_specs=[whole((VEC_ROWS + shard, 3 * width // 2)), whole((shard, 3 * width + half))],
+        in_specs=[pl.BlockSpec(memory_space=pltpu.SMEM)] + [whole(value.shape) for value in values],
+        out_specs=[whole((owners, rows, 3 * part)), whole((shard, 5 * part + half))],
         out_shape=[
-            jax.ShapeDtypeStruct((VEC_ROWS + shard, 3 * width // 2), BF),
-            jax.ShapeDtypeStruct((shard, 3 * width + half), BF),
+            jax.ShapeDtypeStruct((owners, rows, 3 * part), BF),
+            jax.ShapeDtypeStruct((shard, 5 * part + half), BF),
         ],
         compiler_params=params("arbitrary"),
         cost_estimate=cost(0, 5 * shard * width * 8),
         name="pack_weights",
-    )(core, qkv, small, proj, fc1, fc2)
+    )(place, *values)
 
 
 def project_kernel(tok_ref, w_ref, bias_ref, vec_ref, out_ref, out_t_ref):
@@ -685,33 +764,8 @@
     )(tokens, weight, bias, vec)
 
 
-def gather_line(value):
-    owners = lax.axis_size("fsdp")
-    lines = owners // 2
-    at = lax.axis_index("fsdp")
-    line, odd = at // 2, lax.rem(at, 2)
-    other = lax.ppermute(value, "fsdp", [(f, f ^ 1) for f in range(owners)])
-    pair = jnp.stack([jnp.where(odd == 0, value, other), jnp.where(odd == 0, other, value)])
-    ups, downs = [pair], [pair]
-    for hop in range(1, lines):
-        up = [(f, f + 2) for f in range(owners - 2) if f // 2 >= hop - 1]
-        down = [(f, f - 2) for f in range(2, owners) if f // 2 <= lines - hop]
-        ups.append(lax.ppermute(ups[-1], "fsdp", up))
-        downs.append(lax.ppermute(downs[-1], "fsdp", down))
-    gathered = []
-    for target in range(lines):
-        options = [
-            downs[target - here] if here < target else ups[here - target] for here in range(lines)
-        ]
-        gathered.append(choose_at(line, options))
-    return jnp.stack(gathered).reshape(owners, *value.shape)
-
-
-def choose_at(index, options):
-    out = options[-1]
-    for at in range(len(options) - 2, -1, -1):
-        out = jnp.where(index == at, options[at], out)
-    return out
+def exchange(value):
+    return lax.all_to_all(value, "fsdp", split_axis=0, concat_axis=0, tiled=True)
 
 
 def per_device(
@@ -762,21 +816,28 @@
         norm1_gain, norm1_bias, query_bias, value_bias, proj_bias, norm2_gain, norm2_bias,
         fc2_bias, fc1_bias,
     ]
-    small_rows = jnp.stack([jnp.pad(vector, (0, 3 * part - vector.shape[0])) for vector in small])
-    small_rows = jnp.pad(small_rows, ((0, VEC_ROWS - len(small)), (0, 0)))
-    one, two = pack_weights(core_row, qkv_weight, small_rows, proj_weight, fc1_weight, fc2_weight)
+    one, two = pack_weights(
+        place_row, owners, small, qkv_weight, proj_weight, fc1_weight, fc2_weight
+    )
+    mine_one = exchange(one)
+    mine_one, two = lax.optimization_barrier((mine_one, two))
     second = lax.all_gather(two, "fsdp", axis=0, tiled=True)
-    first = gather_line(one)
+    own_rows = mine_one[:, VEC_ROWS:]
+    other_rows = partner(own_rows)
+    w_qkv = jnp.where(
+        image == 0,
+        jnp.stack([own_rows, other_rows], axis=1),
+        jnp.stack([other_rows, own_rows], axis=1),
+    ).reshape(width, 3 * part)
 
     def collect(value, theirs):
         mine = pick(value, image, 0)
         return jnp.concatenate([mine, theirs, sibling(mine), sibling(theirs)], axis=0)
 
     tok = collect(tokens, partner(pick(tokens, 1 - image, 0)))
-    w_qkv = first[:, VEC_ROWS:].reshape(width, 3 * part)
-    vecs = first[:, :8, :shard].astype(F32).transpose(1, 0, 2).reshape(8, width)
+    vecs = mine_one[:, :8, :shard].astype(F32).transpose(1, 0, 2).reshape(8, width)
     g1, b1, qb, vb, pb, g2, b2, f2b = vecs
-    f1b = first[:, 8, :ff_shard].astype(F32)
+    f1b = mine_one[:, 8, :ff_shard].astype(F32)
     f1b = pick(f1b.reshape(owners, 2, 2, quarter), core, 1)
     f1b = f1b.transpose(1, 0, 2).reshape(1, half)
 
@@ -786,18 +847,15 @@
     qkv_bias = jnp.concatenate([mine_of(qb), jnp.zeros((part,), F32), mine_of(vb)])
     vec_one = jnp.concatenate([jnp.stack([g1, b1]), jnp.zeros((6, width), F32)])
     packed, packed_t = project(tok, w_qkv, qkv_bias.reshape(1, 3 * part), vec_one)
-    cot_theirs = partner(pick(cotangent, 1 - image, 0))
-    packed, cot_theirs = lax.optimization_barrier((packed, cot_theirs))
+    cot = collect(cotangent, partner(pick(cotangent, 1 - image, 0)))
+    packed, cot = lax.optimization_barrier((packed, cot))
     mixed, result_t, log_total = attend_forward(counts, place_row, packed, packed_t, slots)
     mixed_sib = sibling(mixed)
 
-    cot = collect(cotangent, cot_theirs)
-    wp = second[:, :width]
-    wp_own = lax.dynamic_slice_in_dim(wp, core * part, part, 0)
-    wp_sib = lax.dynamic_slice_in_dim(wp, (1 - core) * part, part, 0)
+    wp_other = sibling(second[:, :part])
     vec_two = jnp.concatenate([jnp.stack([pb, g2, b2]), jnp.zeros((5, width), F32)])
-    middle, out_part, gn_part, dw_ff, gf1, gf2 = feed_forward(
-        tok, mixed, mixed_sib, cot, wp_own, wp_sib, second, vec_two, f1b
+    middle, out_part, gn_part, dw_ff, gf1, gf2, wp_own = feed_forward(
+        core_row, tok, mixed, mixed_sib, cot, wp_other, second, vec_two, f1b
     )
     scattered_one = lax.psum_scatter(dw_ff, "fsdp", scatter_dimension=0, tiled=True)
     gn_sib = sibling(gn_part)
@@ -823,11 +881,17 @@
         jnp.concatenate([dwp_own, dwp_sib], axis=0),
         jnp.concatenate([dwp_sib, dwp_own], axis=0),
     )
-    grad_mixed, output = lax.optimization_barrier((grad_mixed, output))
-    gq, gk, gv = attend_backward(
-        counts, place_row, packed, packed_t, grad_mixed, grad_mixed_t, result_t, log_total, slots
-    )
-    gn1_own, gn1_send, dw_qkv, vec_first, vec_qv = project_back(tok, gq, gk, gv, w_qkv, vec_one)
+    early, late = 2, 1
+    attend = functools.partial(attend_backward, counts, place_row, packed, packed_t)
+    before = attend(grad_mixed, grad_mixed_t, result_t, log_total, slots, 0, early)
+    dw_early, qv_early = weight_grad(tok, *before, vec_one)
+    block_one = jnp.concatenate([dw_early, dwp], axis=1).reshape(owners, shard, -1)
+    came_one = exchange(block_one)
+    grad_mixed, output, block_one = lax.optimization_barrier((grad_mixed, output, block_one))
+    grads = attend(grad_mixed, grad_mixed_t, result_t, log_total, slots, early, late)
+    gn1_own, gn1_send, dw_late, vec_first, qv_late = project_back(
+        tok, before, grads, w_qkv, vec_one
+    )
 
     def spread(vector):
         both = jnp.zeros((2, part), F32)
@@ -838,28 +902,31 @@
 
     once = (core == 0).astype(F32)
     gg1, gb1 = rows_of(vec_first)
-    gqb, gvb = rows_of(vec_qv)
+    gqb, gvb = rows_of(jnp.concatenate([qv_early, qv_late], axis=1))
     gg2, gb2, gpb = rows_of(vec_back) * once
     gf2b = jnp.sum(gf2, axis=0) * once
     gf1b = jnp.sum(gf1, axis=0).reshape(2, owners, quarter).transpose(1, 0, 2)
     gf1b = lax.dynamic_update_index_in_dim(
         jnp.zeros((owners, 2, 2, quarter), F32), gf1b, core, 1
     ).reshape(owners, ff_shard)
-    wide = 4 * part
+    late_wide = 3 * late * PAIR
     small_grads = jnp.stack(
         [gg1, gb1, spread(gqb), spread(gvb), gpb, gg2, gb2, gf2b]
     ).reshape(8, owners, shard).transpose(1, 0, 2)
     small_block = jnp.concatenate(
         [
-            jnp.pad(small_grads, ((0, 0), (0, 0), (0, wide - shard))),
-            jnp.pad(gf1b[:, None], ((0, 0), (0, VEC_ROWS - 9), (0, wide - ff_shard))),
+            jnp.pad(small_grads, ((0, 0), (0, 0), (0, late_wide - shard))),
+            jnp.pad(gf1b[:, None], ((0, 0), (0, VEC_ROWS - 9), (0, late_wide - ff_shard))),
         ],
         axis=1,
     ).astype(BF)
-    dw_attend = jnp.concatenate([dw_qkv, dwp], axis=1).reshape(owners, shard, wide)
-    block_two = jnp.concatenate([small_block, dw_attend], axis=1)
-    block_two, scattered_one = lax.optimization_barrier((block_two, scattered_one))
-    scattered_two = lax.psum_scatter(block_two, "fsdp", scatter_dimension=0, tiled=False)
+    block_two = jnp.concatenate(
+        [small_block, dw_late.reshape(owners, shard, late_wide)], axis=1
+    )
+    came_two = exchange(block_two)
+
+    def total(came):
+        return jnp.sum(came.astype(F32), axis=0).astype(BF)
 
     gn1 = gn1_own + sibling(gn1_send).astype(F32)
     unit_own, inverse_own = normalised(tok[:rows_own].astype(F32))
@@ -867,9 +934,9 @@
     input_grad = hand_back(input_own, input_own[slots:].astype(BF))
 
     def finish(value):
-        total = value.astype(F32) + partner(value).astype(F32)
-        other = sibling(total.astype(BF)).astype(F32)
-        return total, other
+        summed = value.astype(F32) + partner(value).astype(F32)
+        other = sibling(summed.astype(BF)).astype(F32)
+        return summed, other
 
     def in_order(mine, other):
         return jnp.where(core == 0, mine, other), jnp.where(core == 0, other, mine)
@@ -886,18 +953,25 @@
         return value[:, half:].reshape(quarter, 2, width).transpose(1, 0, 2)
 
     grad_fc2 = jnp.stack([fc2_of(lower), fc2_of(upper)]).reshape(ff_shard, width)
-    two_mine, two_other = finish(scattered_two)
-    lower, upper = in_order(two_mine[VEC_ROWS:], two_other[VEC_ROWS:])
+    early_mine, early_other = finish(total(came_one))
+    early_sum = in_order(early_mine, early_other)
+    late_mine, late_other = finish(total(came_two))
+    late_sum = in_order(late_mine[VEC_ROWS:], late_other[VEC_ROWS:])
+    cut, tail = early * PAIR, late * PAIR
     grad_qkv = jnp.concatenate(
         [
-            value[:, at * part : (at + 1) * part]
+            piece
             for at in range(3)
-            for value in (lower, upper)
+            for of in range(2)
+            for piece in (
+                early_sum[of][:, at * cut : (at + 1) * cut],
+                late_sum[of][:, at * tail : (at + 1) * tail],
+            )
         ],
         axis=1,
     )
-    grad_proj = jnp.concatenate([lower[:, 3 * part :], upper[:, 3 * part :]], axis=1)
-    small_sum = two_mine[:VEC_ROWS] + two_other[:VEC_ROWS]
+    grad_proj = jnp.concatenate([early_sum[0][:, 3 * cut :], early_sum[1][:, 3 * cut :]], axis=1)
+    small_sum = late_mine[:VEC_ROWS] + late_other[:VEC_ROWS]
     s = [small_sum[at, :shard] for at in range(8)]
     grad_f1b = small_sum[8, :ff_shard]
     return (

time: 513 us -> 496 us (0.967)
  waiting for transfers between devices: 186 us -> 103 us
  blocking collectives: 0 us -> 58.7 us
  Pallas kernels: 214 us -> 224 us
  other arithmetic: 36.9 us -> 44.6 us
  starting transfers between devices: 23.6 us -> 18 us
  local copies, waits for them, and re-layouts: 30 us -> 24.7 us
    ppermute x7 -> x0, waiting for transfers between devices: 78.1 us -> none  [the longest x3 74.1 us: gather_line(): downs.append(lax.ppermute(downs[-1], 'fsdp', down))]
    all_to_all x0 -> x2, blocking collectives: none -> 58.7 us  [exchange(): lax.all_to_all(value, 'fsdp', split_axis=0, concat_axis=0, tiled=True)]
    reduce_scatter x1 -> x0, waiting for transfers between devices: 38.1 us -> none  [per_device(): lax.psum_scatter(block_two, 'fsdp', scatter_dimension=0, tiled=False)]
    ppermute x6 -> x8, waiting for transfers between devices: 60 us -> 78.9 us  [partner(): return lax.ppermute(value, 'seq', to_partner)]
    all_to_all x0 -> x1, waiting for transfers between devices: none -> 17.3 us  [exchange(): lax.all_to_all(value, 'fsdp', split_axis=0, concat_axis=0, tiled=True)]
    ppermute x7 -> x0, starting transfers between devices: 14.4 us -> none  [the longest x3 7.53 us: gather_line(): ups.append(lax.ppermute(ups[-1], 'fsdp', up))]
    pallas_call x2 -> x4, Pallas kernels: 122 us -> 135 us  [the longest x2 69.6 us: attend_backward(): pl.pallas_call(kernel, grid=(count, keys // bq), in_specs=[pl.BlockSpec(m...]
    pad x10 -> x0, local copies, waits for them, and re-layouts: 6.71 us -> none  [the longest x9 6.09 us: per_device(): jnp.pad(vector, (0, 3 * part - vector.shape[0]))]
  transfers between devices with their start and end apart: 26 -> 23, of which waited for: 14 -> 13; matrix products, arithmetic and copies ran while one was open for 10% -> 11% of each run, Pallas kernels for 31% -> 34%
where the time goes in v3:
time: 496 us; the launch traced here: 488 us
  Pallas kernels  224 us (45%)
  waiting for transfers between devices  103 us (21%)
  blocking collectives  58.7 us (12%)
  other arithmetic  44.6 us (9%)
  local copies, waits for them, and re-layouts  24.7 us (5%)
  starting transfers between devices  18 us (4%)
  between operations  15.3 us (3%)
    ppermute x8, waiting for transfers between devices, partner(): return lax.ppermute(value, 'seq', to_partner)  78.9 us
    pallas_call x2, Pallas kernels, attend_backward(): pl.pallas_call(kernel, grid=(count, keys // bq), in_specs=[pl.BlockSpec(m...  69.6 us
    all_to_all x2, blocking collectives, exchange(): lax.all_to_all(value, 'fsdp', split_axis=0, concat_axis=0, tiled=True)  58.7 us
    pallas_call x1, Pallas kernels, feed_forward(): pl.pallas_call(kernel, grid=(blocks,), in_specs=[pl.BlockSpec(memory_spac...  55.3 us
    pallas_call x1, Pallas kernels, attend_forward(): pl.pallas_call(kernel, grid=(pairs, keys // bq), in_specs=[pl.BlockSpec(m...  42.2 us
    all_to_all x1, waiting for transfers between devices, exchange(): lax.all_to_all(value, 'fsdp', split_axis=0, concat_axis=0, tiled=True)  17.3 us
    pallas_call x1, Pallas kernels, branch(): pl.pallas_call(branch_kernel, grid=(blocks,), in_specs=[pl.BlockSpec(memo...  16.5 us
    pallas_call x1, Pallas kernels, project_back(): pl.pallas_call(project_back_kernel, grid=(blocks,), in_specs=[pl.BlockSpe...  15.4 us
  transfers between devices with their start and end apart: 23, of which 13 were waited for; matrix products, arithmetic and copies ran while one was open for 11% of the time, Pallas kernels for 34%

profile of v3, /device:TPU:0, one launch (start us, length us, event | category | flops | bytes accessed | tf_op | source)
XLA Modules:
  0.0 487.9 jit_solution(8499653404346039246)
XLA Ops:
  8.6 3.1 pack_weights.1
  11.7 36.2 %all_to_all.15 = bf16[8,64,1152]{2,1,0:T(8,128)(2,1)S(1)} all-to-all(bf16[8,64,1152]{2,1,0:T(8,128)(2,1)} %get-tuple-element.54), channel_id=1, replica_groups=mesh['fsdp'=8,'seq'=4] {'fsdp'}, dimensions={0} | all-to-all | bytes 2359296 | tf_op jit(solution)/shard_map/all_to_all | solution.py:768
  51.9 16.9 %collective-permute-done.4 = bf16[512,768]{1,0:T(8,128)(2,1)} collective-permute-done((bf16[512,768]{1,0:T(8,128)(2,1)S(1)}, bf16[512,768]{1,0:T(8,128)(2,1)}, u32[]{:S(2)}, u32[]{:S(2)}) %collective-permute-start.4) | collective-permute-done | bytes 786464 | tf_op jit(solution)/shard_map/ppermute | solution.py:808
  69.4 13.4 %collective-permute-done = bf16[512,768]{1,0:T(8,128)(2,1)S(1)} collective-permute-done((bf16[512,768]{1,0:T(8,128)(2,1)}, bf16[512,768]{1,0:T(8,128)(2,1)S(1)}, u32[]{:S(2)}, u32[]{:S(2)}) %collective-permute-start) | collective-permute-done | bytes 786464 | tf_op jit(solution)/shard_map/ppermute | solution.py:808
  82.8 3.5 pad_maximum_fusion.1.cot_ref
  89.2 7.4 %pad_maximum_fusion.tok_ref = bf16[2048,768]{1,0:T(8,128)(2,1)} fusion(bf16[512,768]{1,0:T(8,128)(2,1)S(1)} %collective-permute-done.2, bf16[512,768]{1,0:T(8,128)(2,1)} %collective-permute-done.1, bf16[512,768]{1,0:T(8,128)(2,1)S(1)} %collective-permute-done, bf16[512,768]{1,0:T(8,128)(2,1)S(1)} %get-tuple-element.109), kind=kLoop, calls=%fused_computation.11 | loop fusion | flops 12582912 | bytes 6291456 | tf_op jit(solution)/shard_map/concatenate | solution.py:835
  98.9 10.9 %collective-permute-done.3 = bf16[8,48,1152]{2,1,0:T(8,128)(2,1)} collective-permute-done((bf16[8,48,1152]{2,1,0:T(8,128)(2,1)}, bf16[8,48,1152]{2,1,0:T(8,128)(2,1)}, u32[]{:S(2)}, u32[]{:S(2)}) %collective-permute-start.3) | collective-permute-done | bytes 884768 | tf_op jit(solution)/shard_map/ppermute | solution.py:808
  113.4 11.5 %project.1 = (bf16[2048,1152]{1,0:T(8,128)(2,1)}, bf16[1152,2048]{1,0:T(8,128)(2,1)}) custom-call(bf16[2048,768]{1,0:T(8,128)(2,1)} %pad_maximum_fusion.tok_ref, bf16[768,1152]{1,0:T(8,128)(2,1)} %bitcast.85, f32[1,1152]{1,0:T(1,128)} %reshape.186.bias_ref, f32[8,768]{1,0:T(8,128)} %maximum_maximum_fusion.vec_ref), custom_call_target="tpu_custom_call" | custom-call | flops 3623878656 | bytes 18874368 | tf_op jit(solution)/shard_map/project/pallas_call | solution.py:744
  124.9 42.2 %attend_forward.1 = (bf16[2048,384]{1,0:T(8,128)(2,1)}, f32[384,2048]{1,0:T(8,128)}, f32[3,8,2048]{2,1,0:T(8,128)}) custom-call(s32[2,4]{1,0:T(2,128)} %counts_ref.5, s32[1]{0:T(128)} %bitcast.3.place_ref, bf16[2048,1152]{1,0:T(8,128)(2,1)} %get-tuple-element.58.k_ref.q_ref.v_ref, bf16[1152,2048]{1,0:T(8,128)(2,1)} %get-tuple-element.59.qt_ref.vt_ref.kt_ref, ...), custom_call_target="tpu_custom_call" | custom-call | flops 25769803776 | bytes 9437184 | tf_op jit(solution)/shard_map/attend_forward/pallas_call | solution.py:163
  171.9 55.3 %feed_forward.1 = (f32[2048,768]{1,0:T(8,128)}, bf16[2048,768]{1,0:T(8,128)(2,1)}, bf16[2048,768]{1,0:T(8,128)(2,1)}, bf16[768,3072]{1,0:T(8,128)(2,1)}, f32[8,1...) custom-call(s32[1]{0:T(128)} %bitcast.core_ref, bf16[2048,768]{1,0:T(8,128)(2,1)} %pad_maximum_fusion.tok_ref, ...), custom_call_target="tpu_custom_call" | custom-call | flops 31406948352 | bytes 40894464 | tf_op jit(solution)/shard_map/feed_forward/pallas_call | solution.py:394
  230.6 3.2 collective-permute-done.10
  238.8 17.7 %collective-permute-done.11 = bf16[512,768]{1,0:T(8,128)(2,1)S(1)} collective-permute-done((bf16[512,768]{1,0:T(8,128)(2,1)S(1)}, bf16[512,768]{1,0:T(8,128)(2,1)S(1)}, u32[]{:S(2)}, u32[]{:S(2)}) %collective-permute-start.11) | collective-permute-done | bytes 786464 | tf_op jit(solution)/shard_map/ppermute | solution.py:808
  257.9 16.5 %branch.1 = (f32[1024,768]{1,0:T(8,128)}, bf16[2048,384]{1,0:T(8,128)(2,1)}, bf16[384,2048]{1,0:T(8,128)(2,1)}, bf16[384,384]{1,0:T(8,128)(2,1)}, bf16[384,384]{1,0:T(8,128)(2,1)}, /*index=5*/f32[24,768]{1,0:T(8,128)}) custom-call(s32[1]{0:T(128)} %bitcast.core_ref, f32[2048,768]{1,0:T(8,128)} %get-tuple-element.63.mid_ref, ...), custom_call_target="tpu_custom_call" | custom-call | flops 3623878656 | bytes 28311552 | tf_op jit(solution)/shard_map/branch/pallas_call | solution.py:489
  275.8 45.4 %attend_backward.2 = (bf16[2048,256]{1,0:T(8,128)(2,1)}, bf16[2048,256]{1,0:T(8,128)(2,1)}, bf16[2048,256]{1,0:T(8,128)(2,1)}) custom-call(s32[2,4]{1,0:T(2,128)} %counts_ref.5, s32[1]{0:T(128)} %bitcast.3.place_ref, bf16[2048,1152]{1,0:T(8,128)(2,1)} %get-tuple-element.58.k_ref.q_ref.v_ref, bf16[2048,1152]{1,0:T(8,128)(2,1)} %get-tuple-element.58.k_ref.q_ref.v_ref, ...), custom_call_target="tpu_custom_call" | custom-call | flops 42949672960 | bytes 12582912 | tf_op jit(solution)/shard_map/attend_backward/pallas_call | solution.py:263
  321.2 10.0 %weight_grad.1 = (bf16[768,768]{1,0:T(8,128)(2,1)}, f32[16,256]{1,0:T(8,128)}) custom-call(bf16[2048,768]{1,0:T(8,128)(2,1)} %pad_maximum_fusion.tok_ref, bf16[2048,256]{1,0:T(8,128)(2,1)} %get-tuple-element.71.gq_ref.gqa_ref, bf16[2048,256]{1,0:T(8,128)(2,1)} %get-tuple-element.72.gk_ref.gka_ref, bf16[2048,256]{1,0:T(8,128)(2,1)} %get-tuple-element.73.gv_ref.gva_ref, ...), custom_call_target="tpu_custom_call" | custom-call | flops 2415919104 | bytes 6291456 | tf_op jit(solution)/shard_map/weight_grad/pallas_call | solution.py:562
  333.8 24.2 %attend_backward.3 = (bf16[2048,128]{1,0:T(8,128)(2,1)}, bf16[2048,128]{1,0:T(8,128)(2,1)}, bf16[2048,128]{1,0:T(8,128)(2,1)}) custom-call(s32[2,4]{1,0:T(2,128)} %counts_ref.5, s32[1]{0:T(128)} %bitcast.3.place_ref, bf16[2048,1152]{1,0:T(8,128)(2,1)} %get-tuple-element.58.k_ref.q_ref.v_ref, bf16[2048,1152]{1,0:T(8,128)(2,1)} %get-tuple-element.58.k_ref.q_ref.v_ref, ...), custom_call_target="tpu_custom_call" | custom-call | flops 21474836480 | bytes 6291456 | tf_op jit(solution)/shard_map/attend_backward/pallas_call | solution.py:263
  358.3 15.4 %project_back.1 = (f32[1024,768]{1,0:T(8,128)}, bf16[1024,768]{1,0:T(8,128)(2,1)}, bf16[768,384]{1,0:T(8,128)(2,1)}, f32[16,768]{1,0:T(8,128)}, f32[16,128]{1,0:T(8,128)}) custom-call(bf16[2048,768]{1,0:T(8,128)(2,1)} %pad_maximum_fusion.tok_ref, bf16[2048,256]{1,0:T(8,128)(2,1)} %get-tuple-element.71.gq_ref.gqa_ref, ...), custom_call_target="tpu_custom_call" | custom-call | flops 4831838208 | bytes 22020096 | tf_op jit(solution)/shard_map/project_back/pallas_call | solution.py:640
  377.0 22.4 %all_to_all.16 = bf16[8,112,384]{2,1,0:T(8,128)(2,1)} all-to-all(bf16[8,112,384]{2,1,0:T(8,128)(2,1)S(1)} %fusion.15), channel_id=1, replica_groups=mesh['fsdp'=8,'seq'=4] {'fsdp'}, dimensions={0} | all-to-all | bytes 1376256 | tf_op jit(solution)/shard_map/all_to_all | solution.py:768
  399.4 4.0 all-to-all-start.2
  415.4 4.1 fusion.13
  419.7 3.1 fusion.7
  426.7 17.3 %all-to-all-done.2 = bf16[8,96,1152]{2,1,0:T(8,128)(2,1)S(1)} async-done(((bf16[8,96,1152]{2,1,0:T(8,128)(2,1)}), bf16[8,96,1152]{2,1,0:T(8,128)(2,1)S(1)}, u32[]{:S(2)}, u32[]{:S(2)}) %all-to-all-start.2) | async-done | bytes 1769504 | tf_op jit(solution)/shard_map/all_to_all | solution.py:768
  455.3 14.4 %collective-permute-done.18 = bf16[96,3072]{1,0:T(8,128)(2,1)S(1)} collective-permute-done((bf16[96,3072]{1,0:T(8,128)(2,1)}, bf16[96,3072]{1,0:T(8,128)(2,1)S(1)}, u32[]{:S(2)}, u32[]{:S(2)}) %collective-permute-start.18) | collective-permute-done | bytes 589856 | tf_op jit(solution)/shard_map/ppermute | solution.py:808
  477.4 3.2 reshape.196
  (199 shorter events, 71.4 us)
Async XLA Ops:
  7.2 40.8 %copy-start.10 = (bf16[2,512,768]{2,1,0:T(8,128)(2,1)S(1)}, bf16[2,512,768]{2,1,0:T(8,128)(2,1)}, u32[]{:S(2)}) copy-start(bf16[2,512,768]{2,1,0:T(8,128)(2,1)} %param.31) | copy-start | bytes 4718596
  7.2 159.9 %all-gather.2.cloned.1.call-start = ((), (), s32[]{:S(2)}) async-start(), calls=%async_computation.4 | async-start | bytes 5971968 | tf_op jit(solution)/shard_map/all_gather | solution.py:824
  47.9 405.7 %reduce-scatter.2.cloned.1.call-start = ((), (), s32[]{:S(2)}) async-start(), calls=%async_computation.5 | async-start | bytes 5308416 | tf_op jit(solution)/shard_map/reduce_scatter | solution.py:860
  48.2 20.6 %collective-permute-start.4 = (bf16[512,768]{1,0:T(8,128)(2,1)S(1)}, bf16[512,768]{1,0:T(8,128)(2,1)}, u32[]{:S(2)}, u32[]{:S(2)}) collective-permute-start(bf16[512,768]{1,0:T(8,128)(2,1)S(1)} %get-tuple-element.108), channel_id=1, source_target_pairs={{0,2},{1,3},{2,0},{3,1},{4,6},{5,7},{6,4},{7,5},{8,10},{9,11},{10,... | collective-permute-start | bytes 2359304 | tf_op jit(solution)/shard_map/ppermute | solution.py:808
  50.7 32.1 %collective-permute-start = (bf16[512,768]{1,0:T(8,128)(2,1)}, bf16[512,768]{1,0:T(8,128)(2,1)S(1)}, u32[]{:S(2)}, u32[]{:S(2)}) collective-permute-start(bf16[512,768]{1,0:T(8,128)(2,1)} %get-tuple-element.110), channel_id=1, source_target_pairs={{0,2},{1,3},{2,0},{3,1},{4,6},{5,7},{6,4},{7,5},{8,10},{9,11},{10,... | collective-permute-start | bytes 2359304 | tf_op jit(solution)/shard_map/ppermute | solution.py:808
  51.9 30.9 %collective-permute-start.5 = (bf16[512,768]{1,0:T(8,128)(2,1)S(1)}, bf16[512,768]{1,0:T(8,128)(2,1)}, u32[]{:S(2)}, u32[]{:S(2)}) collective-permute-start(bf16[512,768]{1,0:T(8,128)(2,1)S(1)} %get-tuple-element.107), channel_id=1, source_target_pairs={{0,1},{1,0},{2,3},{3,2},{4,5},{5,4},{6,7},{7,6},{8,9},{9,8},{10,11... | collective-permute-start | bytes 2359304 | tf_op jit(solution)/shard_map/ppermute | solution.py:805
  68.8 14.0 %collective-permute-start.6 = (bf16[512,768]{1,0:T(8,128)(2,1)}, bf16[512,768]{1,0:T(8,128)(2,1)}, u32[]{:S(2)}, u32[]{:S(2)}) collective-permute-start(bf16[512,768]{1,0:T(8,128)(2,1)} %collective-permute-done.4), channel_id=1, source_target_pairs={{0,1},{1,0},{2,3},{3,2},{4,5},{5,4},{6,7},{7,6},{8,9},{9,8},{10,11... | collective-permute-start | bytes 2359304 | tf_op jit(solution)/shard_map/ppermute | solution.py:805
  68.8 20.3 %collective-permute-start.1 = (bf16[512,768]{1,0:T(8,128)(2,1)S(1)}, bf16[512,768]{1,0:T(8,128)(2,1)}, u32[]{:S(2)}, u32[]{:S(2)}) collective-permute-start(bf16[512,768]{1,0:T(8,128)(2,1)S(1)} %get-tuple-element.109), channel_id=1, source_target_pairs={{0,1},{1,0},{2,3},{3,2},{4,5},{5,4},{6,7},{7,6},{8,9},{9,8},{10,11... | collective-permute-start | bytes 2359304 | tf_op jit(solution)/shard_map/ppermute | solution.py:805
  82.8 6.4 %collective-permute-start.2 = (bf16[512,768]{1,0:T(8,128)(2,1)S(1)}, bf16[512,768]{1,0:T(8,128)(2,1)S(1)}, u32[]{:S(2)}, u32[]{:S(2)}) collective-permute-start(bf16[512,768]{1,0:T(8,128)(2,1)S(1)} %collective-permute-done), channel_id=1, source_target_pairs={{0,1},{1,0},{2,3},{3,2},{4,5},{5,4},{6,7},{7,6},{8,9},{9,8},{10,11... | collective-permute-start | bytes 2359304 | tf_op jit(solution)/shard_map/ppermute | solution.py:805
  87.6 22.1 %collective-permute-start.3 = (bf16[8,48,1152]{2,1,0:T(8,128)(2,1)}, bf16[8,48,1152]{2,1,0:T(8,128)(2,1)}, u32[]{:S(2)}, u32[]{:S(2)}) collective-permute-start(bf16[8,48,1152]{2,1,0:T(8,128)(2,1)} %get-tuple-element.116), channel_id=1, source_target_pairs={{0,2},{1,3},{2,0},{3,1},{4,6},{5,7},{6,4},{7,5},{8,10},{9,11},{10,... | collective-permute-start | bytes 2654216 | tf_op jit(solution)/shard_map/ppermute | solution.py:808
  167.1 3.6 collective-permute-start.7
  168.3 3.2 collective-permute-start.8
  230.0 3.8 collective-permute-start.10
  230.1 27.7 %collective-permute-start.9 = (bf16[2048,768]{1,0:T(8,128)(2,1)}, bf16[2048,768]{1,0:T(8,128)(2,1)}, u32[]{:S(2)}, u32[]{:S(2)}) collective-permute-start(bf16[2048,768]{1,0:T(8,128)(2,1)} %get-tuple-element.64.ga_ref), channel_id=1, source_target_pairs={{0,1},{1,0},{2,3},{3,2},{4,5},{5,4},{6,7},{7,6},{8,9},{9,8},{10,11... | collective-permute-start | bytes 9437192 | tf_op jit(solution)/shard_map/ppermute | solution.py:805
  236.8 19.6 %collective-permute-start.11 = (bf16[512,768]{1,0:T(8,128)(2,1)S(1)}, bf16[512,768]{1,0:T(8,128)(2,1)S(1)}, u32[]{:S(2)}, u32[]{:S(2)}) collective-permute-start(bf16[512,768]{1,0:T(8,128)(2,1)S(1)} %get-tuple-element.106), channel_id=1, source_target_pairs={{0,2},{1,3},{2,0},{3,1},{4,6},{5,7},{6,4},{7,5},{8,10},{9,11},{10,... | collective-permute-start | bytes 2359304 | tf_op jit(solution)/shard_map/ppermute | solution.py:808
  399.4 44.5 %all-to-all-start.2 = ((bf16[8,96,1152]{2,1,0:T(8,128)(2,1)}), bf16[8,96,1152]{2,1,0:T(8,128)(2,1)S(1)}, u32[]{:S(2)}, u32[]{:S(2)}) async-start(bf16[8,96,1152]{2,1,0:T(8,128)(2,1)} %bitcast.22), calls=%async_computation.2 | async-start | bytes 3538944 | tf_op jit(solution)/shard_map/all_to_all | solution.py:768
  403.7 11.7 %collective-permute-start.12 = (bf16[1024,768]{1,0:T(8,128)(2,1)}, bf16[1024,768]{1,0:T(8,128)(2,1)}, u32[]{:S(2)}, u32[]{:S(2)}) collective-permute-start(bf16[1024,768]{1,0:T(8,128)(2,1)} %get-tuple-element.84), channel_id=1, source_target_pairs={{0,1},{1,0},{2,3},{3,2},{4,5},{5,4},{6,7},{7,6},{8,9},{9,8},{10,11... | collective-permute-start | bytes 4718600 | tf_op jit(solution)/shard_map/ppermute | solution.py:805
  405.0 5.0 %collective-permute-start.14 = (bf16[112,384]{1,0:T(8,128)(2,1)S(1)}, bf16[112,384]{1,0:T(8,128)(2,1)S(1)}, u32[]{:S(2)}, u32[]{:S(2)}) collective-permute-start(bf16[112,384]{1,0:T(8,128)(2,1)S(1)} %reduce_sum.114), channel_id=1, source_target_pairs={{0,2},{1,3},{2,0},{3,1},{4,6},{5,7},{6,4},{7,5},{8,10},{9,11},{10,... | collective-permute-start | bytes 258056 | tf_op jit(solution)/shard_map/ppermute | solution.py:808
  411.6 1.6 collective-permute-start.15
  424.5 25.8 %collective-permute-start.13 = (bf16[512,768]{1,0:T(8,128)(2,1)S(1)}, bf16[512,768]{1,0:T(8,128)(2,1)}, u32[]{:S(2)}, u32[]{:S(2)}) collective-permute-start(bf16[512,768]{1,0:T(8,128)(2,1)S(1)} %slice.253), channel_id=1, source_target_pairs={{0,2},{1,3},{2,0},{3,1},{4,6},{5,7},{6,4},{7,5},{8,10},{9,11},{10,... | collective-permute-start | bytes 2359304 | tf_op jit(solution)/shard_map/ppermute | solution.py:808
  444.2 6.0 %collective-permute-start.16 = (bf16[96,1152]{1,0:T(8,128)(2,1)S(1)}, bf16[96,1152]{1,0:T(8,128)(2,1)S(1)}, u32[]{:S(2)}, u32[]{:S(2)}) collective-permute-start(bf16[96,1152]{1,0:T(8,128)(2,1)S(1)} %reduce_sum.115), channel_id=1, source_target_pairs={{0,2},{1,3},{2,0},{3,1},{4,6},{5,7},{6,4},{7,5},{8,10},{9,11},{10,... | collective-permute-start | bytes 663560 | tf_op jit(solution)/shard_map/ppermute | solution.py:808
  450.2 3.2 collective-permute-start.17
  453.7 16.0 %collective-permute-start.18 = (bf16[96,3072]{1,0:T(8,128)(2,1)}, bf16[96,3072]{1,0:T(8,128)(2,1)S(1)}, u32[]{:S(2)}, u32[]{:S(2)}) collective-permute-start(bf16[96,3072]{1,0:T(8,128)(2,1)} %reduce-scatter.2.cloned.1.call-done), channel_id=1, source_target_pairs={{0,2},{1,3},{2,0},{3,1},{4,6},{5,7},{6,4},{7,5},{8,10},{9,11},{10,... | collective-permute-start | bytes 1769480 | tf_op jit(solution)/shard_map/ppermute | solution.py:808
  470.9 2.1 collective-permute-start.19
  (20 other events, 202.1 us)
Sparse Core Ops, SparseCore 0:
  48.1 85.6 all-gather.1
  238.6 94.3 reduce-scatter.1

commit v4 on v3

--- a/solution.py
+++ b/solution.py
@@ -676,20 +676,18 @@
     shard, width = proj_ref.shape
     part = width // 2
     ff = fc1_ref.shape[1]
-    owners = one_ref.shape[0]
+    owners = width // shard
     quarter = ff // owners // 4
     half = ff // 2
-    one_ref[0, :VEC_ROWS, :] = jnp.zeros((VEC_ROWS, 3 * part), BF)
+    one_ref[:VEC_ROWS, :] = jnp.zeros((VEC_ROWS, 3 * part), BF)
     for at, ref in enumerate(vectors):
-        one_ref[0, at : at + 1, : ref.shape[1]] = ref[...]
+        one_ref[at : at + 1, : ref.shape[1]] = ref[...]
     for at in range(3):
         low = qkv_ref[:, at * width : at * width + part]
         high = qkv_ref[:, at * width + part : (at + 1) * width]
         mine = jnp.where(first_core, low, high)
         mine = jnp.where(first_chip, mine[: shard // 2], mine[shard // 2 :])
-        one_ref[0, VEC_ROWS:, at * part : (at + 1) * part] = mine
-    for owner in range(1, owners):
-        one_ref[owner] = one_ref[0]
+        one_ref[VEC_ROWS:, at * part : (at + 1) * part] = mine
     two_ref[:, :part] = jnp.where(first_core, proj_ref[:, :part], proj_ref[:, part:])
     pieces_low, pieces_high = [], []
     for piece in range(2):
@@ -707,7 +705,7 @@
         two_ref[:, start : start + width] = jnp.where(first_core, low, high)
 
 
-def pack_weights(place, owners, vectors, qkv, proj, fc1, fc2):
+def pack_weights(place, vectors, qkv, proj, fc1, fc2):
     shard, width = proj.shape
     half = fc1.shape[1] // 2
     part = width // 2
@@ -718,9 +716,9 @@
         pack_kernel,
         grid=(1,),
         in_specs=[pl.BlockSpec(memory_space=pltpu.SMEM)] + [whole(value.shape) for value in values],
-        out_specs=[whole((owners, rows, 3 * part)), whole((shard, 5 * part + half))],
+        out_specs=[whole((rows, 3 * part)), whole((shard, 5 * part + half))],
         out_shape=[
-            jax.ShapeDtypeStruct((owners, rows, 3 * part), BF),
+            jax.ShapeDtypeStruct((rows, 3 * part), BF),
             jax.ShapeDtypeStruct((shard, 5 * part + half), BF),
         ],
         compiler_params=params("arbitrary"),
@@ -817,9 +815,9 @@
         fc2_bias, fc1_bias,
     ]
     one, two = pack_weights(
-        place_row, owners, small, qkv_weight, proj_weight, fc1_weight, fc2_weight
-    )
-    mine_one = exchange(one)
+        place_row, small, qkv_weight, proj_weight, fc1_weight, fc2_weight
+    )
+    mine_one = lax.all_gather(one, "fsdp", axis=0, tiled=False)
     mine_one, two = lax.optimization_barrier((mine_one, two))
     second = lax.all_gather(two, "fsdp", axis=0, tiled=True)
     own_rows = mine_one[:, VEC_ROWS:]
@@ -860,19 +858,14 @@
     scattered_one = lax.psum_scatter(dw_ff, "fsdp", scatter_dimension=0, tiled=True)
     gn_sib = sibling(gn_part)
     rows_own = 2 * slots
-    out_sib = sibling(out_part[rows_own:])
-    out_own = (
-        middle[:rows_own] + out_part[:rows_own].astype(F32) + out_sib.astype(F32) + f2b
-    ).astype(BF)
-
-    def hand_back(own, sent):
+
+    def hand_back(own, came):
         kept_part = own[:slots]
-        came = partner(sent).astype(own.dtype)
+        came = came.astype(own.dtype)
         straight = jnp.stack([kept_part, came])
         crossed = jnp.stack([came, kept_part])
         return jnp.where(image == 0, straight, crossed)
 
-    output = hand_back(out_own, out_own[slots:])
     grad_middle, grad_mixed, grad_mixed_t, dwp_own, dwp_sib, vec_back = branch(
         core_row, middle, gn_part, gn_sib, cot, mixed, mixed_sib, wp_own, vec_two
     )
@@ -881,14 +874,23 @@
         jnp.concatenate([dwp_own, dwp_sib], axis=0),
         jnp.concatenate([dwp_sib, dwp_own], axis=0),
     )
+    grad_mixed, out_part = lax.optimization_barrier((grad_mixed, out_part))
+    out_sib = sibling(out_part[rows_own:])
     early, late = 2, 1
     attend = functools.partial(attend_backward, counts, place_row, packed, packed_t)
     before = attend(grad_mixed, grad_mixed_t, result_t, log_total, slots, 0, early)
     dw_early, qv_early = weight_grad(tok, *before, vec_one)
     block_one = jnp.concatenate([dw_early, dwp], axis=1).reshape(owners, shard, -1)
     came_one = exchange(block_one)
-    grad_mixed, output, block_one = lax.optimization_barrier((grad_mixed, output, block_one))
+    out_own = (
+        middle[:rows_own] + out_part[:rows_own].astype(F32) + out_sib.astype(F32) + f2b
+    ).astype(BF)
+    grad_mixed, out_own, block_one = lax.optimization_barrier((grad_mixed, out_own, block_one))
+    out_came = partner(out_own[slots:])
     grads = attend(grad_mixed, grad_mixed_t, result_t, log_total, slots, early, late)
+    vec_one, out_came, scattered_one = lax.optimization_barrier((vec_one, out_came, scattered_one))
+    one_came = partner(scattered_one)
+    output = hand_back(out_own, out_came)
     gn1_own, gn1_send, dw_late, vec_first, qv_late = project_back(
         tok, before, grads, w_qkv, vec_one
     )
@@ -923,25 +925,28 @@
     block_two = jnp.concatenate(
         [small_block, dw_late.reshape(owners, shard, late_wide)], axis=1
     )
-    came_two = exchange(block_two)
-
-    def total(came):
-        return jnp.sum(came.astype(F32), axis=0).astype(BF)
-
     gn1 = gn1_own + sibling(gn1_send).astype(F32)
     unit_own, inverse_own = normalised(tok[:rows_own].astype(F32))
     input_own = grad_middle + norm_pull(gn1, g1, unit_own, inverse_own)
-    input_grad = hand_back(input_own, input_own[slots:].astype(BF))
-
-    def finish(value):
-        summed = value.astype(F32) + partner(value).astype(F32)
+    block_two, came_one, one_came = lax.optimization_barrier((block_two, came_one, one_came))
+    came_two = exchange(block_two)
+    came_two, input_own = lax.optimization_barrier((came_two, input_own))
+
+    def total(came):
+        return jnp.sum(came.astype(F32), axis=0).astype(BF)
+
+    input_grad = hand_back(input_own, partner(input_own[slots:].astype(BF)))
+
+    def finish(value, came=None):
+        came = partner(value) if came is None else came
+        summed = value.astype(F32) + came.astype(F32)
         other = sibling(summed.astype(BF)).astype(F32)
         return summed, other
 
     def in_order(mine, other):
         return jnp.where(core == 0, mine, other), jnp.where(core == 0, other, mine)
 
-    one_mine, one_other = finish(scattered_one)
+    one_mine, one_other = finish(scattered_one, one_came)
     lower, upper = in_order(one_mine, one_other)
 
     def fc1_of(value):

time: 496 us -> 473 us (0.954)
  blocking collectives: 58.7 us -> 0 us
  local copies, waits for them, and re-layouts: 24.7 us -> 42.1 us
  waiting for transfers between devices: 103 us -> 114 us
  other arithmetic: 44.6 us -> 49.6 us
    all_to_all x2 -> x0, blocking collectives: 58.7 us -> none  [exchange(): lax.all_to_all(value, 'fsdp', split_axis=0, concat_axis=0, tiled=True)]
    all_gather x0 -> x1, waiting for transfers between devices: none -> 43.9 us  [per_device(): mine_one = lax.all_gather(one, 'fsdp', axis=0, tiled=False)]
    all_to_all x1 -> x2, waiting for transfers between devices: 17.3 us -> 0.01 us  [exchange(): lax.all_to_all(value, 'fsdp', split_axis=0, concat_axis=0, tiled=True)]
    ppermute x8, waiting for transfers between devices: 78.9 us -> 64.4 us  [partner(): return lax.ppermute(value, 'seq', to_partner)]
    unnamed x59 -> x53, local copies, waits for them, and re-layouts: 2.34 us -> 8.98 us
    all_to_all x1 -> x2, starting transfers between devices: 4.01 us -> 9.68 us  [exchange(): lax.all_to_all(value, 'fsdp', split_axis=0, concat_axis=0, tiled=True)]
  transfers between devices with their start and end apart: 23 -> 25, of which waited for: 13 -> 9; matrix products, arithmetic and copies ran while one was open for 11% -> 19% of each run, Pallas kernels for 34% -> 36%
where the time goes in v4:
time: 473 us; the launch traced here: 464 us
  Pallas kernels  224 us (47%)
  waiting for transfers between devices  114 us (24%)
  other arithmetic  49.6 us (10%)
  local copies, waits for them, and re-layouts  42.1 us (9%)
  starting transfers between devices  20.7 us (4%)
  between operations  14.5 us (3%)
    pallas_call x2, Pallas kernels, attend_backward(): pl.pallas_call(kernel, grid=(count, keys // bq), in_specs=[pl.BlockSpec(m...  69.7 us
    ppermute x8, waiting for transfers between devices, partner(): return lax.ppermute(value, 'seq', to_partner)  64.4 us
    pallas_call x1, Pallas kernels, feed_forward(): pl.pallas_call(kernel, grid=(blocks,), in_specs=[pl.BlockSpec(memory_spac...  55.4 us
    all_gather x1, waiting for transfers between devices, per_device(): mine_one = lax.all_gather(one, 'fsdp', axis=0, tiled=False)  43.9 us
    pallas_call x1, Pallas kernels, attend_forward(): pl.pallas_call(kernel, grid=(pairs, keys // bq), in_specs=[pl.BlockSpec(m...  42.2 us
    pallas_call x1, Pallas kernels, branch(): pl.pallas_call(branch_kernel, grid=(blocks,), in_specs=[pl.BlockSpec(memo...  16.5 us
    pallas_call x1, Pallas kernels, project_back(): pl.pallas_call(project_back_kernel, grid=(blocks,), in_specs=[pl.BlockSpe...  15.4 us
    pallas_call x1, Pallas kernels, project(): pl.pallas_call(project_kernel, grid=(rows // bt,), in_specs=[pl.BlockSpec...  11.5 us
  transfers between devices with their start and end apart: 25, of which 9 were waited for; matrix products, arithmetic and copies ran while one was open for 19% of the time, Pallas kernels for 36%

profile of v4, /device:TPU:0, one launch (start us, length us, event | category | flops | bytes accessed | tf_op | source)
XLA Modules:
  0.0 464.2 jit_solution(13676048814481685909)
XLA Ops:
  11.4 43.9 %all-gather.6.cloned.1.call-done = bf16[512,1152]{1,0:T(8,128)(2,1)} async-done(((bf16[64,1152]{1,0:T(8,128)(2,1)}), bf16[512,1152]{1,0:T(8,128)(2,1)}) %all-gather.6.cloned.1.call-update) | async-done | bytes 1179664 | tf_op jit(solution)/shard_map/all_gather | solution.py:820
  59.2 16.9 %collective-permute-done.4 = bf16[512,768]{1,0:T(8,128)(2,1)} collective-permute-done((bf16[512,768]{1,0:T(8,128)(2,1)S(1)}, bf16[512,768]{1,0:T(8,128)(2,1)}, u32[]{:S(2)}, u32[]{:S(2)}) %collective-permute-start.4) | collective-permute-done | bytes 786464 | tf_op jit(solution)/shard_map/ppermute | solution.py:806
  76.7 13.7 %collective-permute-done = bf16[512,768]{1,0:T(8,128)(2,1)S(1)} collective-permute-done((bf16[512,768]{1,0:T(8,128)(2,1)}, bf16[512,768]{1,0:T(8,128)(2,1)S(1)}, u32[]{:S(2)}, u32[]{:S(2)}) %collective-permute-start) | collective-permute-done | bytes 786464 | tf_op jit(solution)/shard_map/ppermute | solution.py:806
  90.4 3.2 pad_maximum_fusion.1.cot_ref
  96.4 7.4 %pad_maximum_fusion.tok_ref = bf16[2048,768]{1,0:T(8,128)(2,1)} fusion(bf16[512,768]{1,0:T(8,128)(2,1)S(1)} %collective-permute-done.2, bf16[512,768]{1,0:T(8,128)(2,1)} %collective-permute-done.1, bf16[512,768]{1,0:T(8,128)(2,1)S(1)} %collective-permute-done, bf16[512,768]{1,0:T(8,128)(2,1)S(1)} %get-tuple-element.121), kind=kLoop, calls=%fused_computation.11 | loop fusion | flops 12582912 | bytes 6291456 | tf_op jit(solution)/shard_map/concatenate | solution.py:833
  106.2 11.1 %collective-permute-done.3 = bf16[8,48,1152]{2,1,0:T(8,128)(2,1)} collective-permute-done((bf16[8,48,1152]{2,1,0:T(8,128)(2,1)}, bf16[8,48,1152]{2,1,0:T(8,128)(2,1)}, u32[]{:S(2)}, u32[]{:S(2)}) %collective-permute-start.3) | collective-permute-done | bytes 884768 | tf_op jit(solution)/shard_map/ppermute | solution.py:806
  117.3 3.6 maximum_select_fusion.1
  120.9 11.5 %project.1 = (bf16[2048,1152]{1,0:T(8,128)(2,1)}, bf16[1152,2048]{1,0:T(8,128)(2,1)}) custom-call(bf16[2048,768]{1,0:T(8,128)(2,1)} %pad_maximum_fusion.tok_ref, bf16[768,1152]{1,0:T(8,128)(2,1)} %bitcast.89, f32[1,1152]{1,0:T(1,128)} %reshape.186.bias_ref, f32[8,768]{1,0:T(8,128)} %maximum_maximum_fusion.vec_ref), custom_call_target="tpu_custom_call" | custom-call | flops 3623878656 | bytes 18874368 | tf_op jit(solution)/shard_map/project/pallas_call | solution.py:742
  132.4 42.2 %attend_forward.1 = (bf16[2048,384]{1,0:T(8,128)(2,1)}, f32[384,2048]{1,0:T(8,128)}, f32[3,8,2048]{2,1,0:T(8,128)}) custom-call(s32[2,4]{1,0:T(2,128)} %counts_ref.5, s32[1]{0:T(128)} %bitcast.3.place_ref, bf16[2048,1152]{1,0:T(8,128)(2,1)} %get-tuple-element.68.k_ref.q_ref.v_ref, bf16[1152,2048]{1,0:T(8,128)(2,1)} %get-tuple-element.69.qt_ref.vt_ref.kt_ref, ...), custom_call_target="tpu_custom_call" | custom-call | flops 25769803776 | bytes 9437184 | tf_op jit(solution)/shard_map/attend_forward/pallas_call | solution.py:163
  179.1 55.4 %feed_forward.1 = (f32[2048,768]{1,0:T(8,128)}, bf16[2048,768]{1,0:T(8,128)(2,1)}, bf16[2048,768]{1,0:T(8,128)(2,1)}, bf16[768,3072]{1,0:T(8,128)(2,1)}, f32[8,1...) custom-call(s32[1]{0:T(128)} %bitcast.core_ref, bf16[2048,768]{1,0:T(8,128)(2,1)} %pad_maximum_fusion.tok_ref, ...), custom_call_target="tpu_custom_call" | custom-call | flops 31406948352 | bytes 40894464 | tf_op jit(solution)/shard_map/feed_forward/pallas_call | solution.py:394
  236.0 4.5 collective-permute-done.9.gb_ref
  240.5 16.5 %branch.1 = (f32[1024,768]{1,0:T(8,128)}, bf16[2048,384]{1,0:T(8,128)(2,1)}, bf16[384,2048]{1,0:T(8,128)(2,1)}, bf16[384,384]{1,0:T(8,128)(2,1)}, bf16[384,384]{1,0:T(8,128)(2,1)}, /*index=5*/f32[24,768]{1,0:T(8,128)}) custom-call(s32[1]{0:T(128)} %bitcast.core_ref, f32[2048,768]{1,0:T(8,128)} %get-tuple-element.73.mid_ref, ...), custom_call_target="tpu_custom_call" | custom-call | flops 3623878656 | bytes 28311552 | tf_op jit(solution)/shard_map/branch/pallas_call | solution.py:489
  259.9 45.6 %attend_backward.2 = (bf16[2048,256]{1,0:T(8,128)(2,1)}, bf16[2048,256]{1,0:T(8,128)(2,1)}, bf16[2048,256]{1,0:T(8,128)(2,1)}) custom-call(s32[2,4]{1,0:T(2,128)} %counts_ref.5, s32[1]{0:T(128)} %bitcast.3.place_ref, bf16[2048,1152]{1,0:T(8,128)(2,1)} %get-tuple-element.68.k_ref.q_ref.v_ref, bf16[2048,1152]{1,0:T(8,128)(2,1)} %get-tuple-element.68.k_ref.q_ref.v_ref, ...), custom_call_target="tpu_custom_call" | custom-call | flops 42949672960 | bytes 12582912 | tf_op jit(solution)/shard_map/attend_backward/pallas_call | solution.py:263
  306.0 10.1 %weight_grad.1 = (bf16[768,768]{1,0:T(8,128)(2,1)}, f32[16,256]{1,0:T(8,128)}) custom-call(bf16[2048,768]{1,0:T(8,128)(2,1)} %pad_maximum_fusion.tok_ref, bf16[2048,256]{1,0:T(8,128)(2,1)} %get-tuple-element.83.gq_ref.gqa_ref, bf16[2048,256]{1,0:T(8,128)(2,1)} %get-tuple-element.84.gk_ref.gka_ref, bf16[2048,256]{1,0:T(8,128)(2,1)} %get-tuple-element.85.gv_ref.gva_ref, ...), custom_call_target="tpu_custom_call" | custom-call | flops 2415919104 | bytes 6291456 | tf_op jit(solution)/shard_map/weight_grad/pallas_call | solution.py:562
  318.8 3.8 all-to-all-start
  322.5 3.4 add_convert_fusion
  328.9 24.0 %attend_backward.3 = (bf16[2048,128]{1,0:T(8,128)(2,1)}, bf16[2048,128]{1,0:T(8,128)(2,1)}, bf16[2048,128]{1,0:T(8,128)(2,1)}) custom-call(s32[2,4]{1,0:T(2,128)} %counts_ref.5, s32[1]{0:T(128)} %bitcast.3.place_ref, bf16[2048,1152]{1,0:T(8,128)(2,1)} %get-tuple-element.68.k_ref.q_ref.v_ref, bf16[2048,1152]{1,0:T(8,128)(2,1)} %get-tuple-element.68.k_ref.q_ref.v_ref, ...), custom_call_target="tpu_custom_call" | custom-call | flops 21474836480 | bytes 6291456 | tf_op jit(solution)/shard_map/attend_backward/pallas_call | solution.py:263
  353.0 15.4 %project_back.1 = (f32[1024,768]{1,0:T(8,128)}, bf16[1024,768]{1,0:T(8,128)(2,1)}, bf16[768,384]{1,0:T(8,128)(2,1)}, f32[16,768]{1,0:T(8,128)}, f32[16,128]{1,0:T(8,128)}) custom-call(bf16[2048,768]{1,0:T(8,128)(2,1)} %pad_maximum_fusion.tok_ref, bf16[2048,256]{1,0:T(8,128)(2,1)} %get-tuple-element.83.gq_ref.gqa_ref, ...), custom_call_target="tpu_custom_call" | custom-call | flops 4831838208 | bytes 22020096 | tf_op jit(solution)/shard_map/project_back/pallas_call | solution.py:640
  372.7 13.1 %collective-permute-done.12 = bf16[96,3072]{1,0:T(8,128)(2,1)} collective-permute-done((bf16[96,3072]{1,0:T(8,128)(2,1)}, bf16[96,3072]{1,0:T(8,128)(2,1)}, u32[]{:S(2)}, u32[]{:S(2)}) %collective-permute-start.12) | collective-permute-done | bytes 589856 | tf_op jit(solution)/shard_map/ppermute | solution.py:806
  387.2 3.3 maximum_select_fusion.2
  390.5 5.9 %all-to-all-start.1 = ((bf16[8,112,384]{2,1,0:T(8,128)(2,1)}), bf16[8,112,384]{2,1,0:T(8,128)(2,1)}, u32[]{:S(2)}, u32[]{:S(2)}) async-start(bf16[8,112,384]{2,1,0:T(8,128)(2,1)} %fusion.15), calls=%async_computation.2 | async-start | bytes 1376256 | tf_op jit(solution)/shard_map/all_to_all | solution.py:766
  416.8 3.9 fusion.13
  429.2 3.2 reshape.196
  445.9 9.6 %collective-permute-done.14 = bf16[512,768]{1,0:T(8,128)(2,1)S(1)} collective-permute-done((bf16[512,768]{1,0:T(8,128)(2,1)S(1)}, bf16[512,768]{1,0:T(8,128)(2,1)S(1)}, u32[]{:S(2)}, u32[]{:S(2)}) %collective-permute-start.14) | collective-permute-done | bytes 786464 | tf_op jit(solution)/shard_map/ppermute | solution.py:806
  (196 shorter events, 78.5 us)
Async XLA Ops:
  7.2 48.1 %all-gather.6.cloned.1.call-start = ((), (), s32[]{:S(2)}) async-start(), calls=%async_computation.5 | async-start | bytes 1327104 | tf_op jit(solution)/shard_map/all_gather | solution.py:820
  11.3 163.4 %all-gather.4.cloned.1.call-start = ((), (), s32[]{:S(2)}) async-start(), calls=%async_computation.3 | async-start | bytes 5971968 | tf_op jit(solution)/shard_map/all_gather | solution.py:822
  55.3 297.7 %reduce-scatter.2.cloned.1.call-start = ((), (), s32[]{:S(2)}) async-start(), calls=%async_computation.4 | async-start | bytes 5308416 | tf_op jit(solution)/shard_map/reduce_scatter | solution.py:858
  55.5 20.7 %collective-permute-start.4 = (bf16[512,768]{1,0:T(8,128)(2,1)S(1)}, bf16[512,768]{1,0:T(8,128)(2,1)}, u32[]{:S(2)}, u32[]{:S(2)}) collective-permute-start(bf16[512,768]{1,0:T(8,128)(2,1)S(1)} %get-tuple-element.120), channel_id=1, source_target_pairs={{0,2},{1,3},{2,0},{3,1},{4,6},{5,7},{6,4},{7,5},{8,10},{9,11},{10,... | collective-permute-start | bytes 2359304 | tf_op jit(solution)/shard_map/ppermute | solution.py:806
  58.0 32.4 %collective-permute-start = (bf16[512,768]{1,0:T(8,128)(2,1)}, bf16[512,768]{1,0:T(8,128)(2,1)S(1)}, u32[]{:S(2)}, u32[]{:S(2)}) collective-permute-start(bf16[512,768]{1,0:T(8,128)(2,1)} %get-tuple-element.122), channel_id=1, source_target_pairs={{0,2},{1,3},{2,0},{3,1},{4,6},{5,7},{6,4},{7,5},{8,10},{9,11},{10,... | collective-permute-start | bytes 2359304 | tf_op jit(solution)/shard_map/ppermute | solution.py:806
  59.2 31.2 %collective-permute-start.5 = (bf16[512,768]{1,0:T(8,128)(2,1)S(1)}, bf16[512,768]{1,0:T(8,128)(2,1)}, u32[]{:S(2)}, u32[]{:S(2)}) collective-permute-start(bf16[512,768]{1,0:T(8,128)(2,1)S(1)} %get-tuple-element.119), channel_id=1, source_target_pairs={{0,1},{1,0},{2,3},{3,2},{4,5},{5,4},{6,7},{7,6},{8,9},{9,8},{10,11... | collective-permute-start | bytes 2359304 | tf_op jit(solution)/shard_map/ppermute | solution.py:803
  76.1 14.3 %collective-permute-start.6 = (bf16[512,768]{1,0:T(8,128)(2,1)}, bf16[512,768]{1,0:T(8,128)(2,1)}, u32[]{:S(2)}, u32[]{:S(2)}) collective-permute-start(bf16[512,768]{1,0:T(8,128)(2,1)} %collective-permute-done.4), channel_id=1, source_target_pairs={{0,1},{1,0},{2,3},{3,2},{4,5},{5,4},{6,7},{7,6},{8,9},{9,8},{10,11... | collective-permute-start | bytes 2359304 | tf_op jit(solution)/shard_map/ppermute | solution.py:803
  76.1 20.3 %collective-permute-start.1 = (bf16[512,768]{1,0:T(8,128)(2,1)S(1)}, bf16[512,768]{1,0:T(8,128)(2,1)}, u32[]{:S(2)}, u32[]{:S(2)}) collective-permute-start(bf16[512,768]{1,0:T(8,128)(2,1)S(1)} %get-tuple-element.121), channel_id=1, source_target_pairs={{0,1},{1,0},{2,3},{3,2},{4,5},{5,4},{6,7},{7,6},{8,9},{9,8},{10,11... | collective-permute-start | bytes 2359304 | tf_op jit(solution)/shard_map/ppermute | solution.py:803
  90.4 6.0 %collective-permute-start.2 = (bf16[512,768]{1,0:T(8,128)(2,1)S(1)}, bf16[512,768]{1,0:T(8,128)(2,1)S(1)}, u32[]{:S(2)}, u32[]{:S(2)}) collective-permute-start(bf16[512,768]{1,0:T(8,128)(2,1)S(1)} %collective-permute-done), channel_id=1, source_target_pairs={{0,1},{1,0},{2,3},{3,2},{4,5},{5,4},{6,7},{7,6},{8,9},{9,8},{10,11... | collective-permute-start | bytes 2359304 | tf_op jit(solution)/shard_map/ppermute | solution.py:803
  95.0 22.4 %collective-permute-start.3 = (bf16[8,48,1152]{2,1,0:T(8,128)(2,1)}, bf16[8,48,1152]{2,1,0:T(8,128)(2,1)}, u32[]{:S(2)}, u32[]{:S(2)}) collective-permute-start(bf16[8,48,1152]{2,1,0:T(8,128)(2,1)} %get-tuple-element.128), channel_id=1, source_target_pairs={{0,2},{1,3},{2,0},{3,1},{4,6},{5,7},{6,4},{7,5},{8,10},{9,11},{10,... | collective-permute-start | bytes 2654216 | tf_op jit(solution)/shard_map/ppermute | solution.py:806
  174.7 3.8 collective-permute-start.7
  175.8 3.2 collective-permute-start.8
  234.4 6.1 %collective-permute-start.9 = (bf16[2048,768]{1,0:T(8,128)(2,1)}, bf16[2048,768]{1,0:T(8,128)(2,1)}, u32[]{:S(2)}, u32[]{:S(2)}) collective-permute-start(bf16[2048,768]{1,0:T(8,128)(2,1)} %get-tuple-element.74.ga_ref), channel_id=1, source_target_pairs={{0,1},{1,0},{2,3},{3,2},{4,5},{5,4},{6,7},{7,6},{8,9},{9,8},{10,11... | collective-permute-start | bytes 9437192 | tf_op jit(solution)/shard_map/ppermute | solution.py:803
  259.7 62.9 %collective-permute-start.10 = (bf16[1024,768]{1,0:T(8,128)(2,1)}, bf16[1024,768]{1,0:T(8,128)(2,1)}, u32[]{:S(2)}, u32[]{:S(2)}) collective-permute-start(bf16[1024,768]{1,0:T(8,128)(2,1)} %slice.146), channel_id=1, source_target_pairs={{0,1},{1,0},{2,3},{3,2},{4,5},{5,4},{6,7},{7,6},{8,9},{9,8},{10,11... | collective-permute-start | bytes 4718600 | tf_op jit(solution)/shard_map/ppermute | solution.py:803
  318.8 54.0 %all-to-all-start = ((bf16[8,96,1152]{2,1,0:T(8,128)(2,1)}), bf16[8,96,1152]{2,1,0:T(8,128)(2,1)S(1)}, u32[]{:S(2)}, u32[]{:S(2)}) async-start(bf16[8,96,1152]{2,1,0:T(8,128)(2,1)} %bitcast.81), calls=%async_computation.1 | async-start | bytes 3538944 | tf_op jit(solution)/shard_map/all_to_all | solution.py:766
  327.2 25.7 %collective-permute-start.11 = (bf16[512,768]{1,0:T(8,128)(2,1)}, bf16[512,768]{1,0:T(8,128)(2,1)}, u32[]{:S(2)}, u32[]{:S(2)}) collective-permute-start(bf16[512,768]{1,0:T(8,128)(2,1)} %get-tuple-element.118), channel_id=1, source_target_pairs={{0,2},{1,3},{2,0},{3,1},{4,6},{5,7},{6,4},{7,5},{8,10},{9,11},{10,... | collective-permute-start | bytes 2359304 | tf_op jit(solution)/shard_map/ppermute | solution.py:806
  370.3 15.5 %collective-permute-start.12 = (bf16[96,3072]{1,0:T(8,128)(2,1)}, bf16[96,3072]{1,0:T(8,128)(2,1)}, u32[]{:S(2)}, u32[]{:S(2)}) collective-permute-start(bf16[96,3072]{1,0:T(8,128)(2,1)} %reduce-scatter.2.cloned.1.call-done), channel_id=1, source_target_pairs={{0,2},{1,3},{2,0},{3,1},{4,6},{5,7},{6,4},{7,5},{8,10},{9,11},{10,... | collective-permute-start | bytes 1769480 | tf_op jit(solution)/shard_map/ppermute | solution.py:806
  386.8 9.7 %collective-permute-start.17 = (bf16[96,1152]{1,0:T(8,128)(2,1)}, bf16[96,1152]{1,0:T(8,128)(2,1)}, u32[]{:S(2)}, u32[]{:S(2)}) collective-permute-start(bf16[96,1152]{1,0:T(8,128)(2,1)} %reduce_sum.115), channel_id=1, source_target_pairs={{0,2},{1,3},{2,0},{3,1},{4,6},{5,7},{6,4},{7,5},{8,10},{9,11},{10,... | collective-permute-start | bytes 663560 | tf_op jit(solution)/shard_map/ppermute | solution.py:806
  387.2 29.6 %collective-permute-start.13 = (bf16[1024,768]{1,0:T(8,128)(2,1)}, bf16[1024,768]{1,0:T(8,128)(2,1)S(1)}, u32[]{:S(2)}, u32[]{:S(2)}) collective-permute-start(bf16[1024,768]{1,0:T(8,128)(2,1)} %get-tuple-element.108), channel_id=1, source_target_pairs={{0,1},{1,0},{2,3},{3,2},{4,5},{5,4},{6,7},{7,6},{8,9},{9,8},{10,11... | collective-permute-start | bytes 4718600 | tf_op jit(solution)/shard_map/ppermute | solution.py:803
  390.5 33.4 %all-to-all-start.1 = ((bf16[8,112,384]{2,1,0:T(8,128)(2,1)}), bf16[8,112,384]{2,1,0:T(8,128)(2,1)}, u32[]{:S(2)}, u32[]{:S(2)}) async-start(bf16[8,112,384]{2,1,0:T(8,128)(2,1)} %fusion.15), calls=%async_computation.2 | async-start | bytes 1376256 | tf_op jit(solution)/shard_map/all_to_all | solution.py:766
  399.2 2.9 collective-permute-start.19
  425.1 7.3 %collective-permute-start.15 = (bf16[112,384]{1,0:T(8,128)(2,1)S(1)}, bf16[112,384]{1,0:T(8,128)(2,1)S(1)}, u32[]{:S(2)}, u32[]{:S(2)}) collective-permute-start(bf16[112,384]{1,0:T(8,128)(2,1)S(1)} %reduce_sum.114), channel_id=1, source_target_pairs={{0,2},{1,3},{2,0},{3,1},{4,6},{5,7},{6,4},{7,5},{8,10},{9,11},{10,... | collective-permute-start | bytes 258056 | tf_op jit(solution)/shard_map/ppermute | solution.py:806
  432.4 3.5 collective-permute-start.16
  435.5 20.0 %collective-permute-start.14 = (bf16[512,768]{1,0:T(8,128)(2,1)S(1)}, bf16[512,768]{1,0:T(8,128)(2,1)S(1)}, u32[]{:S(2)}, u32[]{:S(2)}) collective-permute-start(bf16[512,768]{1,0:T(8,128)(2,1)S(1)} %slice.251), channel_id=1, source_target_pairs={{0,2},{1,3},{2,0},{3,1},{4,6},{5,7},{6,4},{7,5},{8,10},{9,11},{10,... | collective-permute-start | bytes 2359304 | tf_op jit(solution)/shard_map/ppermute | solution.py:806
  (19 other events, 302.0 us)
Sparse Core Ops, SparseCore 0:
  11.5 43.7 all-gather.5
  58.0 85.8 all-gather.3
  234.8 95.1 reduce-scatter.1

commit v5 on v4

--- a/solution.py
+++ b/solution.py
@@ -317,7 +317,7 @@
 
 def feed_forward_kernel(
     chunk, core_ref, tok_ref, mo_ref, ms_ref, cot_ref, wpx_ref, g2_ref, vec_ref, f1b_ref,
-    mid_ref, out_ref, gn_ref, dw_ref, gf1_ref, gf2_ref, wpo_ref, acc1, acc2, accb, accc, wps_ref
+    mid_ref, out_ref, send_ref, gn_ref, dw_ref, gf1_ref, gf2_ref, wpo_ref, acc1, acc2, accb, accc, wps_ref
 ):
     step = pl.program_id(0)
     steps = pl.num_programs(0)
@@ -370,8 +370,15 @@
         acc2[cols, :] += dot(active, cot, 0, 0)
         accb[:, cols] += fold(grad_hidden.astype(F32))
     accc[...] += fold(cot.astype(F32))
-    out_ref[...] = out.astype(BF)
     gn_ref[...] = grad.astype(BF)
+
+    @pl.when(step < steps // 2)
+    def _():
+        out_ref[...] = middle + out + vec_ref[3:4, :]
+
+    @pl.when(step >= steps // 2)
+    def _():
+        send_ref[...] = out.astype(BF)
 
     @pl.when(step == steps - 1)
     def _():
@@ -407,7 +414,8 @@
         ],
         out_specs=[
             pl.BlockSpec((bt, width), lambda i: (i, 0)),
-            pl.BlockSpec((bt, width), lambda i: (i, 0)),
+            pl.BlockSpec((bt, width), lambda i: (jnp.minimum(i, blocks // 2 - 1), 0)),
+            pl.BlockSpec((bt, width), lambda i: (jnp.maximum(i - blocks // 2, 0), 0)),
             pl.BlockSpec((bt, width), lambda i: (i, 0)),
             whole((width, 2 * half)),
             whole((8, half)),
@@ -416,7 +424,8 @@
         ],
         out_shape=[
             jax.ShapeDtypeStruct((rows, width), F32),
-            jax.ShapeDtypeStruct((rows, width), BF),
+            jax.ShapeDtypeStruct((rows // 2, width), F32),
+            jax.ShapeDtypeStruct((rows // 2, width), BF),
             jax.ShapeDtypeStruct((rows, width), BF),
             jax.ShapeDtypeStruct((width, 2 * half), BF),
             jax.ShapeDtypeStruct((8, half), F32),
@@ -528,7 +537,7 @@
     )(core, middle, grad_own, grad_sib, cot, mixed_own, mixed_sib, wp_own, vec)
 
 
-def weight_grad_kernel(tok_ref, gq_ref, gk_ref, gv_ref, vec_ref, dw_ref, qv_ref, accw, accqv):
+def weight_grad_kernel(normed_ref, gq_ref, gk_ref, gv_ref, dw_ref, qv_ref, accw, accqv):
     step = pl.program_id(0)
     steps = pl.num_programs(0)
     part = gq_ref.shape[1]
@@ -538,8 +547,7 @@
         accw[...] = jnp.zeros_like(accw)
         accqv[...] = jnp.zeros_like(accqv)
 
-    unit, _ = normalised(tok_ref[...].astype(F32))
-    normed_t = (unit * vec_ref[0:1, :] + vec_ref[1:2, :]).astype(BF).T
+    normed_t = normed_ref[...].T
     for at, ref in enumerate((gq_ref, gk_ref, gv_ref)):
         cols = slice(at * part, (at + 1) * part)
         value = ref[...]
@@ -554,8 +562,8 @@
         qv_ref[...] = accqv[...]
 
 
-def weight_grad(tokens, gq, gk, gv, vec):
-    rows, width = tokens.shape
+def weight_grad(normed, gq, gk, gv):
+    rows, width = normed.shape
     part = gq.shape[1]
     bt = 256
     straight = lambda i: (i, 0)
@@ -567,7 +575,6 @@
             pl.BlockSpec((bt, part), straight),
             pl.BlockSpec((bt, part), straight),
             pl.BlockSpec((bt, part), straight),
-            whole(vec.shape),
         ],
         out_specs=[whole((width, 3 * part)), whole((16, part))],
         out_shape=[
@@ -578,11 +585,11 @@
         compiler_params=params("arbitrary"),
         cost_estimate=cost(2 * rows * width * 3 * part, 2 * rows * (width + 3 * part)),
         name="weight_grad",
-    )(tokens, gq, gk, gv, vec)
+    )(normed, gq, gk, gv)
 
 
 def project_back_kernel(
-    tok_ref, gqa_ref, gka_ref, gva_ref, gq_ref, gk_ref, gv_ref, w_ref, vec_ref,
+    tok_ref, normed_ref, gqa_ref, gka_ref, gva_ref, gq_ref, gk_ref, gv_ref, w_ref,
     own_ref, sib_ref, dw_ref, vecs_ref, qv_ref, accw, accv, accqv
 ):
     step = pl.program_id(0)
@@ -598,7 +605,7 @@
         accqv[...] = jnp.zeros_like(accqv)
 
     unit, _ = normalised(tok_ref[...].astype(F32))
-    normed_t = (unit * vec_ref[0:1, :] + vec_ref[1:2, :]).astype(BF).T
+    normed_t = normed_ref[...].T
     grad = None
     before = (gqa_ref, gka_ref, gva_ref)
     for at, ref in enumerate((gq_ref, gk_ref, gv_ref)):
@@ -631,7 +638,7 @@
         qv_ref[...] = accqv[...]
 
 
-def project_back(tokens, before, grads, weight, vec):
+def project_back(tokens, normed, before, grads, weight):
     rows, width = tokens.shape
     early, part = before[0].shape[1], grads[0].shape[1]
     bt = 256
@@ -640,10 +647,10 @@
     return pl.pallas_call(
         project_back_kernel,
         grid=(blocks,),
-        in_specs=[pl.BlockSpec((bt, width), straight)]
+        in_specs=[pl.BlockSpec((bt, width), straight)] * 2
         + [pl.BlockSpec((bt, early), straight)] * 3
         + [pl.BlockSpec((bt, part), straight)] * 3
-        + [whole(weight.shape), whole(vec.shape)],
+        + [whole(weight.shape)],
         out_specs=[
             pl.BlockSpec((bt, width), lambda i: (jnp.minimum(i, blocks // 2 - 1), 0)),
             pl.BlockSpec((bt, width), lambda i: (jnp.maximum(i - blocks // 2, 0), 0)),
@@ -666,7 +673,134 @@
         compiler_params=params("arbitrary"),
         cost_estimate=cost(2 * rows * width * (6 * part + 3 * early), 14 * rows * width),
         name="project_back",
-    )(tokens, *before, *grads, weight, vec)
+    )(tokens, normed, *before, *grads, weight)
+
+
+def input_back_kernel(tok_ref, own_ref, sib_ref, gm_ref, vec_ref, keep_ref, send_ref):
+    unit, inverse = normalised(tok_ref[...].astype(F32))
+    grad = own_ref[...] + sib_ref[...].astype(F32)
+    total = gm_ref[...] + norm_pull(grad, vec_ref[0:1, :], unit, inverse)
+    step = pl.program_id(0)
+    steps = pl.num_programs(0)
+
+    @pl.when(step < steps // 2)
+    def _():
+        keep_ref[...] = total
+
+    @pl.when(step >= steps // 2)
+    def _():
+        send_ref[...] = total.astype(BF)
+
+
+def input_back(tokens, grad_own, grad_sib, grad_middle, vec):
+    rows, width = grad_own.shape
+    bt = 256
+    blocks = rows // bt
+    straight = lambda i: (i, 0)
+    return pl.pallas_call(
+        input_back_kernel,
+        grid=(blocks,),
+        in_specs=[pl.BlockSpec((bt, width), straight)] * 4 + [whole(vec.shape)],
+        out_specs=[
+            pl.BlockSpec((bt, width), lambda i: (jnp.minimum(i, blocks // 2 - 1), 0)),
+            pl.BlockSpec((bt, width), lambda i: (jnp.maximum(i - blocks // 2, 0), 0)),
+        ],
+        out_shape=[
+            jax.ShapeDtypeStruct((rows // 2, width), F32),
+            jax.ShapeDtypeStruct((rows // 2, width), BF),
+        ],
+        compiler_params=params("arbitrary"),
+        cost_estimate=cost(20 * rows * width, 16 * rows * width),
+        name="input_back",
+    )(tokens, grad_own, grad_sib, grad_middle, vec)
+
+
+def finish_ff_kernel(place_ref, mine_ref, other_ref, fc1_ref, fc2_ref):
+    first_core = lax.rem(place_ref[0], 2) == 0
+    shard, ff = fc1_ref.shape
+    half = ff // 2
+    quarter = fc2_ref.shape[0] // 4
+    width = fc2_ref.shape[1]
+    owners = ff // (4 * quarter)
+    mine = mine_ref[...].astype(F32)
+    other = other_ref[...].astype(F32)
+    cores = (jnp.where(first_core, mine, other), jnp.where(first_core, other, mine))
+    pieces = []
+    for owner in range(owners):
+        for value in cores:
+            for piece in range(2):
+                start = (piece * owners + owner) * quarter
+                pieces.append(value[:, start : start + quarter])
+    fc1_ref[...] = jnp.concatenate(pieces, axis=1)
+    for at, value in enumerate(cores):
+        for piece in range(2):
+            row = (2 * at + piece) * quarter
+            start = half + piece * width
+            fc2_ref[row : row + quarter, :] = value[:, start : start + width]
+
+
+def finish_ff(place, mine, other, width, quarter):
+    shard, wide = mine.shape
+    return pl.pallas_call(
+        finish_ff_kernel,
+        grid=(1,),
+        in_specs=[
+            pl.BlockSpec(memory_space=pltpu.SMEM), whole(mine.shape), whole(other.shape)
+        ],
+        out_specs=[whole((shard, wide)), whole((4 * quarter, width))],
+        out_shape=[
+            jax.ShapeDtypeStruct((shard, wide), F32),
+            jax.ShapeDtypeStruct((4 * quarter, width), F32),
+        ],
+        compiler_params=params("arbitrary"),
+        cost_estimate=cost(0, 12 * shard * wide),
+        name="finish_ff",
+    )(place, mine, other)
+
+
+def finish_attend_kernel(place_ref, em_ref, eo_ref, lm_ref, lo_ref, qkv_ref, proj_ref, small_ref):
+    first_core = lax.rem(place_ref[0], 2) == 0
+    shard, width = proj_ref.shape
+    part = width // 2
+    late = lm_ref.shape[1] // 3
+    early = part - late
+    rows = lm_ref.shape[0] - shard
+    lm = lm_ref[...].astype(F32)
+    lo = lo_ref[...].astype(F32)
+    small_ref[...] = lm[:rows] + lo[:rows]
+    em = em_ref[...].astype(F32)
+    eo = eo_ref[...].astype(F32)
+    firsts = (jnp.where(first_core, em, eo), jnp.where(first_core, eo, em))
+    lasts = (jnp.where(first_core, lm, lo)[rows:], jnp.where(first_core, lo, lm)[rows:])
+    for at in range(3):
+        for of in range(2):
+            start = at * width + of * part
+            qkv_ref[:, start : start + early] = firsts[of][:, at * early : (at + 1) * early]
+            qkv_ref[:, start + early : start + part] = lasts[of][:, at * late : (at + 1) * late]
+    for of in range(2):
+        proj_ref[:, of * part : (of + 1) * part] = firsts[of][:, 3 * early :]
+
+
+def finish_attend(place, early_mine, early_other, late_mine, late_other, width):
+    shard = early_mine.shape[0]
+    rows = late_mine.shape[0] - shard
+    return pl.pallas_call(
+        finish_attend_kernel,
+        grid=(1,),
+        in_specs=[pl.BlockSpec(memory_space=pltpu.SMEM)]
+        + [whole(value.shape) for value in (early_mine, early_other, late_mine, late_other)],
+        out_specs=[
+            whole((shard, 3 * width)), whole((shard, width)), whole((rows, late_mine.shape[1]))
+        ],
+        out_shape=[
+            jax.ShapeDtypeStruct((shard, 3 * width), F32),
+            jax.ShapeDtypeStruct((shard, width), F32),
+            jax.ShapeDtypeStruct((rows, late_mine.shape[1]), F32),
+        ],
+        compiler_params=params("arbitrary"),
+        cost_estimate=cost(0, 24 * shard * width),
+        name="finish_attend",
+    )(place, early_mine, early_other, late_mine, late_other)
 
 
 def pack_kernel(place_ref, *refs):
@@ -727,9 +861,10 @@
     )(place, *values)
 
 
-def project_kernel(tok_ref, w_ref, bias_ref, vec_ref, out_ref, out_t_ref):
+def project_kernel(tok_ref, w_ref, bias_ref, vec_ref, out_ref, out_t_ref, normed_ref):
     unit, _ = normalised(tok_ref[...].astype(F32))
     normed = (unit * vec_ref[0:1, :] + vec_ref[1:2, :]).astype(BF)
+    normed_ref[...] = normed
     packed = dot(normed, w_ref[...]) + bias_ref[0:1, :]
     out_ref[...] = packed.astype(BF)
     out_t_ref[...] = packed.T.astype(BF)
@@ -751,10 +886,12 @@
         out_specs=[
             pl.BlockSpec((bt, wide), lambda i: (i, 0)),
             pl.BlockSpec((wide, bt), lambda i: (0, i)),
+            pl.BlockSpec((bt, width), lambda i: (i, 0)),
         ],
         out_shape=[
             jax.ShapeDtypeStruct((rows, wide), BF),
             jax.ShapeDtypeStruct((wide, rows), BF),
+            jax.ShapeDtypeStruct((rows, width), BF),
         ],
         compiler_params=params("arbitrary"),
         cost_estimate=cost(2 * rows * width * wide, 12 * rows * width),
@@ -817,9 +954,21 @@
     one, two = pack_weights(
         place_row, small, qkv_weight, proj_weight, fc1_weight, fc2_weight
     )
+    one, tokens, cotangent = lax.optimization_barrier((one, tokens, cotangent))
     mine_one = lax.all_gather(one, "fsdp", axis=0, tiled=False)
-    mine_one, two = lax.optimization_barrier((mine_one, two))
+    def collect(value, theirs):
+        mine = pick(value, image, 0)
+        return jnp.concatenate([mine, theirs, sibling(mine), sibling(theirs)], axis=0)
+
+    tok_came = partner(pick(tokens, 1 - image, 0))
+    cot_came = partner(pick(cotangent, 1 - image, 0))
+    mine_one, two, tok_came, cot_came = lax.optimization_barrier(
+        (mine_one, two, tok_came, cot_came)
+    )
+    tok = collect(tokens, tok_came)
+    cot = collect(cotangent, cot_came)
     second = lax.all_gather(two, "fsdp", axis=0, tiled=True)
+
     own_rows = mine_one[:, VEC_ROWS:]
     other_rows = partner(own_rows)
     w_qkv = jnp.where(
@@ -828,11 +977,6 @@
         jnp.stack([other_rows, own_rows], axis=1),
     ).reshape(width, 3 * part)
 
-    def collect(value, theirs):
-        mine = pick(value, image, 0)
-        return jnp.concatenate([mine, theirs, sibling(mine), sibling(theirs)], axis=0)
-
-    tok = collect(tokens, partner(pick(tokens, 1 - image, 0)))
     vecs = mine_one[:, :8, :shard].astype(F32).transpose(1, 0, 2).reshape(8, width)
     g1, b1, qb, vb, pb, g2, b2, f2b = vecs
     f1b = mine_one[:, 8, :ff_shard].astype(F32)
@@ -844,15 +988,14 @@
 
     qkv_bias = jnp.concatenate([mine_of(qb), jnp.zeros((part,), F32), mine_of(vb)])
     vec_one = jnp.concatenate([jnp.stack([g1, b1]), jnp.zeros((6, width), F32)])
-    packed, packed_t = project(tok, w_qkv, qkv_bias.reshape(1, 3 * part), vec_one)
-    cot = collect(cotangent, partner(pick(cotangent, 1 - image, 0)))
+    packed, packed_t, normed = project(tok, w_qkv, qkv_bias.reshape(1, 3 * part), vec_one)
     packed, cot = lax.optimization_barrier((packed, cot))
     mixed, result_t, log_total = attend_forward(counts, place_row, packed, packed_t, slots)
     mixed_sib = sibling(mixed)
 
     wp_other = sibling(second[:, :part])
-    vec_two = jnp.concatenate([jnp.stack([pb, g2, b2]), jnp.zeros((5, width), F32)])
-    middle, out_part, gn_part, dw_ff, gf1, gf2, wp_own = feed_forward(
+    vec_two = jnp.concatenate([jnp.stack([pb, g2, b2, f2b]), jnp.zeros((4, width), F32)])
+    middle, out_own, out_send, gn_part, dw_ff, gf1, gf2, wp_own = feed_forward(
         core_row, tok, mixed, mixed_sib, cot, wp_other, second, vec_two, f1b
     )
     scattered_one = lax.psum_scatter(dw_ff, "fsdp", scatter_dimension=0, tiled=True)
@@ -874,26 +1017,36 @@
         jnp.concatenate([dwp_own, dwp_sib], axis=0),
         jnp.concatenate([dwp_sib, dwp_own], axis=0),
     )
-    grad_mixed, out_part = lax.optimization_barrier((grad_mixed, out_part))
-    out_sib = sibling(out_part[rows_own:])
+    out_own = (out_own + sibling(out_send).astype(F32)).astype(BF)
+    grad_mixed, out_own = lax.optimization_barrier((grad_mixed, out_own))
+    out_came = partner(out_own[slots:])
     early, late = 2, 1
     attend = functools.partial(attend_backward, counts, place_row, packed, packed_t)
     before = attend(grad_mixed, grad_mixed_t, result_t, log_total, slots, 0, early)
-    dw_early, qv_early = weight_grad(tok, *before, vec_one)
+    dw_early, qv_early = weight_grad(normed, *before)
     block_one = jnp.concatenate([dw_early, dwp], axis=1).reshape(owners, shard, -1)
     came_one = exchange(block_one)
-    out_own = (
-        middle[:rows_own] + out_part[:rows_own].astype(F32) + out_sib.astype(F32) + f2b
-    ).astype(BF)
-    grad_mixed, out_own, block_one = lax.optimization_barrier((grad_mixed, out_own, block_one))
-    out_came = partner(out_own[slots:])
+    grad_mixed, out_came, block_one, scattered_one = lax.optimization_barrier(
+        (grad_mixed, out_came, block_one, scattered_one)
+    )
+    output = hand_back(out_own, out_came)
+    one_came = partner(scattered_one)
     grads = attend(grad_mixed, grad_mixed_t, result_t, log_total, slots, early, late)
-    vec_one, out_came, scattered_one = lax.optimization_barrier((vec_one, out_came, scattered_one))
-    one_came = partner(scattered_one)
-    output = hand_back(out_own, out_came)
-    gn1_own, gn1_send, dw_late, vec_first, qv_late = project_back(
-        tok, before, grads, w_qkv, vec_one
-    )
+
+    def total(came):
+        return jnp.sum(came.astype(F32), axis=0).astype(BF)
+
+    def join(value, came):
+        return (value.astype(F32) + came.astype(F32)).astype(BF)
+
+    early_total = total(came_one)
+    one_came, early_total, w_qkv, grads = lax.optimization_barrier(
+        (one_came, early_total, w_qkv, grads)
+    )
+    early_came = partner(early_total)
+    one_sum = join(scattered_one, one_came)
+    one_other = sibling(one_sum)
+    gn1_own, gn1_send, dw_late, vec_first, qv_late = project_back(tok, normed, before, grads, w_qkv)
 
     def spread(vector):
         both = jnp.zeros((2, part), F32)
@@ -925,58 +1078,21 @@
     block_two = jnp.concatenate(
         [small_block, dw_late.reshape(owners, shard, late_wide)], axis=1
     )
-    gn1 = gn1_own + sibling(gn1_send).astype(F32)
-    unit_own, inverse_own = normalised(tok[:rows_own].astype(F32))
-    input_own = grad_middle + norm_pull(gn1, g1, unit_own, inverse_own)
-    block_two, came_one, one_came = lax.optimization_barrier((block_two, came_one, one_came))
+    gn1_sib = sibling(gn1_send)
     came_two = exchange(block_two)
-    came_two, input_own = lax.optimization_barrier((came_two, input_own))
-
-    def total(came):
-        return jnp.sum(came.astype(F32), axis=0).astype(BF)
-
-    input_grad = hand_back(input_own, partner(input_own[slots:].astype(BF)))
-
-    def finish(value, came=None):
-        came = partner(value) if came is None else came
-        summed = value.astype(F32) + came.astype(F32)
-        other = sibling(summed.astype(BF)).astype(F32)
-        return summed, other
-
-    def in_order(mine, other):
-        return jnp.where(core == 0, mine, other), jnp.where(core == 0, other, mine)
-
-    one_mine, one_other = finish(scattered_one, one_came)
-    lower, upper = in_order(one_mine, one_other)
-
-    def fc1_of(value):
-        return value[:, :half].reshape(shard, 2, owners, quarter).transpose(0, 2, 1, 3)
-
-    grad_fc1 = jnp.stack([fc1_of(lower), fc1_of(upper)], axis=2).reshape(shard, ff)
-
-    def fc2_of(value):
-        return value[:, half:].reshape(quarter, 2, width).transpose(1, 0, 2)
-
-    grad_fc2 = jnp.stack([fc2_of(lower), fc2_of(upper)]).reshape(ff_shard, width)
-    early_mine, early_other = finish(total(came_one))
-    early_sum = in_order(early_mine, early_other)
-    late_mine, late_other = finish(total(came_two))
-    late_sum = in_order(late_mine[VEC_ROWS:], late_other[VEC_ROWS:])
-    cut, tail = early * PAIR, late * PAIR
-    grad_qkv = jnp.concatenate(
-        [
-            piece
-            for at in range(3)
-            for of in range(2)
-            for piece in (
-                early_sum[of][:, at * cut : (at + 1) * cut],
-                late_sum[of][:, at * tail : (at + 1) * tail],
-            )
-        ],
-        axis=1,
-    )
-    grad_proj = jnp.concatenate([early_sum[0][:, 3 * cut :], early_sum[1][:, 3 * cut :]], axis=1)
-    small_sum = late_mine[:VEC_ROWS] + late_other[:VEC_ROWS]
+    input_own, input_send = input_back(tok, gn1_own, gn1_sib, grad_middle, vec_one)
+    came_two, input_send = lax.optimization_barrier((came_two, input_send))
+    input_grad = hand_back(input_own, partner(input_send))
+
+    grad_fc1, grad_fc2 = finish_ff(place_row, one_sum, one_other, width, quarter)
+    early_sum = join(early_total, early_came)
+    early_other = sibling(early_sum)
+    late_total = total(came_two)
+    late_sum = join(late_total, partner(late_total))
+    late_other = sibling(late_sum)
+    grad_qkv, grad_proj, small_sum = finish_attend(
+        place_row, early_sum, early_other, late_sum, late_other, width
+    )
     s = [small_sum[at, :shard] for at in range(8)]
     grad_f1b = small_sum[8, :ff_shard]
     return (

time: 473 us -> 436 us (0.922); the launches traced: 464 us -> 434 us
  local copies, waits for them, and re-layouts: 42.1 us -> 16.8 us
  other arithmetic: 49.6 us -> 27.6 us
  Pallas kernels: 224 us -> 234 us
  waiting for transfers between devices: 114 us -> 121 us
    all_to_all x2, waiting for transfers between devices: 0.01 us -> 50.6 us  [exchange(): lax.all_to_all(value, 'fsdp', split_axis=0, concat_axis=0, tiled=True)]
    all_gather x1, waiting for transfers between devices: 43.9 us -> 5.46 us  [per_device(): mine_one = lax.all_gather(one, 'fsdp', axis=0, tiled=False)]
    ppermute x8, waiting for transfers between devices: 64.4 us -> 51.9 us  [partner(): return lax.ppermute(value, 'seq', to_partner)]
    reshape x5 -> x0, local copies, waits for them, and re-layouts: 12.2 us -> none  [the longest x2 4.54 us: fc2_of(): return value[:, half:].reshape(quarter, 2, width).transpose(1, 0, 2)]
    pallas_call x0 -> x3, Pallas kernels: none -> 11.9 us  [the longest x1 6.74 us: input_back(): pl.pallas_call(input_back_kernel, grid=(blocks,), in_specs=[pl.BlockSpec(...]
    unnamed x53 -> x42, local copies, waits for them, and re-layouts: 8.98 us -> 2.44 us
    slice x5 -> x0, local copies, waits for them, and re-layouts: 5.64 us -> none  [the longest x1 2.67 us: per_device(): out_sib = sibling(out_part[rows_own:])]
    all_gather x1, waiting for transfers between devices: 0.02 us -> 5.17 us  [per_device(): second = lax.all_gather(two, 'fsdp', axis=0, tiled=True)]
  transfers between devices with their start and end apart: 25 -> 25, of which waited for: 9 -> 11; matrix products, arithmetic and copies ran while one was open for 19% -> 8% of each run, Pallas kernels for 36% -> 37%
where the time goes in v5:
time: 436 us; the launch traced here: 434 us
  Pallas kernels  234 us (54%)
  waiting for transfers between devices  121 us (28%)
  other arithmetic  27.6 us (6%)
  starting transfers between devices  20.5 us (5%)
  local copies, waits for them, and re-layouts  16.8 us (4%)
  between operations  14.3 us (3%)
    pallas_call x2, Pallas kernels, attend_backward(): pl.pallas_call(kernel, grid=(count, keys // bq), in_specs=[pl.BlockSpec(m...  69.3 us
    pallas_call x1, Pallas kernels, feed_forward(): pl.pallas_call(kernel, grid=(blocks,), in_specs=[pl.BlockSpec(memory_spac...  56.2 us
    ppermute x8, waiting for transfers between devices, partner(): return lax.ppermute(value, 'seq', to_partner)  51.9 us
    all_to_all x2, waiting for transfers between devices, exchange(): lax.all_to_all(value, 'fsdp', split_axis=0, concat_axis=0, tiled=True)  50.6 us
    pallas_call x1, Pallas kernels, attend_forward(): pl.pallas_call(kernel, grid=(pairs, keys // bq), in_specs=[pl.BlockSpec(m...  42.2 us
    pallas_call x1, Pallas kernels, branch(): pl.pallas_call(branch_kernel, grid=(blocks,), in_specs=[pl.BlockSpec(memo...  16.7 us
    pallas_call x1, Pallas kernels, project_back(): pl.pallas_call(project_back_kernel, grid=(blocks,), in_specs=[pl.BlockSpe...  14.2 us
    pallas_call x1, Pallas kernels, project(): pl.pallas_call(project_kernel, grid=(rows // bt,), in_specs=[pl.BlockSpec...  11.7 us
  transfers between devices with their start and end apart: 25, of which 11 were waited for; matrix products, arithmetic and copies ran while one was open for 8% of the time, Pallas kernels for 37%

profile of v5, /device:TPU:0, one launch (start us, length us, event | category | flops | bytes accessed | tf_op | source)
XLA Modules:
  0.0 433.8 jit_solution(17068882691600317708)
XLA Ops:
  16.1 17.7 %collective-permute-done = bf16[512,768]{1,0:T(8,128)(2,1)} collective-permute-done((bf16[512,768]{1,0:T(8,128)(2,1)S(1)}, bf16[512,768]{1,0:T(8,128)(2,1)}, u32[]{:S(2)}, u32[]{:S(2)}) %collective-permute-start) | collective-permute-done | bytes 786464 | tf_op jit(solution)/shard_map/ppermute | solution.py:943
  33.8 16.0 %collective-permute-done.1 = bf16[512,768]{1,0:T(8,128)(2,1)} collective-permute-done((bf16[512,768]{1,0:T(8,128)(2,1)S(1)}, bf16[512,768]{1,0:T(8,128)(2,1)}, u32[]{:S(2)}, u32[]{:S(2)}) %collective-permute-start.1) | collective-permute-done | bytes 786464 | tf_op jit(solution)/shard_map/ppermute | solution.py:943
  49.9 5.5 %all-gather.6.cloned.1.call-done = bf16[512,1152]{1,0:T(8,128)(2,1)} async-done(((bf16[64,1152]{1,0:T(8,128)(2,1)}), bf16[512,1152]{1,0:T(8,128)(2,1)}) %all-gather.6.cloned.1.call-update) | async-done | bytes 1179664 | tf_op jit(solution)/shard_map/all_gather | solution.py:958
  62.8 3.6 pad_maximum_fusion.tok_ref
  66.4 3.1 pad_maximum_fusion.1.cot_ref
  69.5 12.3 %collective-permute-done.4 = bf16[8,48,1152]{2,1,0:T(8,128)(2,1)} collective-permute-done((bf16[8,48,1152]{2,1,0:T(8,128)(2,1)}, bf16[8,48,1152]{2,1,0:T(8,128)(2,1)}, u32[]{:S(2)}, u32[]{:S(2)}) %collective-permute-start.4) | collective-permute-done | bytes 884768 | tf_op jit(solution)/shard_map/ppermute | solution.py:943
  81.8 3.0 maximum_select_fusion.1
  84.8 11.7 %project.1 = (bf16[2048,1152]{1,0:T(8,128)(2,1)}, bf16[1152,2048]{1,0:T(8,128)(2,1)}, bf16[2048,768]{1,0:T(8,128)(2,1)}) custom-call(bf16[2048,768]{1,0:T(8,128)(2,1)} %pad_maximum_fusion.tok_ref, bf16[768,1152]{1,0:T(8,128)(2,1)} %bitcast.70, f32[1,1152]{1,0:T(1,128)} %reshape.146.bias_ref, f32[8,768]{1,0:T(8,128)} %maximum_maximum_fusion.vec_ref), custom_call_target="tpu_custom_call" | custom-call | flops 3623878656 | bytes 18874368 | tf_op jit(solution)/shard_map/project/pallas_call | solution.py:877
  96.5 42.2 %attend_forward.1 = (bf16[2048,384]{1,0:T(8,128)(2,1)}, f32[384,2048]{1,0:T(8,128)}, f32[3,8,2048]{2,1,0:T(8,128)}) custom-call(s32[2,4]{1,0:T(2,128)} %counts_ref.5, s32[1]{0:T(128)} %bitcast.1.place_ref, bf16[2048,1152]{1,0:T(8,128)(2,1)} %get-tuple-element.88.k_ref.q_ref.v_ref, bf16[1152,2048]{1,0:T(8,128)(2,1)} %get-tuple-element.89.qt_ref.vt_ref.kt_ref, ...), custom_call_target="tpu_custom_call" | custom-call | flops 25769803776 | bytes 9437184 | tf_op jit(solution)/shard_map/attend_forward/pallas_call | solution.py:163
  138.8 5.2 %all-gather.4.cloned.1.call-done.g2_ref = bf16[768,3456]{1,0:T(8,128)(2,1)} async-done(((bf16[96,3456]{1,0:T(8,128)(2,1)}), bf16[768,3456]{1,0:T(8,128)(2,1)}) %all-gather.4.cloned.1.call-update) | async-done | bytes 5308432 | tf_op jit(solution)/shard_map/all_gather | solution.py:970
  148.1 56.2 %feed_forward.1 = (f32[2048,768]{1,0:T(8,128)}, f32[1024,768]{1,0:T(8,128)}, bf16[1024,768]{1,0:T(8,128)(2,1)}, bf16[2048,768]{1,0:T(8,128)(2,1)}, bf16[768,3072...) custom-call(s32[1]{0:T(128)} %bitcast.core_ref, ...), custom_call_target="tpu_custom_call" | custom-call | flops 31406948352 | bytes 40894464 | tf_op jit(solution)/shard_map/feed_forward/pallas_call | solution.py:401
  205.0 7.5 %collective-permute-done.10 = bf16[1024,768]{1,0:T(8,128)(2,1)S(1)} collective-permute-done((bf16[1024,768]{1,0:T(8,128)(2,1)}, bf16[1024,768]{1,0:T(8,128)(2,1)S(1)}, u32[]{:S(2)}, u32[]{:S(2)}) %collective-permute-start.10) | collective-permute-done | bytes 1572896 | tf_op jit(solution)/shard_map/ppermute | solution.py:940
  214.8 16.7 %branch.1 = (f32[1024,768]{1,0:T(8,128)}, bf16[2048,384]{1,0:T(8,128)(2,1)}, bf16[384,2048]{1,0:T(8,128)(2,1)}, bf16[384,384]{1,0:T(8,128)(2,1)}, bf16[384,384]{1,0:T(8,128)(2,1)}, /*index=5*/f32[24,768]{1,0:T(8,128)}) custom-call(s32[1]{0:T(128)} %bitcast.core_ref, f32[2048,768]{1,0:T(8,128)} %get-tuple-element.93.mid_ref, ...), custom_call_target="tpu_custom_call" | custom-call | flops 3623878656 | bytes 28311552 | tf_op jit(solution)/shard_map/branch/pallas_call | solution.py:498
  232.9 45.3 %attend_backward.2 = (bf16[2048,256]{1,0:T(8,128)(2,1)}, bf16[2048,256]{1,0:T(8,128)(2,1)}, bf16[2048,256]{1,0:T(8,128)(2,1)}) custom-call(s32[2,4]{1,0:T(2,128)} %counts_ref.5, s32[1]{0:T(128)} %bitcast.1.place_ref, bf16[2048,1152]{1,0:T(8,128)(2,1)} %get-tuple-element.88.k_ref.q_ref.v_ref, bf16[2048,1152]{1,0:T(8,128)(2,1)} %get-tuple-element.88.k_ref.q_ref.v_ref, ...), custom_call_target="tpu_custom_call" | custom-call | flops 42949672960 | bytes 12582912 | tf_op jit(solution)/shard_map/attend_backward/pallas_call | solution.py:263
  278.2 8.6 %weight_grad.1 = (bf16[768,768]{1,0:T(8,128)(2,1)}, f32[16,256]{1,0:T(8,128)}) custom-call(bf16[2048,768]{1,0:T(8,128)(2,1)} %get-tuple-element.101.normed_ref, bf16[2048,256]{1,0:T(8,128)(2,1)} %get-tuple-element.105.gq_ref.gqa_ref, bf16[2048,256]{1,0:T(8,128)(2,1)} %get-tuple-element.106.gk_ref.gka_ref, bf16[2048,256]{1,0:T(8,128)(2,1)} %get-tuple-element.107.gv_ref.gva_ref), custom_call_target="tpu_custom_call" | custom-call | flops 2415919104 | bytes 6291456 | tf_op jit(solution)/shard_map/weight_grad/pallas_call | solution.py:570
  289.4 4.0 all-to-all-start
  296.8 39.6 %all-to-all-done = bf16[8,96,1152]{2,1,0:T(8,128)(2,1)S(1)} async-done(((bf16[8,96,1152]{2,1,0:T(8,128)(2,1)}), bf16[8,96,1152]{2,1,0:T(8,128)(2,1)S(1)}, u32[]{:S(2)}, u32[]{:S(2)}) %all-to-all-start) | async-done | bytes 1769504 | tf_op jit(solution)/shard_map/all_to_all | solution.py:903
  338.8 24.0 %attend_backward.3 = (bf16[2048,128]{1,0:T(8,128)(2,1)}, bf16[2048,128]{1,0:T(8,128)(2,1)}, bf16[2048,128]{1,0:T(8,128)(2,1)}) custom-call(s32[2,4]{1,0:T(2,128)} %counts_ref.5, s32[1]{0:T(128)} %bitcast.1.place_ref, bf16[2048,1152]{1,0:T(8,128)(2,1)} %get-tuple-element.88.k_ref.q_ref.v_ref, bf16[2048,1152]{1,0:T(8,128)(2,1)} %get-tuple-element.88.k_ref.q_ref.v_ref, ...), custom_call_target="tpu_custom_call" | custom-call | flops 21474836480 | bytes 6291456 | tf_op jit(solution)/shard_map/attend_backward/pallas_call | solution.py:263
  362.8 14.2 %project_back.1 = (f32[1024,768]{1,0:T(8,128)}, bf16[1024,768]{1,0:T(8,128)(2,1)}, bf16[768,384]{1,0:T(8,128)(2,1)}, f32[16,768]{1,0:T(8,128)}, f32[16,128]{1,0:T(8,128)}) custom-call(bf16[2048,768]{1,0:T(8,128)(2,1)} %pad_maximum_fusion.tok_ref, bf16[2048,768]{1,0:T(8,128)(2,1)} %get-tuple-element.101.normed_ref, ...), custom_call_target="tpu_custom_call" | custom-call | flops 4831838208 | bytes 22020096 | tf_op jit(solution)/shard_map/project_back/pallas_call | solution.py:647
  381.1 3.6 all-to-all-start.1
  385.8 6.7 %input_back.1 = (f32[512,768]{1,0:T(8,128)}, bf16[512,768]{1,0:T(8,128)(2,1)}) custom-call(bf16[2048,768]{1,0:T(8,128)(2,1)} %pad_maximum_fusion.tok_ref, f32[1024,768]{1,0:T(8,128)} %get-tuple-element.122.own_ref, bf16[1024,768]{1,0:T(8,128)(2,1)} %collective-permute-done.13.sib_ref, f32[1024,768]{1,0:T(8,128)} %get-tuple-element.124.gm_ref, ...), custom_call_target="tpu_custom_call" | custom-call | flops 15728640 | bytes 12582912 | tf_op jit(solution)/shard_map/input_back/pallas_call | solution.py:700
  392.5 11.0 %all-to-all-done.1 = bf16[8,112,384]{2,1,0:T(8,128)(2,1)S(1)} async-done(((bf16[8,112,384]{2,1,0:T(8,128)(2,1)}), bf16[8,112,384]{2,1,0:T(8,128)(2,1)S(1)}, u32[]{:S(2)}, u32[]{:S(2)}) %all-to-all-start.1) | async-done | bytes 688160 | tf_op jit(solution)/shard_map/all_to_all | solution.py:903
  413.1 3.0 finish_ff.1
  421.8 3.4 collective-permute-done.14
  (157 shorter events, 55.4 us)
Async XLA Ops:
  7.2 48.1 %all-gather.6.cloned.1.call-start = ((), (), s32[]{:S(2)}) async-start(), calls=%async_computation.5 | async-start | bytes 1327104 | tf_op jit(solution)/shard_map/all_gather | solution.py:958
  11.3 132.6 %all-gather.4.cloned.1.call-start = ((), (), s32[]{:S(2)}) async-start(), calls=%async_computation.3 | async-start | bytes 5971968 | tf_op jit(solution)/shard_map/all_gather | solution.py:970
  12.4 21.4 %collective-permute-start = (bf16[512,768]{1,0:T(8,128)(2,1)S(1)}, bf16[512,768]{1,0:T(8,128)(2,1)}, u32[]{:S(2)}, u32[]{:S(2)}) collective-permute-start(bf16[512,768]{1,0:T(8,128)(2,1)S(1)} %get-tuple-element.148), channel_id=1, source_target_pairs={{0,2},{1,3},{2,0},{3,1},{4,6},{5,7},{6,4},{7,5},{8,10},{9,11},{10,... | collective-permute-start | bytes 2359304 | tf_op jit(solution)/shard_map/ppermute | solution.py:943
  15.5 34.4 %collective-permute-start.1 = (bf16[512,768]{1,0:T(8,128)(2,1)S(1)}, bf16[512,768]{1,0:T(8,128)(2,1)}, u32[]{:S(2)}, u32[]{:S(2)}) collective-permute-start(bf16[512,768]{1,0:T(8,128)(2,1)S(1)} %get-tuple-element.146), channel_id=1, source_target_pairs={{0,2},{1,3},{2,0},{3,1},{4,6},{5,7},{6,4},{7,5},{8,10},{9,11},{10,... | collective-permute-start | bytes 2359304 | tf_op jit(solution)/shard_map/ppermute | solution.py:943
  55.3 282.1 %reduce-scatter.2.cloned.1.call-start = ((), (), s32[]{:S(2)}) async-start(), calls=%async_computation.4 | async-start | bytes 5308416 | tf_op jit(solution)/shard_map/reduce_scatter | solution.py:1001
  55.4 7.4 %collective-permute-start.2 = (bf16[512,768]{1,0:T(8,128)(2,1)}, bf16[512,768]{1,0:T(8,128)(2,1)}, u32[]{:S(2)}, u32[]{:S(2)}) collective-permute-start(bf16[512,768]{1,0:T(8,128)(2,1)} %get-tuple-element.147), channel_id=1, source_target_pairs={{0,1},{1,0},{2,3},{3,2},{4,5},{5,4},{6,7},{7,6},{8,9},{9,8},{10,11... | collective-permute-start | bytes 2359304 | tf_op jit(solution)/shard_map/ppermute | solution.py:940
  55.5 10.9 %collective-permute-start.5 = (bf16[512,768]{1,0:T(8,128)(2,1)S(1)}, bf16[512,768]{1,0:T(8,128)(2,1)}, u32[]{:S(2)}, u32[]{:S(2)}) collective-permute-start(bf16[512,768]{1,0:T(8,128)(2,1)S(1)} %get-tuple-element.145), channel_id=1, source_target_pairs={{0,1},{1,0},{2,3},{3,2},{4,5},{5,4},{6,7},{7,6},{8,9},{9,8},{10,11... | collective-permute-start | bytes 2359304 | tf_op jit(solution)/shard_map/ppermute | solution.py:940
  56.0 6.7 %collective-permute-start.3 = (bf16[512,768]{1,0:T(8,128)(2,1)}, bf16[512,768]{1,0:T(8,128)(2,1)}, u32[]{:S(2)}, u32[]{:S(2)}) collective-permute-start(bf16[512,768]{1,0:T(8,128)(2,1)} %collective-permute-done), channel_id=1, source_target_pairs={{0,1},{1,0},{2,3},{3,2},{4,5},{5,4},{6,7},{7,6},{8,9},{9,8},{10,11... | collective-permute-start | bytes 2359304 | tf_op jit(solution)/shard_map/ppermute | solution.py:940
  56.1 10.2 %collective-permute-start.6 = (bf16[512,768]{1,0:T(8,128)(2,1)}, bf16[512,768]{1,0:T(8,128)(2,1)}, u32[]{:S(2)}, u32[]{:S(2)}) collective-permute-start(bf16[512,768]{1,0:T(8,128)(2,1)} %collective-permute-done.1), channel_id=1, source_target_pairs={{0,1},{1,0},{2,3},{3,2},{4,5},{5,4},{6,7},{7,6},{8,9},{9,8},{10,11... | collective-permute-start | bytes 2359304 | tf_op jit(solution)/shard_map/ppermute | solution.py:940
  59.8 21.9 %collective-permute-start.4 = (bf16[8,48,1152]{2,1,0:T(8,128)(2,1)}, bf16[8,48,1152]{2,1,0:T(8,128)(2,1)}, u32[]{:S(2)}, u32[]{:S(2)}) collective-permute-start(bf16[8,48,1152]{2,1,0:T(8,128)(2,1)} %get-tuple-element.150), channel_id=1, source_target_pairs={{0,2},{1,3},{2,0},{3,1},{4,6},{5,7},{6,4},{7,5},{8,10},{9,11},{10,... | collective-permute-start | bytes 2654216 | tf_op jit(solution)/shard_map/ppermute | solution.py:943
  138.8 8.2 %collective-permute-start.7 = (bf16[2048,384]{1,0:T(8,128)(2,1)}, bf16[2048,384]{1,0:T(8,128)(2,1)S(1)}, u32[]{:S(2)}, u32[]{:S(2)}) collective-permute-start(bf16[2048,384]{1,0:T(8,128)(2,1)} %get-tuple-element.90.mo_ref), channel_id=1, source_target_pairs={{0,1},{1,0},{2,3},{3,2},{4,5},{5,4},{6,7},{7,6},{8,9},{9,8},{10,11... | collective-permute-start | bytes 4718600 | tf_op jit(solution)/shard_map/ppermute | solution.py:940
  204.3 10.4 %collective-permute-start.9 = (bf16[2048,768]{1,0:T(8,128)(2,1)}, bf16[2048,768]{1,0:T(8,128)(2,1)}, u32[]{:S(2)}, u32[]{:S(2)}) collective-permute-start(bf16[2048,768]{1,0:T(8,128)(2,1)} %get-tuple-element.94.ga_ref), channel_id=1, source_target_pairs={{0,1},{1,0},{2,3},{3,2},{4,5},{5,4},{6,7},{7,6},{8,9},{9,8},{10,11... | collective-permute-start | bytes 9437192 | tf_op jit(solution)/shard_map/ppermute | solution.py:940
  204.9 7.6 %collective-permute-start.10 = (bf16[1024,768]{1,0:T(8,128)(2,1)}, bf16[1024,768]{1,0:T(8,128)(2,1)S(1)}, u32[]{:S(2)}, u32[]{:S(2)}) collective-permute-start(bf16[1024,768]{1,0:T(8,128)(2,1)} %get-tuple-element.98), channel_id=1, source_target_pairs={{0,1},{1,0},{2,3},{3,2},{4,5},{5,4},{6,7},{7,6},{8,9},{9,8},{10,11... | collective-permute-start | bytes 4718600 | tf_op jit(solution)/shard_map/ppermute | solution.py:940
  289.4 47.0 %all-to-all-start = ((bf16[8,96,1152]{2,1,0:T(8,128)(2,1)}), bf16[8,96,1152]{2,1,0:T(8,128)(2,1)S(1)}, u32[]{:S(2)}, u32[]{:S(2)}) async-start(bf16[8,96,1152]{2,1,0:T(8,128)(2,1)} %bitcast.22), calls=%async_computation.1 | async-start | bytes 3538944 | tf_op jit(solution)/shard_map/all_to_all | solution.py:903
  294.7 42.7 %collective-permute-start.11 = (bf16[512,768]{1,0:T(8,128)(2,1)}, bf16[512,768]{1,0:T(8,128)(2,1)S(1)}, u32[]{:S(2)}, u32[]{:S(2)}) collective-permute-start(bf16[512,768]{1,0:T(8,128)(2,1)} %get-tuple-element.144), channel_id=1, source_target_pairs={{0,2},{1,3},{2,0},{3,1},{4,6},{5,7},{6,4},{7,5},{8,10},{9,11},{10,... | collective-permute-start | bytes 2359304 | tf_op jit(solution)/shard_map/ppermute | solution.py:943
  337.4 25.3 %collective-permute-start.12 = (bf16[96,3072]{1,0:T(8,128)(2,1)}, bf16[96,3072]{1,0:T(8,128)(2,1)S(1)}, u32[]{:S(2)}, u32[]{:S(2)}) collective-permute-start(bf16[96,3072]{1,0:T(8,128)(2,1)} %reduce-scatter.2.cloned.1.call-done), channel_id=1, source_target_pairs={{0,2},{1,3},{2,0},{3,1},{4,6},{5,7},{6,4},{7,5},{8,10},{9,11},{10,... | collective-permute-start | bytes 1769480 | tf_op jit(solution)/shard_map/ppermute | solution.py:943
  379.0 6.8 %collective-permute-start.13 = (bf16[1024,768]{1,0:T(8,128)(2,1)}, bf16[1024,768]{1,0:T(8,128)(2,1)}, u32[]{:S(2)}, u32[]{:S(2)}) collective-permute-start(bf16[1024,768]{1,0:T(8,128)(2,1)} %get-tuple-element.123), channel_id=1, source_target_pairs={{0,1},{1,0},{2,3},{3,2},{4,5},{5,4},{6,7},{7,6},{8,9},{9,8},{10,11... | collective-permute-start | bytes 4718600 | tf_op jit(solution)/shard_map/ppermute | solution.py:940
  381.1 22.4 %all-to-all-start.1 = ((bf16[8,112,384]{2,1,0:T(8,128)(2,1)}), bf16[8,112,384]{2,1,0:T(8,128)(2,1)S(1)}, u32[]{:S(2)}, u32[]{:S(2)}) async-start(bf16[8,112,384]{2,1,0:T(8,128)(2,1)} %fusion.4), calls=%async_computation.2 | async-start | bytes 1376256 | tf_op jit(solution)/shard_map/all_to_all | solution.py:903
  384.7 21.6 %collective-permute-start.15 = (bf16[96,1152]{1,0:T(8,128)(2,1)}, bf16[96,1152]{1,0:T(8,128)(2,1)}, u32[]{:S(2)}, u32[]{:S(2)}) collective-permute-start(bf16[96,1152]{1,0:T(8,128)(2,1)} %reduce_sum.69), channel_id=1, source_target_pairs={{0,2},{1,3},{2,0},{3,1},{4,6},{5,7},{6,4},{7,5},{8,10},{9,11},{10,... | collective-permute-start | bytes 663560 | tf_op jit(solution)/shard_map/ppermute | solution.py:943
  385.5 26.8 %collective-permute-start.19 = (bf16[96,3072]{1,0:T(8,128)(2,1)S(1)}, bf16[96,3072]{1,0:T(8,128)(2,1)S(1)}, u32[]{:S(2)}, u32[]{:S(2)}) collective-permute-start(bf16[96,3072]{1,0:T(8,128)(2,1)S(1)} %add_convert_fusion.1.mine_ref), channel_id=1, source_target_pairs={{0,1},{1,0},{2,3},{3,2},{4,5},{5,4},{6,7},{7,6},{8,9},{9,8},{10,11... | collective-permute-start | bytes 1769480 | tf_op jit(solution)/shard_map/ppermute | solution.py:940
  404.2 5.7 %collective-permute-start.17 = (bf16[112,384]{1,0:T(8,128)(2,1)}, bf16[112,384]{1,0:T(8,128)(2,1)S(1)}, u32[]{:S(2)}, u32[]{:S(2)}) collective-permute-start(bf16[112,384]{1,0:T(8,128)(2,1)} %reduce_sum.75), channel_id=1, source_target_pairs={{0,2},{1,3},{2,0},{3,1},{4,6},{5,7},{6,4},{7,5},{8,10},{9,11},{10,... | collective-permute-start | bytes 258056 | tf_op jit(solution)/shard_map/ppermute | solution.py:943
  404.9 20.3 %collective-permute-start.14 = (bf16[512,768]{1,0:T(8,128)(2,1)}, bf16[512,768]{1,0:T(8,128)(2,1)S(1)}, u32[]{:S(2)}, u32[]{:S(2)}) collective-permute-start(bf16[512,768]{1,0:T(8,128)(2,1)} %get-tuple-element.134), channel_id=1, source_target_pairs={{0,2},{1,3},{2,0},{3,1},{4,6},{5,7},{6,4},{7,5},{8,10},{9,11},{10,... | collective-permute-start | bytes 2359304 | tf_op jit(solution)/shard_map/ppermute | solution.py:943
  407.4 8.8 %collective-permute-start.16 = (bf16[96,1152]{1,0:T(8,128)(2,1)S(1)}, bf16[96,1152]{1,0:T(8,128)(2,1)S(1)}, u32[]{:S(2)}, u32[]{:S(2)}) collective-permute-start(bf16[96,1152]{1,0:T(8,128)(2,1)S(1)} %add_convert_fusion.2.em_ref), channel_id=1, source_target_pairs={{0,1},{1,0},{2,3},{3,2},{4,5},{5,4},{6,7},{7,6},{8,9},{9,8},{10,11... | collective-permute-start | bytes 663560 | tf_op jit(solution)/shard_map/ppermute | solution.py:940
  410.8 5.3 %collective-permute-start.18 = (bf16[112,384]{1,0:T(8,128)(2,1)S(1)}, bf16[112,384]{1,0:T(8,128)(2,1)}, u32[]{:S(2)}, u32[]{:S(2)}) collective-permute-start(bf16[112,384]{1,0:T(8,128)(2,1)S(1)} %add_convert_fusion.3.lm_ref), channel_id=1, source_target_pairs={{0,1},{1,0},{2,3},{3,2},{4,5},{5,4},{6,7},{7,6},{8,9},{9,8},{10,11... | collective-permute-start | bytes 258056 | tf_op jit(solution)/shard_map/ppermute | solution.py:940
  (19 other events, 141.3 us)
Sparse Core Ops, SparseCore 0:
  11.5 43.8 all-gather.5
  58.1 85.8 all-gather.3
  205.1 94.6 reduce-scatter.1

commit v6 on v5

--- a/solution.py
+++ b/solution.py
@@ -13,15 +13,15 @@
 MASKED = -1e30
 BF = jnp.bfloat16
 F32 = jnp.float32
-VMEM_BYTES = 60 * 1024 * 1024
+MIB = 1024 * 1024
 PAIR = 2 * HEAD_DIM
 VEC_ROWS = 16
 SLOT_ORDER = (0, 2, 1, 3)
 
 
-def params(*semantics):
+def params(mebibytes, *semantics):
     return pltpu.CompilerParams(
-        dimension_semantics=semantics, vmem_limit_bytes=VMEM_BYTES
+        dimension_semantics=semantics, vmem_limit_bytes=mebibytes * MIB
     )
 
 
@@ -188,7 +188,7 @@
             pltpu.VMEM((8, bq), F32),
             pltpu.VMEM((8, bq), F32),
         ],
-        compiler_params=params("arbitrary", "arbitrary"),
+        compiler_params=params(24, "arbitrary", "arbitrary"),
         cost_estimate=cost(
             2 * pairs * 2 * 2 * keys * keys * 256, 12 * keys * width, 2 * pairs * keys * keys
         ),
@@ -230,17 +230,25 @@
     do_pair = do_ref[...]
     q_pair = q_ref[...]
     totals = [None, None]
-    for at in range(keys // chunk):
+    units = [(at, which) for at in range(keys // chunk) for which in range(2)]
+
+    def front(at, which):
         rows = slice(at * chunk, (at + 1) * chunk)
-        for which in range(2):
-            p = jnp.exp(dot(kaug[which, rows, :], queries[which]))
-            dp = dot(vaug[which, rows, :], grads[which])
-            p_low = p.astype(BF)
-            ds = (p * dp).astype(BF)
-            acc_v[which, rows, :] += dot(p_low, do_pair)
-            acc_k[which, rows, :] += dot(ds, q_pair)
-            part = dot(kt_ref[which * HEAD_DIM : (which + 1) * HEAD_DIM, rows], ds)
-            totals[which] = part if totals[which] is None else totals[which] + part
+        return dot(kaug[which, rows, :], queries[which]), dot(vaug[which, rows, :], grads[which])
+
+    ahead = front(*units[0])
+    for unit, (at, which) in enumerate(units):
+        rows = slice(at * chunk, (at + 1) * chunk)
+        scores, dp = ahead
+        if unit + 1 < len(units):
+            ahead = front(*units[unit + 1])
+        p = jnp.exp(scores)
+        p_low = p.astype(BF)
+        ds = (p * dp).astype(BF)
+        acc_v[which, rows, :] += dot(p_low, do_pair)
+        acc_k[which, rows, :] += dot(ds, q_pair)
+        part = dot(kt_ref[which * HEAD_DIM : (which + 1) * HEAD_DIM, rows], ds)
+        totals[which] = part if totals[which] is None else totals[which] + part
     both = jnp.concatenate(totals, axis=0) * scale
     gq_ref[...] = both.T.astype(BF)
 
@@ -288,7 +296,7 @@
             pltpu.VMEM((2, keys, PAIR), F32),
             pltpu.VMEM((2, keys, PAIR), F32),
         ],
-        compiler_params=params("arbitrary", "arbitrary"),
+        compiler_params=params(32, "arbitrary", "arbitrary"),
         cost_estimate=cost(
             2 * count * 5 * 2 * keys * keys * 256, 24 * keys * count * PAIR,
             2 * count * keys * keys,
@@ -351,17 +359,29 @@
     cot = cot_ref[...]
     out = None
     grad = None
-    for at in range(half // chunk):
-        cols = slice(at * chunk, (at + 1) * chunk)
+
+    def weights(at):
         w1 = g2_ref[:, part + at * chunk : part + (at + 1) * chunk]
         piece, row = divmod(at * chunk, width)
         start = part + half + piece * width
-        w2 = g2_ref[row : row + chunk, start : start + width]
-        hidden = dot(normed, w1) + f1b_ref[0:1, cols]
+        return w1, g2_ref[row : row + chunk, start : start + width]
+
+    def front(at):
+        w1, w2 = weights(at)
+        hidden = dot(normed, w1) + f1b_ref[0:1, at * chunk : (at + 1) * chunk]
+        return hidden, dot(cot, w2, 1, 1)
+
+    ahead = front(0)
+    for at in range(half // chunk):
+        cols = slice(at * chunk, (at + 1) * chunk)
+        hidden, grad_active = ahead
+        if at + 1 < half // chunk:
+            ahead = front(at + 1)
+        w1, w2 = weights(at)
         below = 0.5 + 0.5 * lax.erf(hidden * (0.5**0.5))
         slope = below + hidden * (jnp.exp(hidden * hidden * -0.5) * 0.3989422804014327)
         active = (hidden * below).astype(BF)
-        grad_hidden = (dot(cot, w2, 1, 1) * slope).astype(BF)
+        grad_hidden = (grad_active * slope).astype(BF)
         more = dot(active, w2)
         out = more if out is None else out + more
         more = dot(grad_hidden, w1, 1, 1)
@@ -395,7 +415,7 @@
     rows, width = tokens.shape
     half = f1b.shape[1]
     heads = mixed_own.shape[1]
-    bt, chunk = 256, 384
+    bt, chunk = 512, 384
     blocks = rows // bt
     kernel = functools.partial(feed_forward_kernel, chunk)
     return pl.pallas_call(
@@ -439,7 +459,7 @@
             pltpu.VMEM((8, width), F32),
             pltpu.VMEM((width // 2, width), BF),
         ],
-        compiler_params=params("arbitrary"),
+        compiler_params=params(60, "arbitrary"),
         cost_estimate=cost(
             2 * rows * width * (6 * half + width), 20 * rows * width + 8 * width * half,
             2 * rows * half,
@@ -491,7 +511,7 @@
 def branch(core, middle, grad_own, grad_sib, cot, mixed_own, mixed_sib, wp_own, vec):
     rows, width = middle.shape
     half = mixed_own.shape[1]
-    bt = 256
+    bt = 512
     blocks = rows // bt
     swap = lambda i: (lax.rem(i + blocks // 2, blocks), 0)
     straight = lambda i: (i, 0)
@@ -531,7 +551,7 @@
             pltpu.VMEM((24, width), F32),
             pltpu.VMEM((bt, width), BF),
         ],
-        compiler_params=params("arbitrary"),
+        compiler_params=params(40, "arbitrary"),
         cost_estimate=cost(2 * rows * width * 3 * half, 18 * rows * width),
         name="branch",
     )(core, middle, grad_own, grad_sib, cot, mixed_own, mixed_sib, wp_own, vec)
@@ -565,7 +585,7 @@
 def weight_grad(normed, gq, gk, gv):
     rows, width = normed.shape
     part = gq.shape[1]
-    bt = 256
+    bt = 512
     straight = lambda i: (i, 0)
     return pl.pallas_call(
         weight_grad_kernel,
@@ -582,7 +602,7 @@
             jax.ShapeDtypeStruct((16, part), F32),
         ],
         scratch_shapes=[pltpu.VMEM((width, 3 * part), F32), pltpu.VMEM((16, part), F32)],
-        compiler_params=params("arbitrary"),
+        compiler_params=params(24, "arbitrary"),
         cost_estimate=cost(2 * rows * width * 3 * part, 2 * rows * (width + 3 * part)),
         name="weight_grad",
     )(normed, gq, gk, gv)
@@ -641,7 +661,7 @@
 def project_back(tokens, normed, before, grads, weight):
     rows, width = tokens.shape
     early, part = before[0].shape[1], grads[0].shape[1]
-    bt = 256
+    bt = 512
     blocks = rows // bt
     straight = lambda i: (i, 0)
     return pl.pallas_call(
@@ -670,7 +690,7 @@
             pltpu.VMEM((16, width), F32),
             pltpu.VMEM((16, part), F32),
         ],
-        compiler_params=params("arbitrary"),
+        compiler_params=params(40, "arbitrary"),
         cost_estimate=cost(2 * rows * width * (6 * part + 3 * early), 14 * rows * width),
         name="project_back",
     )(tokens, normed, *before, *grads, weight)
@@ -709,7 +729,7 @@
             jax.ShapeDtypeStruct((rows // 2, width), F32),
             jax.ShapeDtypeStruct((rows // 2, width), BF),
         ],
-        compiler_params=params("arbitrary"),
+        compiler_params=params(16, "arbitrary"),
         cost_estimate=cost(20 * rows * width, 16 * rows * width),
         name="input_back",
     )(tokens, grad_own, grad_sib, grad_middle, vec)
@@ -752,7 +772,7 @@
             jax.ShapeDtypeStruct((shard, wide), F32),
             jax.ShapeDtypeStruct((4 * quarter, width), F32),
         ],
-        compiler_params=params("arbitrary"),
+        compiler_params=params(16, "arbitrary"),
         cost_estimate=cost(0, 12 * shard * wide),
         name="finish_ff",
     )(place, mine, other)
@@ -797,7 +817,7 @@
             jax.ShapeDtypeStruct((shard, width), F32),
             jax.ShapeDtypeStruct((rows, late_mine.shape[1]), F32),
         ],
-        compiler_params=params("arbitrary"),
+        compiler_params=params(16, "arbitrary"),
         cost_estimate=cost(0, 24 * shard * width),
         name="finish_attend",
     )(place, early_mine, early_other, late_mine, late_other)
@@ -855,7 +875,7 @@
             jax.ShapeDtypeStruct((rows, 3 * part), BF),
             jax.ShapeDtypeStruct((shard, 5 * part + half), BF),
         ],
-        compiler_params=params("arbitrary"),
+        compiler_params=params(16, "arbitrary"),
         cost_estimate=cost(0, 5 * shard * width * 8),
         name="pack_weights",
     )(place, *values)
@@ -873,7 +893,7 @@
 def project(tokens, weight, bias, vec):
     rows, width = tokens.shape
     wide = weight.shape[1]
-    bt = 256
+    bt = 512
     return pl.pallas_call(
         project_kernel,
         grid=(rows // bt,),
@@ -893,7 +913,7 @@
             jax.ShapeDtypeStruct((wide, rows), BF),
             jax.ShapeDtypeStruct((rows, width), BF),
         ],
-        compiler_params=params("arbitrary"),
+        compiler_params=params(36, "arbitrary"),
         cost_estimate=cost(2 * rows * width * wide, 12 * rows * width),
         name="project",
     )(tokens, weight, bias, vec)
@@ -1039,10 +1059,10 @@
     def join(value, came):
         return (value.astype(F32) + came.astype(F32)).astype(BF)
 
+    one_came, came_one, w_qkv, grads = lax.optimization_barrier(
+        (one_came, came_one, w_qkv, grads)
+    )
     early_total = total(came_one)
-    one_came, early_total, w_qkv, grads = lax.optimization_barrier(
-        (one_came, early_total, w_qkv, grads)
-    )
     early_came = partner(early_total)
     one_sum = join(scattered_one, one_came)
     one_other = sibling(one_sum)
@@ -1081,8 +1101,9 @@
     gn1_sib = sibling(gn1_send)
     came_two = exchange(block_two)
     input_own, input_send = input_back(tok, gn1_own, gn1_sib, grad_middle, vec_one)
-    came_two, input_send = lax.optimization_barrier((came_two, input_send))
-    input_grad = hand_back(input_own, partner(input_send))
+    input_came = partner(input_send)
+    came_two, input_own = lax.optimization_barrier((came_two, input_own))
+    input_grad = hand_back(input_own, input_came)
 
     grad_fc1, grad_fc2 = finish_ff(place_row, one_sum, one_other, width, quarter)
     early_sum = join(early_total, early_came)

time: 436 us -> 439 us (level); the launches traced: 434 us -> 432 us
  local copies, waits for them, and re-layouts: 16.8 us -> 58.5 us
  Pallas kernels: 234 us -> 206 us
  waiting for transfers between devices: 121 us -> 104 us
    all_to_all x2, waiting for transfers between devices: 50.6 us -> 4.32 us  [exchange(): lax.all_to_all(value, 'fsdp', split_axis=0, concat_axis=0, tiled=True)]
    unnamed x42 -> x136, local copies, waits for them, and re-layouts: 2.44 us -> 46.6 us
    ppermute x8, waiting for transfers between devices: 51.9 us -> 75.2 us  [partner(): return lax.ppermute(value, 'seq', to_partner)]
    all_gather x1, waiting for transfers between devices: 5.17 us -> 11.9 us  [per_device(): second = lax.all_gather(two, 'fsdp', axis=0, tiled=True)]
    pallas_call x1, Pallas kernels: 8.57 us -> 3.62 us  [weight_grad(): pl.pallas_call(weight_grad_kernel, grid=(rows // bt,), in_specs=[pl.Block...]
    pallas_call x1, Pallas kernels: 11.7 us -> 7.1 us  [project(): pl.pallas_call(project_kernel, grid=(rows // bt,), in_specs=[pl.BlockSpec...]
  transfers between devices with their start and end apart: 25 -> 25, of which waited for: 11 -> 10; matrix products, arithmetic and copies ran while one was open for 8% -> 8% of each run, Pallas kernels for 37% -> 32%
where the time goes in v6:
time: 439 us; the launch traced here: 432 us
  Pallas kernels  206 us (47%)
  waiting for transfers between devices  104 us (24%)
  local copies, waits for them, and re-layouts  58.5 us (13%)
  other arithmetic  25 us (6%)
  starting transfers between devices  22.8 us (5%)
  between operations  15 us (3%)
    ppermute x8, waiting for transfers between devices, partner(): return lax.ppermute(value, 'seq', to_partner)  75.2 us
    pallas_call x2, Pallas kernels, attend_backward(): pl.pallas_call(kernel, grid=(count, keys // bq), in_specs=[pl.BlockSpec(m...  66.4 us
    pallas_call x1, Pallas kernels, feed_forward(): pl.pallas_call(kernel, grid=(blocks,), in_specs=[pl.BlockSpec(memory_spac...  54.7 us
    unnamed x136, local copies, waits for them, and re-layouts  46.6 us
    pallas_call x1, Pallas kernels, attend_forward(): pl.pallas_call(kernel, grid=(pairs, keys // bq), in_specs=[pl.BlockSpec(m...  41.3 us
    pallas_call x1, Pallas kernels, branch(): pl.pallas_call(branch_kernel, grid=(blocks,), in_specs=[pl.BlockSpec(memo...  13.3 us
    all_gather x1, waiting for transfers between devices, per_device(): second = lax.all_gather(two, 'fsdp', axis=0, tiled=True)  11.9 us
    all_to_all x2, starting transfers between devices, exchange(): lax.all_to_all(value, 'fsdp', split_axis=0, concat_axis=0, tiled=True)  10.7 us
  transfers between devices with their start and end apart: 25, of which 10 were waited for; matrix products, arithmetic and copies ran while one was open for 8% of the time, Pallas kernels for 32%

profile of v6, /device:TPU:0, one launch (start us, length us, event | category | flops | bytes accessed | tf_op | source)
XLA Modules:
  0.0 431.7 jit_solution(6462277026251512628)
XLA Ops:
  23.1 18.2 %collective-permute-done = bf16[512,768]{1,0:T(8,128)(2,1)} collective-permute-done((bf16[512,768]{1,0:T(8,128)(2,1)S(1)}, bf16[512,768]{1,0:T(8,128)(2,1)}, u32[]{:S(2)}, u32[]{:S(2)}) %collective-permute-start) | collective-permute-done | bytes 786464 | tf_op jit(solution)/shard_map/ppermute | solution.py:963
  41.3 16.0 %collective-permute-done.1 = bf16[512,768]{1,0:T(8,128)(2,1)} collective-permute-done((bf16[512,768]{1,0:T(8,128)(2,1)S(1)}, bf16[512,768]{1,0:T(8,128)(2,1)}, u32[]{:S(2)}, u32[]{:S(2)}) %collective-permute-start.1) | collective-permute-done | bytes 786464 | tf_op jit(solution)/shard_map/ppermute | solution.py:963
  57.3 5.1 %all-gather.6.cloned.1.call-done = bf16[512,1152]{1,0:T(8,128)(2,1)} async-done(((bf16[64,1152]{1,0:T(8,128)(2,1)}), bf16[512,1152]{1,0:T(8,128)(2,1)}) %all-gather.6.cloned.1.call-update) | async-done | bytes 1179664 | tf_op jit(solution)/shard_map/all_gather | solution.py:978
  70.7 4.2 pad_maximum_fusion.1.cot_ref
  74.9 13.9 %collective-permute-done.4 = bf16[8,48,1152]{2,1,0:T(8,128)(2,1)S(1)} collective-permute-done((bf16[8,48,1152]{2,1,0:T(8,128)(2,1)}, bf16[8,48,1152]{2,1,0:T(8,128)(2,1)S(1)}, u32[]{:S(2)}, u32[]{:S(2)}) %collective-permute-start.4) | collective-permute-done | bytes 884768 | tf_op jit(solution)/shard_map/ppermute | solution.py:963
  89.1 7.1 %project.1 = (bf16[2048,1152]{1,0:T(8,128)(2,1)S(1)}, bf16[1152,2048]{1,0:T(8,128)(2,1)S(1)}, bf16[2048,768]{1,0:T(8,128)(2,1)S(1)}) custom-call(bf16[2048,768]{1,0:T(8,128)(2,1)S(1)} %pad_maximum_fusion.tok_ref, bf16[768,1152]{1,0:T(8,128)(2,1)S(1)} %bitcast.67, f32[1,1152]{1,0:T(1,128)S(1)} %reshape.146.bias_ref, f32[8,768]{1,0:T(8,128)S(1)} %maximum_maximum_fusion.vec_ref), custom_call_target="tpu_custom_call" | custom-call | flops 3623878656 | bytes 18874368 | tf_op jit(solution)/shard_map/project/pallas_call | solution.py:897
  96.2 41.3 %attend_forward.1 = (bf16[2048,384]{1,0:T(8,128)(2,1)S(1)}, f32[384,2048]{1,0:T(8,128)S(1)}, f32[3,8,2048]{2,1,0:T(8,128)S(1)}) custom-call(s32[2,4]{1,0:T(2,128)S(1)} %copy-done.35, s32[1]{0:T(128)} %bitcast.1.place_ref, bf16[2048,1152]{1,0:T(8,128)(2,1)S(1)} %get-tuple-element.88.k_ref.q_ref.v_ref, ...), custom_call_target="tpu_custom_call" | custom-call | flops 25769803776 | bytes 9437184 | tf_op jit(solution)/shard_map/attend_forward/pallas_call | solution.py:163
  139.2 11.9 %all-gather.4.cloned.1.call-done.g2_ref = bf16[768,3456]{1,0:T(8,128)(2,1)} async-done(((bf16[96,3456]{1,0:T(8,128)(2,1)}), bf16[768,3456]{1,0:T(8,128)(2,1)}) %all-gather.4.cloned.1.call-update) | async-done | bytes 5308432 | tf_op jit(solution)/shard_map/all_gather | solution.py:990
  156.7 54.7 %feed_forward.1 = (f32[2048,768]{1,0:T(8,128)}, f32[1024,768]{1,0:T(8,128)}, bf16[1024,768]{1,0:T(8,128)(2,1)}, bf16[2048,768]{1,0:T(8,128)(2,1)}, bf16[768,3072...) custom-call(s32[1]{0:T(128)} %bitcast.core_ref, bf16[2048,768]{1,0:T(8,128)(2,1)} %copy-done, ...), custom_call_target="tpu_custom_call" | custom-call | flops 31406948352 | bytes 40894464 | tf_op jit(solution)/shard_map/feed_forward/pallas_call | solution.py:421
  213.9 7.7 %collective-permute-done.10 = bf16[1024,768]{1,0:T(8,128)(2,1)} collective-permute-done((bf16[1024,768]{1,0:T(8,128)(2,1)}, bf16[1024,768]{1,0:T(8,128)(2,1)}, u32[]{:S(2)}, u32[]{:S(2)}) %collective-permute-start.10) | collective-permute-done | bytes 1572896 | tf_op jit(solution)/shard_map/ppermute | solution.py:960
  221.6 4.0 add_convert_fusion
  225.7 13.3 %branch.1 = (f32[1024,768]{1,0:T(8,128)S(1)}, bf16[2048,384]{1,0:T(8,128)(2,1)S(1)}, bf16[384,2048]{1,0:T(8,128)(2,1)S(1)}, bf16[384,384]{1,0:T(8,128)(2,1)S(1)}...) custom-call(s32[1]{0:T(128)} %bitcast.core_ref, f32[2048,768]{1,0:T(8,128)} %get-tuple-element.93.mid_ref, ...), custom_call_target="tpu_custom_call" | custom-call | flops 3623878656 | bytes 28311552 | tf_op jit(solution)/shard_map/branch/pallas_call | solution.py:518
  240.8 3.3 copy-done.47
  246.0 44.5 %attend_backward.2 = (bf16[2048,256]{1,0:T(8,128)(2,1)S(1)}, bf16[2048,256]{1,0:T(8,128)(2,1)S(1)}, bf16[2048,256]{1,0:T(8,128)(2,1)S(1)}) custom-call(s32[2,4]{1,0:T(2,128)S(1)} %copy-done.35, s32[1]{0:T(128)} %bitcast.1.place_ref, bf16[2048,1152]{1,0:T(8,128)(2,1)S(1)} %bitcast.80, bf16[2048,1152]{1,0:T(8,128)(2,1)S(1)} %bitcast.80, ...), custom_call_target="tpu_custom_call" | custom-call | flops 42949672960 | bytes 12582912 | tf_op jit(solution)/shard_map/attend_backward/pallas_call | solution.py:271
  290.6 3.6 weight_grad.1
  295.6 4.7 %all-to-all-start = ((bf16[8,96,1152]{2,1,0:T(8,128)(2,1)}), bf16[8,96,1152]{2,1,0:T(8,128)(2,1)}, u32[]{:S(2)}, u32[]{:S(2)}) async-start(bf16[8,96,1152]{2,1,0:T(8,128)(2,1)} %bitcast.22), calls=%async_computation.1 | async-start | bytes 3538944 | tf_op jit(solution)/shard_map/all_to_all | solution.py:923
  303.3 17.6 %collective-permute-done.11 = bf16[512,768]{1,0:T(8,128)(2,1)} collective-permute-done((bf16[512,768]{1,0:T(8,128)(2,1)S(1)}, bf16[512,768]{1,0:T(8,128)(2,1)}, u32[]{:S(2)}, u32[]{:S(2)}) %collective-permute-start.11) | collective-permute-done | bytes 786464 | tf_op jit(solution)/shard_map/ppermute | solution.py:963
  331.8 21.9 %attend_backward.3 = (bf16[2048,128]{1,0:T(8,128)(2,1)S(1)}, bf16[2048,128]{1,0:T(8,128)(2,1)S(1)}, bf16[2048,128]{1,0:T(8,128)(2,1)S(1)}) custom-call(s32[2,4]{1,0:T(2,128)S(1)} %copy-done.35, s32[1]{0:T(128)} %bitcast.1.place_ref, bf16[2048,1152]{1,0:T(8,128)(2,1)S(1)} %copy-done.45, bf16[2048,1152]{1,0:T(8,128)(2,1)S(1)} %copy-done.45, ...), custom_call_target="tpu_custom_call" | custom-call | flops 21474836480 | bytes 6291456 | tf_op jit(solution)/shard_map/attend_backward/pallas_call | solution.py:271
  361.0 10.7 %project_back.1 = (f32[1024,768]{1,0:T(8,128)S(1)}, bf16[1024,768]{1,0:T(8,128)(2,1)S(1)}, bf16[768,384]{1,0:T(8,128)(2,1)S(1)}, f32[16,768]{1,0:T(8,128)S(1)}, f32[16,128]{1,0:T(8,128)S(1)}) custom-call(bf16[2048,768]{1,0:T(8,128)(2,1)} %copy-done, bf16[2048,768]{1,0:T(8,128)(2,1)} %copy-done.36, bf16[2048,256]{1,0:T(8,128)(2,1)S(1)} %copy-done.39, ...), custom_call_target="tpu_custom_call" | custom-call | flops 4831838208 | bytes 22020096 | tf_op jit(solution)/shard_map/project_back/pallas_call | solution.py:667
  376.0 6.0 %all-to-all-start.1 = ((bf16[8,112,384]{2,1,0:T(8,128)(2,1)}), bf16[8,112,384]{2,1,0:T(8,128)(2,1)}, u32[]{:S(2)}, u32[]{:S(2)}) async-start(bf16[8,112,384]{2,1,0:T(8,128)(2,1)} %fusion.4), calls=%async_computation.2 | async-start | bytes 1376256 | tf_op jit(solution)/shard_map/all_to_all | solution.py:923
  390.6 3.8 input_back.1
  396.4 4.3 %all-to-all-done.1 = bf16[8,112,384]{2,1,0:T(8,128)(2,1)} async-done(((bf16[8,112,384]{2,1,0:T(8,128)(2,1)}), bf16[8,112,384]{2,1,0:T(8,128)(2,1)}, u32[]{:S(2)}, u32[]{:S(2)}) %all-to-all-start.1) | async-done | bytes 688160 | tf_op jit(solution)/shard_map/all_to_all | solution.py:923
  410.4 3.0 finish_ff.1
  415.6 7.0 %collective-permute-done.14 = bf16[512,768]{1,0:T(8,128)(2,1)S(1)} collective-permute-done((bf16[512,768]{1,0:T(8,128)(2,1)}, bf16[512,768]{1,0:T(8,128)(2,1)S(1)}, u32[]{:S(2)}, u32[]{:S(2)}) %collective-permute-start.14) | collective-permute-done | bytes 786464 | tf_op jit(solution)/shard_map/ppermute | solution.py:963
  (252 shorter events, 88.9 us)
Async XLA Ops:
  7.2 55.2 %all-gather.6.cloned.1.call-start = ((), (), s32[]{:S(2)}) async-start(), calls=%async_computation.5 | async-start | bytes 1327104 | tf_op jit(solution)/shard_map/all_gather | solution.py:978
  18.5 132.6 %all-gather.4.cloned.1.call-start = ((), (), s32[]{:S(2)}) async-start(), calls=%async_computation.3 | async-start | bytes 5971968 | tf_op jit(solution)/shard_map/all_gather | solution.py:990
  19.9 21.4 %collective-permute-start = (bf16[512,768]{1,0:T(8,128)(2,1)S(1)}, bf16[512,768]{1,0:T(8,128)(2,1)}, u32[]{:S(2)}, u32[]{:S(2)}) collective-permute-start(bf16[512,768]{1,0:T(8,128)(2,1)S(1)} %get-tuple-element.148), channel_id=1, source_target_pairs={{0,2},{1,3},{2,0},{3,1},{4,6},{5,7},{6,4},{7,5},{8,10},{9,11},{10,... | collective-permute-start | bytes 2359304 | tf_op jit(solution)/shard_map/ppermute | solution.py:963
  22.9 34.4 %collective-permute-start.1 = (bf16[512,768]{1,0:T(8,128)(2,1)S(1)}, bf16[512,768]{1,0:T(8,128)(2,1)}, u32[]{:S(2)}, u32[]{:S(2)}) collective-permute-start(bf16[512,768]{1,0:T(8,128)(2,1)S(1)} %get-tuple-element.146), channel_id=1, source_target_pairs={{0,2},{1,3},{2,0},{3,1},{4,6},{5,7},{6,4},{7,5},{8,10},{9,11},{10,... | collective-permute-start | bytes 2359304 | tf_op jit(solution)/shard_map/ppermute | solution.py:963
  62.5 258.5 %reduce-scatter.2.cloned.1.call-start = ((), (), s32[]{:S(2)}) async-start(), calls=%async_computation.4 | async-start | bytes 5308416 | tf_op jit(solution)/shard_map/reduce_scatter | solution.py:1021
  62.5 6.2 %collective-permute-start.2 = (bf16[512,768]{1,0:T(8,128)(2,1)}, bf16[512,768]{1,0:T(8,128)(2,1)}, u32[]{:S(2)}, u32[]{:S(2)}) collective-permute-start(bf16[512,768]{1,0:T(8,128)(2,1)} %get-tuple-element.147), channel_id=1, source_target_pairs={{0,1},{1,0},{2,3},{3,2},{4,5},{5,4},{6,7},{7,6},{8,9},{9,8},{10,11... | collective-permute-start | bytes 2359304 | tf_op jit(solution)/shard_map/ppermute | solution.py:960
  62.6 8.1 %collective-permute-start.5 = (bf16[512,768]{1,0:T(8,128)(2,1)S(1)}, bf16[512,768]{1,0:T(8,128)(2,1)}, u32[]{:S(2)}, u32[]{:S(2)}) collective-permute-start(bf16[512,768]{1,0:T(8,128)(2,1)S(1)} %get-tuple-element.145), channel_id=1, source_target_pairs={{0,1},{1,0},{2,3},{3,2},{4,5},{5,4},{6,7},{7,6},{8,9},{9,8},{10,11... | collective-permute-start | bytes 2359304 | tf_op jit(solution)/shard_map/ppermute | solution.py:960
  63.2 5.5 %collective-permute-start.3 = (bf16[512,768]{1,0:T(8,128)(2,1)}, bf16[512,768]{1,0:T(8,128)(2,1)}, u32[]{:S(2)}, u32[]{:S(2)}) collective-permute-start(bf16[512,768]{1,0:T(8,128)(2,1)} %collective-permute-done), channel_id=1, source_target_pairs={{0,1},{1,0},{2,3},{3,2},{4,5},{5,4},{6,7},{7,6},{8,9},{9,8},{10,11... | collective-permute-start | bytes 2359304 | tf_op jit(solution)/shard_map/ppermute | solution.py:960
  63.2 7.5 %collective-permute-start.6 = (bf16[512,768]{1,0:T(8,128)(2,1)}, bf16[512,768]{1,0:T(8,128)(2,1)}, u32[]{:S(2)}, u32[]{:S(2)}) collective-permute-start(bf16[512,768]{1,0:T(8,128)(2,1)} %collective-permute-done.1), channel_id=1, source_target_pairs={{0,1},{1,0},{2,3},{3,2},{4,5},{5,4},{6,7},{7,6},{8,9},{9,8},{10,11... | collective-permute-start | bytes 2359304 | tf_op jit(solution)/shard_map/ppermute | solution.py:960
  67.0 21.8 %collective-permute-start.4 = (bf16[8,48,1152]{2,1,0:T(8,128)(2,1)}, bf16[8,48,1152]{2,1,0:T(8,128)(2,1)S(1)}, u32[]{:S(2)}, u32[]{:S(2)}) collective-permute-start(bf16[8,48,1152]{2,1,0:T(8,128)(2,1)} %get-tuple-element.150), channel_id=1, source_target_pairs={{0,2},{1,3},{2,0},{3,1},{4,6},{5,7},{6,4},{7,5},{8,10},{9,11},{10,... | collective-permute-start | bytes 2654216 | tf_op jit(solution)/shard_map/ppermute | solution.py:963
  139.2 16.4 %collective-permute-start.7 = (bf16[2048,384]{1,0:T(8,128)(2,1)S(1)}, bf16[2048,384]{1,0:T(8,128)(2,1)S(1)}, u32[]{:S(2)}, u32[]{:S(2)}) collective-permute-start(bf16[2048,384]{1,0:T(8,128)(2,1)S(1)} %get-tuple-element.90.mo_ref), channel_id=1, source_target_pairs={{0,1},{1,0},{2,3},{3,2},{4,5},{5,4},{6,7},{7,6},{8,9},{9,8},{10,11... | collective-permute-start | bytes 4718600 | tf_op jit(solution)/shard_map/ppermute | solution.py:960
  213.4 12.3 %collective-permute-start.9 = (bf16[2048,768]{1,0:T(8,128)(2,1)S(1)}, bf16[2048,768]{1,0:T(8,128)(2,1)}, u32[]{:S(2)}, u32[]{:S(2)}) collective-permute-start(bf16[2048,768]{1,0:T(8,128)(2,1)S(1)} %copy-done.6), channel_id=1, source_target_pairs={{0,1},{1,0},{2,3},{3,2},{4,5},{5,4},{6,7},{7,6},{8,9},{9,8},{10,11... | collective-permute-start | bytes 9437192 | tf_op jit(solution)/shard_map/ppermute | solution.py:960
  213.9 7.7 %collective-permute-start.10 = (bf16[1024,768]{1,0:T(8,128)(2,1)}, bf16[1024,768]{1,0:T(8,128)(2,1)}, u32[]{:S(2)}, u32[]{:S(2)}) collective-permute-start(bf16[1024,768]{1,0:T(8,128)(2,1)} %get-tuple-element.98), channel_id=1, source_target_pairs={{0,1},{1,0},{2,3},{3,2},{4,5},{5,4},{6,7},{7,6},{8,9},{9,8},{10,11... | collective-permute-start | bytes 4718600 | tf_op jit(solution)/shard_map/ppermute | solution.py:960
  295.6 59.7 %all-to-all-start = ((bf16[8,96,1152]{2,1,0:T(8,128)(2,1)}), bf16[8,96,1152]{2,1,0:T(8,128)(2,1)}, u32[]{:S(2)}, u32[]{:S(2)}) async-start(bf16[8,96,1152]{2,1,0:T(8,128)(2,1)} %bitcast.22), calls=%async_computation.1 | async-start | bytes 3538944 | tf_op jit(solution)/shard_map/all_to_all | solution.py:923
  301.3 19.7 %collective-permute-start.11 = (bf16[512,768]{1,0:T(8,128)(2,1)S(1)}, bf16[512,768]{1,0:T(8,128)(2,1)}, u32[]{:S(2)}, u32[]{:S(2)}) collective-permute-start(bf16[512,768]{1,0:T(8,128)(2,1)S(1)} %get-tuple-element.144), channel_id=1, source_target_pairs={{0,2},{1,3},{2,0},{3,1},{4,6},{5,7},{6,4},{7,5},{8,10},{9,11},{10,... | collective-permute-start | bytes 2359304 | tf_op jit(solution)/shard_map/ppermute | solution.py:963
  320.9 34.3 %collective-permute-start.12 = (bf16[96,3072]{1,0:T(8,128)(2,1)}, bf16[96,3072]{1,0:T(8,128)(2,1)}, u32[]{:S(2)}, u32[]{:S(2)}) collective-permute-start(bf16[96,3072]{1,0:T(8,128)(2,1)} %reduce-scatter.2.cloned.1.call-done), channel_id=1, source_target_pairs={{0,2},{1,3},{2,0},{3,1},{4,6},{5,7},{6,4},{7,5},{8,10},{9,11},{10,... | collective-permute-start | bytes 1769480 | tf_op jit(solution)/shard_map/ppermute | solution.py:963
  375.0 11.8 %collective-permute-start.13 = (bf16[1024,768]{1,0:T(8,128)(2,1)}, bf16[1024,768]{1,0:T(8,128)(2,1)}, u32[]{:S(2)}, u32[]{:S(2)}) collective-permute-start(bf16[1024,768]{1,0:T(8,128)(2,1)} %copy-done.33), channel_id=1, source_target_pairs={{0,1},{1,0},{2,3},{3,2},{4,5},{5,4},{6,7},{7,6},{8,9},{9,8},{10,11... | collective-permute-start | bytes 4718600 | tf_op jit(solution)/shard_map/ppermute | solution.py:960
  376.0 24.8 %all-to-all-start.1 = ((bf16[8,112,384]{2,1,0:T(8,128)(2,1)}), bf16[8,112,384]{2,1,0:T(8,128)(2,1)}, u32[]{:S(2)}, u32[]{:S(2)}) async-start(bf16[8,112,384]{2,1,0:T(8,128)(2,1)} %fusion.4), calls=%async_computation.2 | async-start | bytes 1376256 | tf_op jit(solution)/shard_map/all_to_all | solution.py:923
  383.9 20.1 %collective-permute-start.15 = (bf16[96,1152]{1,0:T(8,128)(2,1)S(1)}, bf16[96,1152]{1,0:T(8,128)(2,1)}, u32[]{:S(2)}, u32[]{:S(2)}) collective-permute-start(bf16[96,1152]{1,0:T(8,128)(2,1)S(1)} %reduce_sum.74), channel_id=1, source_target_pairs={{0,2},{1,3},{2,0},{3,1},{4,6},{5,7},{6,4},{7,5},{8,10},{9,11},{10,... | collective-permute-start | bytes 663560 | tf_op jit(solution)/shard_map/ppermute | solution.py:963
  386.8 23.6 %collective-permute-start.19 = (bf16[96,3072]{1,0:T(8,128)(2,1)}, bf16[96,3072]{1,0:T(8,128)(2,1)}, u32[]{:S(2)}, u32[]{:S(2)}) collective-permute-start(bf16[96,3072]{1,0:T(8,128)(2,1)} %add_convert_fusion.1.mine_ref), channel_id=1, source_target_pairs={{0,1},{1,0},{2,3},{3,2},{4,5},{5,4},{6,7},{7,6},{8,9},{9,8},{10,11... | collective-permute-start | bytes 1769480 | tf_op jit(solution)/shard_map/ppermute | solution.py:960
  401.9 5.5 %collective-permute-start.17 = (bf16[112,384]{1,0:T(8,128)(2,1)S(1)}, bf16[112,384]{1,0:T(8,128)(2,1)S(1)}, u32[]{:S(2)}, u32[]{:S(2)}) collective-permute-start(bf16[112,384]{1,0:T(8,128)(2,1)S(1)} %reduce_sum.75), channel_id=1, source_target_pairs={{0,2},{1,3},{2,0},{3,1},{4,6},{5,7},{6,4},{7,5},{8,10},{9,11},{10,... | collective-permute-start | bytes 258056 | tf_op jit(solution)/shard_map/ppermute | solution.py:963
  402.6 20.1 %collective-permute-start.14 = (bf16[512,768]{1,0:T(8,128)(2,1)}, bf16[512,768]{1,0:T(8,128)(2,1)S(1)}, u32[]{:S(2)}, u32[]{:S(2)}) collective-permute-start(bf16[512,768]{1,0:T(8,128)(2,1)} %copy-done.34), channel_id=1, source_target_pairs={{0,2},{1,3},{2,0},{3,1},{4,6},{5,7},{6,4},{7,5},{8,10},{9,11},{10,... | collective-permute-start | bytes 2359304 | tf_op jit(solution)/shard_map/ppermute | solution.py:963
  405.0 8.3 %collective-permute-start.16 = (bf16[96,1152]{1,0:T(8,128)(2,1)S(1)}, bf16[96,1152]{1,0:T(8,128)(2,1)S(1)}, u32[]{:S(2)}, u32[]{:S(2)}) collective-permute-start(bf16[96,1152]{1,0:T(8,128)(2,1)S(1)} %add_convert_fusion.2.em_ref), channel_id=1, source_target_pairs={{0,1},{1,0},{2,3},{3,2},{4,5},{5,4},{6,7},{7,6},{8,9},{9,8},{10,11... | collective-permute-start | bytes 663560 | tf_op jit(solution)/shard_map/ppermute | solution.py:960
  407.5 5.9 %collective-permute-start.18 = (bf16[112,384]{1,0:T(8,128)(2,1)S(1)}, bf16[112,384]{1,0:T(8,128)(2,1)S(1)}, u32[]{:S(2)}, u32[]{:S(2)}) collective-permute-start(bf16[112,384]{1,0:T(8,128)(2,1)S(1)} %add_convert_fusion.3.lm_ref), channel_id=1, source_target_pairs={{0,1},{1,0},{2,3},{3,2},{4,5},{5,4},{6,7},{7,6},{8,9},{9,8},{10,11... | collective-permute-start | bytes 258056 | tf_op jit(solution)/shard_map/ppermute | solution.py:960
  (66 other events, 523.9 us)
Sparse Core Ops, SparseCore 0:
  18.6 43.8 all-gather.5
  65.2 85.8 all-gather.3
  211.6 94.4 reduce-scatter.1

commit v7 on v6

--- a/solution.py
+++ b/solution.py
@@ -188,7 +188,7 @@
             pltpu.VMEM((8, bq), F32),
             pltpu.VMEM((8, bq), F32),
         ],
-        compiler_params=params(24, "arbitrary", "arbitrary"),
+        compiler_params=params(60, "arbitrary", "arbitrary"),
         cost_estimate=cost(
             2 * pairs * 2 * 2 * keys * keys * 256, 12 * keys * width, 2 * pairs * keys * keys
         ),
@@ -296,7 +296,7 @@
             pltpu.VMEM((2, keys, PAIR), F32),
             pltpu.VMEM((2, keys, PAIR), F32),
         ],
-        compiler_params=params(32, "arbitrary", "arbitrary"),
+        compiler_params=params(60, "arbitrary", "arbitrary"),
         cost_estimate=cost(
             2 * count * 5 * 2 * keys * keys * 256, 24 * keys * count * PAIR,
             2 * count * keys * keys,
@@ -551,7 +551,7 @@
             pltpu.VMEM((24, width), F32),
             pltpu.VMEM((bt, width), BF),
         ],
-        compiler_params=params(40, "arbitrary"),
+        compiler_params=params(60, "arbitrary"),
         cost_estimate=cost(2 * rows * width * 3 * half, 18 * rows * width),
         name="branch",
     )(core, middle, grad_own, grad_sib, cot, mixed_own, mixed_sib, wp_own, vec)
@@ -602,7 +602,7 @@
             jax.ShapeDtypeStruct((16, part), F32),
         ],
         scratch_shapes=[pltpu.VMEM((width, 3 * part), F32), pltpu.VMEM((16, part), F32)],
-        compiler_params=params(24, "arbitrary"),
+        compiler_params=params(60, "arbitrary"),
         cost_estimate=cost(2 * rows * width * 3 * part, 2 * rows * (width + 3 * part)),
         name="weight_grad",
     )(normed, gq, gk, gv)
@@ -690,7 +690,7 @@
             pltpu.VMEM((16, width), F32),
             pltpu.VMEM((16, part), F32),
         ],
-        compiler_params=params(40, "arbitrary"),
+        compiler_params=params(60, "arbitrary"),
         cost_estimate=cost(2 * rows * width * (6 * part + 3 * early), 14 * rows * width),
         name="project_back",
     )(tokens, normed, *before, *grads, weight)
@@ -729,7 +729,7 @@
             jax.ShapeDtypeStruct((rows // 2, width), F32),
             jax.ShapeDtypeStruct((rows // 2, width), BF),
         ],
-        compiler_params=params(16, "arbitrary"),
+        compiler_params=params(60, "arbitrary"),
         cost_estimate=cost(20 * rows * width, 16 * rows * width),
         name="input_back",
     )(tokens, grad_own, grad_sib, grad_middle, vec)
@@ -772,7 +772,7 @@
             jax.ShapeDtypeStruct((shard, wide), F32),
             jax.ShapeDtypeStruct((4 * quarter, width), F32),
         ],
-        compiler_params=params(16, "arbitrary"),
+        compiler_params=params(60, "arbitrary"),
         cost_estimate=cost(0, 12 * shard * wide),
         name="finish_ff",
     )(place, mine, other)
@@ -817,7 +817,7 @@
             jax.ShapeDtypeStruct((shard, width), F32),
             jax.ShapeDtypeStruct((rows, late_mine.shape[1]), F32),
         ],
-        compiler_params=params(16, "arbitrary"),
+        compiler_params=params(60, "arbitrary"),
         cost_estimate=cost(0, 24 * shard * width),
         name="finish_attend",
     )(place, early_mine, early_other, late_mine, late_other)
@@ -875,7 +875,7 @@
             jax.ShapeDtypeStruct((rows, 3 * part), BF),
             jax.ShapeDtypeStruct((shard, 5 * part + half), BF),
         ],
-        compiler_params=params(16, "arbitrary"),
+        compiler_params=params(60, "arbitrary"),
         cost_estimate=cost(0, 5 * shard * width * 8),
         name="pack_weights",
     )(place, *values)
@@ -913,7 +913,7 @@
             jax.ShapeDtypeStruct((wide, rows), BF),
             jax.ShapeDtypeStruct((rows, width), BF),
         ],
-        compiler_params=params(36, "arbitrary"),
+        compiler_params=params(60, "arbitrary"),
         cost_estimate=cost(2 * rows * width * wide, 12 * rows * width),
         name="project",
     )(tokens, weight, bias, vec)
@@ -1037,35 +1037,34 @@
         jnp.concatenate([dwp_own, dwp_sib], axis=0),
         jnp.concatenate([dwp_sib, dwp_own], axis=0),
     )
-    out_own = (out_own + sibling(out_send).astype(F32)).astype(BF)
-    grad_mixed, out_own = lax.optimization_barrier((grad_mixed, out_own))
-    out_came = partner(out_own[slots:])
+    grad_mixed, out_send, out_own = lax.optimization_barrier((grad_mixed, out_send, out_own))
+    out_sib = sibling(out_send)
     early, late = 2, 1
     attend = functools.partial(attend_backward, counts, place_row, packed, packed_t)
     before = attend(grad_mixed, grad_mixed_t, result_t, log_total, slots, 0, early)
+    before, out_sib = lax.optimization_barrier((before, out_sib))
     dw_early, qv_early = weight_grad(normed, *before)
+    out_own = (out_own + out_sib.astype(F32)).astype(BF)
     block_one = jnp.concatenate([dw_early, dwp], axis=1).reshape(owners, shard, -1)
+    grad_mixed, out_own, block_one = lax.optimization_barrier((grad_mixed, out_own, block_one))
     came_one = exchange(block_one)
-    grad_mixed, out_came, block_one, scattered_one = lax.optimization_barrier(
-        (grad_mixed, out_came, block_one, scattered_one)
+    out_came = partner(out_own[slots:])
+    grads = attend(grad_mixed, grad_mixed_t, result_t, log_total, slots, early, late)
+
+    def total(came):
+        return jnp.sum(came.astype(F32), axis=0).astype(BF)
+
+    def join(value, came):
+        return (value.astype(F32) + came.astype(F32)).astype(BF)
+
+    scattered_one, came_one, out_came, grads = lax.optimization_barrier(
+        (scattered_one, came_one, out_came, grads)
     )
     output = hand_back(out_own, out_came)
     one_came = partner(scattered_one)
-    grads = attend(grad_mixed, grad_mixed_t, result_t, log_total, slots, early, late)
-
-    def total(came):
-        return jnp.sum(came.astype(F32), axis=0).astype(BF)
-
-    def join(value, came):
-        return (value.astype(F32) + came.astype(F32)).astype(BF)
-
-    one_came, came_one, w_qkv, grads = lax.optimization_barrier(
-        (one_came, came_one, w_qkv, grads)
-    )
     early_total = total(came_one)
     early_came = partner(early_total)
     one_sum = join(scattered_one, one_came)
-    one_other = sibling(one_sum)
     gn1_own, gn1_send, dw_late, vec_first, qv_late = project_back(tok, normed, before, grads, w_qkv)
 
     def spread(vector):
@@ -1102,7 +1101,8 @@
     came_two = exchange(block_two)
     input_own, input_send = input_back(tok, gn1_own, gn1_sib, grad_middle, vec_one)
     input_came = partner(input_send)
-    came_two, input_own = lax.optimization_barrier((came_two, input_own))
+    came_two, input_own, one_sum = lax.optimization_barrier((came_two, input_own, one_sum))
+    one_other = sibling(one_sum)
     input_grad = hand_back(input_own, input_came)
 
     grad_fc1, grad_fc2 = finish_ff(place_row, one_sum, one_other, width, quarter)

time: 439 us -> 413 us (0.941)
  local copies, waits for them, and re-layouts: 58.5 us -> 19.7 us
  Pallas kernels: 206 us -> 228 us
  waiting for transfers between devices: 104 us -> 97 us
    unnamed x136 -> x48, local copies, waits for them, and re-layouts: 46.6 us -> 5.38 us
    all_to_all x2, waiting for transfers between devices: 4.32 us -> 21.7 us  [exchange(): lax.all_to_all(value, 'fsdp', split_axis=0, concat_axis=0, tiled=True)]
    ppermute x8, waiting for transfers between devices: 75.2 us -> 58.1 us  [partner(): return lax.ppermute(value, 'seq', to_partner)]
    all_gather x1, waiting for transfers between devices: 11.9 us -> 6.55 us  [per_device(): second = lax.all_gather(two, 'fsdp', axis=0, tiled=True)]
  transfers between devices with their start and end apart: 25 -> 25, of which waited for: 10 -> 12; matrix products, arithmetic and copies ran while one was open for 8% -> 8% of each run, Pallas kernels for 32% -> 39%
where the time goes in v7:
time: 413 us; the launch traced here: 406 us
  Pallas kernels  228 us (55%)
  waiting for transfers between devices  97 us (23%)
  other arithmetic  25.4 us (6%)
  starting transfers between devices  21.6 us (5%)
  local copies, waits for them, and re-layouts  19.7 us (5%)
  between operations  14.8 us (4%)
    pallas_call x2, Pallas kernels, attend_backward(): pl.pallas_call(kernel, grid=(count, keys // bq), in_specs=[pl.BlockSpec(m...  69.5 us
    ppermute x8, waiting for transfers between devices, partner(): return lax.ppermute(value, 'seq', to_partner)  58.1 us
    pallas_call x1, Pallas kernels, feed_forward(): pl.pallas_call(kernel, grid=(blocks,), in_specs=[pl.BlockSpec(memory_spac...  54.5 us
    pallas_call x1, Pallas kernels, attend_forward(): pl.pallas_call(kernel, grid=(pairs, keys // bq), in_specs=[pl.BlockSpec(m...  42.5 us
    all_to_all x2, waiting for transfers between devices, exchange(): lax.all_to_all(value, 'fsdp', split_axis=0, concat_axis=0, tiled=True)  21.7 us
    pallas_call x1, Pallas kernels, branch(): pl.pallas_call(branch_kernel, grid=(blocks,), in_specs=[pl.BlockSpec(memo...  16.1 us
    pallas_call x1, Pallas kernels, project_back(): pl.pallas_call(project_back_kernel, grid=(blocks,), in_specs=[pl.BlockSpe...  14 us
    ppermute x8, starting transfers between devices, partner(): return lax.ppermute(value, 'seq', to_partner)  10.7 us
  transfers between devices with their start and end apart: 25, of which 12 were waited for; matrix products, arithmetic and copies ran while one was open for 8% of the time, Pallas kernels for 39%

profile of v7, /device:TPU:0, one launch (start us, length us, event | category | flops | bytes accessed | tf_op | source)
XLA Modules:
  0.0 406.5 jit_solution(1328922731448510855)
XLA Ops:
  16.1 17.7 %collective-permute-done = bf16[512,768]{1,0:T(8,128)(2,1)} collective-permute-done((bf16[512,768]{1,0:T(8,128)(2,1)S(1)}, bf16[512,768]{1,0:T(8,128)(2,1)}, u32[]{:S(2)}, u32[]{:S(2)}) %collective-permute-start) | collective-permute-done | bytes 786464 | tf_op jit(solution)/shard_map/ppermute | solution.py:963
  33.8 16.0 %collective-permute-done.1 = bf16[512,768]{1,0:T(8,128)(2,1)} collective-permute-done((bf16[512,768]{1,0:T(8,128)(2,1)S(1)}, bf16[512,768]{1,0:T(8,128)(2,1)}, u32[]{:S(2)}, u32[]{:S(2)}) %collective-permute-start.1) | collective-permute-done | bytes 786464 | tf_op jit(solution)/shard_map/ppermute | solution.py:963
  49.9 5.5 %all-gather.6.cloned.1.call-done = bf16[512,1152]{1,0:T(8,128)(2,1)} async-done(((bf16[64,1152]{1,0:T(8,128)(2,1)}), bf16[512,1152]{1,0:T(8,128)(2,1)}) %all-gather.6.cloned.1.call-update) | async-done | bytes 1179664 | tf_op jit(solution)/shard_map/all_gather | solution.py:978
  62.8 3.4 pad_maximum_fusion.tok_ref
  66.1 3.1 pad_maximum_fusion.1.cot_ref
  69.2 12.6 %collective-permute-done.4 = bf16[8,48,1152]{2,1,0:T(8,128)(2,1)} collective-permute-done((bf16[8,48,1152]{2,1,0:T(8,128)(2,1)}, bf16[8,48,1152]{2,1,0:T(8,128)(2,1)}, u32[]{:S(2)}, u32[]{:S(2)}) %collective-permute-start.4) | collective-permute-done | bytes 884768 | tf_op jit(solution)/shard_map/ppermute | solution.py:963
  81.8 3.0 maximum_select_fusion.1
  84.8 10.0 %project.1 = (bf16[2048,1152]{1,0:T(8,128)(2,1)}, bf16[1152,2048]{1,0:T(8,128)(2,1)}, bf16[2048,768]{1,0:T(8,128)(2,1)}) custom-call(bf16[2048,768]{1,0:T(8,128)(2,1)} %pad_maximum_fusion.tok_ref, bf16[768,1152]{1,0:T(8,128)(2,1)} %bitcast.70, f32[1,1152]{1,0:T(1,128)} %reshape.146.bias_ref, f32[8,768]{1,0:T(8,128)} %maximum_maximum_fusion.vec_ref), custom_call_target="tpu_custom_call" | custom-call | flops 3623878656 | bytes 18874368 | tf_op jit(solution)/shard_map/project/pallas_call | solution.py:897
  94.9 42.5 %attend_forward.1 = (bf16[2048,384]{1,0:T(8,128)(2,1)}, f32[384,2048]{1,0:T(8,128)}, f32[3,8,2048]{2,1,0:T(8,128)}) custom-call(s32[2,4]{1,0:T(2,128)} %counts_ref.5, s32[1]{0:T(128)} %bitcast.1.place_ref, bf16[2048,1152]{1,0:T(8,128)(2,1)} %get-tuple-element.94.k_ref.q_ref.v_ref, bf16[1152,2048]{1,0:T(8,128)(2,1)} %get-tuple-element.95.qt_ref.vt_ref.kt_ref, ...), custom_call_target="tpu_custom_call" | custom-call | flops 25769803776 | bytes 9437184 | tf_op jit(solution)/shard_map/attend_forward/pallas_call | solution.py:163
  137.4 6.5 %all-gather.4.cloned.1.call-done.g2_ref = bf16[768,3456]{1,0:T(8,128)(2,1)} async-done(((bf16[96,3456]{1,0:T(8,128)(2,1)}), bf16[768,3456]{1,0:T(8,128)(2,1)}) %all-gather.4.cloned.1.call-update) | async-done | bytes 5308432 | tf_op jit(solution)/shard_map/all_gather | solution.py:990
  148.1 54.5 %feed_forward.1 = (f32[2048,768]{1,0:T(8,128)}, f32[1024,768]{1,0:T(8,128)}, bf16[1024,768]{1,0:T(8,128)(2,1)}, bf16[2048,768]{1,0:T(8,128)(2,1)}, bf16[768,3072...) custom-call(s32[1]{0:T(128)} %bitcast.core_ref, ...), custom_call_target="tpu_custom_call" | custom-call | flops 31406948352 | bytes 40894464 | tf_op jit(solution)/shard_map/feed_forward/pallas_call | solution.py:421
  203.9 4.7 %collective-permute-done.9.gb_ref = bf16[2048,768]{1,0:T(8,128)(2,1)S(1)} collective-permute-done((bf16[2048,768]{1,0:T(8,128)(2,1)}, bf16[2048,768]{1,0:T(8,128)(2,1)S(1)}, u32[]{:S(2)}, u32[]{:S(2)}) %collective-permute-start.9) | collective-permute-done | bytes 3145760 | tf_op jit(solution)/shard_map/ppermute | solution.py:960
  210.3 16.1 %branch.1 = (f32[1024,768]{1,0:T(8,128)}, bf16[2048,384]{1,0:T(8,128)(2,1)}, bf16[384,2048]{1,0:T(8,128)(2,1)}, bf16[384,384]{1,0:T(8,128)(2,1)}, bf16[384,384]{1,0:T(8,128)(2,1)}, /*index=5*/f32[24,768]{1,0:T(8,128)}) custom-call(s32[1]{0:T(128)} %bitcast.core_ref, f32[2048,768]{1,0:T(8,128)} %get-tuple-element.99.mid_ref, ...), custom_call_target="tpu_custom_call" | custom-call | flops 3623878656 | bytes 28311552 | tf_op jit(solution)/shard_map/branch/pallas_call | solution.py:518
  226.9 45.4 %attend_backward.2 = (bf16[2048,256]{1,0:T(8,128)(2,1)}, bf16[2048,256]{1,0:T(8,128)(2,1)}, bf16[2048,256]{1,0:T(8,128)(2,1)}) custom-call(s32[2,4]{1,0:T(2,128)} %counts_ref.5, s32[1]{0:T(128)} %bitcast.1.place_ref, bf16[2048,1152]{1,0:T(8,128)(2,1)} %get-tuple-element.94.k_ref.q_ref.v_ref, bf16[2048,1152]{1,0:T(8,128)(2,1)} %get-tuple-element.94.k_ref.q_ref.v_ref, ...), custom_call_target="tpu_custom_call" | custom-call | flops 42949672960 | bytes 12582912 | tf_op jit(solution)/shard_map/attend_backward/pallas_call | solution.py:271
  272.5 6.6 %weight_grad.1 = (bf16[768,768]{1,0:T(8,128)(2,1)}, f32[16,256]{1,0:T(8,128)}) custom-call(bf16[2048,768]{1,0:T(8,128)(2,1)} %get-tuple-element.115.normed_ref, bf16[2048,256]{1,0:T(8,128)(2,1)} %get-tuple-element.116.gq_ref.gqa_ref, bf16[2048,256]{1,0:T(8,128)(2,1)} %get-tuple-element.117.gk_ref.gka_ref, bf16[2048,256]{1,0:T(8,128)(2,1)} %get-tuple-element.118.gv_ref.gva_ref), custom_call_target="tpu_custom_call" | custom-call | flops 2415919104 | bytes 6291456 | tf_op jit(solution)/shard_map/weight_grad/pallas_call | solution.py:590
  282.4 4.0 all-to-all-start
  289.7 24.0 %attend_backward.3 = (bf16[2048,128]{1,0:T(8,128)(2,1)}, bf16[2048,128]{1,0:T(8,128)(2,1)}, bf16[2048,128]{1,0:T(8,128)(2,1)}) custom-call(s32[2,4]{1,0:T(2,128)} %counts_ref.5, s32[1]{0:T(128)} %bitcast.1.place_ref, bf16[2048,1152]{1,0:T(8,128)(2,1)} %get-tuple-element.94.k_ref.q_ref.v_ref, bf16[2048,1152]{1,0:T(8,128)(2,1)} %get-tuple-element.94.k_ref.q_ref.v_ref, ...), custom_call_target="tpu_custom_call" | custom-call | flops 21474836480 | bytes 6291456 | tf_op jit(solution)/shard_map/attend_backward/pallas_call | solution.py:271
  313.8 20.7 %all-to-all-done = bf16[8,96,1152]{2,1,0:T(8,128)(2,1)S(1)} async-done(((bf16[8,96,1152]{2,1,0:T(8,128)(2,1)}), bf16[8,96,1152]{2,1,0:T(8,128)(2,1)S(1)}, u32[]{:S(2)}, u32[]{:S(2)}) %all-to-all-start) | async-done | bytes 1769504 | tf_op jit(solution)/shard_map/all_to_all | solution.py:923
  334.5 14.0 %project_back.1 = (f32[1024,768]{1,0:T(8,128)}, bf16[1024,768]{1,0:T(8,128)(2,1)}, bf16[768,384]{1,0:T(8,128)(2,1)}, f32[16,768]{1,0:T(8,128)}, f32[16,128]{1,0:T(8,128)}) custom-call(bf16[2048,768]{1,0:T(8,128)(2,1)} %pad_maximum_fusion.tok_ref, bf16[2048,768]{1,0:T(8,128)(2,1)} %get-tuple-element.115.normed_ref, ...), custom_call_target="tpu_custom_call" | custom-call | flops 4831838208 | bytes 22020096 | tf_op jit(solution)/shard_map/project_back/pallas_call | solution.py:667
  354.0 4.0 all-to-all-start.1
  358.9 8.1 %collective-permute-done.13 = bf16[96,3072]{1,0:T(8,128)(2,1)} collective-permute-done((bf16[96,3072]{1,0:T(8,128)(2,1)}, bf16[96,3072]{1,0:T(8,128)(2,1)}, u32[]{:S(2)}, u32[]{:S(2)}) %collective-permute-start.13) | collective-permute-done | bytes 589856 | tf_op jit(solution)/shard_map/ppermute | solution.py:963
  368.4 6.9 %input_back.1 = (f32[512,768]{1,0:T(8,128)}, bf16[512,768]{1,0:T(8,128)(2,1)}) custom-call(bf16[2048,768]{1,0:T(8,128)(2,1)} %pad_maximum_fusion.tok_ref, f32[1024,768]{1,0:T(8,128)} %get-tuple-element.140.own_ref, bf16[1024,768]{1,0:T(8,128)(2,1)} %collective-permute-done.12.sib_ref, f32[1024,768]{1,0:T(8,128)} %get-tuple-element.142.gm_ref, ...), custom_call_target="tpu_custom_call" | custom-call | flops 15728640 | bytes 12582912 | tf_op jit(solution)/shard_map/input_back/pallas_call | solution.py:720
  379.8 3.0 collective-permute-done.17
  393.8 3.0 finish_ff.1
  (163 shorter events, 56.2 us)
Async XLA Ops:
  7.2 48.1 %all-gather.6.cloned.1.call-start = ((), (), s32[]{:S(2)}) async-start(), calls=%async_computation.5 | async-start | bytes 1327104 | tf_op jit(solution)/shard_map/all_gather | solution.py:978
  11.3 132.6 %all-gather.4.cloned.1.call-start = ((), (), s32[]{:S(2)}) async-start(), calls=%async_computation.3 | async-start | bytes 5971968 | tf_op jit(solution)/shard_map/all_gather | solution.py:990
  12.4 21.4 %collective-permute-start = (bf16[512,768]{1,0:T(8,128)(2,1)S(1)}, bf16[512,768]{1,0:T(8,128)(2,1)}, u32[]{:S(2)}, u32[]{:S(2)}) collective-permute-start(bf16[512,768]{1,0:T(8,128)(2,1)S(1)} %get-tuple-element.160), channel_id=1, source_target_pairs={{0,2},{1,3},{2,0},{3,1},{4,6},{5,7},{6,4},{7,5},{8,10},{9,11},{10,... | collective-permute-start | bytes 2359304 | tf_op jit(solution)/shard_map/ppermute | solution.py:963
  15.5 34.4 %collective-permute-start.1 = (bf16[512,768]{1,0:T(8,128)(2,1)S(1)}, bf16[512,768]{1,0:T(8,128)(2,1)}, u32[]{:S(2)}, u32[]{:S(2)}) collective-permute-start(bf16[512,768]{1,0:T(8,128)(2,1)S(1)} %get-tuple-element.158), channel_id=1, source_target_pairs={{0,2},{1,3},{2,0},{3,1},{4,6},{5,7},{6,4},{7,5},{8,10},{9,11},{10,... | collective-permute-start | bytes 2359304 | tf_op jit(solution)/shard_map/ppermute | solution.py:963
  55.3 279.1 %reduce-scatter.2.cloned.1.call-start = ((), (), s32[]{:S(2)}) async-start(), calls=%async_computation.4 | async-start | bytes 5308416 | tf_op jit(solution)/shard_map/reduce_scatter | solution.py:1021
  55.4 7.4 %collective-permute-start.2 = (bf16[512,768]{1,0:T(8,128)(2,1)}, bf16[512,768]{1,0:T(8,128)(2,1)}, u32[]{:S(2)}, u32[]{:S(2)}) collective-permute-start(bf16[512,768]{1,0:T(8,128)(2,1)} %get-tuple-element.159), channel_id=1, source_target_pairs={{0,1},{1,0},{2,3},{3,2},{4,5},{5,4},{6,7},{7,6},{8,9},{9,8},{10,11... | collective-permute-start | bytes 2359304 | tf_op jit(solution)/shard_map/ppermute | solution.py:960
  55.5 10.7 %collective-permute-start.5 = (bf16[512,768]{1,0:T(8,128)(2,1)S(1)}, bf16[512,768]{1,0:T(8,128)(2,1)}, u32[]{:S(2)}, u32[]{:S(2)}) collective-permute-start(bf16[512,768]{1,0:T(8,128)(2,1)S(1)} %get-tuple-element.157), channel_id=1, source_target_pairs={{0,1},{1,0},{2,3},{3,2},{4,5},{5,4},{6,7},{7,6},{8,9},{9,8},{10,11... | collective-permute-start | bytes 2359304 | tf_op jit(solution)/shard_map/ppermute | solution.py:960
  56.0 6.7 %collective-permute-start.3 = (bf16[512,768]{1,0:T(8,128)(2,1)}, bf16[512,768]{1,0:T(8,128)(2,1)}, u32[]{:S(2)}, u32[]{:S(2)}) collective-permute-start(bf16[512,768]{1,0:T(8,128)(2,1)} %collective-permute-done), channel_id=1, source_target_pairs={{0,1},{1,0},{2,3},{3,2},{4,5},{5,4},{6,7},{7,6},{8,9},{9,8},{10,11... | collective-permute-start | bytes 2359304 | tf_op jit(solution)/shard_map/ppermute | solution.py:960
  56.1 10.0 %collective-permute-start.6 = (bf16[512,768]{1,0:T(8,128)(2,1)}, bf16[512,768]{1,0:T(8,128)(2,1)}, u32[]{:S(2)}, u32[]{:S(2)}) collective-permute-start(bf16[512,768]{1,0:T(8,128)(2,1)} %collective-permute-done.1), channel_id=1, source_target_pairs={{0,1},{1,0},{2,3},{3,2},{4,5},{5,4},{6,7},{7,6},{8,9},{9,8},{10,11... | collective-permute-start | bytes 2359304 | tf_op jit(solution)/shard_map/ppermute | solution.py:960
  59.8 21.9 %collective-permute-start.4 = (bf16[8,48,1152]{2,1,0:T(8,128)(2,1)}, bf16[8,48,1152]{2,1,0:T(8,128)(2,1)}, u32[]{:S(2)}, u32[]{:S(2)}) collective-permute-start(bf16[8,48,1152]{2,1,0:T(8,128)(2,1)} %get-tuple-element.162), channel_id=1, source_target_pairs={{0,2},{1,3},{2,0},{3,1},{4,6},{5,7},{6,4},{7,5},{8,10},{9,11},{10,... | collective-permute-start | bytes 2654216 | tf_op jit(solution)/shard_map/ppermute | solution.py:963
  137.4 9.6 %collective-permute-start.7 = (bf16[2048,384]{1,0:T(8,128)(2,1)}, bf16[2048,384]{1,0:T(8,128)(2,1)S(1)}, u32[]{:S(2)}, u32[]{:S(2)}) collective-permute-start(bf16[2048,384]{1,0:T(8,128)(2,1)} %get-tuple-element.96.mo_ref), channel_id=1, source_target_pairs={{0,1},{1,0},{2,3},{3,2},{4,5},{5,4},{6,7},{7,6},{8,9},{9,8},{10,11... | collective-permute-start | bytes 4718600 | tf_op jit(solution)/shard_map/ppermute | solution.py:960
  202.6 6.0 %collective-permute-start.9 = (bf16[2048,768]{1,0:T(8,128)(2,1)}, bf16[2048,768]{1,0:T(8,128)(2,1)S(1)}, u32[]{:S(2)}, u32[]{:S(2)}) collective-permute-start(bf16[2048,768]{1,0:T(8,128)(2,1)} %get-tuple-element.100.ga_ref), channel_id=1, source_target_pairs={{0,1},{1,0},{2,3},{3,2},{4,5},{5,4},{6,7},{7,6},{8,9},{9,8},{10,11... | collective-permute-start | bytes 9437192 | tf_op jit(solution)/shard_map/ppermute | solution.py:960
  226.4 46.1 %collective-permute-start.10 = (bf16[1024,768]{1,0:T(8,128)(2,1)}, bf16[1024,768]{1,0:T(8,128)(2,1)S(1)}, u32[]{:S(2)}, u32[]{:S(2)}) collective-permute-start(bf16[1024,768]{1,0:T(8,128)(2,1)} %get-tuple-element.113), channel_id=1, source_target_pairs={{0,1},{1,0},{2,3},{3,2},{4,5},{5,4},{6,7},{7,6},{8,9},{9,8},{10,11... | collective-permute-start | bytes 4718600 | tf_op jit(solution)/shard_map/ppermute | solution.py:960
  282.4 52.1 %all-to-all-start = ((bf16[8,96,1152]{2,1,0:T(8,128)(2,1)}), bf16[8,96,1152]{2,1,0:T(8,128)(2,1)S(1)}, u32[]{:S(2)}, u32[]{:S(2)}) async-start(bf16[8,96,1152]{2,1,0:T(8,128)(2,1)} %bitcast.21), calls=%async_computation.1 | async-start | bytes 3538944 | tf_op jit(solution)/shard_map/all_to_all | solution.py:923
  288.2 25.5 %collective-permute-start.11 = (bf16[512,768]{1,0:T(8,128)(2,1)}, bf16[512,768]{1,0:T(8,128)(2,1)S(1)}, u32[]{:S(2)}, u32[]{:S(2)}) collective-permute-start(bf16[512,768]{1,0:T(8,128)(2,1)} %get-tuple-element.156), channel_id=1, source_target_pairs={{0,2},{1,3},{2,0},{3,1},{4,6},{5,7},{6,4},{7,5},{8,10},{9,11},{10,... | collective-permute-start | bytes 2359304 | tf_op jit(solution)/shard_map/ppermute | solution.py:963
  350.4 18.0 %collective-permute-start.12 = (bf16[1024,768]{1,0:T(8,128)(2,1)}, bf16[1024,768]{1,0:T(8,128)(2,1)}, u32[]{:S(2)}, u32[]{:S(2)}) collective-permute-start(bf16[1024,768]{1,0:T(8,128)(2,1)} %get-tuple-element.141), channel_id=1, source_target_pairs={{0,1},{1,0},{2,3},{3,2},{4,5},{5,4},{6,7},{7,6},{8,9},{9,8},{10,11... | collective-permute-start | bytes 4718600 | tf_op jit(solution)/shard_map/ppermute | solution.py:960
  350.5 16.5 %collective-permute-start.13 = (bf16[96,3072]{1,0:T(8,128)(2,1)}, bf16[96,3072]{1,0:T(8,128)(2,1)}, u32[]{:S(2)}, u32[]{:S(2)}) collective-permute-start(bf16[96,3072]{1,0:T(8,128)(2,1)} %reduce-scatter.2.cloned.1.call-done), channel_id=1, source_target_pairs={{0,2},{1,3},{2,0},{3,1},{4,6},{5,7},{6,4},{7,5},{8,10},{9,11},{10,... | collective-permute-start | bytes 1769480 | tf_op jit(solution)/shard_map/ppermute | solution.py:963
  354.0 22.4 %all-to-all-start.1 = ((bf16[8,112,384]{2,1,0:T(8,128)(2,1)}), bf16[8,112,384]{2,1,0:T(8,128)(2,1)S(1)}, u32[]{:S(2)}, u32[]{:S(2)}) async-start(bf16[8,112,384]{2,1,0:T(8,128)(2,1)} %fusion.4), calls=%async_computation.2 | async-start | bytes 1376256 | tf_op jit(solution)/shard_map/all_to_all | solution.py:923
  358.2 20.9 %collective-permute-start.15 = (bf16[96,1152]{1,0:T(8,128)(2,1)S(1)}, bf16[96,1152]{1,0:T(8,128)(2,1)S(1)}, u32[]{:S(2)}, u32[]{:S(2)}) collective-permute-start(bf16[96,1152]{1,0:T(8,128)(2,1)S(1)} %reduce_sum.74), channel_id=1, source_target_pairs={{0,2},{1,3},{2,0},{3,1},{4,6},{5,7},{6,4},{7,5},{8,10},{9,11},{10,... | collective-permute-start | bytes 663560 | tf_op jit(solution)/shard_map/ppermute | solution.py:963
  377.1 5.7 %collective-permute-start.17 = (bf16[112,384]{1,0:T(8,128)(2,1)}, bf16[112,384]{1,0:T(8,128)(2,1)S(1)}, u32[]{:S(2)}, u32[]{:S(2)}) collective-permute-start(bf16[112,384]{1,0:T(8,128)(2,1)} %reduce_sum.75), channel_id=1, source_target_pairs={{0,2},{1,3},{2,0},{3,1},{4,6},{5,7},{6,4},{7,5},{8,10},{9,11},{10,... | collective-permute-start | bytes 258056 | tf_op jit(solution)/shard_map/ppermute | solution.py:963
  377.7 19.8 %collective-permute-start.14 = (bf16[512,768]{1,0:T(8,128)(2,1)}, bf16[512,768]{1,0:T(8,128)(2,1)S(1)}, u32[]{:S(2)}, u32[]{:S(2)}) collective-permute-start(bf16[512,768]{1,0:T(8,128)(2,1)} %get-tuple-element.146), channel_id=1, source_target_pairs={{0,2},{1,3},{2,0},{3,1},{4,6},{5,7},{6,4},{7,5},{8,10},{9,11},{10,... | collective-permute-start | bytes 2359304 | tf_op jit(solution)/shard_map/ppermute | solution.py:963
  379.2 7.4 %collective-permute-start.16 = (bf16[96,1152]{1,0:T(8,128)(2,1)S(1)}, bf16[96,1152]{1,0:T(8,128)(2,1)S(1)}, u32[]{:S(2)}, u32[]{:S(2)}) collective-permute-start(bf16[96,1152]{1,0:T(8,128)(2,1)S(1)} %add_convert_fusion.2.em_ref), channel_id=1, source_target_pairs={{0,1},{1,0},{2,3},{3,2},{4,5},{5,4},{6,7},{7,6},{8,9},{9,8},{10,11... | collective-permute-start | bytes 663560 | tf_op jit(solution)/shard_map/ppermute | solution.py:960
  379.3 13.7 %collective-permute-start.19 = (bf16[96,3072]{1,0:T(8,128)(2,1)S(1)}, bf16[96,3072]{1,0:T(8,128)(2,1)S(1)}, u32[]{:S(2)}, u32[]{:S(2)}) collective-permute-start(bf16[96,3072]{1,0:T(8,128)(2,1)S(1)} %add_convert_fusion.1.mine_ref), channel_id=1, source_target_pairs={{0,1},{1,0},{2,3},{3,2},{4,5},{5,4},{6,7},{7,6},{8,9},{9,8},{10,11... | collective-permute-start | bytes 1769480 | tf_op jit(solution)/shard_map/ppermute | solution.py:960
  383.7 2.9 collective-permute-start.18
  (22 other events, 205.4 us)
Sparse Core Ops, SparseCore 0:
  11.5 43.8 all-gather.5
  58.1 85.8 all-gather.3
  203.3 97.4 reduce-scatter.1

commit v8 on v7

--- a/solution.py
+++ b/solution.py
@@ -121,10 +121,12 @@
         top = jnp.max(s.reshape(chunk // 8, 8, bq), axis=0)
         return top if peak is None else jnp.maximum(peak, top)
 
-    def weigh_chunk(which, at, peak, total):
+    def raise_chunk(which, at, peak):
         rows = slice(at * chunk, (at + 1) * chunk)
-        p = jnp.exp(scores[which][rows, :] - peak).astype(BF)
-        o = dot(vaug[which, :, rows], p)
+        return jnp.exp(scores[which][rows, :] - peak).astype(BF)
+
+    def weigh_chunk(which, at, p, total):
+        o = dot(vaug[which, :, at * chunk : (at + 1) * chunk], p)
         return o if total is None else total + o
 
     @pl.when(step == 0)
@@ -141,10 +143,13 @@
         other = 1 - which
         query = query_block(step if which == 0 else later, other)
         peak = jnp.max(peaks[which][...], axis=0, keepdims=True)
-        next_peak, total = None, None
+        next_peak, total, behind = None, None, None
         for at in range(keys // chunk):
             next_peak = score_chunk(query, other, at, next_peak)
-            total = weigh_chunk(which, at, peak, total)
+            if behind is not None:
+                total = weigh_chunk(which, at - 1, behind, total)
+            behind = raise_chunk(which, at, peak)
+        total = weigh_chunk(which, keys // chunk - 1, behind, total)
         peaks[other][...] = next_peak
         norm = total[HEAD_DIM : HEAD_DIM + 1, :]
         outs.append(total[:HEAD_DIM, :] * (1.0 / norm))
@@ -237,18 +242,22 @@
         return dot(kaug[which, rows, :], queries[which]), dot(vaug[which, rows, :], grads[which])
 
     ahead = front(*units[0])
-    for unit, (at, which) in enumerate(units):
-        rows = slice(at * chunk, (at + 1) * chunk)
-        scores, dp = ahead
+    behind = None
+    for unit in range(len(units) + 1):
+        now = ahead
         if unit + 1 < len(units):
             ahead = front(*units[unit + 1])
-        p = jnp.exp(scores)
-        p_low = p.astype(BF)
-        ds = (p * dp).astype(BF)
-        acc_v[which, rows, :] += dot(p_low, do_pair)
-        acc_k[which, rows, :] += dot(ds, q_pair)
-        part = dot(kt_ref[which * HEAD_DIM : (which + 1) * HEAD_DIM, rows], ds)
-        totals[which] = part if totals[which] is None else totals[which] + part
+        if behind is not None:
+            at, which = units[unit - 1]
+            rows = slice(at * chunk, (at + 1) * chunk)
+            p_low, ds = behind
+            acc_v[which, rows, :] += dot(p_low, do_pair)
+            acc_k[which, rows, :] += dot(ds, q_pair)
+            part = dot(kt_ref[which * HEAD_DIM : (which + 1) * HEAD_DIM, rows], ds)
+            totals[which] = part if totals[which] is None else totals[which] + part
+        if unit < len(units):
+            p = jnp.exp(now[0])
+            behind = p.astype(BF), (p * now[1]).astype(BF)
     both = jnp.concatenate(totals, axis=0) * scale
     gq_ref[...] = both.T.astype(BF)
 
@@ -371,24 +380,31 @@
         hidden = dot(normed, w1) + f1b_ref[0:1, at * chunk : (at + 1) * chunk]
         return hidden, dot(cot, w2, 1, 1)
 
-    ahead = front(0)
-    for at in range(half // chunk):
-        cols = slice(at * chunk, (at + 1) * chunk)
-        hidden, grad_active = ahead
-        if at + 1 < half // chunk:
-            ahead = front(at + 1)
-        w1, w2 = weights(at)
+    def middle_part(hidden, grad_active):
         below = 0.5 + 0.5 * lax.erf(hidden * (0.5**0.5))
         slope = below + hidden * (jnp.exp(hidden * hidden * -0.5) * 0.3989422804014327)
-        active = (hidden * below).astype(BF)
-        grad_hidden = (grad_active * slope).astype(BF)
-        more = dot(active, w2)
-        out = more if out is None else out + more
-        more = dot(grad_hidden, w1, 1, 1)
-        grad = more if grad is None else grad + more
-        acc1[:, cols] += dot(normed_t, grad_hidden)
-        acc2[cols, :] += dot(active, cot, 0, 0)
-        accb[:, cols] += fold(grad_hidden.astype(F32))
+        return (hidden * below).astype(BF), (grad_active * slope).astype(BF)
+
+    chunks = half // chunk
+    ahead = front(0)
+    behind = None
+    for at in range(chunks + 1):
+        now = ahead
+        if at + 1 < chunks:
+            ahead = front(at + 1)
+        if behind is not None:
+            active, grad_hidden = behind
+            cols = slice((at - 1) * chunk, at * chunk)
+            w1, w2 = weights(at - 1)
+            more = dot(active, w2)
+            out = more if out is None else out + more
+            more = dot(grad_hidden, w1, 1, 1)
+            grad = more if grad is None else grad + more
+            acc1[:, cols] += dot(normed_t, grad_hidden)
+            acc2[cols, :] += dot(active, cot, 0, 0)
+            accb[:, cols] += fold(grad_hidden.astype(F32))
+        if at < chunks:
+            behind = middle_part(*now)
     accc[...] += fold(cot.astype(F32))
     gn_ref[...] = grad.astype(BF)
 
@@ -778,15 +794,17 @@
     )(place, mine, other)
 
 
-def finish_attend_kernel(place_ref, em_ref, eo_ref, lm_ref, lo_ref, qkv_ref, proj_ref, small_ref):
+def finish_attend_kernel(
+    place_ref, em_ref, eo_ref, la_ref, lb_ref, lc_ref, ld_ref, qkv_ref, proj_ref, small_ref
+):
     first_core = lax.rem(place_ref[0], 2) == 0
     shard, width = proj_ref.shape
     part = width // 2
-    late = lm_ref.shape[1] // 3
+    late = la_ref.shape[1] // 3
     early = part - late
-    rows = lm_ref.shape[0] - shard
-    lm = lm_ref[...].astype(F32)
-    lo = lo_ref[...].astype(F32)
+    rows = la_ref.shape[0] - shard
+    lm = la_ref[...].astype(F32) + lb_ref[...].astype(F32)
+    lo = lc_ref[...].astype(F32) + ld_ref[...].astype(F32)
     small_ref[...] = lm[:rows] + lo[:rows]
     em = em_ref[...].astype(F32)
     eo = eo_ref[...].astype(F32)
@@ -801,14 +819,15 @@
         proj_ref[:, of * part : (of + 1) * part] = firsts[of][:, 3 * early :]
 
 
-def finish_attend(place, early_mine, early_other, late_mine, late_other, width):
+def finish_attend(place, early_mine, early_other, late_mine, late_b, late_c, late_d, width):
     shard = early_mine.shape[0]
     rows = late_mine.shape[0] - shard
     return pl.pallas_call(
         finish_attend_kernel,
         grid=(1,),
         in_specs=[pl.BlockSpec(memory_space=pltpu.SMEM)]
-        + [whole(value.shape) for value in (early_mine, early_other, late_mine, late_other)],
+        + [whole(value.shape) for value in (early_mine, early_other)]
+        + [whole(late_mine.shape)] * 4,
         out_specs=[
             whole((shard, 3 * width)), whole((shard, width)), whole((rows, late_mine.shape[1]))
         ],
@@ -820,7 +839,7 @@
         compiler_params=params(60, "arbitrary"),
         cost_estimate=cost(0, 24 * shard * width),
         name="finish_attend",
-    )(place, early_mine, early_other, late_mine, late_other)
+    )(place, early_mine, early_other, late_mine, late_b, late_c, late_d)
 
 
 def pack_kernel(place_ref, *refs):
@@ -1057,13 +1076,9 @@
     def join(value, came):
         return (value.astype(F32) + came.astype(F32)).astype(BF)
 
-    scattered_one, came_one, out_came, grads = lax.optimization_barrier(
-        (scattered_one, came_one, out_came, grads)
-    )
+    scattered_one, out_came, grads = lax.optimization_barrier((scattered_one, out_came, grads))
     output = hand_back(out_own, out_came)
     one_came = partner(scattered_one)
-    early_total = total(came_one)
-    early_came = partner(early_total)
     one_sum = join(scattered_one, one_came)
     gn1_own, gn1_send, dw_late, vec_first, qv_late = project_back(tok, normed, before, grads, w_qkv)
 
@@ -1098,21 +1113,29 @@
         [small_block, dw_late.reshape(owners, shard, late_wide)], axis=1
     )
     gn1_sib = sibling(gn1_send)
+    block_two, came_one = lax.optimization_barrier((block_two, came_one))
+    early_total = total(came_one)
+    early_came = partner(early_total)
     came_two = exchange(block_two)
     input_own, input_send = input_back(tok, gn1_own, gn1_sib, grad_middle, vec_one)
     input_came = partner(input_send)
-    came_two, input_own, one_sum = lax.optimization_barrier((came_two, input_own, one_sum))
+    came_two, input_own, one_sum, output = lax.optimization_barrier(
+        (came_two, input_own, one_sum, output)
+    )
     one_other = sibling(one_sum)
+    grad_fc1, grad_fc2 = finish_ff(place_row, one_sum, one_other, width, quarter)
     input_grad = hand_back(input_own, input_came)
 
-    grad_fc1, grad_fc2 = finish_ff(place_row, one_sum, one_other, width, quarter)
     early_sum = join(early_total, early_came)
     early_other = sibling(early_sum)
     late_total = total(came_two)
-    late_sum = join(late_total, partner(late_total))
-    late_other = sibling(late_sum)
+    late_came = [
+        lax.ppermute(late_total, "seq", [(at, at ^ flip) for at in range(seq)])
+        for flip in (2, 1, 3)
+    ]
+    late_came, grad_fc1, grad_fc2 = lax.optimization_barrier((late_came, grad_fc1, grad_fc2))
     grad_qkv, grad_proj, small_sum = finish_attend(
-        place_row, early_sum, early_other, late_sum, late_other, width
+        place_row, early_sum, early_other, late_total, *late_came, width
     )
     s = [small_sum[at, :shard] for at in range(8)]
     grad_f1b = small_sum[8, :ff_shard]

time: 413 us -> 402 us (0.973)
  waiting for transfers between devices: 97 us -> 90 us
    all_to_all x2, waiting for transfers between devices: 21.7 us -> 4.62 us  [exchange(): lax.all_to_all(value, 'fsdp', split_axis=0, concat_axis=0, tiled=True)]
    ppermute x0 -> x3, waiting for transfers between devices: none -> 15.8 us  [per_device(): lax.ppermute(late_total, 'seq', [(at, at ^ flip) for at in range(seq)])]
    ppermute x8 -> x7, waiting for transfers between devices: 58.1 us -> 49.2 us  [partner(): return lax.ppermute(value, 'seq', to_partner)]
    ppermute x8 -> x7, starting transfers between devices: 10.7 us -> 10.2 us  [partner(): return lax.ppermute(value, 'seq', to_partner)]
  transfers between devices with their start and end apart: 25 -> 26, of which waited for: 12 -> 12; matrix products, arithmetic and copies ran while one was open for 8% -> 9% of each run, Pallas kernels for 39% -> 42%
where the time goes in v8:
time: 402 us; the launch traced here: 396 us
  Pallas kernels  225 us (56%)
  waiting for transfers between devices  90 us (22%)
  other arithmetic  24.8 us (6%)
  starting transfers between devices  23.1 us (6%)
  local copies, waits for them, and re-layouts  18.2 us (5%)
  between operations  14.7 us (4%)
    pallas_call x2, Pallas kernels, attend_backward(): pl.pallas_call(kernel, grid=(count, keys // bq), in_specs=[pl.BlockSpec(m...  69.4 us
    pallas_call x1, Pallas kernels, feed_forward(): pl.pallas_call(kernel, grid=(blocks,), in_specs=[pl.BlockSpec(memory_spac...  54.6 us
    ppermute x7, waiting for transfers between devices, partner(): return lax.ppermute(value, 'seq', to_partner)  49.2 us
    pallas_call x1, Pallas kernels, attend_forward(): pl.pallas_call(kernel, grid=(pairs, keys // bq), in_specs=[pl.BlockSpec(m...  38.8 us
    pallas_call x1, Pallas kernels, branch(): pl.pallas_call(branch_kernel, grid=(blocks,), in_specs=[pl.BlockSpec(memo...  16.1 us
    ppermute x3, waiting for transfers between devices, per_device(): lax.ppermute(late_total, 'seq', [(at, at ^ flip) for at in range(seq)])  15.8 us
    pallas_call x1, Pallas kernels, project_back(): pl.pallas_call(project_back_kernel, grid=(blocks,), in_specs=[pl.BlockSpe...  14.2 us
    ppermute x7, starting transfers between devices, partner(): return lax.ppermute(value, 'seq', to_partner)  10.2 us
  transfers between devices with their start and end apart: 26, of which 12 were waited for; matrix products, arithmetic and copies ran while one was open for 9% of the time, Pallas kernels for 42%

profile of v8, /device:TPU:0, one launch (start us, length us, event | category | flops | bytes accessed | tf_op | source)
XLA Modules:
  0.0 395.6 jit_solution(10527369738785541661)
XLA Ops:
  12.4 2.9 collective-permute-start
  16.1 17.7 %collective-permute-done = bf16[512,768]{1,0:T(8,128)(2,1)} collective-permute-done((bf16[512,768]{1,0:T(8,128)(2,1)S(1)}, bf16[512,768]{1,0:T(8,128)(2,1)}, u32[]{:S(2)}, u32[]{:S(2)}) %collective-permute-start) | collective-permute-done | bytes 786464 | tf_op jit(solution)/shard_map/ppermute | solution.py:982
  33.8 16.0 %collective-permute-done.1 = bf16[512,768]{1,0:T(8,128)(2,1)} collective-permute-done((bf16[512,768]{1,0:T(8,128)(2,1)S(1)}, bf16[512,768]{1,0:T(8,128)(2,1)}, u32[]{:S(2)}, u32[]{:S(2)}) %collective-permute-start.1) | collective-permute-done | bytes 786464 | tf_op jit(solution)/shard_map/ppermute | solution.py:982
  49.9 5.5 %all-gather.6.cloned.1.call-done = bf16[512,1152]{1,0:T(8,128)(2,1)} async-done(((bf16[64,1152]{1,0:T(8,128)(2,1)}), bf16[512,1152]{1,0:T(8,128)(2,1)}) %all-gather.6.cloned.1.call-update) | async-done | bytes 1179664 | tf_op jit(solution)/shard_map/all_gather | solution.py:997
  62.8 3.4 pad_maximum_fusion.tok_ref
  66.2 3.1 pad_maximum_fusion.1.cot_ref
  69.2 12.6 %collective-permute-done.4 = bf16[8,48,1152]{2,1,0:T(8,128)(2,1)} collective-permute-done((bf16[8,48,1152]{2,1,0:T(8,128)(2,1)}, bf16[8,48,1152]{2,1,0:T(8,128)(2,1)}, u32[]{:S(2)}, u32[]{:S(2)}) %collective-permute-start.4) | collective-permute-done | bytes 884768 | tf_op jit(solution)/shard_map/ppermute | solution.py:982
  81.8 3.1 maximum_select_fusion.1
  84.9 10.1 %project.1 = (bf16[2048,1152]{1,0:T(8,128)(2,1)}, bf16[1152,2048]{1,0:T(8,128)(2,1)}, bf16[2048,768]{1,0:T(8,128)(2,1)}) custom-call(bf16[2048,768]{1,0:T(8,128)(2,1)} %pad_maximum_fusion.tok_ref, bf16[768,1152]{1,0:T(8,128)(2,1)} %bitcast.70, f32[1,1152]{1,0:T(1,128)} %reshape.145.bias_ref, f32[8,768]{1,0:T(8,128)} %maximum_maximum_fusion.vec_ref), custom_call_target="tpu_custom_call" | custom-call | flops 3623878656 | bytes 18874368 | tf_op jit(solution)/shard_map/project/pallas_call | solution.py:916
  94.9 38.8 %attend_forward.1 = (bf16[2048,384]{1,0:T(8,128)(2,1)}, f32[384,2048]{1,0:T(8,128)}, f32[3,8,2048]{2,1,0:T(8,128)}) custom-call(s32[2,4]{1,0:T(2,128)} %counts_ref.5, s32[1]{0:T(128)} %bitcast.place_ref, bf16[2048,1152]{1,0:T(8,128)(2,1)} %get-tuple-element.102.k_ref.q_ref.v_ref, bf16[1152,2048]{1,0:T(8,128)(2,1)} %get-tuple-element.103.qt_ref.vt_ref.kt_ref, ...), custom_call_target="tpu_custom_call" | custom-call | flops 25769803776 | bytes 9437184 | tf_op jit(solution)/shard_map/attend_forward/pallas_call | solution.py:168
  133.7 10.2 %all-gather.4.cloned.1.call-done.g2_ref = bf16[768,3456]{1,0:T(8,128)(2,1)} async-done(((bf16[96,3456]{1,0:T(8,128)(2,1)}), bf16[768,3456]{1,0:T(8,128)(2,1)}) %all-gather.4.cloned.1.call-update) | async-done | bytes 5308432 | tf_op jit(solution)/shard_map/all_gather | solution.py:1009
  148.1 54.6 %feed_forward.1 = (f32[2048,768]{1,0:T(8,128)}, f32[1024,768]{1,0:T(8,128)}, bf16[1024,768]{1,0:T(8,128)(2,1)}, bf16[2048,768]{1,0:T(8,128)(2,1)}, bf16[768,3072...) custom-call(s32[1]{0:T(128)} %bitcast.18.core_ref, ...), custom_call_target="tpu_custom_call" | custom-call | flops 31406948352 | bytes 40894464 | tf_op jit(solution)/shard_map/feed_forward/pallas_call | solution.py:437
  204.4 4.4 %collective-permute-done.9.gb_ref = bf16[2048,768]{1,0:T(8,128)(2,1)S(1)} collective-permute-done((bf16[2048,768]{1,0:T(8,128)(2,1)}, bf16[2048,768]{1,0:T(8,128)(2,1)S(1)}, u32[]{:S(2)}, u32[]{:S(2)}) %collective-permute-start.9) | collective-permute-done | bytes 3145760 | tf_op jit(solution)/shard_map/ppermute | solution.py:979
  210.4 16.1 %branch.1 = (f32[1024,768]{1,0:T(8,128)}, bf16[2048,384]{1,0:T(8,128)(2,1)}, bf16[384,2048]{1,0:T(8,128)(2,1)}, bf16[384,384]{1,0:T(8,128)(2,1)}, bf16[384,384]{1,0:T(8,128)(2,1)}, /*index=5*/f32[24,768]{1,0:T(8,128)}) custom-call(s32[1]{0:T(128)} %bitcast.18.core_ref, f32[2048,768]{1,0:T(8,128)} %get-tuple-element.107.mid_ref, ...), custom_call_target="tpu_custom_call" | custom-call | flops 3623878656 | bytes 28311552 | tf_op jit(solution)/shard_map/branch/pallas_call | solution.py:534
  227.0 45.4 %attend_backward.2 = (bf16[2048,256]{1,0:T(8,128)(2,1)}, bf16[2048,256]{1,0:T(8,128)(2,1)}, bf16[2048,256]{1,0:T(8,128)(2,1)}) custom-call(s32[2,4]{1,0:T(2,128)} %counts_ref.5, s32[1]{0:T(128)} %bitcast.place_ref, bf16[2048,1152]{1,0:T(8,128)(2,1)} %get-tuple-element.102.k_ref.q_ref.v_ref, bf16[2048,1152]{1,0:T(8,128)(2,1)} %get-tuple-element.102.k_ref.q_ref.v_ref, ...), custom_call_target="tpu_custom_call" | custom-call | flops 42949672960 | bytes 12582912 | tf_op jit(solution)/shard_map/attend_backward/pallas_call | solution.py:280
  272.9 6.6 %weight_grad.1 = (bf16[768,768]{1,0:T(8,128)(2,1)}, f32[16,256]{1,0:T(8,128)}) custom-call(bf16[2048,768]{1,0:T(8,128)(2,1)} %get-tuple-element.99.normed_ref, bf16[2048,256]{1,0:T(8,128)(2,1)} %get-tuple-element.121.gq_ref.gqa_ref, bf16[2048,256]{1,0:T(8,128)(2,1)} %get-tuple-element.122.gk_ref.gka_ref, bf16[2048,256]{1,0:T(8,128)(2,1)} %get-tuple-element.123.gv_ref.gva_ref), custom_call_target="tpu_custom_call" | custom-call | flops 2415919104 | bytes 6291456 | tf_op jit(solution)/shard_map/weight_grad/pallas_call | solution.py:606
  282.7 3.9 all-to-all-start
  289.3 24.0 %attend_backward.3 = (bf16[2048,128]{1,0:T(8,128)(2,1)}, bf16[2048,128]{1,0:T(8,128)(2,1)}, bf16[2048,128]{1,0:T(8,128)(2,1)}) custom-call(s32[2,4]{1,0:T(2,128)} %counts_ref.5, s32[1]{0:T(128)} %bitcast.place_ref, bf16[2048,1152]{1,0:T(8,128)(2,1)} %get-tuple-element.102.k_ref.q_ref.v_ref, bf16[2048,1152]{1,0:T(8,128)(2,1)} %get-tuple-element.102.k_ref.q_ref.v_ref, ...), custom_call_target="tpu_custom_call" | custom-call | flops 21474836480 | bytes 6291456 | tf_op jit(solution)/shard_map/attend_backward/pallas_call | solution.py:280
  313.4 14.2 %project_back.1 = (f32[1024,768]{1,0:T(8,128)}, bf16[1024,768]{1,0:T(8,128)(2,1)}, bf16[768,384]{1,0:T(8,128)(2,1)}, f32[16,768]{1,0:T(8,128)}, f32[16,128]{1,0:T(8,128)}) custom-call(bf16[2048,768]{1,0:T(8,128)(2,1)} %pad_maximum_fusion.tok_ref, bf16[2048,768]{1,0:T(8,128)(2,1)} %get-tuple-element.99.normed_ref, ...), custom_call_target="tpu_custom_call" | custom-call | flops 4831838208 | bytes 22020096 | tf_op jit(solution)/shard_map/project_back/pallas_call | solution.py:683
  334.4 4.2 %all-to-all-start.1 = ((bf16[8,112,384]{2,1,0:T(8,128)(2,1)}), bf16[8,112,384]{2,1,0:T(8,128)(2,1)S(1)}, u32[]{:S(2)}, u32[]{:S(2)}) async-start(bf16[8,112,384]{2,1,0:T(8,128)(2,1)} %fusion.4), calls=%async_computation.2 | async-start | bytes 1376256 | tf_op jit(solution)/shard_map/all_to_all | solution.py:942
  340.5 2.8 maximum_select_fusion.2
  347.6 6.9 %input_back.1 = (f32[512,768]{1,0:T(8,128)}, bf16[512,768]{1,0:T(8,128)(2,1)}) custom-call(bf16[2048,768]{1,0:T(8,128)(2,1)} %pad_maximum_fusion.tok_ref, f32[1024,768]{1,0:T(8,128)} %get-tuple-element.147.own_ref, bf16[1024,768]{1,0:T(8,128)(2,1)} %collective-permute-done.12.sib_ref, f32[1024,768]{1,0:T(8,128)} %get-tuple-element.149.gm_ref, ...), custom_call_target="tpu_custom_call" | custom-call | flops 15728640 | bytes 12582912 | tf_op jit(solution)/shard_map/input_back/pallas_call | solution.py:736
  362.1 3.0 finish_ff.1
  365.1 13.5 %collective-permute-done.19.ld_ref = bf16[112,384]{1,0:T(8,128)(2,1)S(1)} collective-permute-done((bf16[112,384]{1,0:T(8,128)(2,1)S(1)}, bf16[112,384]{1,0:T(8,128)(2,1)S(1)}, u32[]{:S(2)}, u32[]{:S(2)}) %collective-permute-start.19) | collective-permute-done | bytes 86048 | tf_op jit(solution)/shard_map/ppermute | solution.py:1133
  (166 shorter events, 57.8 us)
Async XLA Ops:
  7.2 48.1 %all-gather.6.cloned.1.call-start = ((), (), s32[]{:S(2)}) async-start(), calls=%async_computation.5 | async-start | bytes 1327104 | tf_op jit(solution)/shard_map/all_gather | solution.py:997
  11.3 132.6 %all-gather.4.cloned.1.call-start = ((), (), s32[]{:S(2)}) async-start(), calls=%async_computation.3 | async-start | bytes 5971968 | tf_op jit(solution)/shard_map/all_gather | solution.py:1009
  12.4 21.4 %collective-permute-start = (bf16[512,768]{1,0:T(8,128)(2,1)S(1)}, bf16[512,768]{1,0:T(8,128)(2,1)}, u32[]{:S(2)}, u32[]{:S(2)}) collective-permute-start(bf16[512,768]{1,0:T(8,128)(2,1)S(1)} %get-tuple-element.174), channel_id=1, source_target_pairs={{0,2},{1,3},{2,0},{3,1},{4,6},{5,7},{6,4},{7,5},{8,10},{9,11},{10,... | collective-permute-start | bytes 2359304 | tf_op jit(solution)/shard_map/ppermute | solution.py:982
  15.5 34.4 %collective-permute-start.1 = (bf16[512,768]{1,0:T(8,128)(2,1)S(1)}, bf16[512,768]{1,0:T(8,128)(2,1)}, u32[]{:S(2)}, u32[]{:S(2)}) collective-permute-start(bf16[512,768]{1,0:T(8,128)(2,1)S(1)} %get-tuple-element.172), channel_id=1, source_target_pairs={{0,2},{1,3},{2,0},{3,1},{4,6},{5,7},{6,4},{7,5},{8,10},{9,11},{10,... | collective-permute-start | bytes 2359304 | tf_op jit(solution)/shard_map/ppermute | solution.py:982
  55.3 258.1 %reduce-scatter.2.cloned.1.call-start = ((), (), s32[]{:S(2)}) async-start(), calls=%async_computation.4 | async-start | bytes 5308416 | tf_op jit(solution)/shard_map/reduce_scatter | solution.py:1040
  55.4 7.4 %collective-permute-start.2 = (bf16[512,768]{1,0:T(8,128)(2,1)}, bf16[512,768]{1,0:T(8,128)(2,1)}, u32[]{:S(2)}, u32[]{:S(2)}) collective-permute-start(bf16[512,768]{1,0:T(8,128)(2,1)} %get-tuple-element.173), channel_id=1, source_target_pairs={{0,1},{1,0},{2,3},{3,2},{4,5},{5,4},{6,7},{7,6},{8,9},{9,8},{10,11... | collective-permute-start | bytes 2359304 | tf_op jit(solution)/shard_map/ppermute | solution.py:979
  55.5 10.7 %collective-permute-start.5 = (bf16[512,768]{1,0:T(8,128)(2,1)S(1)}, bf16[512,768]{1,0:T(8,128)(2,1)}, u32[]{:S(2)}, u32[]{:S(2)}) collective-permute-start(bf16[512,768]{1,0:T(8,128)(2,1)S(1)} %get-tuple-element.171), channel_id=1, source_target_pairs={{0,1},{1,0},{2,3},{3,2},{4,5},{5,4},{6,7},{7,6},{8,9},{9,8},{10,11... | collective-permute-start | bytes 2359304 | tf_op jit(solution)/shard_map/ppermute | solution.py:979
  56.0 6.7 %collective-permute-start.3 = (bf16[512,768]{1,0:T(8,128)(2,1)}, bf16[512,768]{1,0:T(8,128)(2,1)}, u32[]{:S(2)}, u32[]{:S(2)}) collective-permute-start(bf16[512,768]{1,0:T(8,128)(2,1)} %collective-permute-done), channel_id=1, source_target_pairs={{0,1},{1,0},{2,3},{3,2},{4,5},{5,4},{6,7},{7,6},{8,9},{9,8},{10,11... | collective-permute-start | bytes 2359304 | tf_op jit(solution)/shard_map/ppermute | solution.py:979
  56.1 10.0 %collective-permute-start.6 = (bf16[512,768]{1,0:T(8,128)(2,1)}, bf16[512,768]{1,0:T(8,128)(2,1)}, u32[]{:S(2)}, u32[]{:S(2)}) collective-permute-start(bf16[512,768]{1,0:T(8,128)(2,1)} %collective-permute-done.1), channel_id=1, source_target_pairs={{0,1},{1,0},{2,3},{3,2},{4,5},{5,4},{6,7},{7,6},{8,9},{9,8},{10,11... | collective-permute-start | bytes 2359304 | tf_op jit(solution)/shard_map/ppermute | solution.py:979
  59.8 21.9 %collective-permute-start.4 = (bf16[8,48,1152]{2,1,0:T(8,128)(2,1)}, bf16[8,48,1152]{2,1,0:T(8,128)(2,1)}, u32[]{:S(2)}, u32[]{:S(2)}) collective-permute-start(bf16[8,48,1152]{2,1,0:T(8,128)(2,1)} %get-tuple-element.176), channel_id=1, source_target_pairs={{0,2},{1,3},{2,0},{3,1},{4,6},{5,7},{6,4},{7,5},{8,10},{9,11},{10,... | collective-permute-start | bytes 2654216 | tf_op jit(solution)/shard_map/ppermute | solution.py:982
  133.7 13.2 %collective-permute-start.7 = (bf16[2048,384]{1,0:T(8,128)(2,1)}, bf16[2048,384]{1,0:T(8,128)(2,1)S(1)}, u32[]{:S(2)}, u32[]{:S(2)}) collective-permute-start(bf16[2048,384]{1,0:T(8,128)(2,1)} %get-tuple-element.104.mo_ref), channel_id=1, source_target_pairs={{0,1},{1,0},{2,3},{3,2},{4,5},{5,4},{6,7},{7,6},{8,9},{9,8},{10,11... | collective-permute-start | bytes 4718600 | tf_op jit(solution)/shard_map/ppermute | solution.py:979
  202.7 6.0 %collective-permute-start.9 = (bf16[2048,768]{1,0:T(8,128)(2,1)}, bf16[2048,768]{1,0:T(8,128)(2,1)S(1)}, u32[]{:S(2)}, u32[]{:S(2)}) collective-permute-start(bf16[2048,768]{1,0:T(8,128)(2,1)} %get-tuple-element.108.ga_ref), channel_id=1, source_target_pairs={{0,1},{1,0},{2,3},{3,2},{4,5},{5,4},{6,7},{7,6},{8,9},{9,8},{10,11... | collective-permute-start | bytes 9437192 | tf_op jit(solution)/shard_map/ppermute | solution.py:979
  226.5 46.3 %collective-permute-start.10 = (bf16[1024,768]{1,0:T(8,128)(2,1)}, bf16[1024,768]{1,0:T(8,128)(2,1)S(1)}, u32[]{:S(2)}, u32[]{:S(2)}) collective-permute-start(bf16[1024,768]{1,0:T(8,128)(2,1)} %get-tuple-element.120), channel_id=1, source_target_pairs={{0,1},{1,0},{2,3},{3,2},{4,5},{5,4},{6,7},{7,6},{8,9},{9,8},{10,11... | collective-permute-start | bytes 4718600 | tf_op jit(solution)/shard_map/ppermute | solution.py:979
  282.7 51.7 %all-to-all-start = ((bf16[8,96,1152]{2,1,0:T(8,128)(2,1)}), bf16[8,96,1152]{2,1,0:T(8,128)(2,1)S(1)}, u32[]{:S(2)}, u32[]{:S(2)}) async-start(bf16[8,96,1152]{2,1,0:T(8,128)(2,1)} %bitcast.21), calls=%async_computation.1 | async-start | bytes 3538944 | tf_op jit(solution)/shard_map/all_to_all | solution.py:942
  287.8 25.5 %collective-permute-start.11 = (bf16[512,768]{1,0:T(8,128)(2,1)}, bf16[512,768]{1,0:T(8,128)(2,1)S(1)}, u32[]{:S(2)}, u32[]{:S(2)}) collective-permute-start(bf16[512,768]{1,0:T(8,128)(2,1)} %get-tuple-element.170), channel_id=1, source_target_pairs={{0,2},{1,3},{2,0},{3,1},{4,6},{5,7},{6,4},{7,5},{8,10},{9,11},{10,... | collective-permute-start | bytes 2359304 | tf_op jit(solution)/shard_map/ppermute | solution.py:982
  329.6 18.0 %collective-permute-start.12 = (bf16[1024,768]{1,0:T(8,128)(2,1)}, bf16[1024,768]{1,0:T(8,128)(2,1)}, u32[]{:S(2)}, u32[]{:S(2)}) collective-permute-start(bf16[1024,768]{1,0:T(8,128)(2,1)} %get-tuple-element.148), channel_id=1, source_target_pairs={{0,1},{1,0},{2,3},{3,2},{4,5},{5,4},{6,7},{7,6},{8,9},{9,8},{10,11... | collective-permute-start | bytes 4718600 | tf_op jit(solution)/shard_map/ppermute | solution.py:979
  329.7 16.5 %collective-permute-start.13 = (bf16[96,3072]{1,0:T(8,128)(2,1)}, bf16[96,3072]{1,0:T(8,128)(2,1)}, u32[]{:S(2)}, u32[]{:S(2)}) collective-permute-start(bf16[96,3072]{1,0:T(8,128)(2,1)} %reduce-scatter.2.cloned.1.call-done), channel_id=1, source_target_pairs={{0,2},{1,3},{2,0},{3,1},{4,6},{5,7},{6,4},{7,5},{8,10},{9,11},{10,... | collective-permute-start | bytes 1769480 | tf_op jit(solution)/shard_map/ppermute | solution.py:982
  334.4 22.6 %all-to-all-start.1 = ((bf16[8,112,384]{2,1,0:T(8,128)(2,1)}), bf16[8,112,384]{2,1,0:T(8,128)(2,1)S(1)}, u32[]{:S(2)}, u32[]{:S(2)}) async-start(bf16[8,112,384]{2,1,0:T(8,128)(2,1)} %fusion.4), calls=%async_computation.2 | async-start | bytes 1376256 | tf_op jit(solution)/shard_map/all_to_all | solution.py:942
  338.9 19.5 %collective-permute-start.15 = (bf16[96,1152]{1,0:T(8,128)(2,1)S(1)}, bf16[96,1152]{1,0:T(8,128)(2,1)}, u32[]{:S(2)}, u32[]{:S(2)}) collective-permute-start(bf16[96,1152]{1,0:T(8,128)(2,1)S(1)} %reduce_sum.74), channel_id=1, source_target_pairs={{0,2},{1,3},{2,0},{3,1},{4,6},{5,7},{6,4},{7,5},{8,10},{9,11},{10,... | collective-permute-start | bytes 663560 | tf_op jit(solution)/shard_map/ppermute | solution.py:982
  357.0 29.6 %collective-permute-start.14 = (bf16[512,768]{1,0:T(8,128)(2,1)}, bf16[512,768]{1,0:T(8,128)(2,1)S(1)}, u32[]{:S(2)}, u32[]{:S(2)}) collective-permute-start(bf16[512,768]{1,0:T(8,128)(2,1)} %get-tuple-element.155), channel_id=1, source_target_pairs={{0,2},{1,3},{2,0},{3,1},{4,6},{5,7},{6,4},{7,5},{8,10},{9,11},{10,... | collective-permute-start | bytes 2359304 | tf_op jit(solution)/shard_map/ppermute | solution.py:982
  359.5 21.4 %collective-permute-start.16 = (bf16[96,1152]{1,0:T(8,128)(2,1)S(1)}, bf16[96,1152]{1,0:T(8,128)(2,1)}, u32[]{:S(2)}, u32[]{:S(2)}) collective-permute-start(bf16[96,1152]{1,0:T(8,128)(2,1)S(1)} %add_convert_fusion.2.em_ref), channel_id=1, source_target_pairs={{0,1},{1,0},{2,3},{3,2},{4,5},{5,4},{6,7},{7,6},{8,9},{9,8},{10,11... | collective-permute-start | bytes 663560 | tf_op jit(solution)/shard_map/ppermute | solution.py:979
  359.9 18.7 %collective-permute-start.19 = (bf16[112,384]{1,0:T(8,128)(2,1)S(1)}, bf16[112,384]{1,0:T(8,128)(2,1)S(1)}, u32[]{:S(2)}, u32[]{:S(2)}) collective-permute-start(bf16[112,384]{1,0:T(8,128)(2,1)S(1)} %reduce_sum.75.la_ref), channel_id=1, source_target_pairs={{0,3},{1,2},{2,1},{3,0},{4,7},{5,6},{6,5},{7,4},{8,11},{9,10},{10,... | collective-permute-start | bytes 258056 | tf_op jit(solution)/shard_map/ppermute | solution.py:1133
  360.4 18.2 %collective-permute-start.18 = (bf16[112,384]{1,0:T(8,128)(2,1)S(1)}, bf16[112,384]{1,0:T(8,128)(2,1)S(1)}, u32[]{:S(2)}, u32[]{:S(2)}) collective-permute-start(bf16[112,384]{1,0:T(8,128)(2,1)S(1)} %reduce_sum.75.la_ref), channel_id=1, source_target_pairs={{0,1},{1,0},{2,3},{3,2},{4,5},{5,4},{6,7},{7,6},{8,9},{9,8},{10,11... | collective-permute-start | bytes 258056 | tf_op jit(solution)/shard_map/ppermute | solution.py:1133
  360.6 20.2 %collective-permute-start.17 = (bf16[112,384]{1,0:T(8,128)(2,1)S(1)}, bf16[112,384]{1,0:T(8,128)(2,1)S(1)}, u32[]{:S(2)}, u32[]{:S(2)}) collective-permute-start(bf16[112,384]{1,0:T(8,128)(2,1)S(1)} %reduce_sum.75.la_ref), channel_id=1, source_target_pairs={{0,2},{1,3},{2,0},{3,1},{4,6},{5,7},{6,4},{7,5},{8,10},{9,11},{10,... | collective-permute-start | bytes 258056 | tf_op jit(solution)/shard_map/ppermute | solution.py:1133
  (24 other events, 278.8 us)
Sparse Core Ops, SparseCore 0:
  11.5 43.8 all-gather.5
  58.1 85.8 all-gather.3
  203.4 96.9 reduce-scatter.1

commit v9 on v8

--- a/solution.py
+++ b/solution.py
@@ -334,13 +334,20 @@
 
 def feed_forward_kernel(
     chunk, core_ref, tok_ref, mo_ref, ms_ref, cot_ref, wpx_ref, g2_ref, vec_ref, f1b_ref,
-    mid_ref, out_ref, send_ref, gn_ref, dw_ref, gf1_ref, gf2_ref, wpo_ref, acc1, acc2, accb, accc, wps_ref
+    mid_ref, out_ref, send_ref, gn_ref, dw_ref, gf1_ref, gf2_ref, wpo_ref, acc1, acc2, accb, accc, wps_ref,
+    w1t_ref, w2t_ref
 ):
     step = pl.program_id(0)
     steps = pl.num_programs(0)
     width = tok_ref.shape[1]
     half = f1b_ref.shape[1]
     part = width // 2
+
+    def weights(at):
+        w1 = g2_ref[:, part + at * chunk : part + (at + 1) * chunk]
+        piece, row = divmod(at * chunk, width)
+        start = part + half + piece * width
+        return w1, g2_ref[row : row + chunk, start : start + width]
 
     @pl.when(step == 0)
     def _():
@@ -354,6 +361,11 @@
         wpo_ref[:, there] = wpx_ref[here, :]
         wps_ref[:, here] = g2_ref[there, :part]
         wps_ref[:, there] = wpx_ref[there, :]
+        for at in range(half // chunk):
+            cols = slice(at * chunk, (at + 1) * chunk)
+            w1, w2 = weights(at)
+            w1t_ref[cols, :] = w1.T
+            w2t_ref[:, cols] = w2.T
 
     middle = (
         tok_ref[...].astype(F32)
@@ -369,16 +381,10 @@
     out = None
     grad = None
 
-    def weights(at):
-        w1 = g2_ref[:, part + at * chunk : part + (at + 1) * chunk]
-        piece, row = divmod(at * chunk, width)
-        start = part + half + piece * width
-        return w1, g2_ref[row : row + chunk, start : start + width]
-
     def front(at):
-        w1, w2 = weights(at)
+        w1, _ = weights(at)
         hidden = dot(normed, w1) + f1b_ref[0:1, at * chunk : (at + 1) * chunk]
-        return hidden, dot(cot, w2, 1, 1)
+        return hidden, dot(cot, w2t_ref[:, at * chunk : (at + 1) * chunk])
 
     def middle_part(hidden, grad_active):
         below = 0.5 + 0.5 * lax.erf(hidden * (0.5**0.5))
@@ -395,10 +401,10 @@
         if behind is not None:
             active, grad_hidden = behind
             cols = slice((at - 1) * chunk, at * chunk)
-            w1, w2 = weights(at - 1)
+            _, w2 = weights(at - 1)
             more = dot(active, w2)
             out = more if out is None else out + more
-            more = dot(grad_hidden, w1, 1, 1)
+            more = dot(grad_hidden, w1t_ref[cols, :])
             grad = more if grad is None else grad + more
             acc1[:, cols] += dot(normed_t, grad_hidden)
             acc2[cols, :] += dot(active, cot, 0, 0)
@@ -474,6 +480,8 @@
             pltpu.VMEM((8, half), F32),
             pltpu.VMEM((8, width), F32),
             pltpu.VMEM((width // 2, width), BF),
+            pltpu.VMEM((half, width), BF),
+            pltpu.VMEM((width, half), BF),
         ],
         compiler_params=params(60, "arbitrary"),
         cost_estimate=cost(
@@ -486,7 +494,7 @@
 
 def branch_kernel(
     core_ref, mid_ref, ga_ref, gb_ref, cot_ref, mo_ref, ms_ref, wpo_ref, vec_ref,
-    gm_ref, do_ref, dot_ref, dwo_ref, dws_ref, vecs_ref, acco, accs, accv, low_ref
+    gm_ref, do_ref, dot_ref, dwo_ref, dws_ref, vecs_ref, acco, accs, accv, low_ref, wpt_ref
 ):
     step = pl.program_id(0)
     steps = pl.num_programs(0)
@@ -496,6 +504,7 @@
     def _():
         acco[...] = jnp.zeros_like(acco)
         accs[...] = jnp.zeros_like(accs)
+        wpt_ref[...] = wpo_ref[...].T
         accv[...] = jnp.zeros_like(accv)
 
     unit, inverse = normalised(mid_ref[...])
@@ -511,10 +520,11 @@
     low = grad_middle.astype(BF)
     low_ref[...] = low
     accv[16:24, :] += fold(low.astype(F32))
-    do_ref[...] = dot(low, wpo_ref[...], 1, 1).astype(BF)
-    dot_ref[...] = dot(wpo_ref[...], low, 1, 1).astype(BF)
+    back = dot(low, wpt_ref[...])
+    do_ref[...] = back.astype(BF)
+    dot_ref[...] = back.T.astype(BF)
     mine = low_ref[:, pl.ds(pl.multiple_of(core_ref[0] * half, half), half)]
-    acco[...] += dot(mo_ref[...], mine, 0, 0)
+    acco[...] += dot(mo_ref[...].astype(BF), mine)
     accs[...] += dot(ms_ref[...], mine, 0, 0)
 
     @pl.when(step == steps - 1)
@@ -524,9 +534,9 @@
         vecs_ref[...] = accv[...]
 
 
-def branch(core, middle, grad_own, grad_sib, cot, mixed_own, mixed_sib, wp_own, vec):
+def branch(core, middle, grad_own, grad_sib, cot, result_t, mixed_sib, wp_own, vec):
     rows, width = middle.shape
-    half = mixed_own.shape[1]
+    half = mixed_sib.shape[1]
     bt = 512
     blocks = rows // bt
     swap = lambda i: (lax.rem(i + blocks // 2, blocks), 0)
@@ -540,7 +550,7 @@
             pl.BlockSpec((bt, width), straight),
             pl.BlockSpec((bt, width), swap),
             pl.BlockSpec((bt, width), straight),
-            pl.BlockSpec((bt, half), straight),
+            pl.BlockSpec((half, bt), lambda i: (0, i)),
             pl.BlockSpec((bt, half), swap),
             whole(wp_own.shape),
             whole(vec.shape),
@@ -566,11 +576,12 @@
             pltpu.VMEM((half, half), F32),
             pltpu.VMEM((24, width), F32),
             pltpu.VMEM((bt, width), BF),
+            pltpu.VMEM((width, half), BF),
         ],
         compiler_params=params(60, "arbitrary"),
         cost_estimate=cost(2 * rows * width * 3 * half, 18 * rows * width),
         name="branch",
-    )(core, middle, grad_own, grad_sib, cot, mixed_own, mixed_sib, wp_own, vec)
+    )(core, middle, grad_own, grad_sib, cot, result_t, mixed_sib, wp_own, vec)
 
 
 def weight_grad_kernel(normed_ref, gq_ref, gk_ref, gv_ref, dw_ref, qv_ref, accw, accqv):
@@ -626,7 +637,7 @@
 
 def project_back_kernel(
     tok_ref, normed_ref, gqa_ref, gka_ref, gva_ref, gq_ref, gk_ref, gv_ref, w_ref,
-    own_ref, sib_ref, dw_ref, vecs_ref, qv_ref, accw, accv, accqv
+    own_ref, sib_ref, dw_ref, vecs_ref, qv_ref, accw, accv, accqv, wt_ref
 ):
     step = pl.program_id(0)
     steps = pl.num_programs(0)
@@ -639,6 +650,7 @@
         accw[...] = jnp.zeros_like(accw)
         accv[...] = jnp.zeros_like(accv)
         accqv[...] = jnp.zeros_like(accqv)
+        wt_ref[...] = w_ref[...].T
 
     unit, _ = normalised(tok_ref[...].astype(F32))
     normed_t = normed_ref[...].T
@@ -649,7 +661,7 @@
         value = ref[...]
         more = dot(
             jnp.concatenate([before[at][...], value], axis=1),
-            w_ref[:, at * wide : (at + 1) * wide], 1, 1,
+            wt_ref[at * wide : (at + 1) * wide, :],
         )
         grad = more if grad is None else grad + more
         accw[:, cols] += dot(normed_t, value)
@@ -705,6 +717,7 @@
             pltpu.VMEM((width, 3 * part), F32),
             pltpu.VMEM((16, width), F32),
             pltpu.VMEM((16, part), F32),
+            pltpu.VMEM((3 * (early + part), width), BF),
         ],
         compiler_params=params(60, "arbitrary"),
         cost_estimate=cost(2 * rows * width * (6 * part + 3 * early), 14 * rows * width),
@@ -1049,7 +1062,7 @@
         return jnp.where(image == 0, straight, crossed)
 
     grad_middle, grad_mixed, grad_mixed_t, dwp_own, dwp_sib, vec_back = branch(
-        core_row, middle, gn_part, gn_sib, cot, mixed, mixed_sib, wp_own, vec_two
+        core_row, middle, gn_part, gn_sib, cot, result_t, mixed_sib, wp_own, vec_two
     )
     dwp = jnp.where(
         core == 0,
@@ -1114,21 +1127,21 @@
     )
     gn1_sib = sibling(gn1_send)
     block_two, came_one = lax.optimization_barrier((block_two, came_one))
-    early_total = total(came_one)
-    early_came = partner(early_total)
     came_two = exchange(block_two)
     input_own, input_send = input_back(tok, gn1_own, gn1_sib, grad_middle, vec_one)
     input_came = partner(input_send)
-    came_two, input_own, one_sum, output = lax.optimization_barrier(
-        (came_two, input_own, one_sum, output)
-    )
+    early_total = total(came_one)
+    early_came = partner(early_total)
+    one_came, input_own, output = lax.optimization_barrier((one_came, input_own, output))
+    one_sum = join(scattered_one, one_came)
+    came_two, one_sum = lax.optimization_barrier((came_two, one_sum))
     one_other = sibling(one_sum)
     grad_fc1, grad_fc2 = finish_ff(place_row, one_sum, one_other, width, quarter)
-    input_grad = hand_back(input_own, input_came)
 
     early_sum = join(early_total, early_came)
     early_other = sibling(early_sum)
-    late_total = total(came_two)
+    late_total, input_came = lax.optimization_barrier((total(came_two), input_came))
+    input_grad = hand_back(input_own, input_came)
     late_came = [
         lax.ppermute(late_total, "seq", [(at, at ^ flip) for at in range(seq)])
         for flip in (2, 1, 3)

time: 402 us -> 396 us (0.985)
  waiting for transfers between devices: 90 us -> 84.2 us
    ppermute x3, waiting for transfers between devices: 15.8 us -> 0.17 us  [per_device(): lax.ppermute(late_total, 'seq', [(at, at ^ flip) for at in range(seq)])]
    ppermute x7, waiting for transfers between devices: 49.2 us -> 53.5 us  [partner(): return lax.ppermute(value, 'seq', to_partner)]
  transfers between devices with their start and end apart: 26 -> 26, of which waited for: 12 -> 13; matrix products, arithmetic and copies ran while one was open for 9% -> 9% of each run, Pallas kernels for 42% -> 42%
where the time goes in v9:
time: 396 us; the launch traced here: 389 us
  Pallas kernels  226 us (57%)
  waiting for transfers between devices  84.2 us (21%)
  other arithmetic  24.8 us (6%)
  starting transfers between devices  21.9 us (6%)
  local copies, waits for them, and re-layouts  17.8 us (4%)
  between operations  14.4 us (4%)
    pallas_call x2, Pallas kernels, attend_backward(): pl.pallas_call(kernel, grid=(count, keys // bq), in_specs=[pl.BlockSpec(m...  69.6 us
    pallas_call x1, Pallas kernels, feed_forward(): pl.pallas_call(kernel, grid=(blocks,), in_specs=[pl.BlockSpec(memory_spac...  56.1 us
    ppermute x7, waiting for transfers between devices, partner(): return lax.ppermute(value, 'seq', to_partner)  53.5 us
    pallas_call x1, Pallas kernels, attend_forward(): pl.pallas_call(kernel, grid=(pairs, keys // bq), in_specs=[pl.BlockSpec(m...  39 us
    pallas_call x1, Pallas kernels, branch(): pl.pallas_call(branch_kernel, grid=(blocks,), in_specs=[pl.BlockSpec(memo...  15.4 us
    pallas_call x1, Pallas kernels, project_back(): pl.pallas_call(project_back_kernel, grid=(blocks,), in_specs=[pl.BlockSpe...  14.5 us
    all_gather x1, waiting for transfers between devices, per_device(): second = lax.all_gather(two, 'fsdp', axis=0, tiled=True)  10.5 us
    pallas_call x1, Pallas kernels, project(): pl.pallas_call(project_kernel, grid=(rows // bt,), in_specs=[pl.BlockSpec...  10 us
  transfers between devices with their start and end apart: 26, of which 13 were waited for; matrix products, arithmetic and copies ran while one was open for 9% of the time, Pallas kernels for 42%

profile of v9, /device:TPU:0, one launch (start us, length us, event | category | flops | bytes accessed | tf_op | source)
XLA Modules:
  0.0 389.1 jit_solution(360205787137841584)
XLA Ops:
  16.1 17.7 %collective-permute-done = bf16[512,768]{1,0:T(8,128)(2,1)} collective-permute-done((bf16[512,768]{1,0:T(8,128)(2,1)S(1)}, bf16[512,768]{1,0:T(8,128)(2,1)}, u32[]{:S(2)}, u32[]{:S(2)}) %collective-permute-start) | collective-permute-done | bytes 786464 | tf_op jit(solution)/shard_map/ppermute | solution.py:995
  33.8 16.0 %collective-permute-done.1 = bf16[512,768]{1,0:T(8,128)(2,1)} collective-permute-done((bf16[512,768]{1,0:T(8,128)(2,1)S(1)}, bf16[512,768]{1,0:T(8,128)(2,1)}, u32[]{:S(2)}, u32[]{:S(2)}) %collective-permute-start.1) | collective-permute-done | bytes 786464 | tf_op jit(solution)/shard_map/ppermute | solution.py:995
  49.9 5.5 %all-gather.6.cloned.1.call-done = bf16[512,1152]{1,0:T(8,128)(2,1)} async-done(((bf16[64,1152]{1,0:T(8,128)(2,1)}), bf16[512,1152]{1,0:T(8,128)(2,1)}) %all-gather.6.cloned.1.call-update) | async-done | bytes 1179664 | tf_op jit(solution)/shard_map/all_gather | solution.py:1010
  62.5 3.3 pad_maximum_fusion.tok_ref
  65.8 3.2 pad_maximum_fusion.1.cot_ref
  69.0 12.4 %collective-permute-done.4 = bf16[8,48,1152]{2,1,0:T(8,128)(2,1)} collective-permute-done((bf16[8,48,1152]{2,1,0:T(8,128)(2,1)}, bf16[8,48,1152]{2,1,0:T(8,128)(2,1)}, u32[]{:S(2)}, u32[]{:S(2)}) %collective-permute-start.4) | collective-permute-done | bytes 884768 | tf_op jit(solution)/shard_map/ppermute | solution.py:995
  81.4 3.0 maximum_select_fusion.1
  84.5 10.0 %project.1 = (bf16[2048,1152]{1,0:T(8,128)(2,1)}, bf16[1152,2048]{1,0:T(8,128)(2,1)}, bf16[2048,768]{1,0:T(8,128)(2,1)}) custom-call(bf16[2048,768]{1,0:T(8,128)(2,1)} %pad_maximum_fusion.tok_ref, bf16[768,1152]{1,0:T(8,128)(2,1)} %bitcast.70, f32[1,1152]{1,0:T(1,128)} %reshape.146.bias_ref, f32[8,768]{1,0:T(8,128)} %maximum_maximum_fusion.vec_ref), custom_call_target="tpu_custom_call" | custom-call | flops 3623878656 | bytes 18874368 | tf_op jit(solution)/shard_map/project/pallas_call | solution.py:929
  94.5 39.0 %attend_forward.1 = (bf16[2048,384]{1,0:T(8,128)(2,1)}, f32[384,2048]{1,0:T(8,128)}, f32[3,8,2048]{2,1,0:T(8,128)}) custom-call(s32[2,4]{1,0:T(2,128)} %counts_ref.5, s32[1]{0:T(128)} %bitcast.1.place_ref, bf16[2048,1152]{1,0:T(8,128)(2,1)} %get-tuple-element.104.k_ref.q_ref.v_ref, bf16[1152,2048]{1,0:T(8,128)(2,1)} %get-tuple-element.105.qt_ref.vt_ref.kt_ref, ...), custom_call_target="tpu_custom_call" | custom-call | flops 25769803776 | bytes 9437184 | tf_op jit(solution)/shard_map/attend_forward/pallas_call | solution.py:168
  133.5 10.5 %all-gather.4.cloned.1.call-done.g2_ref = bf16[768,3456]{1,0:T(8,128)(2,1)} async-done(((bf16[96,3456]{1,0:T(8,128)(2,1)}), bf16[768,3456]{1,0:T(8,128)(2,1)}) %all-gather.4.cloned.1.call-update) | async-done | bytes 5308432 | tf_op jit(solution)/shard_map/all_gather | solution.py:1022
  148.1 56.1 %feed_forward.1 = (f32[2048,768]{1,0:T(8,128)}, f32[1024,768]{1,0:T(8,128)}, bf16[1024,768]{1,0:T(8,128)(2,1)}, bf16[2048,768]{1,0:T(8,128)(2,1)}, bf16[768,3072...) custom-call(s32[1]{0:T(128)} %bitcast.core_ref, ...), custom_call_target="tpu_custom_call" | custom-call | flops 31406948352 | bytes 40894464 | tf_op jit(solution)/shard_map/feed_forward/pallas_call | solution.py:443
  206.0 4.3 %collective-permute-done.9.gb_ref = bf16[2048,768]{1,0:T(8,128)(2,1)S(1)} collective-permute-done((bf16[2048,768]{1,0:T(8,128)(2,1)}, bf16[2048,768]{1,0:T(8,128)(2,1)S(1)}, u32[]{:S(2)}, u32[]{:S(2)}) %collective-permute-start.9) | collective-permute-done | bytes 3145760 | tf_op jit(solution)/shard_map/ppermute | solution.py:992
  212.0 15.4 %branch.1 = (f32[1024,768]{1,0:T(8,128)}, bf16[2048,384]{1,0:T(8,128)(2,1)}, bf16[384,2048]{1,0:T(8,128)(2,1)}, bf16[384,384]{1,0:T(8,128)(2,1)}, bf16[384,384]{1,0:T(8,128)(2,1)}, /*index=5*/f32[24,768]{1,0:T(8,128)}) custom-call(s32[1]{0:T(128)} %bitcast.core_ref, f32[2048,768]{1,0:T(8,128)} %get-tuple-element.110.mid_ref, ...), custom_call_target="tpu_custom_call" | custom-call | flops 3623878656 | bytes 28311552 | tf_op jit(solution)/shard_map/branch/pallas_call | solution.py:544
  227.8 45.5 %attend_backward.2 = (bf16[2048,256]{1,0:T(8,128)(2,1)}, bf16[2048,256]{1,0:T(8,128)(2,1)}, bf16[2048,256]{1,0:T(8,128)(2,1)}) custom-call(s32[2,4]{1,0:T(2,128)} %counts_ref.5, s32[1]{0:T(128)} %bitcast.1.place_ref, bf16[2048,1152]{1,0:T(8,128)(2,1)} %get-tuple-element.104.k_ref.q_ref.v_ref, bf16[2048,1152]{1,0:T(8,128)(2,1)} %get-tuple-element.104.k_ref.q_ref.v_ref, ...), custom_call_target="tpu_custom_call" | custom-call | flops 42949672960 | bytes 12582912 | tf_op jit(solution)/shard_map/attend_backward/pallas_call | solution.py:280
  273.8 6.6 %weight_grad.1 = (bf16[768,768]{1,0:T(8,128)(2,1)}, f32[16,256]{1,0:T(8,128)}) custom-call(bf16[2048,768]{1,0:T(8,128)(2,1)} %get-tuple-element.126.normed_ref, bf16[2048,256]{1,0:T(8,128)(2,1)} %get-tuple-element.127.gq_ref.gqa_ref, bf16[2048,256]{1,0:T(8,128)(2,1)} %get-tuple-element.128.gk_ref.gka_ref, bf16[2048,256]{1,0:T(8,128)(2,1)} %get-tuple-element.129.gv_ref.gva_ref), custom_call_target="tpu_custom_call" | custom-call | flops 2415919104 | bytes 6291456 | tf_op jit(solution)/shard_map/weight_grad/pallas_call | solution.py:617
  285.3 4.0 %all-to-all-start = ((bf16[8,96,1152]{2,1,0:T(8,128)(2,1)}), bf16[8,96,1152]{2,1,0:T(8,128)(2,1)S(1)}, u32[]{:S(2)}, u32[]{:S(2)}) async-start(bf16[8,96,1152]{2,1,0:T(8,128)(2,1)} %bitcast.21), calls=%async_computation.1 | async-start | bytes 3538944 | tf_op jit(solution)/shard_map/all_to_all | solution.py:955
  289.3 24.1 %attend_backward.3 = (bf16[2048,128]{1,0:T(8,128)(2,1)}, bf16[2048,128]{1,0:T(8,128)(2,1)}, bf16[2048,128]{1,0:T(8,128)(2,1)}) custom-call(s32[2,4]{1,0:T(2,128)} %counts_ref.5, s32[1]{0:T(128)} %bitcast.1.place_ref, bf16[2048,1152]{1,0:T(8,128)(2,1)} %get-tuple-element.104.k_ref.q_ref.v_ref, bf16[2048,1152]{1,0:T(8,128)(2,1)} %get-tuple-element.104.k_ref.q_ref.v_ref, ...), custom_call_target="tpu_custom_call" | custom-call | flops 21474836480 | bytes 6291456 | tf_op jit(solution)/shard_map/attend_backward/pallas_call | solution.py:280
  314.0 14.5 %project_back.1 = (f32[1024,768]{1,0:T(8,128)}, bf16[1024,768]{1,0:T(8,128)(2,1)}, bf16[768,384]{1,0:T(8,128)(2,1)}, f32[16,768]{1,0:T(8,128)}, f32[16,128]{1,0:T(8,128)}) custom-call(bf16[2048,768]{1,0:T(8,128)(2,1)} %pad_maximum_fusion.tok_ref, bf16[2048,768]{1,0:T(8,128)(2,1)} %get-tuple-element.126.normed_ref, ...), custom_call_target="tpu_custom_call" | custom-call | flops 4831838208 | bytes 22020096 | tf_op jit(solution)/shard_map/project_back/pallas_call | solution.py:695
  332.5 3.4 all-to-all-done
  336.0 3.8 all-to-all-start.1
  344.3 6.8 %input_back.1 = (f32[512,768]{1,0:T(8,128)}, bf16[512,768]{1,0:T(8,128)(2,1)}) custom-call(bf16[2048,768]{1,0:T(8,128)(2,1)} %pad_maximum_fusion.tok_ref, f32[1024,768]{1,0:T(8,128)} %get-tuple-element.142.own_ref, bf16[1024,768]{1,0:T(8,128)(2,1)} %collective-permute-done.13.sib_ref, f32[1024,768]{1,0:T(8,128)} %get-tuple-element.144.gm_ref, ...), custom_call_target="tpu_custom_call" | custom-call | flops 15728640 | bytes 12582912 | tf_op jit(solution)/shard_map/input_back/pallas_call | solution.py:749
  352.9 5.1 %all-to-all-done.1 = bf16[8,112,384]{2,1,0:T(8,128)(2,1)S(1)} async-done(((bf16[8,112,384]{2,1,0:T(8,128)(2,1)}), bf16[8,112,384]{2,1,0:T(8,128)(2,1)S(1)}, u32[]{:S(2)}, u32[]{:S(2)}) %all-to-all-start.1) | async-done | bytes 688160 | tf_op jit(solution)/shard_map/all_to_all | solution.py:955
  360.2 3.0 finish_ff.1
  363.2 7.3 %collective-permute-done.14 = bf16[512,768]{1,0:T(8,128)(2,1)} collective-permute-done((bf16[512,768]{1,0:T(8,128)(2,1)}, bf16[512,768]{1,0:T(8,128)(2,1)}, u32[]{:S(2)}, u32[]{:S(2)}) %collective-permute-start.14) | collective-permute-done | bytes 786464 | tf_op jit(solution)/shard_map/ppermute | solution.py:995
  (164 shorter events, 54.1 us)
Async XLA Ops:
  7.2 48.1 %all-gather.6.cloned.1.call-start = ((), (), s32[]{:S(2)}) async-start(), calls=%async_computation.5 | async-start | bytes 1327104 | tf_op jit(solution)/shard_map/all_gather | solution.py:1010
  11.3 132.6 %all-gather.4.cloned.1.call-start = ((), (), s32[]{:S(2)}) async-start(), calls=%async_computation.3 | async-start | bytes 5971968 | tf_op jit(solution)/shard_map/all_gather | solution.py:1022
  12.4 21.4 %collective-permute-start = (bf16[512,768]{1,0:T(8,128)(2,1)S(1)}, bf16[512,768]{1,0:T(8,128)(2,1)}, u32[]{:S(2)}, u32[]{:S(2)}) collective-permute-start(bf16[512,768]{1,0:T(8,128)(2,1)S(1)} %get-tuple-element.180), channel_id=1, source_target_pairs={{0,2},{1,3},{2,0},{3,1},{4,6},{5,7},{6,4},{7,5},{8,10},{9,11},{10,... | collective-permute-start | bytes 2359304 | tf_op jit(solution)/shard_map/ppermute | solution.py:995
  15.5 34.4 %collective-permute-start.1 = (bf16[512,768]{1,0:T(8,128)(2,1)S(1)}, bf16[512,768]{1,0:T(8,128)(2,1)}, u32[]{:S(2)}, u32[]{:S(2)}) collective-permute-start(bf16[512,768]{1,0:T(8,128)(2,1)S(1)} %get-tuple-element.178), channel_id=1, source_target_pairs={{0,2},{1,3},{2,0},{3,1},{4,6},{5,7},{6,4},{7,5},{8,10},{9,11},{10,... | collective-permute-start | bytes 2359304 | tf_op jit(solution)/shard_map/ppermute | solution.py:995
  55.3 258.0 %reduce-scatter.2.cloned.1.call-start = ((), (), s32[]{:S(2)}) async-start(), calls=%async_computation.4 | async-start | bytes 5308416 | tf_op jit(solution)/shard_map/reduce_scatter | solution.py:1053
  55.4 7.1 %collective-permute-start.2 = (bf16[512,768]{1,0:T(8,128)(2,1)}, bf16[512,768]{1,0:T(8,128)(2,1)}, u32[]{:S(2)}, u32[]{:S(2)}) collective-permute-start(bf16[512,768]{1,0:T(8,128)(2,1)} %get-tuple-element.179), channel_id=1, source_target_pairs={{0,1},{1,0},{2,3},{3,2},{4,5},{5,4},{6,7},{7,6},{8,9},{9,8},{10,11... | collective-permute-start | bytes 2359304 | tf_op jit(solution)/shard_map/ppermute | solution.py:992
  55.5 10.3 %collective-permute-start.5 = (bf16[512,768]{1,0:T(8,128)(2,1)S(1)}, bf16[512,768]{1,0:T(8,128)(2,1)}, u32[]{:S(2)}, u32[]{:S(2)}) collective-permute-start(bf16[512,768]{1,0:T(8,128)(2,1)S(1)} %get-tuple-element.177), channel_id=1, source_target_pairs={{0,1},{1,0},{2,3},{3,2},{4,5},{5,4},{6,7},{7,6},{8,9},{9,8},{10,11... | collective-permute-start | bytes 2359304 | tf_op jit(solution)/shard_map/ppermute | solution.py:992
  56.0 6.5 %collective-permute-start.3 = (bf16[512,768]{1,0:T(8,128)(2,1)}, bf16[512,768]{1,0:T(8,128)(2,1)}, u32[]{:S(2)}, u32[]{:S(2)}) collective-permute-start(bf16[512,768]{1,0:T(8,128)(2,1)} %collective-permute-done), channel_id=1, source_target_pairs={{0,1},{1,0},{2,3},{3,2},{4,5},{5,4},{6,7},{7,6},{8,9},{9,8},{10,11... | collective-permute-start | bytes 2359304 | tf_op jit(solution)/shard_map/ppermute | solution.py:992
  59.1 22.3 %collective-permute-start.4 = (bf16[8,48,1152]{2,1,0:T(8,128)(2,1)}, bf16[8,48,1152]{2,1,0:T(8,128)(2,1)}, u32[]{:S(2)}, u32[]{:S(2)}) collective-permute-start(bf16[8,48,1152]{2,1,0:T(8,128)(2,1)} %get-tuple-element.182), channel_id=1, source_target_pairs={{0,2},{1,3},{2,0},{3,1},{4,6},{5,7},{6,4},{7,5},{8,10},{9,11},{10,... | collective-permute-start | bytes 2654216 | tf_op jit(solution)/shard_map/ppermute | solution.py:995
  60.6 5.2 %collective-permute-start.6 = (bf16[512,768]{1,0:T(8,128)(2,1)}, bf16[512,768]{1,0:T(8,128)(2,1)}, u32[]{:S(2)}, u32[]{:S(2)}) collective-permute-start(bf16[512,768]{1,0:T(8,128)(2,1)} %collective-permute-done.1), channel_id=1, source_target_pairs={{0,1},{1,0},{2,3},{3,2},{4,5},{5,4},{6,7},{7,6},{8,9},{9,8},{10,11... | collective-permute-start | bytes 2359304 | tf_op jit(solution)/shard_map/ppermute | solution.py:992
  133.5 13.5 %collective-permute-start.7 = (bf16[2048,384]{1,0:T(8,128)(2,1)}, bf16[2048,384]{1,0:T(8,128)(2,1)S(1)}, u32[]{:S(2)}, u32[]{:S(2)}) collective-permute-start(bf16[2048,384]{1,0:T(8,128)(2,1)} %get-tuple-element.106.mo_ref), channel_id=1, source_target_pairs={{0,1},{1,0},{2,3},{3,2},{4,5},{5,4},{6,7},{7,6},{8,9},{9,8},{10,11... | collective-permute-start | bytes 4718600 | tf_op jit(solution)/shard_map/ppermute | solution.py:992
  204.3 6.0 %collective-permute-start.9 = (bf16[2048,768]{1,0:T(8,128)(2,1)}, bf16[2048,768]{1,0:T(8,128)(2,1)S(1)}, u32[]{:S(2)}, u32[]{:S(2)}) collective-permute-start(bf16[2048,768]{1,0:T(8,128)(2,1)} %get-tuple-element.111.ga_ref), channel_id=1, source_target_pairs={{0,1},{1,0},{2,3},{3,2},{4,5},{5,4},{6,7},{7,6},{8,9},{9,8},{10,11... | collective-permute-start | bytes 9437192 | tf_op jit(solution)/shard_map/ppermute | solution.py:992
  227.4 46.4 %collective-permute-start.10 = (bf16[1024,768]{1,0:T(8,128)(2,1)}, bf16[1024,768]{1,0:T(8,128)(2,1)S(1)}, u32[]{:S(2)}, u32[]{:S(2)}) collective-permute-start(bf16[1024,768]{1,0:T(8,128)(2,1)} %get-tuple-element.124), channel_id=1, source_target_pairs={{0,1},{1,0},{2,3},{3,2},{4,5},{5,4},{6,7},{7,6},{8,9},{9,8},{10,11... | collective-permute-start | bytes 4718600 | tf_op jit(solution)/shard_map/ppermute | solution.py:992
  283.7 29.6 %collective-permute-start.11 = (bf16[512,768]{1,0:T(8,128)(2,1)S(1)}, bf16[512,768]{1,0:T(8,128)(2,1)}, u32[]{:S(2)}, u32[]{:S(2)}) collective-permute-start(bf16[512,768]{1,0:T(8,128)(2,1)S(1)} %get-tuple-element.176), channel_id=1, source_target_pairs={{0,2},{1,3},{2,0},{3,1},{4,6},{5,7},{6,4},{7,5},{8,10},{9,11},{10,... | collective-permute-start | bytes 2359304 | tf_op jit(solution)/shard_map/ppermute | solution.py:995
  285.3 50.7 %all-to-all-start = ((bf16[8,96,1152]{2,1,0:T(8,128)(2,1)}), bf16[8,96,1152]{2,1,0:T(8,128)(2,1)S(1)}, u32[]{:S(2)}, u32[]{:S(2)}) async-start(bf16[8,96,1152]{2,1,0:T(8,128)(2,1)} %bitcast.21), calls=%async_computation.1 | async-start | bytes 3538944 | tf_op jit(solution)/shard_map/all_to_all | solution.py:955
  313.4 37.7 %collective-permute-start.12 = (bf16[96,3072]{1,0:T(8,128)(2,1)}, bf16[96,3072]{1,0:T(8,128)(2,1)}, u32[]{:S(2)}, u32[]{:S(2)}) collective-permute-start(bf16[96,3072]{1,0:T(8,128)(2,1)} %reduce-scatter.2.cloned.1.call-done), channel_id=1, source_target_pairs={{0,2},{1,3},{2,0},{3,1},{4,6},{5,7},{6,4},{7,5},{8,10},{9,11},{10,... | collective-permute-start | bytes 1769480 | tf_op jit(solution)/shard_map/ppermute | solution.py:995
  328.5 15.8 %collective-permute-start.13 = (bf16[1024,768]{1,0:T(8,128)(2,1)}, bf16[1024,768]{1,0:T(8,128)(2,1)}, u32[]{:S(2)}, u32[]{:S(2)}) collective-permute-start(bf16[1024,768]{1,0:T(8,128)(2,1)} %get-tuple-element.143), channel_id=1, source_target_pairs={{0,1},{1,0},{2,3},{3,2},{4,5},{5,4},{6,7},{7,6},{8,9},{9,8},{10,11... | collective-permute-start | bytes 4718600 | tf_op jit(solution)/shard_map/ppermute | solution.py:992
  336.0 22.1 %all-to-all-start.1 = ((bf16[8,112,384]{2,1,0:T(8,128)(2,1)}), bf16[8,112,384]{2,1,0:T(8,128)(2,1)S(1)}, u32[]{:S(2)}, u32[]{:S(2)}) async-start(bf16[8,112,384]{2,1,0:T(8,128)(2,1)} %fusion.4), calls=%async_computation.2 | async-start | bytes 1376256 | tf_op jit(solution)/shard_map/all_to_all | solution.py:955
  340.0 18.0 %collective-permute-start.15 = (bf16[96,1152]{1,0:T(8,128)(2,1)S(1)}, bf16[96,1152]{1,0:T(8,128)(2,1)S(1)}, u32[]{:S(2)}, u32[]{:S(2)}) collective-permute-start(bf16[96,1152]{1,0:T(8,128)(2,1)S(1)} %reduce_sum.75), channel_id=1, source_target_pairs={{0,2},{1,3},{2,0},{3,1},{4,6},{5,7},{6,4},{7,5},{8,10},{9,11},{10,... | collective-permute-start | bytes 663560 | tf_op jit(solution)/shard_map/ppermute | solution.py:995
  351.1 19.4 %collective-permute-start.14 = (bf16[512,768]{1,0:T(8,128)(2,1)}, bf16[512,768]{1,0:T(8,128)(2,1)}, u32[]{:S(2)}, u32[]{:S(2)}) collective-permute-start(bf16[512,768]{1,0:T(8,128)(2,1)} %get-tuple-element.160), channel_id=1, source_target_pairs={{0,2},{1,3},{2,0},{3,1},{4,6},{5,7},{6,4},{7,5},{8,10},{9,11},{10,... | collective-permute-start | bytes 2359304 | tf_op jit(solution)/shard_map/ppermute | solution.py:995
  358.1 17.9 %collective-permute-start.16 = (bf16[96,1152]{1,0:T(8,128)(2,1)S(1)}, bf16[96,1152]{1,0:T(8,128)(2,1)S(1)}, u32[]{:S(2)}, u32[]{:S(2)}) collective-permute-start(bf16[96,1152]{1,0:T(8,128)(2,1)S(1)} %add_convert_fusion.2.em_ref), channel_id=1, source_target_pairs={{0,1},{1,0},{2,3},{3,2},{4,5},{5,4},{6,7},{7,6},{8,9},{9,8},{10,11... | collective-permute-start | bytes 663560 | tf_op jit(solution)/shard_map/ppermute | solution.py:992
  370.5 5.3 %collective-permute-start.17 = (bf16[112,384]{1,0:T(8,128)(2,1)S(1)}, bf16[112,384]{1,0:T(8,128)(2,1)S(1)}, u32[]{:S(2)}, u32[]{:S(2)}) collective-permute-start(bf16[112,384]{1,0:T(8,128)(2,1)S(1)} %reduce_sum.74.la_ref), channel_id=1, source_target_pairs={{0,2},{1,3},{2,0},{3,1},{4,6},{5,7},{6,4},{7,5},{8,10},{9,11},{10,... | collective-permute-start | bytes 258056 | tf_op jit(solution)/shard_map/ppermute | solution.py:1146
  371.1 4.7 %collective-permute-start.18 = (bf16[112,384]{1,0:T(8,128)(2,1)S(1)}, bf16[112,384]{1,0:T(8,128)(2,1)S(1)}, u32[]{:S(2)}, u32[]{:S(2)}) collective-permute-start(bf16[112,384]{1,0:T(8,128)(2,1)S(1)} %reduce_sum.74.la_ref), channel_id=1, source_target_pairs={{0,1},{1,0},{2,3},{3,2},{4,5},{5,4},{6,7},{7,6},{8,9},{9,8},{10,11... | collective-permute-start | bytes 258056 | tf_op jit(solution)/shard_map/ppermute | solution.py:1146
  371.1 4.8 %collective-permute-start.19 = (bf16[112,384]{1,0:T(8,128)(2,1)S(1)}, bf16[112,384]{1,0:T(8,128)(2,1)S(1)}, u32[]{:S(2)}, u32[]{:S(2)}) collective-permute-start(bf16[112,384]{1,0:T(8,128)(2,1)S(1)} %reduce_sum.74.la_ref), channel_id=1, source_target_pairs={{0,3},{1,2},{2,1},{3,0},{4,7},{5,6},{6,5},{7,4},{8,11},{9,10},{10,... | collective-permute-start | bytes 258056 | tf_op jit(solution)/shard_map/ppermute | solution.py:1146
  (23 other events, 239.3 us)
Sparse Core Ops, SparseCore 0:
  11.5 43.8 all-gather.5
  58.1 85.8 all-gather.3
  205.0 96.0 reduce-scatter.1

commit v10 on v9

--- a/solution.py
+++ b/solution.py
@@ -17,6 +17,9 @@
 PAIR = 2 * HEAD_DIM
 VEC_ROWS = 16
 SLOT_ORDER = (0, 2, 1, 3)
+ERF_TERMS = tuple(
+    0.5 * term for term in (0.254829592, -0.284496736, 1.421413741, -1.453152027, 1.061405429)
+)
 
 
 def params(mebibytes, *semantics):
@@ -387,8 +390,14 @@
         return hidden, dot(cot, w2t_ref[:, at * chunk : (at + 1) * chunk])
 
     def middle_part(hidden, grad_active):
-        below = 0.5 + 0.5 * lax.erf(hidden * (0.5**0.5))
-        slope = below + hidden * (jnp.exp(hidden * hidden * -0.5) * 0.3989422804014327)
+        bell = jnp.exp(hidden * hidden * -0.5)
+        inverse = pl.reciprocal(1.0 + jnp.abs(hidden) * (0.3275911 * 0.5**0.5), approx=False)
+        tail = ERF_TERMS[4]
+        for term in ERF_TERMS[3::-1]:
+            tail = tail * inverse + term
+        tail = tail * inverse * bell
+        below = jnp.where(hidden >= 0.0, 1.0 - tail, tail)
+        slope = below + hidden * (bell * 0.3989422804014327)
         return (hidden * below).astype(BF), (grad_active * slope).astype(BF)
 
     chunks = half // chunk
@@ -437,7 +446,7 @@
     rows, width = tokens.shape
     half = f1b.shape[1]
     heads = mixed_own.shape[1]
-    bt, chunk = 512, 384
+    bt, chunk = 512, 768
     blocks = rows // bt
     kernel = functools.partial(feed_forward_kernel, chunk)
     return pl.pallas_call(
@@ -584,7 +593,9 @@
     )(core, middle, grad_own, grad_sib, cot, result_t, mixed_sib, wp_own, vec)
 
 
-def weight_grad_kernel(normed_ref, gq_ref, gk_ref, gv_ref, dw_ref, qv_ref, accw, accqv):
+def weight_grad_kernel(
+    core_ref, normed_ref, gq_ref, gk_ref, gv_ref, dwo_ref, dws_ref, dw_ref, qv_ref, accw, accqv
+):
     step = pl.program_id(0)
     steps = pl.num_programs(0)
     part = gq_ref.shape[1]
@@ -605,34 +616,43 @@
 
     @pl.when(step == steps - 1)
     def _():
-        dw_ref[...] = accw[...].astype(BF)
+        dw_ref[:, : 3 * part] = accw[...].astype(BF)
+        rows = dwo_ref.shape[0]
+        first_core = core_ref[0] == 0
+        dwo, dws = dwo_ref[...], dws_ref[...]
+        dw_ref[:rows, 3 * part :] = jnp.where(first_core, dwo, dws)
+        dw_ref[rows:, 3 * part :] = jnp.where(first_core, dws, dwo)
         qv_ref[...] = accqv[...]
 
 
-def weight_grad(normed, gq, gk, gv):
+def weight_grad(core, normed, gq, gk, gv, dw_own, dw_sib):
     rows, width = normed.shape
     part = gq.shape[1]
     bt = 512
+    wide = 3 * part + dw_own.shape[1]
     straight = lambda i: (i, 0)
     return pl.pallas_call(
         weight_grad_kernel,
         grid=(rows // bt,),
         in_specs=[
+            pl.BlockSpec(memory_space=pltpu.SMEM),
             pl.BlockSpec((bt, width), straight),
             pl.BlockSpec((bt, part), straight),
             pl.BlockSpec((bt, part), straight),
             pl.BlockSpec((bt, part), straight),
-        ],
-        out_specs=[whole((width, 3 * part)), whole((16, part))],
+            whole(dw_own.shape),
+            whole(dw_sib.shape),
+        ],
+        out_specs=[whole((width, wide)), whole((16, part))],
         out_shape=[
-            jax.ShapeDtypeStruct((width, 3 * part), BF),
+            jax.ShapeDtypeStruct((width, wide), BF),
             jax.ShapeDtypeStruct((16, part), F32),
         ],
         scratch_shapes=[pltpu.VMEM((width, 3 * part), F32), pltpu.VMEM((16, part), F32)],
         compiler_params=params(60, "arbitrary"),
         cost_estimate=cost(2 * rows * width * 3 * part, 2 * rows * (width + 3 * part)),
         name="weight_grad",
-    )(normed, gq, gk, gv)
+    )(core, normed, gq, gk, gv, dw_own, dw_sib)
 
 
 def project_back_kernel(
@@ -1064,20 +1084,15 @@
     grad_middle, grad_mixed, grad_mixed_t, dwp_own, dwp_sib, vec_back = branch(
         core_row, middle, gn_part, gn_sib, cot, result_t, mixed_sib, wp_own, vec_two
     )
-    dwp = jnp.where(
-        core == 0,
-        jnp.concatenate([dwp_own, dwp_sib], axis=0),
-        jnp.concatenate([dwp_sib, dwp_own], axis=0),
-    )
     grad_mixed, out_send, out_own = lax.optimization_barrier((grad_mixed, out_send, out_own))
     out_sib = sibling(out_send)
     early, late = 2, 1
     attend = functools.partial(attend_backward, counts, place_row, packed, packed_t)
     before = attend(grad_mixed, grad_mixed_t, result_t, log_total, slots, 0, early)
     before, out_sib = lax.optimization_barrier((before, out_sib))
-    dw_early, qv_early = weight_grad(normed, *before)
+    block_one, qv_early = weight_grad(core_row, normed, *before, dwp_own, dwp_sib)
     out_own = (out_own + out_sib.astype(F32)).astype(BF)
-    block_one = jnp.concatenate([dw_early, dwp], axis=1).reshape(owners, shard, -1)
+    block_one = block_one.reshape(owners, shard, -1)
     grad_mixed, out_own, block_one = lax.optimization_barrier((grad_mixed, out_own, block_one))
     came_one = exchange(block_one)
     out_came = partner(out_own[slots:])
@@ -1092,7 +1107,6 @@
     scattered_one, out_came, grads = lax.optimization_barrier((scattered_one, out_came, grads))
     output = hand_back(out_own, out_came)
     one_came = partner(scattered_one)
-    one_sum = join(scattered_one, one_came)
     gn1_own, gn1_send, dw_late, vec_first, qv_late = project_back(tok, normed, before, grads, w_qkv)
 
     def spread(vector):
@@ -1132,7 +1146,7 @@
     input_came = partner(input_send)
     early_total = total(came_one)
     early_came = partner(early_total)
-    one_came, input_own, output = lax.optimization_barrier((one_came, input_own, output))
+    one_came, input_own = lax.optimization_barrier((one_came, input_own))
     one_sum = join(scattered_one, one_came)
     came_two, one_sum = lax.optimization_barrier((came_two, one_sum))
     one_other = sibling(one_sum)
@@ -1140,7 +1154,9 @@
 
     early_sum = join(early_total, early_came)
     early_other = sibling(early_sum)
-    late_total, input_came = lax.optimization_barrier((total(came_two), input_came))
+    late_total, input_came, output = lax.optimization_barrier(
+        (total(came_two), input_came, output)
+    )
     input_grad = hand_back(input_own, input_came)
     late_came = [
         lax.ppermute(late_total, "seq", [(at, at ^ flip) for at in range(seq)])

time: 396 us -> 392 us (0.990)
  transfers between devices with their start and end apart: 26 -> 26, of which waited for: 13 -> 11; matrix products, arithmetic and copies ran while one was open for 9% -> 8% of each run, Pallas kernels for 42% -> 43%
where the time goes in v10:
time: 392 us; the launch traced here: 386 us
  Pallas kernels  225 us (57%)
  waiting for transfers between devices  82.5 us (21%)
  other arithmetic  22.4 us (6%)
  starting transfers between devices  22.1 us (6%)
  local copies, waits for them, and re-layouts  18.9 us (5%)
  between operations  14.7 us (4%)
    pallas_call x2, Pallas kernels, attend_backward(): pl.pallas_call(kernel, grid=(count, keys // bq), in_specs=[pl.BlockSpec(m...  69.5 us
    pallas_call x1, Pallas kernels, feed_forward(): pl.pallas_call(kernel, grid=(blocks,), in_specs=[pl.BlockSpec(memory_spac...  54.4 us
    ppermute x7, waiting for transfers between devices, partner(): return lax.ppermute(value, 'seq', to_partner)  50.7 us
    pallas_call x1, Pallas kernels, attend_forward(): pl.pallas_call(kernel, grid=(pairs, keys // bq), in_specs=[pl.BlockSpec(m...  38.9 us
    pallas_call x1, Pallas kernels, branch(): pl.pallas_call(branch_kernel, grid=(blocks,), in_specs=[pl.BlockSpec(memo...  15.6 us
    pallas_call x1, Pallas kernels, project_back(): pl.pallas_call(project_back_kernel, grid=(blocks,), in_specs=[pl.BlockSpe...  14.5 us
    all_to_all x2, waiting for transfers between devices, exchange(): lax.all_to_all(value, 'fsdp', split_axis=0, concat_axis=0, tiled=True)  10.8 us
    all_gather x1, waiting for transfers between devices, per_device(): second = lax.all_gather(two, 'fsdp', axis=0, tiled=True)  10.2 us
  transfers between devices with their start and end apart: 26, of which 11 were waited for; matrix products, arithmetic and copies ran while one was open for 8% of the time, Pallas kernels for 43%

profile of v10, /device:TPU:0, one launch (start us, length us, event | category | flops | bytes accessed | tf_op | source)
XLA Modules:
  0.0 385.6 jit_solution(15560268736842734127)
XLA Ops:
  16.1 17.7 %collective-permute-done = bf16[512,768]{1,0:T(8,128)(2,1)} collective-permute-done((bf16[512,768]{1,0:T(8,128)(2,1)S(1)}, bf16[512,768]{1,0:T(8,128)(2,1)}, u32[]{:S(2)}, u32[]{:S(2)}) %collective-permute-start) | collective-permute-done | bytes 786464 | tf_op jit(solution)/shard_map/ppermute | solution.py:1015
  33.8 16.0 %collective-permute-done.1 = bf16[512,768]{1,0:T(8,128)(2,1)} collective-permute-done((bf16[512,768]{1,0:T(8,128)(2,1)S(1)}, bf16[512,768]{1,0:T(8,128)(2,1)}, u32[]{:S(2)}, u32[]{:S(2)}) %collective-permute-start.1) | collective-permute-done | bytes 786464 | tf_op jit(solution)/shard_map/ppermute | solution.py:1015
  49.9 5.5 %all-gather.6.cloned.1.call-done = bf16[512,1152]{1,0:T(8,128)(2,1)} async-done(((bf16[64,1152]{1,0:T(8,128)(2,1)}), bf16[512,1152]{1,0:T(8,128)(2,1)}) %all-gather.6.cloned.1.call-update) | async-done | bytes 1179664 | tf_op jit(solution)/shard_map/all_gather | solution.py:1030
  62.8 3.4 pad_maximum_fusion.tok_ref
  66.2 3.2 pad_maximum_fusion.1.cot_ref
  69.3 12.5 %collective-permute-done.4 = bf16[8,48,1152]{2,1,0:T(8,128)(2,1)} collective-permute-done((bf16[8,48,1152]{2,1,0:T(8,128)(2,1)}, bf16[8,48,1152]{2,1,0:T(8,128)(2,1)}, u32[]{:S(2)}, u32[]{:S(2)}) %collective-permute-start.4) | collective-permute-done | bytes 884768 | tf_op jit(solution)/shard_map/ppermute | solution.py:1015
  81.8 3.0 maximum_select_fusion.1
  84.8 10.1 %project.1 = (bf16[2048,1152]{1,0:T(8,128)(2,1)}, bf16[1152,2048]{1,0:T(8,128)(2,1)}, bf16[2048,768]{1,0:T(8,128)(2,1)}) custom-call(bf16[2048,768]{1,0:T(8,128)(2,1)} %pad_maximum_fusion.tok_ref, bf16[768,1152]{1,0:T(8,128)(2,1)} %bitcast.71, f32[1,1152]{1,0:T(1,128)} %reshape.145.bias_ref, f32[8,768]{1,0:T(8,128)} %maximum_maximum_fusion.vec_ref), custom_call_target="tpu_custom_call" | custom-call | flops 3623878656 | bytes 18874368 | tf_op jit(solution)/shard_map/project/pallas_call | solution.py:949
  94.9 38.9 %attend_forward.1 = (bf16[2048,384]{1,0:T(8,128)(2,1)}, f32[384,2048]{1,0:T(8,128)}, f32[3,8,2048]{2,1,0:T(8,128)}) custom-call(s32[2,4]{1,0:T(2,128)} %counts_ref.5, s32[1]{0:T(128)} %bitcast.place_ref, bf16[2048,1152]{1,0:T(8,128)(2,1)} %get-tuple-element.105.k_ref.q_ref.v_ref, bf16[1152,2048]{1,0:T(8,128)(2,1)} %get-tuple-element.106.qt_ref.vt_ref.kt_ref, ...), custom_call_target="tpu_custom_call" | custom-call | flops 25769803776 | bytes 9437184 | tf_op jit(solution)/shard_map/attend_forward/pallas_call | solution.py:171
  133.8 10.2 %all-gather.4.cloned.1.call-done.g2_ref = bf16[768,3456]{1,0:T(8,128)(2,1)} async-done(((bf16[96,3456]{1,0:T(8,128)(2,1)}), bf16[768,3456]{1,0:T(8,128)(2,1)}) %all-gather.4.cloned.1.call-update) | async-done | bytes 5308432 | tf_op jit(solution)/shard_map/all_gather | solution.py:1042
  148.1 54.4 %feed_forward.1 = (f32[2048,768]{1,0:T(8,128)}, f32[1024,768]{1,0:T(8,128)}, bf16[1024,768]{1,0:T(8,128)(2,1)}, bf16[2048,768]{1,0:T(8,128)(2,1)}, bf16[768,3072...) custom-call(s32[1]{0:T(128)} %bitcast.18.core_ref, ...), custom_call_target="tpu_custom_call" | custom-call | flops 31406948352 | bytes 40894464 | tf_op jit(solution)/shard_map/feed_forward/pallas_call | solution.py:452
  204.1 4.4 %collective-permute-done.9.gb_ref = bf16[2048,768]{1,0:T(8,128)(2,1)S(1)} collective-permute-done((bf16[2048,768]{1,0:T(8,128)(2,1)}, bf16[2048,768]{1,0:T(8,128)(2,1)S(1)}, u32[]{:S(2)}, u32[]{:S(2)}) %collective-permute-start.9) | collective-permute-done | bytes 3145760 | tf_op jit(solution)/shard_map/ppermute | solution.py:1012
  210.2 15.6 %branch.1 = (f32[1024,768]{1,0:T(8,128)}, bf16[2048,384]{1,0:T(8,128)(2,1)}, bf16[384,2048]{1,0:T(8,128)(2,1)}, bf16[384,384]{1,0:T(8,128)(2,1)}, bf16[384,384]{1,0:T(8,128)(2,1)}, /*index=5*/f32[24,768]{1,0:T(8,128)}) custom-call(s32[1]{0:T(128)} %bitcast.18.core_ref, f32[2048,768]{1,0:T(8,128)} %get-tuple-element.110.mid_ref, ...), custom_call_target="tpu_custom_call" | custom-call | flops 3623878656 | bytes 28311552 | tf_op jit(solution)/shard_map/branch/pallas_call | solution.py:553
  226.2 45.5 %attend_backward.2 = (bf16[2048,256]{1,0:T(8,128)(2,1)}, bf16[2048,256]{1,0:T(8,128)(2,1)}, bf16[2048,256]{1,0:T(8,128)(2,1)}) custom-call(s32[2,4]{1,0:T(2,128)} %counts_ref.5, s32[1]{0:T(128)} %bitcast.place_ref, bf16[2048,1152]{1,0:T(8,128)(2,1)} %get-tuple-element.105.k_ref.q_ref.v_ref, bf16[2048,1152]{1,0:T(8,128)(2,1)} %get-tuple-element.105.k_ref.q_ref.v_ref, ...), custom_call_target="tpu_custom_call" | custom-call | flops 42949672960 | bytes 12582912 | tf_op jit(solution)/shard_map/attend_backward/pallas_call | solution.py:283
  272.0 7.2 %weight_grad.1 = (bf16[768,1152]{1,0:T(8,128)(2,1)}, f32[16,256]{1,0:T(8,128)}) custom-call(s32[1]{0:T(128)} %bitcast.18.core_ref, bf16[2048,768]{1,0:T(8,128)(2,1)} %get-tuple-element.102.normed_ref, bf16[2048,256]{1,0:T(8,128)(2,1)} %get-tuple-element.124.gq_ref.gqa_ref, bf16[2048,256]{1,0:T(8,128)(2,1)} %get-tuple-element.125.gk_ref.gka_ref, ...), custom_call_target="tpu_custom_call" | custom-call | flops 2415919104 | bytes 6291456 | tf_op jit(solution)/shard_map/weight_grad/pallas_call | solution.py:634
  281.4 3.9 %all-to-all-start = ((bf16[8,96,1152]{2,1,0:T(8,128)(2,1)}), bf16[8,96,1152]{2,1,0:T(8,128)(2,1)S(1)}, u32[]{:S(2)}, u32[]{:S(2)}) async-start(bf16[8,96,1152]{2,1,0:T(8,128)(2,1)} %bitcast.70), calls=%async_computation.1 | async-start | bytes 3538944 | tf_op jit(solution)/shard_map/all_to_all | solution.py:975
  288.0 24.0 %attend_backward.3 = (bf16[2048,128]{1,0:T(8,128)(2,1)}, bf16[2048,128]{1,0:T(8,128)(2,1)}, bf16[2048,128]{1,0:T(8,128)(2,1)}) custom-call(s32[2,4]{1,0:T(2,128)} %counts_ref.5, s32[1]{0:T(128)} %bitcast.place_ref, bf16[2048,1152]{1,0:T(8,128)(2,1)} %get-tuple-element.105.k_ref.q_ref.v_ref, bf16[2048,1152]{1,0:T(8,128)(2,1)} %get-tuple-element.105.k_ref.q_ref.v_ref, ...), custom_call_target="tpu_custom_call" | custom-call | flops 21474836480 | bytes 6291456 | tf_op jit(solution)/shard_map/attend_backward/pallas_call | solution.py:283
  312.1 14.5 %project_back.1 = (f32[1024,768]{1,0:T(8,128)}, bf16[1024,768]{1,0:T(8,128)(2,1)}, bf16[768,384]{1,0:T(8,128)(2,1)}, f32[16,768]{1,0:T(8,128)}, f32[16,128]{1,0:T(8,128)}) custom-call(bf16[2048,768]{1,0:T(8,128)(2,1)} %pad_maximum_fusion.tok_ref, bf16[2048,768]{1,0:T(8,128)(2,1)} %get-tuple-element.102.normed_ref, ...), custom_call_target="tpu_custom_call" | custom-call | flops 4831838208 | bytes 22020096 | tf_op jit(solution)/shard_map/project_back/pallas_call | solution.py:715
  331.3 3.1 all-to-all-done
  334.4 3.9 %all-to-all-start.1 = ((bf16[8,112,384]{2,1,0:T(8,128)(2,1)}), bf16[8,112,384]{2,1,0:T(8,128)(2,1)S(1)}, u32[]{:S(2)}, u32[]{:S(2)}) async-start(bf16[8,112,384]{2,1,0:T(8,128)(2,1)} %fusion.4), calls=%async_computation.2 | async-start | bytes 1376256 | tf_op jit(solution)/shard_map/all_to_all | solution.py:975
  340.1 6.7 %input_back.1 = (f32[512,768]{1,0:T(8,128)}, bf16[512,768]{1,0:T(8,128)(2,1)}) custom-call(bf16[2048,768]{1,0:T(8,128)(2,1)} %pad_maximum_fusion.tok_ref, f32[1024,768]{1,0:T(8,128)} %get-tuple-element.151.own_ref, bf16[1024,768]{1,0:T(8,128)(2,1)} %collective-permute-done.13.sib_ref, f32[1024,768]{1,0:T(8,128)} %get-tuple-element.153.gm_ref, ...), custom_call_target="tpu_custom_call" | custom-call | flops 15728640 | bytes 12582912 | tf_op jit(solution)/shard_map/input_back/pallas_call | solution.py:769
  348.9 7.7 %all-to-all-done.1 = bf16[8,112,384]{2,1,0:T(8,128)(2,1)S(1)} async-done(((bf16[8,112,384]{2,1,0:T(8,128)(2,1)}), bf16[8,112,384]{2,1,0:T(8,128)(2,1)S(1)}, u32[]{:S(2)}, u32[]{:S(2)}) %all-to-all-start.1) | async-done | bytes 688160 | tf_op jit(solution)/shard_map/all_to_all | solution.py:975
  358.7 3.1 finish_ff.1
  361.8 4.5 %collective-permute-done.14 = bf16[512,768]{1,0:T(8,128)(2,1)} collective-permute-done((bf16[512,768]{1,0:T(8,128)(2,1)}, bf16[512,768]{1,0:T(8,128)(2,1)}, u32[]{:S(2)}, u32[]{:S(2)}) %collective-permute-start.14) | collective-permute-done | bytes 786464 | tf_op jit(solution)/shard_map/ppermute | solution.py:1015
  (156 shorter events, 52.1 us)
Async XLA Ops:
  7.2 48.1 %all-gather.6.cloned.1.call-start = ((), (), s32[]{:S(2)}) async-start(), calls=%async_computation.5 | async-start | bytes 1327104 | tf_op jit(solution)/shard_map/all_gather | solution.py:1030
  11.3 132.6 %all-gather.4.cloned.1.call-start = ((), (), s32[]{:S(2)}) async-start(), calls=%async_computation.3 | async-start | bytes 5971968 | tf_op jit(solution)/shard_map/all_gather | solution.py:1042
  12.4 21.4 %collective-permute-start = (bf16[512,768]{1,0:T(8,128)(2,1)S(1)}, bf16[512,768]{1,0:T(8,128)(2,1)}, u32[]{:S(2)}, u32[]{:S(2)}) collective-permute-start(bf16[512,768]{1,0:T(8,128)(2,1)S(1)} %get-tuple-element.180), channel_id=1, source_target_pairs={{0,2},{1,3},{2,0},{3,1},{4,6},{5,7},{6,4},{7,5},{8,10},{9,11},{10,... | collective-permute-start | bytes 2359304 | tf_op jit(solution)/shard_map/ppermute | solution.py:1015
  15.5 34.4 %collective-permute-start.1 = (bf16[512,768]{1,0:T(8,128)(2,1)S(1)}, bf16[512,768]{1,0:T(8,128)(2,1)}, u32[]{:S(2)}, u32[]{:S(2)}) collective-permute-start(bf16[512,768]{1,0:T(8,128)(2,1)S(1)} %get-tuple-element.178), channel_id=1, source_target_pairs={{0,2},{1,3},{2,0},{3,1},{4,6},{5,7},{6,4},{7,5},{8,10},{9,11},{10,... | collective-permute-start | bytes 2359304 | tf_op jit(solution)/shard_map/ppermute | solution.py:1015
  55.3 256.7 %reduce-scatter.2.cloned.1.call-start = ((), (), s32[]{:S(2)}) async-start(), calls=%async_computation.4 | async-start | bytes 5308416 | tf_op jit(solution)/shard_map/reduce_scatter | solution.py:1073
  55.4 7.4 %collective-permute-start.2 = (bf16[512,768]{1,0:T(8,128)(2,1)}, bf16[512,768]{1,0:T(8,128)(2,1)}, u32[]{:S(2)}, u32[]{:S(2)}) collective-permute-start(bf16[512,768]{1,0:T(8,128)(2,1)} %get-tuple-element.179), channel_id=1, source_target_pairs={{0,1},{1,0},{2,3},{3,2},{4,5},{5,4},{6,7},{7,6},{8,9},{9,8},{10,11... | collective-permute-start | bytes 2359304 | tf_op jit(solution)/shard_map/ppermute | solution.py:1012
  55.5 10.7 %collective-permute-start.5 = (bf16[512,768]{1,0:T(8,128)(2,1)S(1)}, bf16[512,768]{1,0:T(8,128)(2,1)}, u32[]{:S(2)}, u32[]{:S(2)}) collective-permute-start(bf16[512,768]{1,0:T(8,128)(2,1)S(1)} %get-tuple-element.177), channel_id=1, source_target_pairs={{0,1},{1,0},{2,3},{3,2},{4,5},{5,4},{6,7},{7,6},{8,9},{9,8},{10,11... | collective-permute-start | bytes 2359304 | tf_op jit(solution)/shard_map/ppermute | solution.py:1012
  56.0 6.7 %collective-permute-start.3 = (bf16[512,768]{1,0:T(8,128)(2,1)}, bf16[512,768]{1,0:T(8,128)(2,1)}, u32[]{:S(2)}, u32[]{:S(2)}) collective-permute-start(bf16[512,768]{1,0:T(8,128)(2,1)} %collective-permute-done), channel_id=1, source_target_pairs={{0,1},{1,0},{2,3},{3,2},{4,5},{5,4},{6,7},{7,6},{8,9},{9,8},{10,11... | collective-permute-start | bytes 2359304 | tf_op jit(solution)/shard_map/ppermute | solution.py:1012
  56.1 10.0 %collective-permute-start.6 = (bf16[512,768]{1,0:T(8,128)(2,1)}, bf16[512,768]{1,0:T(8,128)(2,1)}, u32[]{:S(2)}, u32[]{:S(2)}) collective-permute-start(bf16[512,768]{1,0:T(8,128)(2,1)} %collective-permute-done.1), channel_id=1, source_target_pairs={{0,1},{1,0},{2,3},{3,2},{4,5},{5,4},{6,7},{7,6},{8,9},{9,8},{10,11... | collective-permute-start | bytes 2359304 | tf_op jit(solution)/shard_map/ppermute | solution.py:1012
  59.8 21.9 %collective-permute-start.4 = (bf16[8,48,1152]{2,1,0:T(8,128)(2,1)}, bf16[8,48,1152]{2,1,0:T(8,128)(2,1)}, u32[]{:S(2)}, u32[]{:S(2)}) collective-permute-start(bf16[8,48,1152]{2,1,0:T(8,128)(2,1)} %get-tuple-element.182), channel_id=1, source_target_pairs={{0,2},{1,3},{2,0},{3,1},{4,6},{5,7},{6,4},{7,5},{8,10},{9,11},{10,... | collective-permute-start | bytes 2654216 | tf_op jit(solution)/shard_map/ppermute | solution.py:1015
  133.8 13.2 %collective-permute-start.7 = (bf16[2048,384]{1,0:T(8,128)(2,1)}, bf16[2048,384]{1,0:T(8,128)(2,1)S(1)}, u32[]{:S(2)}, u32[]{:S(2)}) collective-permute-start(bf16[2048,384]{1,0:T(8,128)(2,1)} %get-tuple-element.107.mo_ref), channel_id=1, source_target_pairs={{0,1},{1,0},{2,3},{3,2},{4,5},{5,4},{6,7},{7,6},{8,9},{9,8},{10,11... | collective-permute-start | bytes 4718600 | tf_op jit(solution)/shard_map/ppermute | solution.py:1012
  202.5 6.0 %collective-permute-start.9 = (bf16[2048,768]{1,0:T(8,128)(2,1)}, bf16[2048,768]{1,0:T(8,128)(2,1)S(1)}, u32[]{:S(2)}, u32[]{:S(2)}) collective-permute-start(bf16[2048,768]{1,0:T(8,128)(2,1)} %get-tuple-element.111.ga_ref), channel_id=1, source_target_pairs={{0,1},{1,0},{2,3},{3,2},{4,5},{5,4},{6,7},{7,6},{8,9},{9,8},{10,11... | collective-permute-start | bytes 9437192 | tf_op jit(solution)/shard_map/ppermute | solution.py:1012
  225.8 46.2 %collective-permute-start.10 = (bf16[1024,768]{1,0:T(8,128)(2,1)}, bf16[1024,768]{1,0:T(8,128)(2,1)S(1)}, u32[]{:S(2)}, u32[]{:S(2)}) collective-permute-start(bf16[1024,768]{1,0:T(8,128)(2,1)} %get-tuple-element.123), channel_id=1, source_target_pairs={{0,1},{1,0},{2,3},{3,2},{4,5},{5,4},{6,7},{7,6},{8,9},{9,8},{10,11... | collective-permute-start | bytes 4718600 | tf_op jit(solution)/shard_map/ppermute | solution.py:1012
  281.4 53.0 %all-to-all-start = ((bf16[8,96,1152]{2,1,0:T(8,128)(2,1)}), bf16[8,96,1152]{2,1,0:T(8,128)(2,1)S(1)}, u32[]{:S(2)}, u32[]{:S(2)}) async-start(bf16[8,96,1152]{2,1,0:T(8,128)(2,1)} %bitcast.70), calls=%async_computation.1 | async-start | bytes 3538944 | tf_op jit(solution)/shard_map/all_to_all | solution.py:975
  286.5 25.5 %collective-permute-start.11 = (bf16[512,768]{1,0:T(8,128)(2,1)}, bf16[512,768]{1,0:T(8,128)(2,1)S(1)}, u32[]{:S(2)}, u32[]{:S(2)}) collective-permute-start(bf16[512,768]{1,0:T(8,128)(2,1)} %get-tuple-element.176), channel_id=1, source_target_pairs={{0,2},{1,3},{2,0},{3,1},{4,6},{5,7},{6,4},{7,5},{8,10},{9,11},{10,... | collective-permute-start | bytes 2359304 | tf_op jit(solution)/shard_map/ppermute | solution.py:1015
  326.6 13.5 %collective-permute-start.13 = (bf16[1024,768]{1,0:T(8,128)(2,1)}, bf16[1024,768]{1,0:T(8,128)(2,1)}, u32[]{:S(2)}, u32[]{:S(2)}) collective-permute-start(bf16[1024,768]{1,0:T(8,128)(2,1)} %get-tuple-element.152), channel_id=1, source_target_pairs={{0,1},{1,0},{2,3},{3,2},{4,5},{5,4},{6,7},{7,6},{8,9},{9,8},{10,11... | collective-permute-start | bytes 4718600 | tf_op jit(solution)/shard_map/ppermute | solution.py:1012
  328.7 18.2 %collective-permute-start.12 = (bf16[96,3072]{1,0:T(8,128)(2,1)}, bf16[96,3072]{1,0:T(8,128)(2,1)}, u32[]{:S(2)}, u32[]{:S(2)}) collective-permute-start(bf16[96,3072]{1,0:T(8,128)(2,1)} %reduce-scatter.2.cloned.1.call-done), channel_id=1, source_target_pairs={{0,2},{1,3},{2,0},{3,1},{4,6},{5,7},{6,4},{7,5},{8,10},{9,11},{10,... | collective-permute-start | bytes 1769480 | tf_op jit(solution)/shard_map/ppermute | solution.py:1015
  334.4 22.2 %all-to-all-start.1 = ((bf16[8,112,384]{2,1,0:T(8,128)(2,1)}), bf16[8,112,384]{2,1,0:T(8,128)(2,1)S(1)}, u32[]{:S(2)}, u32[]{:S(2)}) async-start(bf16[8,112,384]{2,1,0:T(8,128)(2,1)} %fusion.4), calls=%async_computation.2 | async-start | bytes 1376256 | tf_op jit(solution)/shard_map/all_to_all | solution.py:975
  338.6 19.4 %collective-permute-start.15 = (bf16[96,1152]{1,0:T(8,128)(2,1)S(1)}, bf16[96,1152]{1,0:T(8,128)(2,1)S(1)}, u32[]{:S(2)}, u32[]{:S(2)}) collective-permute-start(bf16[96,1152]{1,0:T(8,128)(2,1)S(1)} %reduce_sum.75), channel_id=1, source_target_pairs={{0,2},{1,3},{2,0},{3,1},{4,6},{5,7},{6,4},{7,5},{8,10},{9,11},{10,... | collective-permute-start | bytes 663560 | tf_op jit(solution)/shard_map/ppermute | solution.py:1015
  346.9 19.5 %collective-permute-start.14 = (bf16[512,768]{1,0:T(8,128)(2,1)}, bf16[512,768]{1,0:T(8,128)(2,1)}, u32[]{:S(2)}, u32[]{:S(2)}) collective-permute-start(bf16[512,768]{1,0:T(8,128)(2,1)} %get-tuple-element.157), channel_id=1, source_target_pairs={{0,2},{1,3},{2,0},{3,1},{4,6},{5,7},{6,4},{7,5},{8,10},{9,11},{10,... | collective-permute-start | bytes 2359304 | tf_op jit(solution)/shard_map/ppermute | solution.py:1015
  358.0 14.1 %collective-permute-start.16 = (bf16[96,1152]{1,0:T(8,128)(2,1)S(1)}, bf16[96,1152]{1,0:T(8,128)(2,1)S(1)}, u32[]{:S(2)}, u32[]{:S(2)}) collective-permute-start(bf16[96,1152]{1,0:T(8,128)(2,1)S(1)} %add_convert_fusion.2.em_ref), channel_id=1, source_target_pairs={{0,1},{1,0},{2,3},{3,2},{4,5},{5,4},{6,7},{7,6},{8,9},{9,8},{10,11... | collective-permute-start | bytes 663560 | tf_op jit(solution)/shard_map/ppermute | solution.py:1012
  366.4 5.3 %collective-permute-start.19 = (bf16[112,384]{1,0:T(8,128)(2,1)S(1)}, bf16[112,384]{1,0:T(8,128)(2,1)S(1)}, u32[]{:S(2)}, u32[]{:S(2)}) collective-permute-start(bf16[112,384]{1,0:T(8,128)(2,1)S(1)} %reduce_sum.74.la_ref), channel_id=1, source_target_pairs={{0,3},{1,2},{2,1},{3,0},{4,7},{5,6},{6,5},{7,4},{8,11},{9,10},{10,... | collective-permute-start | bytes 258056 | tf_op jit(solution)/shard_map/ppermute | solution.py:1162
  366.4 5.3 %collective-permute-start.18 = (bf16[112,384]{1,0:T(8,128)(2,1)S(1)}, bf16[112,384]{1,0:T(8,128)(2,1)S(1)}, u32[]{:S(2)}, u32[]{:S(2)}) collective-permute-start(bf16[112,384]{1,0:T(8,128)(2,1)S(1)} %reduce_sum.74.la_ref), channel_id=1, source_target_pairs={{0,1},{1,0},{2,3},{3,2},{4,5},{5,4},{6,7},{7,6},{8,9},{9,8},{10,11... | collective-permute-start | bytes 258056 | tf_op jit(solution)/shard_map/ppermute | solution.py:1162
  367.1 5.1 %collective-permute-start.17 = (bf16[112,384]{1,0:T(8,128)(2,1)S(1)}, bf16[112,384]{1,0:T(8,128)(2,1)S(1)}, u32[]{:S(2)}, u32[]{:S(2)}) collective-permute-start(bf16[112,384]{1,0:T(8,128)(2,1)S(1)} %reduce_sum.74.la_ref), channel_id=1, source_target_pairs={{0,2},{1,3},{2,0},{3,1},{4,6},{5,7},{6,4},{7,5},{8,10},{9,11},{10,... | collective-permute-start | bytes 258056 | tf_op jit(solution)/shard_map/ppermute | solution.py:1162
  (20 other events, 136.5 us)
Sparse Core Ops, SparseCore 0:
  11.5 43.8 all-gather.5
  58.1 85.8 all-gather.3
  203.2 98.5 reduce-scatter.1

commit v11 on v10

--- a/solution.py
+++ b/solution.py
@@ -745,41 +745,30 @@
     )(tokens, normed, *before, *grads, weight)
 
 
-def input_back_kernel(tok_ref, own_ref, sib_ref, gm_ref, vec_ref, keep_ref, send_ref):
+def input_back_kernel(tok_ref, own_ref, sib_ref, gm_ref, vec_ref, *out_refs):
     unit, inverse = normalised(tok_ref[...].astype(F32))
     grad = own_ref[...] + sib_ref[...].astype(F32)
     total = gm_ref[...] + norm_pull(grad, vec_ref[0:1, :], unit, inverse)
     step = pl.program_id(0)
-    steps = pl.num_programs(0)
-
-    @pl.when(step < steps // 2)
-    def _():
-        keep_ref[...] = total
-
-    @pl.when(step >= steps // 2)
-    def _():
-        send_ref[...] = total.astype(BF)
-
-
-def input_back(tokens, grad_own, grad_sib, grad_middle, vec):
+    for at, ref in enumerate(out_refs):
+
+        @pl.when(step == at)
+        def _():
+            ref[...] = total.astype(ref.dtype)
+
+
+def input_back(tokens, grad_own, grad_sib, grad_middle, vec, part, dtype):
     rows, width = grad_own.shape
-    bt = 256
-    blocks = rows // bt
-    straight = lambda i: (i, 0)
+    bt = rows // 4
+    here = lambda i: (2 * part + i, 0)
     return pl.pallas_call(
         input_back_kernel,
-        grid=(blocks,),
-        in_specs=[pl.BlockSpec((bt, width), straight)] * 4 + [whole(vec.shape)],
-        out_specs=[
-            pl.BlockSpec((bt, width), lambda i: (jnp.minimum(i, blocks // 2 - 1), 0)),
-            pl.BlockSpec((bt, width), lambda i: (jnp.maximum(i - blocks // 2, 0), 0)),
-        ],
-        out_shape=[
-            jax.ShapeDtypeStruct((rows // 2, width), F32),
-            jax.ShapeDtypeStruct((rows // 2, width), BF),
-        ],
+        grid=(2,),
+        in_specs=[pl.BlockSpec((bt, width), here)] * 4 + [whole(vec.shape)],
+        out_specs=[whole((bt, width))] * 2,
+        out_shape=[jax.ShapeDtypeStruct((bt, width), dtype)] * 2,
         compiler_params=params(60, "arbitrary"),
-        cost_estimate=cost(20 * rows * width, 16 * rows * width),
+        cost_estimate=cost(10 * rows * width, 8 * rows * width),
         name="input_back",
     )(tokens, grad_own, grad_sib, grad_middle, vec)
 
@@ -1142,11 +1131,13 @@
     gn1_sib = sibling(gn1_send)
     block_two, came_one = lax.optimization_barrier((block_two, came_one))
     came_two = exchange(block_two)
-    input_own, input_send = input_back(tok, gn1_own, gn1_sib, grad_middle, vec_one)
-    input_came = partner(input_send)
+    pull = functools.partial(input_back, tok, gn1_own, gn1_sib, grad_middle, vec_one)
+    input_send = pull(1, BF)
+    came_a, came_b = partner(input_send[0]), partner(input_send[1])
     early_total = total(came_one)
     early_came = partner(early_total)
-    one_came, input_own = lax.optimization_barrier((one_came, input_own))
+    one_came, input_send, gn1_own = lax.optimization_barrier((one_came, input_send, gn1_own))
+    input_own = input_back(tok, gn1_own, gn1_sib, grad_middle, vec_one, 0, F32)
     one_sum = join(scattered_one, one_came)
     came_two, one_sum = lax.optimization_barrier((came_two, one_sum))
     one_other = sibling(one_sum)
@@ -1154,15 +1145,20 @@
 
     early_sum = join(early_total, early_came)
     early_other = sibling(early_sum)
-    late_total, input_came, output = lax.optimization_barrier(
-        (total(came_two), input_came, output)
-    )
-    input_grad = hand_back(input_own, input_came)
+    late_total, came_a, input_own, output = lax.optimization_barrier(
+        (total(came_two), came_a, input_own, output)
+    )
     late_came = [
         lax.ppermute(late_total, "seq", [(at, at ^ flip) for at in range(seq)])
         for flip in (2, 1, 3)
     ]
-    late_came, grad_fc1, grad_fc2 = lax.optimization_barrier((late_came, grad_fc1, grad_fc2))
+    kept = jnp.stack(input_own)
+    late_came, grad_fc1, grad_fc2, came_b, kept = lax.optimization_barrier(
+        (late_came, grad_fc1, grad_fc2, came_b, kept)
+    )
+    came = jnp.stack([came_a, came_b]).astype(F32)
+    input_grad = jnp.where(image == 0, jnp.stack([kept, came]), jnp.stack([came, kept]))
+    input_grad = input_grad.reshape(images, slots, width)
     grad_qkv, grad_proj, small_sum = finish_attend(
         place_row, early_sum, early_other, late_total, *late_came, width
     )

time: 392 us -> 395 us (level)
  waiting for transfers between devices: 82.5 us -> 76.9 us
  other arithmetic: 22.4 us -> 26.7 us
    ppermute x7 -> x8, waiting for transfers between devices: 50.7 us -> 46.3 us  [partner(): return lax.ppermute(value, 'seq', to_partner)]
    ppermute x7 -> x8, starting transfers between devices: 9.35 us -> 10.7 us  [partner(): return lax.ppermute(value, 'seq', to_partner)]
    pallas_call x1 -> x2, Pallas kernels: 6.75 us -> 7.96 us  [input_back(): pl.pallas_call(input_back_kernel, grid=(2,), in_specs=[pl.BlockSpec((bt,...]
  transfers between devices with their start and end apart: 26 -> 27, of which waited for: 11 -> 9; matrix products, arithmetic and copies ran while one was open for 8% -> 9% of each run, Pallas kernels for 43% -> 43%
where the time goes in v11:
time: 395 us; the launch traced here: 389 us
  Pallas kernels  226 us (57%)
  waiting for transfers between devices  76.9 us (19%)
  other arithmetic  26.7 us (7%)
  starting transfers between devices  24.2 us (6%)
  local copies, waits for them, and re-layouts  20.2 us (5%)
  between operations  14.4 us (4%)
    pallas_call x2, Pallas kernels, attend_backward(): pl.pallas_call(kernel, grid=(count, keys // bq), in_specs=[pl.BlockSpec(m...  69.6 us
    pallas_call x1, Pallas kernels, feed_forward(): pl.pallas_call(kernel, grid=(blocks,), in_specs=[pl.BlockSpec(memory_spac...  54.4 us
    ppermute x8, waiting for transfers between devices, partner(): return lax.ppermute(value, 'seq', to_partner)  46.3 us
    pallas_call x1, Pallas kernels, attend_forward(): pl.pallas_call(kernel, grid=(pairs, keys // bq), in_specs=[pl.BlockSpec(m...  38.9 us
    pallas_call x1, Pallas kernels, branch(): pl.pallas_call(branch_kernel, grid=(blocks,), in_specs=[pl.BlockSpec(memo...  15.6 us
    pallas_call x1, Pallas kernels, project_back(): pl.pallas_call(project_back_kernel, grid=(blocks,), in_specs=[pl.BlockSpe...  14.7 us
    ppermute x8, starting transfers between devices, partner(): return lax.ppermute(value, 'seq', to_partner)  10.7 us
    all_gather x1, waiting for transfers between devices, per_device(): second = lax.all_gather(two, 'fsdp', axis=0, tiled=True)  10.2 us
  transfers between devices with their start and end apart: 27, of which 9 were waited for; matrix products, arithmetic and copies ran while one was open for 9% of the time, Pallas kernels for 43%

profile of v11, /device:TPU:0, one launch (start us, length us, event | category | flops | bytes accessed | tf_op | source)
XLA Modules:
  0.0 388.6 jit_solution(999554617715022126)
XLA Ops:
  12.4 2.9 collective-permute-start
  16.1 17.7 %collective-permute-done = bf16[512,768]{1,0:T(8,128)(2,1)} collective-permute-done((bf16[512,768]{1,0:T(8,128)(2,1)S(1)}, bf16[512,768]{1,0:T(8,128)(2,1)}, u32[]{:S(2)}, u32[]{:S(2)}) %collective-permute-start) | collective-permute-done | bytes 786464 | tf_op jit(solution)/shard_map/ppermute | solution.py:1004
  33.8 16.0 %collective-permute-done.1 = bf16[512,768]{1,0:T(8,128)(2,1)} collective-permute-done((bf16[512,768]{1,0:T(8,128)(2,1)S(1)}, bf16[512,768]{1,0:T(8,128)(2,1)}, u32[]{:S(2)}, u32[]{:S(2)}) %collective-permute-start.1) | collective-permute-done | bytes 786464 | tf_op jit(solution)/shard_map/ppermute | solution.py:1004
  49.9 5.5 %all-gather.6.cloned.1.call-done = bf16[512,1152]{1,0:T(8,128)(2,1)} async-done(((bf16[64,1152]{1,0:T(8,128)(2,1)}), bf16[512,1152]{1,0:T(8,128)(2,1)}) %all-gather.6.cloned.1.call-update) | async-done | bytes 1179664 | tf_op jit(solution)/shard_map/all_gather | solution.py:1019
  62.8 3.4 pad_maximum_fusion.tok_ref
  66.1 3.2 pad_maximum_fusion.1.cot_ref
  69.3 12.5 %collective-permute-done.4 = bf16[8,48,1152]{2,1,0:T(8,128)(2,1)} collective-permute-done((bf16[8,48,1152]{2,1,0:T(8,128)(2,1)}, bf16[8,48,1152]{2,1,0:T(8,128)(2,1)}, u32[]{:S(2)}, u32[]{:S(2)}) %collective-permute-start.4) | collective-permute-done | bytes 884768 | tf_op jit(solution)/shard_map/ppermute | solution.py:1004
  81.8 3.0 maximum_select_fusion.1
  84.8 10.0 %project.1 = (bf16[2048,1152]{1,0:T(8,128)(2,1)}, bf16[1152,2048]{1,0:T(8,128)(2,1)}, bf16[2048,768]{1,0:T(8,128)(2,1)}) custom-call(bf16[2048,768]{1,0:T(8,128)(2,1)} %pad_maximum_fusion.tok_ref, bf16[768,1152]{1,0:T(8,128)(2,1)} %bitcast.76, f32[1,1152]{1,0:T(1,128)} %reshape.174.bias_ref, f32[8,768]{1,0:T(8,128)} %maximum_maximum_fusion.vec_ref), custom_call_target="tpu_custom_call" | custom-call | flops 3623878656 | bytes 18874368 | tf_op jit(solution)/shard_map/project/pallas_call | solution.py:938
  94.8 38.9 %attend_forward.1 = (bf16[2048,384]{1,0:T(8,128)(2,1)}, f32[384,2048]{1,0:T(8,128)}, f32[3,8,2048]{2,1,0:T(8,128)}) custom-call(s32[2,4]{1,0:T(2,128)} %counts_ref.5, s32[1]{0:T(128)} %bitcast.place_ref, bf16[2048,1152]{1,0:T(8,128)(2,1)} %get-tuple-element.111.k_ref.q_ref.v_ref, bf16[1152,2048]{1,0:T(8,128)(2,1)} %get-tuple-element.112.qt_ref.vt_ref.kt_ref, ...), custom_call_target="tpu_custom_call" | custom-call | flops 25769803776 | bytes 9437184 | tf_op jit(solution)/shard_map/attend_forward/pallas_call | solution.py:171
  133.7 10.2 %all-gather.4.cloned.1.call-done.g2_ref = bf16[768,3456]{1,0:T(8,128)(2,1)} async-done(((bf16[96,3456]{1,0:T(8,128)(2,1)}), bf16[768,3456]{1,0:T(8,128)(2,1)}) %all-gather.4.cloned.1.call-update) | async-done | bytes 5308432 | tf_op jit(solution)/shard_map/all_gather | solution.py:1031
  148.1 54.4 %feed_forward.1 = (f32[2048,768]{1,0:T(8,128)}, f32[1024,768]{1,0:T(8,128)}, bf16[1024,768]{1,0:T(8,128)(2,1)}, bf16[2048,768]{1,0:T(8,128)(2,1)}, bf16[768,3072...) custom-call(s32[1]{0:T(128)} %bitcast.18.core_ref, ...), custom_call_target="tpu_custom_call" | custom-call | flops 31406948352 | bytes 40894464 | tf_op jit(solution)/shard_map/feed_forward/pallas_call | solution.py:452
  204.2 4.4 %collective-permute-done.9.gb_ref = bf16[2048,768]{1,0:T(8,128)(2,1)S(1)} collective-permute-done((bf16[2048,768]{1,0:T(8,128)(2,1)}, bf16[2048,768]{1,0:T(8,128)(2,1)S(1)}, u32[]{:S(2)}, u32[]{:S(2)}) %collective-permute-start.9) | collective-permute-done | bytes 3145760 | tf_op jit(solution)/shard_map/ppermute | solution.py:1001
  210.2 15.6 %branch.1 = (f32[1024,768]{1,0:T(8,128)}, bf16[2048,384]{1,0:T(8,128)(2,1)}, bf16[384,2048]{1,0:T(8,128)(2,1)}, bf16[384,384]{1,0:T(8,128)(2,1)}, bf16[384,384]{1,0:T(8,128)(2,1)}, /*index=5*/f32[24,768]{1,0:T(8,128)}) custom-call(s32[1]{0:T(128)} %bitcast.18.core_ref, f32[2048,768]{1,0:T(8,128)} %get-tuple-element.116.mid_ref, ...), custom_call_target="tpu_custom_call" | custom-call | flops 3623878656 | bytes 28311552 | tf_op jit(solution)/shard_map/branch/pallas_call | solution.py:553
  226.3 45.5 %attend_backward.2 = (bf16[2048,256]{1,0:T(8,128)(2,1)}, bf16[2048,256]{1,0:T(8,128)(2,1)}, bf16[2048,256]{1,0:T(8,128)(2,1)}) custom-call(s32[2,4]{1,0:T(2,128)} %counts_ref.5, s32[1]{0:T(128)} %bitcast.place_ref, bf16[2048,1152]{1,0:T(8,128)(2,1)} %get-tuple-element.111.k_ref.q_ref.v_ref, bf16[2048,1152]{1,0:T(8,128)(2,1)} %get-tuple-element.111.k_ref.q_ref.v_ref, ...), custom_call_target="tpu_custom_call" | custom-call | flops 42949672960 | bytes 12582912 | tf_op jit(solution)/shard_map/attend_backward/pallas_call | solution.py:283
  272.0 7.2 %weight_grad.1 = (bf16[768,1152]{1,0:T(8,128)(2,1)}, f32[16,256]{1,0:T(8,128)}) custom-call(s32[1]{0:T(128)} %bitcast.18.core_ref, bf16[2048,768]{1,0:T(8,128)(2,1)} %get-tuple-element.108.normed_ref, bf16[2048,256]{1,0:T(8,128)(2,1)} %get-tuple-element.130.gq_ref.gqa_ref, bf16[2048,256]{1,0:T(8,128)(2,1)} %get-tuple-element.131.gk_ref.gka_ref, ...), custom_call_target="tpu_custom_call" | custom-call | flops 2415919104 | bytes 6291456 | tf_op jit(solution)/shard_map/weight_grad/pallas_call | solution.py:634
  281.4 4.0 %all-to-all-start = ((bf16[8,96,1152]{2,1,0:T(8,128)(2,1)}), bf16[8,96,1152]{2,1,0:T(8,128)(2,1)S(1)}, u32[]{:S(2)}, u32[]{:S(2)}) async-start(bf16[8,96,1152]{2,1,0:T(8,128)(2,1)} %bitcast.75), calls=%async_computation.1 | async-start | bytes 3538944 | tf_op jit(solution)/shard_map/all_to_all | solution.py:964
  288.2 24.1 %attend_backward.3 = (bf16[2048,128]{1,0:T(8,128)(2,1)}, bf16[2048,128]{1,0:T(8,128)(2,1)}, bf16[2048,128]{1,0:T(8,128)(2,1)}) custom-call(s32[2,4]{1,0:T(2,128)} %counts_ref.5, s32[1]{0:T(128)} %bitcast.place_ref, bf16[2048,1152]{1,0:T(8,128)(2,1)} %get-tuple-element.111.k_ref.q_ref.v_ref, bf16[2048,1152]{1,0:T(8,128)(2,1)} %get-tuple-element.111.k_ref.q_ref.v_ref, ...), custom_call_target="tpu_custom_call" | custom-call | flops 21474836480 | bytes 6291456 | tf_op jit(solution)/shard_map/attend_backward/pallas_call | solution.py:283
  312.3 14.7 %project_back.1 = (f32[1024,768]{1,0:T(8,128)}, bf16[1024,768]{1,0:T(8,128)(2,1)}, bf16[768,384]{1,0:T(8,128)(2,1)}, f32[16,768]{1,0:T(8,128)}, f32[16,128]{1,0:T(8,128)}) custom-call(bf16[2048,768]{1,0:T(8,128)(2,1)} %pad_maximum_fusion.tok_ref, bf16[2048,768]{1,0:T(8,128)(2,1)} %get-tuple-element.108.normed_ref, ...), custom_call_target="tpu_custom_call" | custom-call | flops 4831838208 | bytes 22020096 | tf_op jit(solution)/shard_map/project_back/pallas_call | solution.py:715
  334.2 4.4 %all-to-all-start.1 = ((bf16[8,112,384]{2,1,0:T(8,128)(2,1)}), bf16[8,112,384]{2,1,0:T(8,128)(2,1)}, u32[]{:S(2)}, u32[]{:S(2)}) async-start(bf16[8,112,384]{2,1,0:T(8,128)(2,1)} %fusion.4), calls=%async_computation.2 | async-start | bytes 1376256 | tf_op jit(solution)/shard_map/all_to_all | solution.py:964
  342.2 3.8 input_back.2
  349.5 7.7 %all-to-all-done.1 = bf16[8,112,384]{2,1,0:T(8,128)(2,1)} async-done(((bf16[8,112,384]{2,1,0:T(8,128)(2,1)}), bf16[8,112,384]{2,1,0:T(8,128)(2,1)}, u32[]{:S(2)}, u32[]{:S(2)}) %all-to-all-start.1) | async-done | bytes 688160 | tf_op jit(solution)/shard_map/all_to_all | solution.py:964
  361.4 4.2 %input_back.3 = (f32[256,768]{1,0:T(8,128)}, f32[256,768]{1,0:T(8,128)}) custom-call(bf16[2048,768]{1,0:T(8,128)(2,1)} %pad_maximum_fusion.tok_ref, f32[1024,768]{1,0:T(8,128)} %get-tuple-element.164.own_ref, bf16[1024,768]{1,0:T(8,128)(2,1)} %copy-done, f32[1024,768]{1,0:T(8,128)} %get-tuple-element.159.gm_ref, f32[8,768]{1,0:T(8,128)} %maximum_maximum_fusion.vec_ref), custom_call_target="tpu_custom_call" | custom-call | flops 7864320 | bytes 6291456 | tf_op jit(solution)/shard_map/input_back/pallas_call | solution.py:764
  369.2 3.0 finish_ff.1
  (169 shorter events, 58.1 us)
Async XLA Ops:
  7.2 48.1 %all-gather.6.cloned.1.call-start = ((), (), s32[]{:S(2)}) async-start(), calls=%async_computation.5 | async-start | bytes 1327104 | tf_op jit(solution)/shard_map/all_gather | solution.py:1019
  11.3 132.6 %all-gather.4.cloned.1.call-start = ((), (), s32[]{:S(2)}) async-start(), calls=%async_computation.3 | async-start | bytes 5971968 | tf_op jit(solution)/shard_map/all_gather | solution.py:1031
  12.4 21.4 %collective-permute-start = (bf16[512,768]{1,0:T(8,128)(2,1)S(1)}, bf16[512,768]{1,0:T(8,128)(2,1)}, u32[]{:S(2)}, u32[]{:S(2)}) collective-permute-start(bf16[512,768]{1,0:T(8,128)(2,1)S(1)} %get-tuple-element.192), channel_id=1, source_target_pairs={{0,2},{1,3},{2,0},{3,1},{4,6},{5,7},{6,4},{7,5},{8,10},{9,11},{10,... | collective-permute-start | bytes 2359304 | tf_op jit(solution)/shard_map/ppermute | solution.py:1004
  15.5 34.4 %collective-permute-start.1 = (bf16[512,768]{1,0:T(8,128)(2,1)S(1)}, bf16[512,768]{1,0:T(8,128)(2,1)}, u32[]{:S(2)}, u32[]{:S(2)}) collective-permute-start(bf16[512,768]{1,0:T(8,128)(2,1)S(1)} %get-tuple-element.190), channel_id=1, source_target_pairs={{0,2},{1,3},{2,0},{3,1},{4,6},{5,7},{6,4},{7,5},{8,10},{9,11},{10,... | collective-permute-start | bytes 2359304 | tf_op jit(solution)/shard_map/ppermute | solution.py:1004
  55.3 257.0 %reduce-scatter.2.cloned.1.call-start = ((), (), s32[]{:S(2)}) async-start(), calls=%async_computation.4 | async-start | bytes 5308416 | tf_op jit(solution)/shard_map/reduce_scatter | solution.py:1062
  55.4 7.4 %collective-permute-start.2 = (bf16[512,768]{1,0:T(8,128)(2,1)}, bf16[512,768]{1,0:T(8,128)(2,1)}, u32[]{:S(2)}, u32[]{:S(2)}) collective-permute-start(bf16[512,768]{1,0:T(8,128)(2,1)} %get-tuple-element.191), channel_id=1, source_target_pairs={{0,1},{1,0},{2,3},{3,2},{4,5},{5,4},{6,7},{7,6},{8,9},{9,8},{10,11... | collective-permute-start | bytes 2359304 | tf_op jit(solution)/shard_map/ppermute | solution.py:1001
  55.5 10.7 %collective-permute-start.5 = (bf16[512,768]{1,0:T(8,128)(2,1)S(1)}, bf16[512,768]{1,0:T(8,128)(2,1)}, u32[]{:S(2)}, u32[]{:S(2)}) collective-permute-start(bf16[512,768]{1,0:T(8,128)(2,1)S(1)} %get-tuple-element.189), channel_id=1, source_target_pairs={{0,1},{1,0},{2,3},{3,2},{4,5},{5,4},{6,7},{7,6},{8,9},{9,8},{10,11... | collective-permute-start | bytes 2359304 | tf_op jit(solution)/shard_map/ppermute | solution.py:1001
  56.0 6.7 %collective-permute-start.3 = (bf16[512,768]{1,0:T(8,128)(2,1)}, bf16[512,768]{1,0:T(8,128)(2,1)}, u32[]{:S(2)}, u32[]{:S(2)}) collective-permute-start(bf16[512,768]{1,0:T(8,128)(2,1)} %collective-permute-done), channel_id=1, source_target_pairs={{0,1},{1,0},{2,3},{3,2},{4,5},{5,4},{6,7},{7,6},{8,9},{9,8},{10,11... | collective-permute-start | bytes 2359304 | tf_op jit(solution)/shard_map/ppermute | solution.py:1001
  56.1 10.0 %collective-permute-start.6 = (bf16[512,768]{1,0:T(8,128)(2,1)}, bf16[512,768]{1,0:T(8,128)(2,1)}, u32[]{:S(2)}, u32[]{:S(2)}) collective-permute-start(bf16[512,768]{1,0:T(8,128)(2,1)} %collective-permute-done.1), channel_id=1, source_target_pairs={{0,1},{1,0},{2,3},{3,2},{4,5},{5,4},{6,7},{7,6},{8,9},{9,8},{10,11... | collective-permute-start | bytes 2359304 | tf_op jit(solution)/shard_map/ppermute | solution.py:1001
  59.8 21.9 %collective-permute-start.4 = (bf16[8,48,1152]{2,1,0:T(8,128)(2,1)}, bf16[8,48,1152]{2,1,0:T(8,128)(2,1)}, u32[]{:S(2)}, u32[]{:S(2)}) collective-permute-start(bf16[8,48,1152]{2,1,0:T(8,128)(2,1)} %get-tuple-element.194), channel_id=1, source_target_pairs={{0,2},{1,3},{2,0},{3,1},{4,6},{5,7},{6,4},{7,5},{8,10},{9,11},{10,... | collective-permute-start | bytes 2654216 | tf_op jit(solution)/shard_map/ppermute | solution.py:1004
  133.7 13.3 %collective-permute-start.7 = (bf16[2048,384]{1,0:T(8,128)(2,1)}, bf16[2048,384]{1,0:T(8,128)(2,1)S(1)}, u32[]{:S(2)}, u32[]{:S(2)}) collective-permute-start(bf16[2048,384]{1,0:T(8,128)(2,1)} %get-tuple-element.113.mo_ref), channel_id=1, source_target_pairs={{0,1},{1,0},{2,3},{3,2},{4,5},{5,4},{6,7},{7,6},{8,9},{9,8},{10,11... | collective-permute-start | bytes 4718600 | tf_op jit(solution)/shard_map/ppermute | solution.py:1001
  202.5 6.0 %collective-permute-start.9 = (bf16[2048,768]{1,0:T(8,128)(2,1)}, bf16[2048,768]{1,0:T(8,128)(2,1)S(1)}, u32[]{:S(2)}, u32[]{:S(2)}) collective-permute-start(bf16[2048,768]{1,0:T(8,128)(2,1)} %get-tuple-element.117.ga_ref), channel_id=1, source_target_pairs={{0,1},{1,0},{2,3},{3,2},{4,5},{5,4},{6,7},{7,6},{8,9},{9,8},{10,11... | collective-permute-start | bytes 9437192 | tf_op jit(solution)/shard_map/ppermute | solution.py:1001
  225.8 46.2 %collective-permute-start.10 = (bf16[1024,768]{1,0:T(8,128)(2,1)}, bf16[1024,768]{1,0:T(8,128)(2,1)S(1)}, u32[]{:S(2)}, u32[]{:S(2)}) collective-permute-start(bf16[1024,768]{1,0:T(8,128)(2,1)} %get-tuple-element.129), channel_id=1, source_target_pairs={{0,1},{1,0},{2,3},{3,2},{4,5},{5,4},{6,7},{7,6},{8,9},{9,8},{10,11... | collective-permute-start | bytes 4718600 | tf_op jit(solution)/shard_map/ppermute | solution.py:1001
  281.4 52.8 %all-to-all-start = ((bf16[8,96,1152]{2,1,0:T(8,128)(2,1)}), bf16[8,96,1152]{2,1,0:T(8,128)(2,1)S(1)}, u32[]{:S(2)}, u32[]{:S(2)}) async-start(bf16[8,96,1152]{2,1,0:T(8,128)(2,1)} %bitcast.75), calls=%async_computation.1 | async-start | bytes 3538944 | tf_op jit(solution)/shard_map/all_to_all | solution.py:964
  286.7 25.6 %collective-permute-start.11 = (bf16[512,768]{1,0:T(8,128)(2,1)}, bf16[512,768]{1,0:T(8,128)(2,1)S(1)}, u32[]{:S(2)}, u32[]{:S(2)}) collective-permute-start(bf16[512,768]{1,0:T(8,128)(2,1)} %get-tuple-element.188), channel_id=1, source_target_pairs={{0,2},{1,3},{2,0},{3,1},{4,6},{5,7},{6,4},{7,5},{8,10},{9,11},{10,... | collective-permute-start | bytes 2359304 | tf_op jit(solution)/shard_map/ppermute | solution.py:1004
  327.0 14.0 %collective-permute-start.13 = (bf16[1024,768]{1,0:T(8,128)(2,1)}, bf16[1024,768]{1,0:T(8,128)(2,1)S(1)}, u32[]{:S(2)}, u32[]{:S(2)}) collective-permute-start(bf16[1024,768]{1,0:T(8,128)(2,1)} %get-tuple-element.158), channel_id=1, source_target_pairs={{0,1},{1,0},{2,3},{3,2},{4,5},{5,4},{6,7},{7,6},{8,9},{9,8},{10,11... | collective-permute-start | bytes 4718600 | tf_op jit(solution)/shard_map/ppermute | solution.py:1001
  329.1 19.0 %collective-permute-start.12 = (bf16[96,3072]{1,0:T(8,128)(2,1)}, bf16[96,3072]{1,0:T(8,128)(2,1)}, u32[]{:S(2)}, u32[]{:S(2)}) collective-permute-start(bf16[96,3072]{1,0:T(8,128)(2,1)} %reduce-scatter.2.cloned.1.call-done), channel_id=1, source_target_pairs={{0,2},{1,3},{2,0},{3,1},{4,6},{5,7},{6,4},{7,5},{8,10},{9,11},{10,... | collective-permute-start | bytes 1769480 | tf_op jit(solution)/shard_map/ppermute | solution.py:1004
  334.2 22.9 %all-to-all-start.1 = ((bf16[8,112,384]{2,1,0:T(8,128)(2,1)}), bf16[8,112,384]{2,1,0:T(8,128)(2,1)}, u32[]{:S(2)}, u32[]{:S(2)}) async-start(bf16[8,112,384]{2,1,0:T(8,128)(2,1)} %fusion.4), calls=%async_computation.2 | async-start | bytes 1376256 | tf_op jit(solution)/shard_map/all_to_all | solution.py:964
  339.6 17.6 %collective-permute-start.20 = (bf16[96,1152]{1,0:T(8,128)(2,1)}, bf16[96,1152]{1,0:T(8,128)(2,1)}, u32[]{:S(2)}, u32[]{:S(2)}) collective-permute-start(bf16[96,1152]{1,0:T(8,128)(2,1)} %reduce_sum.75), channel_id=1, source_target_pairs={{0,2},{1,3},{2,0},{3,1},{4,6},{5,7},{6,4},{7,5},{8,10},{9,11},{10,... | collective-permute-start | bytes 663560 | tf_op jit(solution)/shard_map/ppermute | solution.py:1004
  346.0 19.5 %collective-permute-start.14 = (bf16[256,768]{1,0:T(8,128)(2,1)}, bf16[256,768]{1,0:T(8,128)(2,1)}, u32[]{:S(2)}, u32[]{:S(2)}) collective-permute-start(bf16[256,768]{1,0:T(8,128)(2,1)} %get-tuple-element.160), channel_id=1, source_target_pairs={{0,2},{1,3},{2,0},{3,1},{4,6},{5,7},{6,4},{7,5},{8,10},{9,11},{10,... | collective-permute-start | bytes 1179656 | tf_op jit(solution)/shard_map/ppermute | solution.py:1004
  346.6 25.6 %collective-permute-start.19 = (bf16[256,768]{1,0:T(8,128)(2,1)}, bf16[256,768]{1,0:T(8,128)(2,1)}, u32[]{:S(2)}, u32[]{:S(2)}) collective-permute-start(bf16[256,768]{1,0:T(8,128)(2,1)} %get-tuple-element.161), channel_id=1, source_target_pairs={{0,2},{1,3},{2,0},{3,1},{4,6},{5,7},{6,4},{7,5},{8,10},{9,11},{10,... | collective-permute-start | bytes 1179656 | tf_op jit(solution)/shard_map/ppermute | solution.py:1004
  357.2 10.0 %collective-permute-start.18 = (bf16[96,3072]{1,0:T(8,128)(2,1)S(1)}, bf16[96,3072]{1,0:T(8,128)(2,1)S(1)}, u32[]{:S(2)}, u32[]{:S(2)}) collective-permute-start(bf16[96,3072]{1,0:T(8,128)(2,1)S(1)} %add_convert_fusion.1.mine_ref), channel_id=1, source_target_pairs={{0,1},{1,0},{2,3},{3,2},{4,5},{5,4},{6,7},{7,6},{8,9},{9,8},{10,11... | collective-permute-start | bytes 1769480 | tf_op jit(solution)/shard_map/ppermute | solution.py:1001
  358.2 14.1 %collective-permute-start.21 = (bf16[96,1152]{1,0:T(8,128)(2,1)S(1)}, bf16[96,1152]{1,0:T(8,128)(2,1)S(1)}, u32[]{:S(2)}, u32[]{:S(2)}) collective-permute-start(bf16[96,1152]{1,0:T(8,128)(2,1)S(1)} %add_convert_fusion.2.em_ref), channel_id=1, source_target_pairs={{0,1},{1,0},{2,3},{3,2},{4,5},{5,4},{6,7},{7,6},{8,9},{9,8},{10,11... | collective-permute-start | bytes 663560 | tf_op jit(solution)/shard_map/ppermute | solution.py:1001
  365.5 6.7 %collective-permute-start.17 = (bf16[112,384]{1,0:T(8,128)(2,1)S(1)}, bf16[112,384]{1,0:T(8,128)(2,1)S(1)}, u32[]{:S(2)}, u32[]{:S(2)}) collective-permute-start(bf16[112,384]{1,0:T(8,128)(2,1)S(1)} %reduce_sum.74.la_ref), channel_id=1, source_target_pairs={{0,3},{1,2},{2,1},{3,0},{4,7},{5,6},{6,5},{7,4},{8,11},{9,10},{10,... | collective-permute-start | bytes 258056 | tf_op jit(solution)/shard_map/ppermute | solution.py:1152
  (25 other events, 166.9 us)
Sparse Core Ops, SparseCore 0:
  11.5 43.8 all-gather.5
  58.1 85.8 all-gather.3
  203.2 98.0 reduce-scatter.1
